TPU v7x, 32 devices: a whole 2x2x4 slice. The times are simulated.
32 devices in a mesh: gx: 4 (over z), gy: 2 (over x), gz: 4 (over y, core).
Axes of the slice: x: 2, y: 2, z: 4, core: 2. Of those that a mesh axis runs over, the one named last changes fastest.
Arguments:
- vel_x: float32 [64, 32, 256], P('gx', 'gz', 'gy'), may hold values from -6 to 6
- vel_y: float32 [64, 32, 256], P('gx', 'gz', 'gy'), may hold values from -6 to 6
- vel_z: float32 [64, 32, 256], P('gx', 'gz', 'gy'), may hold values from -6 to 6
- pressure: float32 [64, 32, 256], P('gx', 'gz', 'gy'), may hold values from -6 to 6
- phase: int32 [64, 32, 256], P('gx', 'gz', 'gy'), may hold values from 0 to 3
- visc_scale: float32 [4], replicated, may hold values from 0.5 to 2
- power_n: float32 [4], replicated, may hold values from 1 to 4
- density: float32 [4], replicated, may hold values from 0.5 to 1.5
Outputs:
- out_vx: float32 [64, 32, 256], P('gx', 'gz', 'gy')
- out_vy: float32 [64, 32, 256], P('gx', 'gz', 'gy')
- out_vz: float32 [64, 32, 256], P('gx', 'gz', 'gy')
- out_p: float32 [64, 32, 256], P('gx', 'gz', 'gy')
- out_eta: float32 [64, 32, 256], P('gx', 'gz', 'gy')
All inputs are finite; a program needn't handle non-finite values.
Results may differ from a plain program's by a relative error of at most 0.00013.
Values sent between devices are 32-bit elements; how exact they have to be, the bound alone decides.
No kernel may reach another device: no remote copies, remote signals or barrier semaphores. Data moves between devices by JAX's collectives and lax.ppermute only.
A program may use at most 64 MiB of HBM per device.

v0:
```python
import jax
import jax.numpy as jnp
from jax import lax
from jax.sharding import PartitionSpec as P

ITERS = 4
PHASES = 4


strain_floor = 1.0
pressure_step = 0.5
velocity_step = 0.1


def padded_2(block, sides, width):
    for axis, dim in sides:
        count = lax.axis_size(axis)
        forward = [(i, i + 1) for i in range(count - 1)]
        backward = [(target, source) for source, target in forward]
        low = lax.ppermute(
            lax.slice_in_dim(block, block.shape[dim] - width, None, axis=dim), axis, forward
        )
        high = lax.ppermute(lax.slice_in_dim(block, 0, width, axis=dim), axis, backward)
        block = jnp.concatenate([low, block, high], axis=dim)
    return block


def lookup(phase, table):
    out = jnp.zeros(phase.shape, jnp.float32)
    for index in range(PHASES):
        out = out + jnp.where(phase == index, table[index], jnp.float32(0.0))
    return out


def strain_rate_list(padded):
    strain_rate_first = padded[0, 2:, 1:-1, 1:-1] - padded[0, 1:-1, 1:-1, 1:-1]
    strain_rate_second = padded[1, 1:-1, 2:, 1:-1] - padded[1, 1:-1, 1:-1, 1:-1]
    strain_rate_third = padded[2, 1:-1, 1:-1, 2:] - padded[2, 1:-1, 1:-1, 1:-1]
    return (strain_rate_first, strain_rate_second, strain_rate_third)


def viscosity(strain_rate_first, strain_rate_second, strain_rate_third, prefactor, exponent):
    div = strain_rate_first + strain_rate_second + strain_rate_third
    third = div / 3.0
    inv = (
        0.5
        * (
            (strain_rate_first - third) ** 2
            + (strain_rate_second - third) ** 2
            + (strain_rate_third - third) ** 2
        )
        + strain_floor
    )
    eta = prefactor * jnp.exp(0.5 * (1.0 / exponent - 1.0) * jnp.log(inv))
    return (eta, div)


def slice_along(field, offset, grid_extent):
    return field[
        1 + offset[0] : 1 + offset[0] + grid_extent[0],
        1 + offset[1] : 1 + offset[1] + grid_extent[1],
        1 + offset[2] : 1 + offset[2] + grid_extent[2],
    ]


def unit(sweep_heading, sign):
    offset = [0, 0, 0]
    offset[sweep_heading] = sign
    return tuple(offset)


def joined(first, second):
    return tuple((first[n] + second[n] for n in range(3)))


def residual_field(sweep_heading, padded_velocity, padded_pressure, padded_viscosity, grid_extent):
    zero_scalar = (0, 0, 0)
    backward_neighbor = unit(sweep_heading, -1)
    middle_slice = slice_along(padded_velocity, zero_scalar, grid_extent)
    viscosity_current = slice_along(padded_viscosity, zero_scalar, grid_extent)
    viscosity_backward = slice_along(padded_viscosity, backward_neighbor, grid_extent)
    momentum_residual = -(
        slice_along(padded_pressure, zero_scalar, grid_extent)
        - slice_along(padded_pressure, backward_neighbor, grid_extent)
    )
    for other in range(3):
        upper_neighbor = unit(other, 1)
        lower_neighbor = unit(other, -1)
        if other == sweep_heading:
            momentum_residual = (
                momentum_residual
                + viscosity_current
                * (slice_along(padded_velocity, upper_neighbor, grid_extent) - middle_slice)
                - viscosity_backward
                * (middle_slice - slice_along(padded_velocity, backward_neighbor, grid_extent))
            )
        else:
            viscosity_above = 0.25 * (
                viscosity_current
                + viscosity_backward
                + slice_along(padded_viscosity, upper_neighbor, grid_extent)
                + slice_along(
                    padded_viscosity, joined(backward_neighbor, upper_neighbor), grid_extent
                )
            )
            viscosity_below = 0.25 * (
                viscosity_current
                + viscosity_backward
                + slice_along(padded_viscosity, lower_neighbor, grid_extent)
                + slice_along(
                    padded_viscosity, joined(backward_neighbor, lower_neighbor), grid_extent
                )
            )
            momentum_residual = (
                momentum_residual
                + viscosity_above
                * (slice_along(padded_velocity, upper_neighbor, grid_extent) - middle_slice)
                - viscosity_below
                * (middle_slice - slice_along(padded_velocity, lower_neighbor, grid_extent))
            )
    return (momentum_residual, 0.5 * (viscosity_current + viscosity_backward))


def pressure_sum(values):
    return lax.psum(jnp.sum(values), ("gx", "gy", "gz"))


def local(vel_x, vel_y, vel_z, pressure, phase, visc_scale, power_n, density):
    grid_extent = pressure.shape
    counts = (lax.axis_size("gx"), lax.axis_size("gz"), lax.axis_size("gy"))
    starts = (
        lax.axis_index("gx") * grid_extent[0],
        lax.axis_index("gz") * grid_extent[1],
        lax.axis_index("gy") * grid_extent[2],
    )

    def coord(sweep_heading, extra):
        length = grid_extent[sweep_heading] + 2 * extra
        index = starts[sweep_heading] - extra + lax.iota(jnp.int32, length)
        dims = [1, 1, 1]
        dims[sweep_heading] = length
        return index.reshape(dims)

    velocity = [
        jnp.where(coord(axis_number, 0) == 0, jnp.float32(0.0), v)
        for axis_number, v in enumerate((vel_x, vel_z, vel_y))
    ]
    rho = lookup(phase, density)
    total_cells = float(
        grid_extent[0] * grid_extent[1] * grid_extent[2] * counts[0] * counts[1] * counts[2]
    )
    inside = jnp.ones((1, 1, 1), jnp.bool_)
    for axis_number in range(3):
        place = coord(axis_number, 1)
        inside = inside & (place >= 0) & (place < grid_extent[axis_number] * counts[axis_number])
    prefactor = lookup(phase, visc_scale)
    exponent = lookup(phase, power_n)
    eta = prefactor
    for step in range(ITERS):
        stacked_rates = jnp.stack(velocity)
        padded_velocity = padded_2(stacked_rates, (("gx", 1), ("gy", 3), ("gz", 2)), 1)
        strain_rate_first, strain_rate_second, strain_rate_third = strain_rate_list(padded_velocity)
        eta, div = viscosity(
            strain_rate_first, strain_rate_second, strain_rate_third, prefactor, exponent
        )
        pressure = pressure - pressure_step * eta * div
        pressure = pressure - pressure_sum(pressure) / total_cells
        both = padded_2(jnp.stack([pressure, eta]), (("gx", 1), ("gy", 3), ("gz", 2)), 1)
        padded_pressure = both[0]
        padded_viscosity = both[1]
        updated = []
        for axis_number in range(3):
            momentum_residual, face_slice = residual_field(
                axis_number,
                padded_velocity[axis_number],
                padded_pressure,
                padded_viscosity,
                grid_extent,
            )
            if axis_number == 1:
                momentum_residual = momentum_residual - rho
            fresh = velocity[axis_number] + velocity_step * momentum_residual / face_slice
            updated.append(jnp.where(coord(axis_number, 0) == 0, jnp.float32(0.0), fresh))
        velocity = updated
    return (velocity[0], velocity[2], velocity[1], pressure, eta)


def solution(mesh):
    return jax.shard_map(
        local,
        mesh=mesh,
        in_specs=(
            P("gx", "gz", "gy"),
            P("gx", "gz", "gy"),
            P("gx", "gz", "gy"),
            P("gx", "gz", "gy"),
            P("gx", "gz", "gy"),
            P(),
            P(),
            P(),
        ),
        out_specs=(
            P("gx", "gz", "gy"),
            P("gx", "gz", "gy"),
            P("gx", "gz", "gy"),
            P("gx", "gz", "gy"),
            P("gx", "gz", "gy"),
        ),
        check_vma=False,
    )
```

profile of v0, /device:TPU:0, one launch (start us, length us, event | category | flops | bytes accessed | tf_op | source)
XLA Modules:
  0.0 415.9 jit_solution(4144427377314365745)
XLA Ops:
  3.1 5.6 %collective-permute-start.1 = (f32[3,1,8,128]{3,2,1,0:T(8,128)S(1)}, f32[3,1,8,128]{3,2,1,0:T(8,128)S(1)}, u32[]{:S(2)}, u32[]{:S(2)}) collective-permute-start(f32[3,1,8,128]{3,2,1,0:T(8,128)S(1)} %get-tuple-element.79), channel_id=1, source_target_pairs={{0,8},{8,16},{16,24},{1,9},{9,17},{17,25},{2,10},{10,18},{18,26},{... | collective-permute-start | bytes 36872 | tf_op jit(solution)/shard_map/ppermute | solution.py:20
  11.5 4.6 %collective-permute-start.2 = (f32[3,18,8,1]{3,2,1,0:T(8,128)S(1)}, f32[3,18,8,1]{3,2,1,0:T(8,128)S(1)}, u32[]{:S(2)}, u32[]{:S(2)}) collective-permute-start(f32[3,18,8,1]{3,2,1,0:T(8,128)S(1)} %get-tuple-element.71), channel_id=1, source_target_pairs={{0,4},{1,5},{2,6},{3,7},{8,12},{9,13},{10,14},{11,15},{16,20},{17,... | collective-permute-start | bytes 5192 | tf_op jit(solution)/shard_map/ppermute | solution.py:20
  23.1 5.9 %fusion.286 = (f32[]{:T(128)}, f32[16,8,128]{2,1,0:T(8,128)S(1)}, pred[16,8,128]{2,1,0:T(8,128)(4,1)S(1)}, pred[16,8,128]{2,1,0:T(8,128)(4,1)S(1)}, pred[16,8,12...) fusion(f32[16,8,128]{2,1,0:T(8,128)S(1)} %copy-done.4, ...), kind=kLoop, calls=%fused_computation.583 | loop fusion | flops 999423 | bytes 908268 | tf_op jit(solution)/shard_map/reduce_sum | solution.py:125
  29.1 43.4 %psum.28 = f32[]{:T(128)} all-reduce(f32[]{:T(128)} %get-tuple-element.18), channel_id=1, replica_groups=mesh['gx'=4,'gy'=2,'gz'=4] {'gx','gy','gz'}, use_global_device_ids=true, to_apply=%region_1.2 | all-reduce | flops 1 | bytes 8 | tf_op jit(solution)/shard_map/psum | solution.py:125
  73.2 5.2 %fusion.276 = f32[1,16,8,128]{3,2,1,0:T(8,128)S(1)} fusion(f32[16,8,128]{2,1,0:T(8,128)S(1)} %get-tuple-element.26, f32[16,8,128]{2,1,0:T(8,128)S(1)} %get-tuple-element.25, f32[16,8,128]{2,1,0:T(8,128)S(1)} %get-tuple-element.24, pred[16,8,128]{2,1,0:T(8,128)(4,1)S(1)} %get-tuple-element.23, f32[]{:T(128)} %bitcast.3, ...), kind=kLoop, calls=%fused_computation.577 | loop fusion | flops 524288 | bytes 327712 | tf_op jit(solution)/shard_map/stack | solution.py:168
  87.7 4.6 %collective-permute-start.7 = (f32[2,18,8,1]{3,2,1,0:T(8,128)S(1)}, f32[2,18,8,1]{3,2,1,0:T(8,128)S(1)}, u32[]{:S(2)}, u32[]{:S(2)}) collective-permute-start(f32[2,18,8,1]{3,2,1,0:T(8,128)S(1)} %get-tuple-element.87), channel_id=1, source_target_pairs={{0,4},{1,5},{2,6},{3,7},{8,12},{9,13},{10,14},{11,15},{16,20},{17,... | collective-permute-start | bytes 3464 | tf_op jit(solution)/shard_map/ppermute | solution.py:20
  96.6 4.7 %collective-permute-start.9 = (f32[2,18,1,130]{3,2,1,0:T(1,128)S(1)}, f32[2,18,1,130]{3,2,1,0:T(1,128)S(1)}, u32[]{:S(2)}, u32[]{:S(2)}) collective-permute-start(f32[2,18,1,130]{3,2,1,0:T(1,128)S(1)} %get-tuple-element.63), channel_id=1, source_target_pairs={{0,1},{1,2},{2,3},{4,5},{5,6},{6,7},{8,9},{9,10},{10,11},{12,13},{... | collective-permute-start | bytes 56168 | tf_op jit(solution)/shard_map/ppermute | solution.py:20
  107.3 4.5 %collective-permute-start.13 = (f32[3,1,8,128]{3,2,1,0:T(8,128)S(1)}, f32[3,1,8,128]{3,2,1,0:T(8,128)S(1)}, u32[]{:S(2)}, u32[]{:S(2)}) collective-permute-start(f32[3,1,8,128]{3,2,1,0:T(8,128)S(1)} %get-tuple-element.77), channel_id=1, source_target_pairs={{0,8},{8,16},{16,24},{1,9},{9,17},{17,25},{2,10},{10,18},{18,26},{... | collective-permute-start | bytes 36872 | tf_op jit(solution)/shard_map/ppermute | solution.py:20
  114.7 4.6 %collective-permute-start.14 = (f32[3,18,8,1]{3,2,1,0:T(8,128)S(1)}, f32[3,18,8,1]{3,2,1,0:T(8,128)S(1)}, u32[]{:S(2)}, u32[]{:S(2)}) collective-permute-start(f32[3,18,8,1]{3,2,1,0:T(8,128)S(1)} %get-tuple-element.69), channel_id=1, source_target_pairs={{0,4},{1,5},{2,6},{3,7},{8,12},{9,13},{10,14},{11,15},{16,20},{17,... | collective-permute-start | bytes 5192 | tf_op jit(solution)/shard_map/ppermute | solution.py:20
  128.1 6.0 %fusion.283 = (f32[]{:T(128)}, f32[16,8,128]{2,1,0:T(8,128)S(1)}, f32[16,8,128]{2,1,0:T(8,128)S(1)}, f32[16,8,128]{2,1,0:T(8,128)S(1)}, f32[16,8,128]{2,1,0:T(8,128)S(1)}) fusion(pred[16,8,128]{2,1,0:T(8,128)(4,1)S(1)} %get-tuple-element.23, f32[]{:T(128)} %bitcast.7, pred[16,8,128]{2,1,0:T(8,128)(4,1)S(1)} %get-tuple-element.22, f32[]{:T(128)} %bitcast.6, ...), kind=kLoop, calls=%fused_computation.582 | loop fusion | flops 901119 | bytes 842584 | tf_op jit(solution)/shard_map/reduce_sum | solution.py:125
  134.1 43.7 %psum.29 = f32[]{:T(128)} all-reduce(f32[]{:T(128)} %get-tuple-element.13), channel_id=1, replica_groups=mesh['gx'=4,'gy'=2,'gz'=4] {'gx','gy','gz'}, use_global_device_ids=true, to_apply=%region_3.4 | all-reduce | flops 1 | bytes 8 | tf_op jit(solution)/shard_map/psum | solution.py:125
  178.4 5.2 %fusion.277 = f32[1,16,8,128]{3,2,1,0:T(8,128)S(1)} fusion(f32[16,8,128]{2,1,0:T(8,128)S(1)} %get-tuple-element.17, f32[16,8,128]{2,1,0:T(8,128)S(1)} %get-tuple-element.16, f32[16,8,128]{2,1,0:T(8,128)S(1)} %get-tuple-element.15, pred[16,8,128]{2,1,0:T(8,128)(4,1)S(1)} %get-tuple-element.23, f32[]{:T(128)} %bitcast.3, ...), kind=kLoop, calls=%fused_computation.578 | loop fusion | flops 524288 | bytes 327712 | tf_op jit(solution)/shard_map/stack | solution.py:168
  192.3 4.6 %collective-permute-start.19 = (f32[2,18,8,1]{3,2,1,0:T(8,128)S(1)}, f32[2,18,8,1]{3,2,1,0:T(8,128)S(1)}, u32[]{:S(2)}, u32[]{:S(2)}) collective-permute-start(f32[2,18,8,1]{3,2,1,0:T(8,128)S(1)} %get-tuple-element.85), channel_id=1, source_target_pairs={{0,4},{1,5},{2,6},{3,7},{8,12},{9,13},{10,14},{11,15},{16,20},{17,... | collective-permute-start | bytes 3464 | tf_op jit(solution)/shard_map/ppermute | solution.py:20
  201.1 4.6 %collective-permute-start.21 = (f32[2,18,1,130]{3,2,1,0:T(1,128)S(1)}, f32[2,18,1,130]{3,2,1,0:T(1,128)S(1)}, u32[]{:S(2)}, u32[]{:S(2)}) collective-permute-start(f32[2,18,1,130]{3,2,1,0:T(1,128)S(1)} %get-tuple-element.61), channel_id=1, source_target_pairs={{0,1},{1,2},{2,3},{4,5},{5,6},{6,7},{8,9},{9,10},{10,11},{12,13},{... | collective-permute-start | bytes 56168 | tf_op jit(solution)/shard_map/ppermute | solution.py:20
  219.1 4.6 %collective-permute-start.26 = (f32[3,18,8,1]{3,2,1,0:T(8,128)S(1)}, f32[3,18,8,1]{3,2,1,0:T(8,128)S(1)}, u32[]{:S(2)}, u32[]{:S(2)}) collective-permute-start(f32[3,18,8,1]{3,2,1,0:T(8,128)S(1)} %get-tuple-element.67), channel_id=1, source_target_pairs={{0,4},{1,5},{2,6},{3,7},{8,12},{9,13},{10,14},{11,15},{16,20},{17,... | collective-permute-start | bytes 5192 | tf_op jit(solution)/shard_map/ppermute | solution.py:20
  232.8 6.0 %fusion.280 = (f32[]{:T(128)}, f32[16,8,128]{2,1,0:T(8,128)S(1)}, f32[16,8,128]{2,1,0:T(8,128)S(1)}, f32[16,8,128]{2,1,0:T(8,128)S(1)}, f32[16,8,128]{2,1,0:T(8,128)S(1)}) fusion(pred[16,8,128]{2,1,0:T(8,128)(4,1)S(1)} %get-tuple-element.23, f32[]{:T(128)} %bitcast.7, pred[16,8,128]{2,1,0:T(8,128)(4,1)S(1)} %get-tuple-element.22, f32[]{:T(128)} %bitcast.6, ...), kind=kLoop, calls=%fused_computation.581 | loop fusion | flops 901119 | bytes 842584 | tf_op jit(solution)/shard_map/reduce_sum | solution.py:125
  238.7 44.0 %psum.30 = f32[]{:T(128)} all-reduce(f32[]{:T(128)} %get-tuple-element.8), channel_id=1, replica_groups=mesh['gx'=4,'gy'=2,'gz'=4] {'gx','gy','gz'}, use_global_device_ids=true, to_apply=%region_5.6 | all-reduce | flops 1 | bytes 8 | tf_op jit(solution)/shard_map/psum | solution.py:125
  283.3 5.2 %fusion.278 = f32[1,16,8,128]{3,2,1,0:T(8,128)S(1)} fusion(f32[16,8,128]{2,1,0:T(8,128)S(1)} %get-tuple-element.12, f32[16,8,128]{2,1,0:T(8,128)S(1)} %get-tuple-element.11, f32[16,8,128]{2,1,0:T(8,128)S(1)} %get-tuple-element.10, pred[16,8,128]{2,1,0:T(8,128)(4,1)S(1)} %get-tuple-element.23, f32[]{:T(128)} %bitcast.3, ...), kind=kLoop, calls=%fused_computation.579 | loop fusion | flops 524288 | bytes 327712 | tf_op jit(solution)/shard_map/stack | solution.py:168
  297.1 4.6 %collective-permute-start.31 = (f32[2,18,8,1]{3,2,1,0:T(8,128)S(1)}, f32[2,18,8,1]{3,2,1,0:T(8,128)S(1)}, u32[]{:S(2)}, u32[]{:S(2)}) collective-permute-start(f32[2,18,8,1]{3,2,1,0:T(8,128)S(1)} %get-tuple-element.83), channel_id=1, source_target_pairs={{0,4},{1,5},{2,6},{3,7},{8,12},{9,13},{10,14},{11,15},{16,20},{17,... | collective-permute-start | bytes 3464 | tf_op jit(solution)/shard_map/ppermute | solution.py:20
  306.0 4.6 %collective-permute-start.33 = (f32[2,18,1,130]{3,2,1,0:T(1,128)S(1)}, f32[2,18,1,130]{3,2,1,0:T(1,128)S(1)}, u32[]{:S(2)}, u32[]{:S(2)}) collective-permute-start(f32[2,18,1,130]{3,2,1,0:T(1,128)S(1)} %get-tuple-element.59), channel_id=1, source_target_pairs={{0,1},{1,2},{2,3},{4,5},{5,6},{6,7},{8,9},{9,10},{10,11},{12,13},{... | collective-permute-start | bytes 56168 | tf_op jit(solution)/shard_map/ppermute | solution.py:20
  324.0 4.6 %collective-permute-start.38 = (f32[3,18,8,1]{3,2,1,0:T(8,128)S(1)}, f32[3,18,8,1]{3,2,1,0:T(8,128)S(1)}, u32[]{:S(2)}, u32[]{:S(2)}) collective-permute-start(f32[3,18,8,1]{3,2,1,0:T(8,128)S(1)} %get-tuple-element.65), channel_id=1, source_target_pairs={{0,4},{1,5},{2,6},{3,7},{8,12},{9,13},{10,14},{11,15},{16,20},{17,... | collective-permute-start | bytes 5192 | tf_op jit(solution)/shard_map/ppermute | solution.py:20
  339.0 5.9 %fusion.279 = (f32[]{:T(128)}, f32[16,8,128]{2,1,0:T(8,128)S(1)}, f32[16,8,128]{2,1,0:T(8,128)S(1)}) fusion(f32[16,8,128]{2,1,0:T(8,128)S(1)} %get-tuple-element.58, f32[16,8,128]{2,1,0:T(8,128)S(1)} %get-tuple-element.57, f32[16,8,128]{2,1,0:T(8,128)S(1)} %get-tuple-element.9, f32[]{:T(128)S(6)} %div.78, pred[16,8,128]{2,1,0:T(8,128)(4,1)S(1)} %get-tuple-element.23, ...), kind=kLoop, calls=%fused_computation.580 | loop fusion | flops 671743 | bytes 667688 | tf_op jit(solution)/shard_map/reduce_sum | solution.py:125
  344.9 43.2 %psum.31 = f32[]{:T(128)} all-reduce(f32[]{:T(128)} %get-tuple-element.5), channel_id=1, replica_groups=mesh['gx'=4,'gy'=2,'gz'=4] {'gx','gy','gz'}, use_global_device_ids=true, to_apply=%region_7.8 | all-reduce | flops 1 | bytes 8 | tf_op jit(solution)/shard_map/psum | solution.py:125
  397.4 4.6 %collective-permute-start.43 = (f32[2,18,8,1]{3,2,1,0:T(8,128)S(1)}, f32[2,18,8,1]{3,2,1,0:T(8,128)S(1)}, u32[]{:S(2)}, u32[]{:S(2)}) collective-permute-start(f32[2,18,8,1]{3,2,1,0:T(8,128)S(1)} %get-tuple-element.81), channel_id=1, source_target_pairs={{0,4},{1,5},{2,6},{3,7},{8,12},{9,13},{10,14},{11,15},{16,20},{17,... | collective-permute-start | bytes 3464 | tf_op jit(solution)/shard_map/ppermute | solution.py:20
  (175 shorter events, 137.4 us)
Async XLA Ops:
  3.1 7.0 %collective-permute-start.1 = (f32[3,1,8,128]{3,2,1,0:T(8,128)S(1)}, f32[3,1,8,128]{3,2,1,0:T(8,128)S(1)}, u32[]{:S(2)}, u32[]{:S(2)}) collective-permute-start(f32[3,1,8,128]{3,2,1,0:T(8,128)S(1)} %get-tuple-element.79), channel_id=1, source_target_pairs={{0,8},{8,16},{16,24},{1,9},{9,17},{17,25},{2,10},{10,18},{18,26},{... | collective-permute-start | bytes 36872 | tf_op jit(solution)/shard_map/ppermute | solution.py:20
  10.2 8.2 %collective-permute-start.3 = (f32[3,18,8,1]{3,2,1,0:T(8,128)S(1)}, f32[3,18,8,1]{3,2,1,0:T(8,128)S(1)}, u32[]{:S(2)}, u32[]{:S(2)}) collective-permute-start(f32[3,18,8,1]{3,2,1,0:T(8,128)S(1)} %get-tuple-element.72), channel_id=1, source_target_pairs={{4,0},{5,1},{6,2},{7,3},{12,8},{13,9},{14,10},{15,11},{20,16},{21,... | collective-permute-start | bytes 5192 | tf_op jit(solution)/shard_map/ppermute | solution.py:23
  11.5 8.1 %collective-permute-start.2 = (f32[3,18,8,1]{3,2,1,0:T(8,128)S(1)}, f32[3,18,8,1]{3,2,1,0:T(8,128)S(1)}, u32[]{:S(2)}, u32[]{:S(2)}) collective-permute-start(f32[3,18,8,1]{3,2,1,0:T(8,128)S(1)} %get-tuple-element.71), channel_id=1, source_target_pairs={{0,4},{1,5},{2,6},{3,7},{8,12},{9,13},{10,14},{11,15},{16,20},{17,... | collective-permute-start | bytes 5192 | tf_op jit(solution)/shard_map/ppermute | solution.py:20
  78.5 7.8 %collective-permute-start.6 = (f32[2,1,8,128]{3,2,1,0:T(8,128)S(1)}, f32[2,1,8,128]{3,2,1,0:T(8,128)S(1)}, u32[]{:S(2)}, u32[]{:S(2)}) collective-permute-start(f32[2,1,8,128]{3,2,1,0:T(8,128)S(1)} %get-tuple-element.96), channel_id=1, source_target_pairs={{8,0},{16,8},{24,16},{9,1},{17,9},{25,17},{10,2},{18,10},{26,18},{... | collective-permute-start | bytes 24584 | tf_op jit(solution)/shard_map/ppermute | solution.py:23
  85.0 7.3 %collective-permute-start.11 = (f32[3,18,1,130]{3,2,1,0:T(1,128)S(1)}, f32[3,18,1,130]{3,2,1,0:T(1,128)S(1)}, u32[]{:S(2)}, u32[]{:S(2)}) collective-permute-start(f32[3,18,1,130]{3,2,1,0:T(1,128)S(1)} %get-tuple-element.45), channel_id=1, source_target_pairs={{0,1},{1,2},{2,3},{4,5},{5,6},{6,7},{8,9},{9,10},{10,11},{12,13},{... | collective-permute-start | bytes 84248 | tf_op jit(solution)/shard_map/ppermute | solution.py:20
  86.4 7.0 %collective-permute-start.8 = (f32[2,18,8,1]{3,2,1,0:T(8,128)S(1)}, f32[2,18,8,1]{3,2,1,0:T(8,128)S(1)}, u32[]{:S(2)}, u32[]{:S(2)}) collective-permute-start(f32[2,18,8,1]{3,2,1,0:T(8,128)S(1)} %get-tuple-element.88), channel_id=1, source_target_pairs={{4,0},{5,1},{6,2},{7,3},{12,8},{13,9},{14,10},{15,11},{20,16},{21,... | collective-permute-start | bytes 3464 | tf_op jit(solution)/shard_map/ppermute | solution.py:23
  87.7 7.2 %collective-permute-start.7 = (f32[2,18,8,1]{3,2,1,0:T(8,128)S(1)}, f32[2,18,8,1]{3,2,1,0:T(8,128)S(1)}, u32[]{:S(2)}, u32[]{:S(2)}) collective-permute-start(f32[2,18,8,1]{3,2,1,0:T(8,128)S(1)} %get-tuple-element.87), channel_id=1, source_target_pairs={{0,4},{1,5},{2,6},{3,7},{8,12},{9,13},{10,14},{11,15},{16,20},{17,... | collective-permute-start | bytes 3464 | tf_op jit(solution)/shard_map/ppermute | solution.py:20
  113.4 10.0 %collective-permute-start.15 = (f32[3,18,8,1]{3,2,1,0:T(8,128)S(1)}, f32[3,18,8,1]{3,2,1,0:T(8,128)S(1)}, u32[]{:S(2)}, u32[]{:S(2)}) collective-permute-start(f32[3,18,8,1]{3,2,1,0:T(8,128)S(1)} %get-tuple-element.70), channel_id=1, source_target_pairs={{4,0},{5,1},{6,2},{7,3},{12,8},{13,9},{14,10},{15,11},{20,16},{21,... | collective-permute-start | bytes 5192 | tf_op jit(solution)/shard_map/ppermute | solution.py:23
  114.7 9.9 %collective-permute-start.14 = (f32[3,18,8,1]{3,2,1,0:T(8,128)S(1)}, f32[3,18,8,1]{3,2,1,0:T(8,128)S(1)}, u32[]{:S(2)}, u32[]{:S(2)}) collective-permute-start(f32[3,18,8,1]{3,2,1,0:T(8,128)S(1)} %get-tuple-element.69), channel_id=1, source_target_pairs={{0,4},{1,5},{2,6},{3,7},{8,12},{9,13},{10,14},{11,15},{16,20},{17,... | collective-permute-start | bytes 5192 | tf_op jit(solution)/shard_map/ppermute | solution.py:20
  183.7 7.2 %collective-permute-start.18 = (f32[2,1,8,128]{3,2,1,0:T(8,128)S(1)}, f32[2,1,8,128]{3,2,1,0:T(8,128)S(1)}, u32[]{:S(2)}, u32[]{:S(2)}) collective-permute-start(f32[2,1,8,128]{3,2,1,0:T(8,128)S(1)} %get-tuple-element.94), channel_id=1, source_target_pairs={{8,0},{16,8},{24,16},{9,1},{17,9},{25,17},{10,2},{18,10},{26,18},{... | collective-permute-start | bytes 24584 | tf_op jit(solution)/shard_map/ppermute | solution.py:23
  189.5 7.3 %collective-permute-start.23 = (f32[3,18,1,130]{3,2,1,0:T(1,128)S(1)}, f32[3,18,1,130]{3,2,1,0:T(1,128)S(1)}, u32[]{:S(2)}, u32[]{:S(2)}) collective-permute-start(f32[3,18,1,130]{3,2,1,0:T(1,128)S(1)} %get-tuple-element.43), channel_id=1, source_target_pairs={{0,1},{1,2},{2,3},{4,5},{5,6},{6,7},{8,9},{9,10},{10,11},{12,13},{... | collective-permute-start | bytes 84248 | tf_op jit(solution)/shard_map/ppermute | solution.py:20
  191.0 7.0 %collective-permute-start.20 = (f32[2,18,8,1]{3,2,1,0:T(8,128)S(1)}, f32[2,18,8,1]{3,2,1,0:T(8,128)S(1)}, u32[]{:S(2)}, u32[]{:S(2)}) collective-permute-start(f32[2,18,8,1]{3,2,1,0:T(8,128)S(1)} %get-tuple-element.86), channel_id=1, source_target_pairs={{4,0},{5,1},{6,2},{7,3},{12,8},{13,9},{14,10},{15,11},{20,16},{21,... | collective-permute-start | bytes 3464 | tf_op jit(solution)/shard_map/ppermute | solution.py:23
  192.3 7.2 %collective-permute-start.19 = (f32[2,18,8,1]{3,2,1,0:T(8,128)S(1)}, f32[2,18,8,1]{3,2,1,0:T(8,128)S(1)}, u32[]{:S(2)}, u32[]{:S(2)}) collective-permute-start(f32[2,18,8,1]{3,2,1,0:T(8,128)S(1)} %get-tuple-element.85), channel_id=1, source_target_pairs={{0,4},{1,5},{2,6},{3,7},{8,12},{9,13},{10,14},{11,15},{16,20},{17,... | collective-permute-start | bytes 3464 | tf_op jit(solution)/shard_map/ppermute | solution.py:20
  217.8 10.2 %collective-permute-start.27 = (f32[3,18,8,1]{3,2,1,0:T(8,128)S(1)}, f32[3,18,8,1]{3,2,1,0:T(8,128)S(1)}, u32[]{:S(2)}, u32[]{:S(2)}) collective-permute-start(f32[3,18,8,1]{3,2,1,0:T(8,128)S(1)} %get-tuple-element.68), channel_id=1, source_target_pairs={{4,0},{5,1},{6,2},{7,3},{12,8},{13,9},{14,10},{15,11},{20,16},{21,... | collective-permute-start | bytes 5192 | tf_op jit(solution)/shard_map/ppermute | solution.py:23
  219.1 10.1 %collective-permute-start.26 = (f32[3,18,8,1]{3,2,1,0:T(8,128)S(1)}, f32[3,18,8,1]{3,2,1,0:T(8,128)S(1)}, u32[]{:S(2)}, u32[]{:S(2)}) collective-permute-start(f32[3,18,8,1]{3,2,1,0:T(8,128)S(1)} %get-tuple-element.67), channel_id=1, source_target_pairs={{0,4},{1,5},{2,6},{3,7},{8,12},{9,13},{10,14},{11,15},{16,20},{17,... | collective-permute-start | bytes 5192 | tf_op jit(solution)/shard_map/ppermute | solution.py:20
  288.5 7.2 %collective-permute-start.30 = (f32[2,1,8,128]{3,2,1,0:T(8,128)S(1)}, f32[2,1,8,128]{3,2,1,0:T(8,128)S(1)}, u32[]{:S(2)}, u32[]{:S(2)}) collective-permute-start(f32[2,1,8,128]{3,2,1,0:T(8,128)S(1)} %get-tuple-element.92), channel_id=1, source_target_pairs={{8,0},{16,8},{24,16},{9,1},{17,9},{25,17},{10,2},{18,10},{26,18},{... | collective-permute-start | bytes 24584 | tf_op jit(solution)/shard_map/ppermute | solution.py:23
  294.4 7.3 %collective-permute-start.35 = (f32[3,18,1,130]{3,2,1,0:T(1,128)S(1)}, f32[3,18,1,130]{3,2,1,0:T(1,128)S(1)}, u32[]{:S(2)}, u32[]{:S(2)}) collective-permute-start(f32[3,18,1,130]{3,2,1,0:T(1,128)S(1)} %get-tuple-element.41), channel_id=1, source_target_pairs={{0,1},{1,2},{2,3},{4,5},{5,6},{6,7},{8,9},{9,10},{10,11},{12,13},{... | collective-permute-start | bytes 84248 | tf_op jit(solution)/shard_map/ppermute | solution.py:20
  295.8 7.0 %collective-permute-start.32 = (f32[2,18,8,1]{3,2,1,0:T(8,128)S(1)}, f32[2,18,8,1]{3,2,1,0:T(8,128)S(1)}, u32[]{:S(2)}, u32[]{:S(2)}) collective-permute-start(f32[2,18,8,1]{3,2,1,0:T(8,128)S(1)} %get-tuple-element.84), channel_id=1, source_target_pairs={{4,0},{5,1},{6,2},{7,3},{12,8},{13,9},{14,10},{15,11},{20,16},{21,... | collective-permute-start | bytes 3464 | tf_op jit(solution)/shard_map/ppermute | solution.py:23
  297.1 7.2 %collective-permute-start.31 = (f32[2,18,8,1]{3,2,1,0:T(8,128)S(1)}, f32[2,18,8,1]{3,2,1,0:T(8,128)S(1)}, u32[]{:S(2)}, u32[]{:S(2)}) collective-permute-start(f32[2,18,8,1]{3,2,1,0:T(8,128)S(1)} %get-tuple-element.83), channel_id=1, source_target_pairs={{0,4},{1,5},{2,6},{3,7},{8,12},{9,13},{10,14},{11,15},{16,20},{17,... | collective-permute-start | bytes 3464 | tf_op jit(solution)/shard_map/ppermute | solution.py:20
  322.7 10.2 %collective-permute-start.39 = (f32[3,18,8,1]{3,2,1,0:T(8,128)S(1)}, f32[3,18,8,1]{3,2,1,0:T(8,128)S(1)}, u32[]{:S(2)}, u32[]{:S(2)}) collective-permute-start(f32[3,18,8,1]{3,2,1,0:T(8,128)S(1)} %get-tuple-element.66), channel_id=1, source_target_pairs={{4,0},{5,1},{6,2},{7,3},{12,8},{13,9},{14,10},{15,11},{20,16},{21,... | collective-permute-start | bytes 5192 | tf_op jit(solution)/shard_map/ppermute | solution.py:23
  324.0 10.1 %collective-permute-start.38 = (f32[3,18,8,1]{3,2,1,0:T(8,128)S(1)}, f32[3,18,8,1]{3,2,1,0:T(8,128)S(1)}, u32[]{:S(2)}, u32[]{:S(2)}) collective-permute-start(f32[3,18,8,1]{3,2,1,0:T(8,128)S(1)} %get-tuple-element.65), channel_id=1, source_target_pairs={{0,4},{1,5},{2,6},{3,7},{8,12},{9,13},{10,14},{11,15},{16,20},{17,... | collective-permute-start | bytes 5192 | tf_op jit(solution)/shard_map/ppermute | solution.py:20
  335.8 58.9 %collective-permute-start.47 = (f32[3,18,1,130]{3,2,1,0:T(1,128)S(1)}, f32[3,18,1,130]{3,2,1,0:T(1,128)S(1)}, u32[]{:S(2)}, u32[]{:S(2)}) collective-permute-start(f32[3,18,1,130]{3,2,1,0:T(1,128)S(1)} %get-tuple-element.39), channel_id=1, source_target_pairs={{0,1},{1,2},{2,3},{4,5},{5,6},{6,7},{8,9},{9,10},{10,11},{12,13},{... | collective-permute-start | bytes 84248 | tf_op jit(solution)/shard_map/ppermute | solution.py:20
  396.1 7.0 %collective-permute-start.44 = (f32[2,18,8,1]{3,2,1,0:T(8,128)S(1)}, f32[2,18,8,1]{3,2,1,0:T(8,128)S(1)}, u32[]{:S(2)}, u32[]{:S(2)}) collective-permute-start(f32[2,18,8,1]{3,2,1,0:T(8,128)S(1)} %get-tuple-element.82), channel_id=1, source_target_pairs={{4,0},{5,1},{6,2},{7,3},{12,8},{13,9},{14,10},{15,11},{20,16},{21,... | collective-permute-start | bytes 3464 | tf_op jit(solution)/shard_map/ppermute | solution.py:23
  397.4 7.2 %collective-permute-start.43 = (f32[2,18,8,1]{3,2,1,0:T(8,128)S(1)}, f32[2,18,8,1]{3,2,1,0:T(8,128)S(1)}, u32[]{:S(2)}, u32[]{:S(2)}) collective-permute-start(f32[2,18,8,1]{3,2,1,0:T(8,128)S(1)} %get-tuple-element.81), channel_id=1, source_target_pairs={{0,4},{1,5},{2,6},{3,7},{8,12},{9,13},{10,14},{11,15},{16,20},{17,... | collective-permute-start | bytes 3464 | tf_op jit(solution)/shard_map/ppermute | solution.py:20
  (33 other events, 220.8 us)
where the time goes:
time: 422 us; the launch traced here: 416 us
  blocking collectives  174 us (41%)
  starting transfers between devices  129 us (31%)
  other arithmetic  63.1 us (15%)
  waiting for transfers between devices  42.3 us (10%)
    psum x4, blocking collectives, pressure_sum(): return lax.psum(jnp.sum(values), ('gx', 'gy', 'gz'))  174 us
    ppermute x24, starting transfers between devices, padded_2(): lax.ppermute(lax.slice_in_dim(block, block.shape[dim] - width, None, axis...  97.7 us
    ppermute x24, starting transfers between devices, padded_2(): lax.ppermute(lax.slice_in_dim(block, 0, width, axis=dim), axis, backward)  31 us
    reduce_sum x4, other arithmetic, pressure_sum(): return lax.psum(jnp.sum(values), ('gx', 'gy', 'gz'))  23.7 us
    ppermute x24, waiting for transfers between devices, padded_2(): lax.ppermute(lax.slice_in_dim(block, 0, width, axis=dim), axis, backward)  22.6 us
    ppermute x24, waiting for transfers between devices, padded_2(): lax.ppermute(lax.slice_in_dim(block, block.shape[dim] - width, None, axis...  19.7 us
    select_n x12, other arithmetic, local(): jnp.where(coord(axis_number, 0) == 0, jnp.float32(0.0), fresh)  15.9 us
    another operation x7, other arithmetic, local(): jnp.stack([pressure, eta])  15.7 us
  transfers between devices with their start and end apart: 48, of which 28 were waited for; matrix products, arithmetic and copies ran while one was open for 3% of the time, Pallas kernels for 0%

commit v1 on v0

v1 whole, which is shorter than its diff:
```python
import math

import jax
import jax.numpy as jnp
from jax import lax
from jax.experimental import pallas as pl
from jax.experimental.pallas import tpu as pltpu
from jax.sharding import PartitionSpec as P

ITERS = 4
PHASES = 4
LOW = ITERS
HIGH = 2 * ITERS
FIELDS = 5
LANE_STEP = 16

VMEM = pl.BlockSpec(memory_space=pltpu.VMEM)
SMEM = pl.BlockSpec(memory_space=pltpu.SMEM)


def z_up(a):
    return pltpu.roll(a, a.shape[0] - 1, 0)


def z_down(a):
    return pltpu.roll(a, 1, 0)


def y_up(a):
    return pltpu.roll(a, a.shape[1] - 1, 1)


def y_down(a):
    return pltpu.roll(a, 1, 1)


def reciprocal(a):
    r = pl.reciprocal(a, approx=True)
    return r * (2.0 - a * r)


def pack_kernel(vx_ref, vz_ref, vy_ref, p_ref, phase_ref, stack_ref, edge_ref):
    bx, bz, by = p_ref.shape
    ix, iz, iy = lax.axis_index("gx"), lax.axis_index("gz"), lax.axis_index("gy")
    lane = lax.broadcasted_iota(jnp.int32, (bz, by), 1)
    row = lax.broadcasted_iota(jnp.int32, (bz, by), 0)
    keep_z = (row > 0) | (iz > 0)
    keep_y = (lane > 0) | (iy > 0)

    def plane(i, carry):
        vx = vx_ref[i] * jnp.where((i > 0) | (ix > 0), 1.0, 0.0)
        vz = jnp.where(keep_z, vz_ref[i], 0.0)
        vy = jnp.where(keep_y, vy_ref[i], 0.0)
        fields = (vx, vz, vy, p_ref[i], phase_ref[i].astype(jnp.float32))
        edge = jnp.zeros((bz, by), jnp.float32)
        for f, a in enumerate(fields):
            stack_ref[i, f] = a
            at = LANE_STEP * f
            first = pltpu.roll(a, at, 1) if at else a
            edge = jnp.where((lane >= at) & (lane < at + HIGH), first, edge)
            last = pltpu.roll(a, at + LANE_STEP, 1)
            edge = jnp.where((lane >= at + LANE_STEP - LOW) & (lane < at + LANE_STEP), last, edge)
        edge_ref[i] = edge
        return carry

    lax.fori_loop(0, bx, plane, 0)


def main_kernel(
    own_ref, above_ref, below_ref, scale_ref, power_ref, rho_table_ref,
    out_vx_ref, out_vz_ref, out_vy_ref, out_p_ref, out_eta_ref, sum_ref,
    va_ref, vb_ref, p_ref, pre_ref, power_field_ref, rho_ref, weight_ref,
):
    bz, by = own_ref.shape[2:]
    bx = own_ref.shape[0] - LOW - HIGH
    rows, lanes = 3 * bz, 2 * by
    nx, nz, ny = lax.axis_size("gx"), lax.axis_size("gz"), lax.axis_size("gy")
    ix, iz, iy = lax.axis_index("gx"), lax.axis_index("gz"), lax.axis_index("gy")

    lane = lax.broadcasted_iota(jnp.int32, (bz, by), 1)
    right = (lane < HIGH) & (iy < ny - 1)
    left = (lane >= by - LOW) & (iy > 0)

    def unpack(i, carry):
        x_in = (i + ix * bx >= LOW) & (i + ix * bx < LOW + nx * bx)
        for t, (ref, z_in) in enumerate(((own_ref, None), (above_ref, iz < nz - 1), (below_ref, iz > 0))):
            at = pl.ds(t * bz, bz)
            ok = x_in if z_in is None else x_in & z_in
            ok = jnp.where(ok, 1.0, 0.0)
            edge = ref[i, FIELDS]
            for f in range(FIELDS):
                middle = ref[i, f]
                shift = LANE_STEP * f
                a = pltpu.roll(edge, (by - shift) % by, 1) if shift else edge
                b = pltpu.roll(edge, (by - LANE_STEP - shift) % by, 1)
                side = jnp.where(right, a, jnp.where(left, b, 0.0))
                if f < 3:
                    va_ref[f, i, at, 0:by] = middle
                    va_ref[f, i, at, by:lanes] = side
                elif f == 3:
                    p_ref[i, at, 0:by] = middle
                    p_ref[i, at, by:lanes] = side
                else:
                    for part, (ph, keep) in enumerate(((middle, None), (side, right | left))):
                        to = pl.ds(part * by, by)
                        values = []
                        for table in (scale_ref, power_ref, rho_table_ref):
                            value = table[0]
                            for index in range(1, PHASES):
                                value = jnp.where(ph == float(index), table[index], value)
                            values.append(jnp.broadcast_to(value, (bz, by)))
                        pre = values[0] * ok
                        if keep is not None:
                            pre = jnp.where(keep, pre, 0.0)
                        pre_ref[i, at, to] = pre
                        power_field_ref[i, at, to] = values[1]
                        rho_ref[i, at, to] = values[2]
        return carry

    lax.fori_loop(0, bx + LOW + HIGH, unpack, 0)

    r = lax.broadcasted_iota(jnp.int32, (rows, lanes), 0)
    c = lax.broadcasted_iota(jnp.int32, (rows, lanes), 1)
    zg = iz * bz + jnp.where(r < 2 * bz, r, r - rows)
    yg = iy * by + jnp.where(c < by + HIGH, c, c - lanes)
    filled = (c < by + HIGH) | (c >= lanes - LOW)
    inside = filled & (zg >= 0) & (zg < nz * bz) & (yg >= 0) & (yg < ny * by)
    weight_ref[0] = jnp.where(inside, 0.05, 0.0)
    weight_ref[1] = jnp.where(inside & (zg > 0), 0.05, 0.0)
    weight_ref[2] = jnp.where(inside & (yg > 0), 0.05, 0.0)
    weight_ref[3] = jnp.where(inside, 0.0, 1.0)

    for k in range(1, ITERS + 1):
        old, new = (va_ref, vb_ref) if k % 2 else (vb_ref, va_ref)
        last = k == ITERS

        def cell(j):
            vx, vz, vy = old[0, j], old[1, j], old[2, j]
            rx = old[0, j + 1] - vx
            rz = z_up(vz) - vz
            ry = y_up(vy) - vy
            a = rx - ry
            b = ry - rz
            inv = (a * (a + b) + b * b) * (1.0 / 3.0) + 1.0
            eta = pre_ref[j] * jnp.exp2(power_field_ref[j] * jnp.log(inv))
            quarter = 0.25 * eta
            div = rx + ry + rz
            p = p_ref[j] - quarter * (div + div)
            p_ref[j] = p
            tx, tz, ty = eta * rx - p, eta * rz - p, eta * ry - p
            sz = quarter + z_down(quarter)
            sy = quarter + y_down(quarter)
            return eta, p, quarter, tx, tz, ty, sz, sy

        def step(j, carry):
            quarter0, tx0, sz0, sy0, part_z0, part_y0, scale_z0, scale_y0 = carry
            eta, p, quarter, tx, tz, ty, sz, sy = cell(j)
            vx, vz, vy = old[0, j], old[1, j], old[2, j]
            vz0, vy0 = old[1, j - 1], old[2, j - 1]
            bias = weight_ref[3]
            sx = quarter + quarter0
            exz = sz + sz0
            exy = sy + sy0
            ezy = sz + y_down(sz)
            fxz = exz * (vx - z_down(vx))
            fxy = exy * (vx - y_down(vx))
            gzx = exz * (vz - vz0)
            hyx = exy * (vy - vy0)
            gzy = ezy * (vz - y_down(vz))
            hyz = ezy * (vy - z_down(vy))
            res_x = (tx - tx0) + ((z_up(fxz) - fxz) + (y_up(fxy) - fxy))
            new_vx = vx + weight_ref[0] * reciprocal(sx + bias) * res_x
            new_vz = vz0 + scale_z0 * (part_z0 + gzx)
            new_vy = vy0 + scale_y0 * (part_y0 + hyx)
            part_z = (tz - z_down(tz)) - rho_ref[j] + ((y_up(gzy) - gzy) - gzx)
            part_y = (ty - y_down(ty)) + ((z_up(hyz) - hyz) - hyx)
            scale_z = weight_ref[1] * reciprocal(sz + bias)
            scale_y = weight_ref[2] * reciprocal(sy + bias)
            if last:
                out_vx_ref[j - LOW] = new_vx[0:bz, 0:by]
                out_p_ref[j - LOW] = p[0:bz, 0:by]
                out_eta_ref[j - LOW] = eta[0:bz, 0:by]
                sum_ref[...] += p[0:bz, 0:by]
            else:
                new[0, j] = new_vx

            def finish():
                if last:
                    out_vz_ref[j - 1 - LOW] = new_vz[0:bz, 0:by]
                    out_vy_ref[j - 1 - LOW] = new_vy[0:bz, 0:by]
                else:
                    new[1, j - 1] = new_vz
                    new[2, j - 1] = new_vy

            return (quarter, tx, sz, sy, part_z, part_y, scale_z, scale_y), finish

        first, count = k, bx + LOW + HIGH - 3 * k
        if last:
            sum_ref[...] = jnp.zeros((bz, by), jnp.float32)
        eta, p, quarter, tx, tz, ty, sz, sy = cell(first - 1)
        zero = jnp.zeros((rows, lanes), jnp.float32)
        carry, _ = step(first, (quarter, tx, sz, sy, zero, zero, zero, zero))

        def loop(j, carry):
            carry, finish = step(j, carry)
            finish()
            return carry

        carry = lax.fori_loop(first + 1, first + count, loop, carry)
        j = first + count
        quarter0, tx0, sz0, sy0, part_z0, part_y0, scale_z0, scale_y0 = carry
        eta, p, quarter, tx, tz, ty, sz, sy = cell(j)
        gzx = (sz + sz0) * (old[1, j] - old[1, j - 1])
        hyx = (sy + sy0) * (old[2, j] - old[2, j - 1])
        new_vz = old[1, j - 1] + scale_z0 * (part_z0 + gzx)
        new_vy = old[2, j - 1] + scale_y0 * (part_y0 + hyx)
        if last:
            out_vz_ref[j - 1 - LOW] = new_vz[0:bz, 0:by]
            out_vy_ref[j - 1 - LOW] = new_vy[0:bz, 0:by]
        else:
            new[1, j - 1] = new_vz
            new[2, j - 1] = new_vy

        if last:
            @pl.when(ix == 0)
            def _():
                out_vx_ref[0] = jnp.zeros((bz, by), jnp.float32)
        else:
            plane = jnp.zeros((rows, lanes), jnp.float32)

            @pl.when(ix == 0)
            def _():
                for i in range(k, LOW):
                    for d in range(3):
                        new[d, i] = plane
                new[0, LOW] = plane

            @pl.when(ix == nx - 1)
            def _():
                for i in range(LOW + bx, first + count):
                    for d in range(3):
                        new[d, i] = plane


def final_kernel(p_ref, sum_ref, out_ref, *, cells):
    mean = jnp.sum(sum_ref[...]) * (1.0 / cells)
    out_ref[...] = p_ref[...] - mean


def shift(a, axis, step):
    count = lax.axis_size(axis)
    return lax.ppermute(a, axis, [(i, i + step) for i in range(count) if 0 <= i + step < count])


def swap_sum(a, axis):
    count = lax.axis_size(axis)
    if count & (count - 1):
        return lax.psum(a, axis)
    bit = 1
    while bit < count:
        a = a + lax.ppermute(a, axis, [(i, i ^ bit) for i in range(count)])
        bit *= 2
    return a


def local(vel_x, vel_y, vel_z, pressure, phase, visc_scale, power_n, density):
    bx, bz, by = pressure.shape
    f32 = jnp.float32
    counts = [lax.axis_size(a) for a in ("gx", "gz", "gy")]
    cells = bx * bz * by * math.prod(counts)
    deep = bx + LOW + HIGH
    block = jax.ShapeDtypeStruct((bx, bz, by), f32)

    stack, edge = pl.pallas_call(
        pack_kernel,
        out_shape=(jax.ShapeDtypeStruct((bx, FIELDS, bz, by), f32), block),
        in_specs=[VMEM] * 5,
        out_specs=(VMEM, VMEM),
    )(vel_x, vel_z, vel_y, pressure, phase)

    lane = lax.broadcasted_iota(jnp.int32, (bx, bz, by), 2)
    if counts[2] == 2:
        side = lax.ppermute(edge, "gy", [(0, 1), (1, 0)])
    else:
        side = jnp.where(lane % LANE_STEP < HIGH, shift(edge, "gy", -1), shift(edge, "gy", 1))
    stack = jnp.concatenate([stack, side[:, None]], axis=1)
    low = shift(stack[bx - LOW :], "gx", 1)
    high = shift(stack[:HIGH], "gx", -1)
    stack = jnp.concatenate([low, stack, high], axis=0)
    above = shift(stack, "gz", -1)
    below = shift(stack, "gz", 1)

    power = (0.5 / math.log(2.0)) * (1.0 / power_n - 1.0)
    scratch = lambda *shape: pltpu.VMEM(shape, f32)
    rows, lanes = 3 * bz, 2 * by
    vx, vz, vy, p, eta, total = pl.pallas_call(
        main_kernel,
        out_shape=(block,) * 5 + (jax.ShapeDtypeStruct((bz, by), f32),),
        in_specs=[VMEM] * 3 + [SMEM] * 3,
        out_specs=(VMEM,) * 6,
        scratch_shapes=[
            scratch(3, deep, rows, lanes),
            scratch(3, deep, rows, lanes),
            scratch(deep, rows, lanes),
            scratch(deep, rows, lanes),
            scratch(deep, rows, lanes),
            scratch(deep, rows, lanes),
            scratch(4, rows, lanes),
        ],
        compiler_params=pltpu.CompilerParams(vmem_limit_bytes=32 * 1024 * 1024),
    )(stack, above, below, visc_scale, power, density)

    for axis in ("gz", "gy", "gx"):
        total = swap_sum(total, axis)
    p = pl.pallas_call(
        lambda *refs: final_kernel(*refs, cells=float(cells)),
        out_shape=block,
        in_specs=[VMEM] * 2,
        out_specs=VMEM,
    )(p, total)
    return (vx, vy, vz, p, eta)


def solution(mesh):
    spec = P("gx", "gz", "gy")
    return jax.shard_map(
        local,
        mesh=mesh,
        in_specs=(spec,) * 5 + (P(),) * 3,
        out_specs=(spec,) * 5,
        check_vma=False,
    )
```

time: 422 us -> 80.9 us (0.19); the launches traced: 416 us -> 80.6 us
  blocking collectives: 174 us -> 0 us
  starting transfers between devices: 129 us -> 27.2 us
  other arithmetic: 63.1 us -> 1.6 us
  Pallas kernels: 0 us -> 31.3 us
  waiting for transfers between devices: 42.3 us -> 19.2 us
    psum x4 -> x0, blocking collectives: 174 us -> none  [pressure_sum(): return lax.psum(jnp.sum(values), ('gx', 'gy', 'gz'))]
    ppermute x48 -> x10, starting transfers between devices: 129 us -> 27.2 us  [the longest x5 15.7 us: swap_sum(): a = a + lax.ppermute(a, axis, [(i, i ^ bit) for i in range(count)])]
    pallas_call x0 -> x3, Pallas kernels: none -> 31.3 us  [the longest x1 26.7 us: local(): pl.pallas_call(main_kernel, out_shape=(block,) * 5 + (jax.ShapeDtypeStruc...]
    reduce_sum x4 -> x0, other arithmetic: 23.7 us -> none  [pressure_sum(): return lax.psum(jnp.sum(values), ('gx', 'gy', 'gz'))]
    ppermute x48 -> x10, waiting for transfers between devices: 42.3 us -> 19.2 us  [the longest x5 9.65 us: swap_sum(): a = a + lax.ppermute(a, axis, [(i, i ^ bit) for i in range(count)])]
    another operation x13 -> x0, other arithmetic: 16.8 us -> none  [the longest x7 15.7 us: local(): jnp.stack([pressure, eta])]
    select_n x12 -> x0, other arithmetic: 15.9 us -> none  [local(): jnp.where(coord(axis_number, 0) == 0, jnp.float32(0.0), fresh)]
  transfers between devices with their start and end apart: 48 -> 10, of which waited for: 28 -> 9; matrix products, arithmetic and copies ran while one was open for 3% -> 0% of each run, Pallas kernels for 0% -> 0%
where the time goes in v1:
time: 80.9 us; the launch traced here: 80.6 us
  Pallas kernels  31.3 us (39%)
  starting transfers between devices  27.2 us (34%)
  waiting for transfers between devices  19.2 us (24%)
  other arithmetic  1.6 us (2%)
    pallas_call x1, Pallas kernels, local(): pl.pallas_call(main_kernel, out_shape=(block,) * 5 + (jax.ShapeDtypeStruc...  26.7 us
    ppermute x5, starting transfers between devices, swap_sum(): a = a + lax.ppermute(a, axis, [(i, i ^ bit) for i in range(count)])  15.7 us
    ppermute x5, waiting for transfers between devices, swap_sum(): a = a + lax.ppermute(a, axis, [(i, i ^ bit) for i in range(count)])  9.65 us
    ppermute x4, starting transfers between devices, shift(): lax.ppermute(a, axis, [(i, i + step) for i in range(count) if 0 <= i + st...  8.56 us
    ppermute x4, waiting for transfers between devices, shift(): lax.ppermute(a, axis, [(i, i + step) for i in range(count) if 0 <= i + st...  7.06 us
    pallas_call x1, Pallas kernels, local(): pl.pallas_call(pack_kernel, out_shape=(jax.ShapeDtypeStruct((bx, FIELDS,...  2.97 us
    ppermute x1, starting transfers between devices, local(): side = lax.ppermute(edge, 'gy', [(0, 1), (1, 0)])  2.94 us
    ppermute x1, waiting for transfers between devices, local(): side = lax.ppermute(edge, 'gy', [(0, 1), (1, 0)])  2.45 us
  transfers between devices with their start and end apart: 10, of which 9 were waited for; matrix products, arithmetic and copies ran while one was open for 0% of the time, Pallas kernels for 0%

profile of v1, /device:TPU:0, one launch (start us, length us, event | category | flops | bytes accessed | tf_op | source)
XLA Modules:
  0.0 80.6 jit_solution(2326651755313159912)
XLA Ops:
  0.6 3.0 %shard_map.119 = (f32[16,5,8,128]{3,2,1,0:T(8,128)}, f32[16,8,128]{2,1,0:T(8,128)}) custom-call(f32[16,8,128]{2,1,0:T(8,128)} %vx_ref.1, f32[16,8,128]{2,1,0:T(8,128)} %vz_ref.1, f32[16,8,128]{2,1,0:T(8,128)} %vy_ref.1, f32[16,8,128]{2,1,0:T(8,128)} %p_ref.1, s32[16,8,128]{2,1,0:T(8,128)} %phase_ref.1), custom_call_target="tpu_custom_call" | custom-call | tf_op jit(solution)/shard_map/pallas_call | solution.py:274
  3.6 2.9 %collective-permute-start = (f32[16,8,128]{2,1,0:T(8,128)}, f32[16,8,128]{2,1,0:T(8,128)S(1)}, u32[]{:S(2)}, u32[]{:S(2)}) collective-permute-start(f32[16,8,128]{2,1,0:T(8,128)} %get-tuple-element.14), channel_id=1, source_target_pairs={{0,4},{4,0},{1,5},{5,1},{2,6},{6,2},{3,7},{7,3},{8,12},{12,8},{9,1... | collective-permute-start | bytes 196616 | tf_op jit(solution)/shard_map/ppermute | solution.py:283
  6.5 2.5 %collective-permute-done = f32[16,8,128]{2,1,0:T(8,128)S(1)} collective-permute-done((f32[16,8,128]{2,1,0:T(8,128)}, f32[16,8,128]{2,1,0:T(8,128)S(1)}, u32[]{:S(2)}, u32[]{:S(2)}) %collective-permute-start) | collective-permute-done | bytes 65568 | tf_op jit(solution)/shard_map/ppermute | solution.py:283
  9.0 0.9 %pad_maximum_fusion.1 = f32[8,6,8,128]{3,2,1,0:T(8,128)S(1)} fusion(f32[16,1,8,128]{3,2,1,0:T(8,128)S(1)} %bitcast.1, f32[16,5,8,128]{3,2,1,0:T(8,128)} %get-tuple-element.13), kind=kLoop, calls=%fused_computation.1 | loop fusion | flops 49152 | bytes 589824 | tf_op jit(solution)/shard_map/concatenate | solution.py:286
  9.9 1.3 %collective-permute-start.2 = (f32[8,6,8,128]{3,2,1,0:T(8,128)S(1)}, f32[8,6,8,128]{3,2,1,0:T(8,128)S(1)}, u32[]{:S(2)}, u32[]{:S(2)}) collective-permute-start(f32[8,6,8,128]{3,2,1,0:T(8,128)S(1)} %pad_maximum_fusion.1), channel_id=1, source_target_pairs={{8,0},{16,8},{24,16},{9,1},{17,9},{25,17},{10,2},{18,10},{26,18},{... | collective-permute-start | bytes 589832 | tf_op jit(solution)/shard_map/ppermute | solution.py:252
  11.3 4.6 %collective-permute-start.1 = (f32[4,6,8,128]{3,2,1,0:T(8,128)S(1)}, f32[4,6,8,128]{3,2,1,0:T(8,128)S(1)}, u32[]{:S(2)}, u32[]{:S(2)}) collective-permute-start(f32[4,6,8,128]{3,2,1,0:T(8,128)S(1)} %pad_maximum_fusion.2), channel_id=1, source_target_pairs={{0,8},{8,16},{16,24},{1,9},{9,17},{17,25},{2,10},{10,18},{18,26},{... | collective-permute-start | bytes 294920 | tf_op jit(solution)/shard_map/ppermute | solution.py:252
  15.9 2.2 %collective-permute-done.1 = f32[4,6,8,128]{3,2,1,0:T(8,128)S(1)} collective-permute-done((f32[4,6,8,128]{3,2,1,0:T(8,128)S(1)}, f32[4,6,8,128]{3,2,1,0:T(8,128)S(1)}, u32[]{:S(2)}, u32[]{:S(2)}) %collective-permute-start.1) | collective-permute-done | bytes 98336 | tf_op jit(solution)/shard_map/ppermute | solution.py:252
  18.2 1.3 %collective-permute-start.4 = (f32[28,6,8,128]{3,2,1,0:T(8,128)S(1)}, f32[28,6,8,128]{3,2,1,0:T(8,128)S(1)}, u32[]{:S(2)}, u32[]{:S(2)}) collective-permute-start(f32[28,6,8,128]{3,2,1,0:T(8,128)S(1)} %pad_maximum_fusion.own_ref), channel_id=1, source_target_pairs={{0,1},{1,2},{2,3},{4,5},{5,6},{6,7},{8,9},{9,10},{10,11},{12,13},{... | collective-permute-start | bytes 2064392 | tf_op jit(solution)/shard_map/ppermute | solution.py:252
  19.5 1.3 %collective-permute-start.3 = (f32[28,6,8,128]{3,2,1,0:T(8,128)S(1)}, f32[28,6,8,128]{3,2,1,0:T(8,128)S(1)}, u32[]{:S(2)}, u32[]{:S(2)}) collective-permute-start(f32[28,6,8,128]{3,2,1,0:T(8,128)S(1)} %pad_maximum_fusion.own_ref), channel_id=1, source_target_pairs={{1,0},{2,1},{3,2},{5,4},{6,5},{7,6},{9,8},{10,9},{11,10},{13,12},{... | collective-permute-start | bytes 2064392 | tf_op jit(solution)/shard_map/ppermute | solution.py:252
  20.9 0.4 collective-permute-done.4.below_ref
  21.2 4.5 %collective-permute-done.3.above_ref = f32[28,6,8,128]{3,2,1,0:T(8,128)S(1)} collective-permute-done((f32[28,6,8,128]{3,2,1,0:T(8,128)S(1)}, f32[28,6,8,128]{3,2,1,0:T(8,128)S(1)}, u32[]{:S(2)}, u32[]{:S(2)}) %collective-permute-start.3) | collective-permute-done | bytes 688160 | tf_op jit(solution)/shard_map/ppermute | solution.py:252
  25.7 26.7 %shard_map.120 = (f32[16,8,128]{2,1,0:T(8,128)}, f32[16,8,128]{2,1,0:T(8,128)}, f32[16,8,128]{2,1,0:T(8,128)}, f32[16,8,128]{2,1,0:T(8,128)S(1)}, f32[16,8,128]{2,1,0:T(8,128)}, /*index=5*/f32[8,128]{1,0:T(8,128)S(1)}) custom-call(f32[28,6,8,128]{3,2,1,0:T(8,128)S(1)} %pad_maximum_fusion.own_ref, f32[28,6,8,128]{3,2,1,0:T(8,128)S(1)} %collective-permute-done.3.above_ref, ...), custom_call_target="tpu_custom_call" | custom-call | tf_op jit(solution)/shard_map/pallas_call | solution.py:296
  52.4 0.6 copy-done
  53.0 8.7 %collective-permute-start.5 = (f32[8,128]{1,0:T(8,128)S(1)}, f32[8,128]{1,0:T(8,128)S(1)}, u32[]{:S(2)}, u32[]{:S(2)}) collective-permute-start(f32[8,128]{1,0:T(8,128)S(1)} %get-tuple-element.19), channel_id=1, source_target_pairs={{0,1},{1,0},{2,3},{3,2},{4,5},{5,4},{6,7},{7,6},{8,9},{9,8},{10,11... | collective-permute-start | bytes 12296 | tf_op jit(solution)/shard_map/ppermute | solution.py:261
  61.8 0.8 %collective-permute-done.5 = f32[8,128]{1,0:T(8,128)S(1)} collective-permute-done((f32[8,128]{1,0:T(8,128)S(1)}, f32[8,128]{1,0:T(8,128)S(1)}, u32[]{:S(2)}, u32[]{:S(2)}) %collective-permute-start.5) | collective-permute-done | bytes 4128 | tf_op jit(solution)/shard_map/ppermute | solution.py:261
  62.7 3.5 %collective-permute-done.6 = f32[8,128]{1,0:T(8,128)S(1)} collective-permute-done((f32[8,128]{1,0:T(8,128)S(1)}, f32[8,128]{1,0:T(8,128)S(1)}, u32[]{:S(2)}, u32[]{:S(2)}) %collective-permute-start.6) | collective-permute-done | bytes 4128 | tf_op jit(solution)/shard_map/ppermute | solution.py:261
  66.2 1.5 %collective-permute-start.7 = (f32[8,128]{1,0:T(8,128)S(1)}, f32[8,128]{1,0:T(8,128)S(1)}, u32[]{:S(2)}, u32[]{:S(2)}) collective-permute-start(f32[8,128]{1,0:T(8,128)S(1)} %add.17), channel_id=1, source_target_pairs={{0,4},{4,0},{1,5},{5,1},{2,6},{6,2},{3,7},{7,3},{8,12},{12,8},{9,1... | collective-permute-start | bytes 12296 | tf_op jit(solution)/shard_map/ppermute | solution.py:261
  67.7 2.1 %collective-permute-done.7 = f32[8,128]{1,0:T(8,128)S(1)} collective-permute-done((f32[8,128]{1,0:T(8,128)S(1)}, f32[8,128]{1,0:T(8,128)S(1)}, u32[]{:S(2)}, u32[]{:S(2)}) %collective-permute-start.7) | collective-permute-done | bytes 4128 | tf_op jit(solution)/shard_map/ppermute | solution.py:261
  69.8 2.4 %collective-permute-start.8 = (f32[8,128]{1,0:T(8,128)S(1)}, f32[8,128]{1,0:T(8,128)S(1)}, u32[]{:S(2)}, u32[]{:S(2)}) collective-permute-start(f32[8,128]{1,0:T(8,128)S(1)} %add.18), channel_id=1, source_target_pairs={{0,8},{8,0},{16,24},{24,16},{1,9},{9,1},{17,25},{25,17},{2,10},{10... | collective-permute-start | bytes 12296 | tf_op jit(solution)/shard_map/ppermute | solution.py:261
  72.2 1.6 %collective-permute-done.8 = f32[8,128]{1,0:T(8,128)S(1)} collective-permute-done((f32[8,128]{1,0:T(8,128)S(1)}, f32[8,128]{1,0:T(8,128)S(1)}, u32[]{:S(2)}, u32[]{:S(2)}) %collective-permute-start.8) | collective-permute-done | bytes 4128 | tf_op jit(solution)/shard_map/ppermute | solution.py:261
  73.8 3.0 %collective-permute-start.9 = (f32[8,128]{1,0:T(8,128)S(1)}, f32[8,128]{1,0:T(8,128)S(1)}, u32[]{:S(2)}, u32[]{:S(2)}) collective-permute-start(f32[8,128]{1,0:T(8,128)S(1)} %add.19), channel_id=1, source_target_pairs={{0,16},{8,24},{16,0},{24,8},{1,17},{9,25},{17,1},{25,9},{2,18},{10... | collective-permute-start | bytes 12296 | tf_op jit(solution)/shard_map/ppermute | solution.py:261
  76.8 1.6 %collective-permute-done.9 = f32[8,128]{1,0:T(8,128)S(1)} collective-permute-done((f32[8,128]{1,0:T(8,128)S(1)}, f32[8,128]{1,0:T(8,128)S(1)}, u32[]{:S(2)}, u32[]{:S(2)}) %collective-permute-start.9) | collective-permute-done | bytes 4128 | tf_op jit(solution)/shard_map/ppermute | solution.py:261
  78.4 0.6 add.20.refs_1_
  79.0 1.6 %shard_map.121 = f32[16,8,128]{2,1,0:T(8,128)} custom-call(f32[16,8,128]{2,1,0:T(8,128)} %copy-done, f32[8,128]{1,0:T(8,128)} %add.20.refs_1_), custom_call_target="tpu_custom_call" | custom-call | tf_op jit(solution)/shard_map/pallas_call | solution.py:315
  (18 shorter events, 0.2 us)
Async XLA Ops:
  3.6 7.6 %copy-start.3 = (f32[16,5,8,128]{3,2,1,0:T(8,128)S(1)}, f32[16,5,8,128]{3,2,1,0:T(8,128)}, u32[]{:S(2)}) copy-start(f32[16,5,8,128]{3,2,1,0:T(8,128)} %get-tuple-element.13) | copy-start | bytes 983044
  3.6 5.4 %collective-permute-start = (f32[16,8,128]{2,1,0:T(8,128)}, f32[16,8,128]{2,1,0:T(8,128)S(1)}, u32[]{:S(2)}, u32[]{:S(2)}) collective-permute-start(f32[16,8,128]{2,1,0:T(8,128)} %get-tuple-element.14), channel_id=1, source_target_pairs={{0,4},{4,0},{1,5},{5,1},{2,6},{6,2},{3,7},{7,3},{8,12},{12,8},{9,1... | collective-permute-start | bytes 196616 | tf_op jit(solution)/shard_map/ppermute | solution.py:283
  9.9 8.2 %collective-permute-start.2 = (f32[8,6,8,128]{3,2,1,0:T(8,128)S(1)}, f32[8,6,8,128]{3,2,1,0:T(8,128)S(1)}, u32[]{:S(2)}, u32[]{:S(2)}) collective-permute-start(f32[8,6,8,128]{3,2,1,0:T(8,128)S(1)} %pad_maximum_fusion.1), channel_id=1, source_target_pairs={{8,0},{16,8},{24,16},{9,1},{17,9},{25,17},{10,2},{18,10},{26,18},{... | collective-permute-start | bytes 589832 | tf_op jit(solution)/shard_map/ppermute | solution.py:252
  11.3 9.6 %copy-start.4 = (f32[4]{0:T(128)S(1)}, f32[4]{0:T(128)}, u32[]{:S(2)}) copy-start(f32[4]{0:T(128)} %param.14) | copy-start | bytes 52
  11.3 6.8 %collective-permute-start.1 = (f32[4,6,8,128]{3,2,1,0:T(8,128)S(1)}, f32[4,6,8,128]{3,2,1,0:T(8,128)S(1)}, u32[]{:S(2)}, u32[]{:S(2)}) collective-permute-start(f32[4,6,8,128]{3,2,1,0:T(8,128)S(1)} %pad_maximum_fusion.2), channel_id=1, source_target_pairs={{0,8},{8,16},{16,24},{1,9},{9,17},{17,25},{2,10},{10,18},{18,26},{... | collective-permute-start | bytes 294920 | tf_op jit(solution)/shard_map/ppermute | solution.py:252
  18.2 7.6 %copy-start.1 = (f32[4]{0:T(128)S(1)}, f32[4]{0:T(128)}, u32[]{:S(2)}) copy-start(f32[4]{0:T(128)} %scale_ref.1) | copy-start | bytes 52
  18.2 7.5 %copy-start.2 = (f32[4]{0:T(128)S(1)}, f32[4]{0:T(128)}, u32[]{:S(2)}) copy-start(f32[4]{0:T(128)} %rho_table_ref.1) | copy-start | bytes 52
  18.2 3.1 %collective-permute-start.4 = (f32[28,6,8,128]{3,2,1,0:T(8,128)S(1)}, f32[28,6,8,128]{3,2,1,0:T(8,128)S(1)}, u32[]{:S(2)}, u32[]{:S(2)}) collective-permute-start(f32[28,6,8,128]{3,2,1,0:T(8,128)S(1)} %pad_maximum_fusion.own_ref), channel_id=1, source_target_pairs={{0,1},{1,2},{2,3},{4,5},{5,6},{6,7},{8,9},{9,10},{10,11},{12,13},{... | collective-permute-start | bytes 2064392 | tf_op jit(solution)/shard_map/ppermute | solution.py:252
  19.5 6.2 %collective-permute-start.3 = (f32[28,6,8,128]{3,2,1,0:T(8,128)S(1)}, f32[28,6,8,128]{3,2,1,0:T(8,128)S(1)}, u32[]{:S(2)}, u32[]{:S(2)}) collective-permute-start(f32[28,6,8,128]{3,2,1,0:T(8,128)S(1)} %pad_maximum_fusion.own_ref), channel_id=1, source_target_pairs={{1,0},{2,1},{3,2},{5,4},{6,5},{7,6},{9,8},{10,9},{11,10},{13,12},{... | collective-permute-start | bytes 2064392 | tf_op jit(solution)/shard_map/ppermute | solution.py:252
  52.4 0.6 copy-start
  53.0 9.5 %collective-permute-start.5 = (f32[8,128]{1,0:T(8,128)S(1)}, f32[8,128]{1,0:T(8,128)S(1)}, u32[]{:S(2)}, u32[]{:S(2)}) collective-permute-start(f32[8,128]{1,0:T(8,128)S(1)} %get-tuple-element.19), channel_id=1, source_target_pairs={{0,1},{1,0},{2,3},{3,2},{4,5},{5,4},{6,7},{7,6},{8,9},{9,8},{10,11... | collective-permute-start | bytes 12296 | tf_op jit(solution)/shard_map/ppermute | solution.py:261
  62.6 3.6 %collective-permute-start.6 = (f32[8,128]{1,0:T(8,128)S(1)}, f32[8,128]{1,0:T(8,128)S(1)}, u32[]{:S(2)}, u32[]{:S(2)}) collective-permute-start(f32[8,128]{1,0:T(8,128)S(1)} %add.16), channel_id=1, source_target_pairs={{0,2},{1,3},{2,0},{3,1},{4,6},{5,7},{6,4},{7,5},{8,10},{9,11},{10,... | collective-permute-start | bytes 12296 | tf_op jit(solution)/shard_map/ppermute | solution.py:261
  66.2 3.6 %collective-permute-start.7 = (f32[8,128]{1,0:T(8,128)S(1)}, f32[8,128]{1,0:T(8,128)S(1)}, u32[]{:S(2)}, u32[]{:S(2)}) collective-permute-start(f32[8,128]{1,0:T(8,128)S(1)} %add.17), channel_id=1, source_target_pairs={{0,4},{4,0},{1,5},{5,1},{2,6},{6,2},{3,7},{7,3},{8,12},{12,8},{9,1... | collective-permute-start | bytes 12296 | tf_op jit(solution)/shard_map/ppermute | solution.py:261
  69.8 4.0 %collective-permute-start.8 = (f32[8,128]{1,0:T(8,128)S(1)}, f32[8,128]{1,0:T(8,128)S(1)}, u32[]{:S(2)}, u32[]{:S(2)}) collective-permute-start(f32[8,128]{1,0:T(8,128)S(1)} %add.18), channel_id=1, source_target_pairs={{0,8},{8,0},{16,24},{24,16},{1,9},{9,1},{17,25},{25,17},{2,10},{10... | collective-permute-start | bytes 12296 | tf_op jit(solution)/shard_map/ppermute | solution.py:261
  73.8 4.6 %collective-permute-start.9 = (f32[8,128]{1,0:T(8,128)S(1)}, f32[8,128]{1,0:T(8,128)S(1)}, u32[]{:S(2)}, u32[]{:S(2)}) collective-permute-start(f32[8,128]{1,0:T(8,128)S(1)} %add.19), channel_id=1, source_target_pairs={{0,16},{8,24},{16,0},{24,8},{1,17},{9,25},{17,1},{25,9},{2,18},{10... | collective-permute-start | bytes 12296 | tf_op jit(solution)/shard_map/ppermute | solution.py:261

commit v2 on v1

--- a/solution.py
+++ b/solution.py
@@ -13,30 +13,35 @@
 HIGH = 2 * ITERS
 FIELDS = 5
 LANE_STEP = 16
+UNROLL = 3
 
 VMEM = pl.BlockSpec(memory_space=pltpu.VMEM)
 SMEM = pl.BlockSpec(memory_space=pltpu.SMEM)
 
 
 def z_up(a):
-    return pltpu.roll(a, a.shape[0] - 1, 0)
+    return pltpu.roll(a, a.shape[-2] - 1, a.ndim - 2)
 
 
 def z_down(a):
-    return pltpu.roll(a, 1, 0)
+    return pltpu.roll(a, 1, a.ndim - 2)
 
 
 def y_up(a):
-    return pltpu.roll(a, a.shape[1] - 1, 1)
+    return pltpu.roll(a, a.shape[-1] - 1, a.ndim - 1)
 
 
 def y_down(a):
-    return pltpu.roll(a, 1, 1)
+    return pltpu.roll(a, 1, a.ndim - 1)
 
 
 def reciprocal(a):
     r = pl.reciprocal(a, approx=True)
     return r * (2.0 - a * r)
+
+
+def merged(k, bz):
+    return 3 * (ITERS - k + 1) <= bz
 
 
 def pack_kernel(vx_ref, vz_ref, vy_ref, p_ref, phase_ref, stack_ref, edge_ref):
@@ -69,11 +74,12 @@
 def main_kernel(
     own_ref, above_ref, below_ref, scale_ref, power_ref, rho_table_ref,
     out_vx_ref, out_vz_ref, out_vy_ref, out_p_ref, out_eta_ref, sum_ref,
-    va_ref, vb_ref, p_ref, pre_ref, power_field_ref, rho_ref, weight_ref,
+    va_ref, vb_ref, p_ref, pre_ref, power_field_ref, rho_ref, pre2_ref, power2_field_ref, rho2_ref,
+    weight_ref, weight2_ref,
 ):
     bz, by = own_ref.shape[2:]
     bx = own_ref.shape[0] - LOW - HIGH
-    rows, lanes = 3 * bz, 2 * by
+    lanes = 2 * by
     nx, nz, ny = lax.axis_size("gx"), lax.axis_size("gz"), lax.axis_size("gy")
     ix, iz, iy = lax.axis_index("gx"), lax.axis_index("gz"), lax.axis_index("gy")
 
@@ -115,118 +121,149 @@
                         pre_ref[i, at, to] = pre
                         power_field_ref[i, at, to] = values[1]
                         rho_ref[i, at, to] = values[2]
+        row = lax.broadcasted_iota(jnp.int32, (bz, lanes), 0)
+        for full, half in ((pre_ref, pre2_ref), (power_field_ref, power2_field_ref), (rho_ref, rho2_ref)):
+            half[i, 0:bz] = full[i, 0:bz]
+            half[i, bz : 2 * bz] = jnp.where(row < bz // 2, full[i, bz : 2 * bz], full[i, 2 * bz :])
         return carry
 
     lax.fori_loop(0, bx + LOW + HIGH, unpack, 0)
 
-    r = lax.broadcasted_iota(jnp.int32, (rows, lanes), 0)
-    c = lax.broadcasted_iota(jnp.int32, (rows, lanes), 1)
-    zg = iz * bz + jnp.where(r < 2 * bz, r, r - rows)
-    yg = iy * by + jnp.where(c < by + HIGH, c, c - lanes)
-    filled = (c < by + HIGH) | (c >= lanes - LOW)
-    inside = filled & (zg >= 0) & (zg < nz * bz) & (yg >= 0) & (yg < ny * by)
-    weight_ref[0] = jnp.where(inside, 0.05, 0.0)
-    weight_ref[1] = jnp.where(inside & (zg > 0), 0.05, 0.0)
-    weight_ref[2] = jnp.where(inside & (yg > 0), 0.05, 0.0)
-    weight_ref[3] = jnp.where(inside, 0.0, 1.0)
+    for ref, high in ((weight_ref, 2 * bz), (weight2_ref, bz + bz // 2)):
+        shape = ref.shape[1:]
+        r = lax.broadcasted_iota(jnp.int32, shape, 0)
+        c = lax.broadcasted_iota(jnp.int32, shape, 1)
+        zg = iz * bz + jnp.where(r < high, r, r - shape[0])
+        yg = iy * by + jnp.where(c < by + HIGH, c, c - lanes)
+        filled = (c < by + HIGH) | (c >= lanes - LOW)
+        inside = filled & (zg >= 0) & (zg < nz * bz) & (yg >= 0) & (yg < ny * by)
+        ref[0] = jnp.where(inside, 0.05, 0.0)
+        ref[1] = jnp.where(inside & (zg > 0), 0.05, 0.0)
+        ref[2] = jnp.where(inside & (yg > 0), 0.05, 0.0)
+        ref[3] = jnp.where(inside, 0.0, 1.0)
 
     for k in range(1, ITERS + 1):
         old, new = (va_ref, vb_ref) if k % 2 else (vb_ref, va_ref)
         last = k == ITERS
-
-        def cell(j):
-            vx, vz, vy = old[0, j], old[1, j], old[2, j]
-            rx = old[0, j + 1] - vx
+        rows = 2 * bz if merged(k, bz) else 3 * bz
+        constants = (pre2_ref, power2_field_ref, rho2_ref) if merged(k, bz) else (pre_ref, power_field_ref, rho_ref)
+        weight = weight2_ref if merged(k, bz) else weight_ref
+        narrow = merged(k + 1, bz) and not merged(k, bz)
+        all_rows = pl.ds(0, rows)
+
+        def keep(value):
+            if narrow:
+                row = lax.broadcasted_iota(jnp.int32, (bz, lanes), 0)
+                halo = jnp.where(row < bz // 2, value[..., bz : 2 * bz, :], value[..., 2 * bz :, :])
+                return [(pl.ds(0, bz), value[..., 0:bz, :]), (pl.ds(bz, bz), halo)]
+            return [(all_rows, value)]
+
+        def store(d, j, count, value):
+            for at, part in keep(value):
+                new[d, pl.ds(j, count), at, :] = part
+
+        def cells(j, count):
+            planes = pl.ds(j, count)
+            vx1 = old[0, pl.ds(j, count + 1), all_rows, :]
+            vx = vx1[:count]
+            vz, vy = old[1, planes, all_rows, :], old[2, planes, all_rows, :]
+            p = p_ref[planes, all_rows, :]
+            rx = vx1[1:] - vx
             rz = z_up(vz) - vz
             ry = y_up(vy) - vy
             a = rx - ry
             b = ry - rz
             inv = (a * (a + b) + b * b) * (1.0 / 3.0) + 1.0
-            eta = pre_ref[j] * jnp.exp2(power_field_ref[j] * jnp.log(inv))
+            eta = constants[0][planes] * jnp.exp2(constants[1][planes] * jnp.log(inv))
             quarter = 0.25 * eta
             div = rx + ry + rz
-            p = p_ref[j] - quarter * (div + div)
-            p_ref[j] = p
+            p = p - quarter * (div + div)
             tx, tz, ty = eta * rx - p, eta * rz - p, eta * ry - p
             sz = quarter + z_down(quarter)
             sy = quarter + y_down(quarter)
-            return eta, p, quarter, tx, tz, ty, sz, sy
-
-        def step(j, carry):
+            return vx, vz, vy, eta, p, quarter, tx, tz, ty, sz, sy
+
+        def chunk(j, count, carry, start=False):
+            planes = pl.ds(j, count)
+            vx, vz, vy, eta, p, quarter, tx, tz, ty, sz, sy = cells(j, count)
+            vz0, vy0 = old[1, pl.ds(j - 1, 1), all_rows, :], old[2, pl.ds(j - 1, 1), all_rows, :]
             quarter0, tx0, sz0, sy0, part_z0, part_y0, scale_z0, scale_y0 = carry
-            eta, p, quarter, tx, tz, ty, sz, sy = cell(j)
-            vx, vz, vy = old[0, j], old[1, j], old[2, j]
-            vz0, vy0 = old[1, j - 1], old[2, j - 1]
-            bias = weight_ref[3]
-            sx = quarter + quarter0
-            exz = sz + sz0
-            exy = sy + sy0
+            join = lambda first, rest: jnp.concatenate([first, rest[:-1]], axis=0) if count > 1 else first
+            bias = weight[3:4]
+            sx = quarter + join(quarter0, quarter)
+            exz = sz + join(sz0, sz)
+            exy = sy + join(sy0, sy)
             ezy = sz + y_down(sz)
             fxz = exz * (vx - z_down(vx))
             fxy = exy * (vx - y_down(vx))
-            gzx = exz * (vz - vz0)
-            hyx = exy * (vy - vy0)
+            low_vz, low_vy = join(vz0, vz), join(vy0, vy)
+            gzx = exz * (vz - low_vz)
+            hyx = exy * (vy - low_vy)
             gzy = ezy * (vz - y_down(vz))
             hyz = ezy * (vy - z_down(vy))
-            res_x = (tx - tx0) + ((z_up(fxz) - fxz) + (y_up(fxy) - fxy))
-            new_vx = vx + weight_ref[0] * reciprocal(sx + bias) * res_x
-            new_vz = vz0 + scale_z0 * (part_z0 + gzx)
-            new_vy = vy0 + scale_y0 * (part_y0 + hyx)
-            part_z = (tz - z_down(tz)) - rho_ref[j] + ((y_up(gzy) - gzy) - gzx)
+            res_x = (tx - join(tx0, tx)) + ((z_up(fxz) - fxz) + (y_up(fxy) - fxy))
+            new_vx = vx + weight[0:1] * reciprocal(sx + bias) * res_x
+            part_z = (tz - z_down(tz)) - constants[2][planes] + ((y_up(gzy) - gzy) - gzx)
             part_y = (ty - y_down(ty)) + ((z_up(hyz) - hyz) - hyx)
-            scale_z = weight_ref[1] * reciprocal(sz + bias)
-            scale_y = weight_ref[2] * reciprocal(sy + bias)
+            scale_z = weight[1:2] * reciprocal(sz + bias)
+            scale_y = weight[2:3] * reciprocal(sy + bias)
+            new_vz = low_vz + join(scale_z0, scale_z) * (join(part_z0, part_z) + gzx)
+            new_vy = low_vy + join(scale_y0, scale_y) * (join(part_y0, part_y) + hyx)
             if last:
-                out_vx_ref[j - LOW] = new_vx[0:bz, 0:by]
-                out_p_ref[j - LOW] = p[0:bz, 0:by]
-                out_eta_ref[j - LOW] = eta[0:bz, 0:by]
-                sum_ref[...] += p[0:bz, 0:by]
+                at = pl.ds(j - LOW, count)
+                out_vx_ref[at] = new_vx[:, 0:bz, 0:by]
+                out_p_ref[at] = p[:, 0:bz, 0:by]
+                out_eta_ref[at] = eta[:, 0:bz, 0:by]
+                sum_ref[...] += jnp.sum(p[:, 0:bz, 0:by], axis=0)
+                if not start:
+                    at = pl.ds(j - 1 - LOW, count)
+                    out_vz_ref[at] = new_vz[:, 0:bz, 0:by]
+                    out_vy_ref[at] = new_vy[:, 0:bz, 0:by]
             else:
-                new[0, j] = new_vx
-
-            def finish():
-                if last:
-                    out_vz_ref[j - 1 - LOW] = new_vz[0:bz, 0:by]
-                    out_vy_ref[j - 1 - LOW] = new_vy[0:bz, 0:by]
-                else:
-                    new[1, j - 1] = new_vz
-                    new[2, j - 1] = new_vy
-
-            return (quarter, tx, sz, sy, part_z, part_y, scale_z, scale_y), finish
+                for at, part in keep(p):
+                    p_ref[planes, at, :] = part
+                store(0, j, count, new_vx)
+                if not start:
+                    store(1, j - 1, count, new_vz)
+                    store(2, j - 1, count, new_vy)
+            return tuple(a[-1:] for a in (quarter, tx, sz, sy, part_z, part_y, scale_z, scale_y))
 
         first, count = k, bx + LOW + HIGH - 3 * k
         if last:
             sum_ref[...] = jnp.zeros((bz, by), jnp.float32)
-        eta, p, quarter, tx, tz, ty, sz, sy = cell(first - 1)
-        zero = jnp.zeros((rows, lanes), jnp.float32)
-        carry, _ = step(first, (quarter, tx, sz, sy, zero, zero, zero, zero))
-
-        def loop(j, carry):
-            carry, finish = step(j, carry)
-            finish()
-            return carry
-
-        carry = lax.fori_loop(first + 1, first + count, loop, carry)
+        _, _, _, _, p, quarter, tx, _, _, sz, sy = cells(first - 1, 1)
+        if not last:
+            for at, part in keep(p):
+                p_ref[pl.ds(first - 1, 1), at, :] = part
+        zero = jnp.zeros((1, rows, lanes), jnp.float32)
+        carry = chunk(first, 1, (quarter, tx, sz, sy, zero, zero, zero, zero), start=True)
+        steps, rest = divmod(count - 1, UNROLL)
+        carry = lax.fori_loop(
+            0, steps, lambda s, carry: chunk(first + 1 + s * UNROLL, UNROLL, carry), carry
+        )
+        if rest:
+            carry = chunk(first + 1 + steps * UNROLL, rest, carry)
         j = first + count
         quarter0, tx0, sz0, sy0, part_z0, part_y0, scale_z0, scale_y0 = carry
-        eta, p, quarter, tx, tz, ty, sz, sy = cell(j)
-        gzx = (sz + sz0) * (old[1, j] - old[1, j - 1])
-        hyx = (sy + sy0) * (old[2, j] - old[2, j - 1])
-        new_vz = old[1, j - 1] + scale_z0 * (part_z0 + gzx)
-        new_vy = old[2, j - 1] + scale_y0 * (part_y0 + hyx)
+        _, vz, vy, _, p, quarter, tx, _, _, sz, sy = cells(j, 1)
+        vz0, vy0 = old[1, pl.ds(j - 1, 1), all_rows, :], old[2, pl.ds(j - 1, 1), all_rows, :]
+        new_vz = vz0 + scale_z0 * (part_z0 + (sz + sz0) * (vz - vz0))
+        new_vy = vy0 + scale_y0 * (part_y0 + (sy + sy0) * (vy - vy0))
         if last:
-            out_vz_ref[j - 1 - LOW] = new_vz[0:bz, 0:by]
-            out_vy_ref[j - 1 - LOW] = new_vy[0:bz, 0:by]
+            out_vz_ref[pl.ds(j - 1 - LOW, 1)] = new_vz[:, 0:bz, 0:by]
+            out_vy_ref[pl.ds(j - 1 - LOW, 1)] = new_vy[:, 0:bz, 0:by]
         else:
-            new[1, j - 1] = new_vz
-            new[2, j - 1] = new_vy
+            for at, part in keep(p):
+                p_ref[pl.ds(j, 1), at, :] = part
+            store(1, j - 1, 1, new_vz)
+            store(2, j - 1, 1, new_vy)
 
         if last:
             @pl.when(ix == 0)
             def _():
                 out_vx_ref[0] = jnp.zeros((bz, by), jnp.float32)
         else:
-            plane = jnp.zeros((rows, lanes), jnp.float32)
+            plane = jnp.zeros((3 * bz, lanes), jnp.float32)
 
             @pl.when(ix == 0)
             def _():
@@ -276,6 +313,7 @@
         out_shape=(jax.ShapeDtypeStruct((bx, FIELDS, bz, by), f32), block),
         in_specs=[VMEM] * 5,
         out_specs=(VMEM, VMEM),
+        compiler_params=pltpu.CompilerParams(vmem_limit_bytes=4 * 1024 * 1024),
     )(vel_x, vel_z, vel_y, pressure, phase)
 
     lane = lax.broadcasted_iota(jnp.int32, (bx, bz, by), 2)
@@ -305,7 +343,11 @@
             scratch(deep, rows, lanes),
             scratch(deep, rows, lanes),
             scratch(deep, rows, lanes),
+            scratch(deep, 2 * bz, lanes),
+            scratch(deep, 2 * bz, lanes),
+            scratch(deep, 2 * bz, lanes),
             scratch(4, rows, lanes),
+            scratch(4, 2 * bz, lanes),
         ],
         compiler_params=pltpu.CompilerParams(vmem_limit_bytes=32 * 1024 * 1024),
     )(stack, above, below, visc_scale, power, density)
@@ -317,6 +359,7 @@
         out_shape=block,
         in_specs=[VMEM] * 2,
         out_specs=VMEM,
+        compiler_params=pltpu.CompilerParams(vmem_limit_bytes=4 * 1024 * 1024),
     )(p, total)
     return (vx, vy, vz, p, eta)
 

time: 80.9 us -> 68.3 us (0.84)
  Pallas kernels: 31.3 us -> 16.6 us
  local copies, waits for them, and re-layouts: 0.64 us -> 4.21 us
  other arithmetic: 1.6 us -> 0.09 us
    pallas_call x1, Pallas kernels: 26.7 us -> 14.5 us  [local(): pl.pallas_call(main_kernel, out_shape=(block,) * 5 + (jax.ShapeDtypeStruc...]
    unnamed x10 -> x16, local copies, waits for them, and re-layouts: 0.64 us -> 4.21 us
    pallas_call x1, Pallas kernels: 2.97 us -> 1.34 us  [local(): pl.pallas_call(pack_kernel, out_shape=(jax.ShapeDtypeStruct((bx, FIELDS,...]
    concatenate x1, other arithmetic: 0.93 us -> 0.01 us  [local(): stack = jnp.concatenate([stack, side[:, None]], axis=1)]
    pallas_call x1, Pallas kernels: 1.59 us -> 0.75 us  [local(): pl.pallas_call(lambda *refs: final_kernel(*refs, cells=float(cells)), out...]
where the time goes in v2:
time: 68.3 us; the launch traced here: 67.9 us
  starting transfers between devices  27.2 us (40%)
  waiting for transfers between devices  19 us (28%)
  Pallas kernels  16.6 us (24%)
  local copies, waits for them, and re-layouts  4.21 us (6%)
  between operations  0.75 us (1%)
    ppermute x5, starting transfers between devices, swap_sum(): a = a + lax.ppermute(a, axis, [(i, i ^ bit) for i in range(count)])  15.7 us
    pallas_call x1, Pallas kernels, local(): pl.pallas_call(main_kernel, out_shape=(block,) * 5 + (jax.ShapeDtypeStruc...  14.5 us
    ppermute x5, waiting for transfers between devices, swap_sum(): a = a + lax.ppermute(a, axis, [(i, i ^ bit) for i in range(count)])  9.65 us
    ppermute x4, starting transfers between devices, shift(): lax.ppermute(a, axis, [(i, i + step) for i in range(count) if 0 <= i + st...  8.56 us
    ppermute x4, waiting for transfers between devices, shift(): lax.ppermute(a, axis, [(i, i + step) for i in range(count) if 0 <= i + st...  7.06 us
    unnamed x16, local copies, waits for them, and re-layouts  4.21 us
    ppermute x1, starting transfers between devices, local(): side = lax.ppermute(edge, 'gy', [(0, 1), (1, 0)])  3 us
    ppermute x1, waiting for transfers between devices, local(): side = lax.ppermute(edge, 'gy', [(0, 1), (1, 0)])  2.25 us
  transfers between devices with their start and end apart: 10, of which 9 were waited for; matrix products, arithmetic and copies ran while one was open for 0% of the time, Pallas kernels for 0%

profile of v2, /device:TPU:0, one launch (start us, length us, event | category | flops | bytes accessed | tf_op | source)
XLA Modules:
  0.0 67.9 jit_solution(10696287964227293385)
XLA Ops:
  0.6 0.8 %copy-done = f32[16,8,128]{2,1,0:T(8,128)S(1)} copy-done((f32[16,8,128]{2,1,0:T(8,128)S(1)}, f32[16,8,128]{2,1,0:T(8,128)}, u32[]{:S(2)}) %copy-start) | copy-done | bytes 65560
  1.5 0.8 %copy-done.1 = f32[16,8,128]{2,1,0:T(8,128)S(1)} copy-done((f32[16,8,128]{2,1,0:T(8,128)S(1)}, f32[16,8,128]{2,1,0:T(8,128)}, u32[]{:S(2)}) %copy-start.1) | copy-done | bytes 65560
  2.3 0.8 %copy-done.2 = f32[16,8,128]{2,1,0:T(8,128)S(1)} copy-done((f32[16,8,128]{2,1,0:T(8,128)S(1)}, f32[16,8,128]{2,1,0:T(8,128)}, u32[]{:S(2)}) %copy-start.2) | copy-done | bytes 65560
  3.2 0.8 %copy-done.3 = f32[16,8,128]{2,1,0:T(8,128)S(1)} copy-done((f32[16,8,128]{2,1,0:T(8,128)S(1)}, f32[16,8,128]{2,1,0:T(8,128)}, u32[]{:S(2)}) %copy-start.3) | copy-done | bytes 65560
  4.0 0.8 %copy-done.4 = s32[16,8,128]{2,1,0:T(8,128)S(1)} copy-done((s32[16,8,128]{2,1,0:T(8,128)S(1)}, s32[16,8,128]{2,1,0:T(8,128)}, u32[]{:S(2)}) %copy-start.4) | copy-done | bytes 65560
  4.8 1.3 %shard_map.119 = (f32[16,5,8,128]{3,2,1,0:T(8,128)S(1)}, f32[16,8,128]{2,1,0:T(8,128)S(1)}) custom-call(f32[16,8,128]{2,1,0:T(8,128)S(1)} %copy-done, f32[16,8,128]{2,1,0:T(8,128)S(1)} %copy-done.1, f32[16,8,128]{2,1,0:T(8,128)S(1)} %copy-done.2, f32[16,8,128]{2,1,0:T(8,128)S(1)} %copy-done.3, s32[16,8,128]{2,1,0:T(8,128)S(1)} %copy-done.4), custom_call_target="tpu_custom_call" | custom-call | tf_op jit(solution)/shard_map/pallas_call | solution.py:311
  6.2 3.0 %collective-permute-start = (f32[16,8,128]{2,1,0:T(8,128)S(1)}, f32[16,8,128]{2,1,0:T(8,128)S(1)}, u32[]{:S(2)}, u32[]{:S(2)}) collective-permute-start(f32[16,8,128]{2,1,0:T(8,128)S(1)} %get-tuple-element.14), channel_id=1, source_target_pairs={{0,4},{4,0},{1,5},{5,1},{2,6},{6,2},{3,7},{7,3},{8,12},{12,8},{9,1... | collective-permute-start | bytes 196616 | tf_op jit(solution)/shard_map/ppermute | solution.py:321
  9.2 2.2 %collective-permute-done = f32[16,8,128]{2,1,0:T(8,128)S(1)} collective-permute-done((f32[16,8,128]{2,1,0:T(8,128)S(1)}, f32[16,8,128]{2,1,0:T(8,128)S(1)}, u32[]{:S(2)}, u32[]{:S(2)}) %collective-permute-start) | collective-permute-done | bytes 65568 | tf_op jit(solution)/shard_map/ppermute | solution.py:321
  11.4 1.3 %collective-permute-start.2 = (f32[8,6,8,128]{3,2,1,0:T(8,128)S(1)}, f32[8,6,8,128]{3,2,1,0:T(8,128)S(1)}, u32[]{:S(2)}, u32[]{:S(2)}) collective-permute-start(f32[8,6,8,128]{3,2,1,0:T(8,128)S(1)} %pad_maximum_fusion.1), channel_id=1, source_target_pairs={{8,0},{16,8},{24,16},{9,1},{17,9},{25,17},{10,2},{18,10},{26,18},{... | collective-permute-start | bytes 589832 | tf_op jit(solution)/shard_map/ppermute | solution.py:289
  12.8 4.6 %collective-permute-start.1 = (f32[4,6,8,128]{3,2,1,0:T(8,128)S(1)}, f32[4,6,8,128]{3,2,1,0:T(8,128)S(1)}, u32[]{:S(2)}, u32[]{:S(2)}) collective-permute-start(f32[4,6,8,128]{3,2,1,0:T(8,128)S(1)} %pad_maximum_fusion.2), channel_id=1, source_target_pairs={{0,8},{8,16},{16,24},{1,9},{9,17},{17,25},{2,10},{10,18},{18,26},{... | collective-permute-start | bytes 294920 | tf_op jit(solution)/shard_map/ppermute | solution.py:289
  17.4 2.2 %collective-permute-done.1 = f32[4,6,8,128]{3,2,1,0:T(8,128)S(1)} collective-permute-done((f32[4,6,8,128]{3,2,1,0:T(8,128)S(1)}, f32[4,6,8,128]{3,2,1,0:T(8,128)S(1)}, u32[]{:S(2)}, u32[]{:S(2)}) %collective-permute-start.1) | collective-permute-done | bytes 98336 | tf_op jit(solution)/shard_map/ppermute | solution.py:289
  19.7 1.3 %collective-permute-start.4 = (f32[28,6,8,128]{3,2,1,0:T(8,128)S(1)}, f32[28,6,8,128]{3,2,1,0:T(8,128)S(1)}, u32[]{:S(2)}, u32[]{:S(2)}) collective-permute-start(f32[28,6,8,128]{3,2,1,0:T(8,128)S(1)} %pad_maximum_fusion.own_ref), channel_id=1, source_target_pairs={{0,1},{1,2},{2,3},{4,5},{5,6},{6,7},{8,9},{9,10},{10,11},{12,13},{... | collective-permute-start | bytes 2064392 | tf_op jit(solution)/shard_map/ppermute | solution.py:289
  21.0 1.3 %collective-permute-start.3 = (f32[28,6,8,128]{3,2,1,0:T(8,128)S(1)}, f32[28,6,8,128]{3,2,1,0:T(8,128)S(1)}, u32[]{:S(2)}, u32[]{:S(2)}) collective-permute-start(f32[28,6,8,128]{3,2,1,0:T(8,128)S(1)} %pad_maximum_fusion.own_ref), channel_id=1, source_target_pairs={{1,0},{2,1},{3,2},{5,4},{6,5},{7,6},{9,8},{10,9},{11,10},{13,12},{... | collective-permute-start | bytes 2064392 | tf_op jit(solution)/shard_map/ppermute | solution.py:289
  22.7 4.5 %collective-permute-done.3.above_ref = f32[28,6,8,128]{3,2,1,0:T(8,128)S(1)} collective-permute-done((f32[28,6,8,128]{3,2,1,0:T(8,128)S(1)}, f32[28,6,8,128]{3,2,1,0:T(8,128)S(1)}, u32[]{:S(2)}, u32[]{:S(2)}) %collective-permute-start.3) | collective-permute-done | bytes 688160 | tf_op jit(solution)/shard_map/ppermute | solution.py:289
  27.2 14.5 %shard_map.120 = (f32[16,8,128]{2,1,0:T(8,128)}, f32[16,8,128]{2,1,0:T(8,128)}, f32[16,8,128]{2,1,0:T(8,128)}, f32[16,8,128]{2,1,0:T(8,128)S(1)}, f32[16,8,128]{2,1,0:T(8,128)}, /*index=5*/f32[8,128]{1,0:T(8,128)S(1)}) custom-call(f32[28,6,8,128]{3,2,1,0:T(8,128)S(1)} %pad_maximum_fusion.own_ref, f32[28,6,8,128]{3,2,1,0:T(8,128)S(1)} %collective-permute-done.3.above_ref, ...), custom_call_target="tpu_custom_call" | custom-call | tf_op jit(solution)/shard_map/pallas_call | solution.py:334
  41.8 8.7 %collective-permute-start.5 = (f32[8,128]{1,0:T(8,128)S(1)}, f32[8,128]{1,0:T(8,128)S(1)}, u32[]{:S(2)}, u32[]{:S(2)}) collective-permute-start(f32[8,128]{1,0:T(8,128)S(1)} %get-tuple-element.19), channel_id=1, source_target_pairs={{0,1},{1,0},{2,3},{3,2},{4,5},{5,4},{6,7},{7,6},{8,9},{9,8},{10,11... | collective-permute-start | bytes 12296 | tf_op jit(solution)/shard_map/ppermute | solution.py:298
  50.5 0.8 %collective-permute-done.5 = f32[8,128]{1,0:T(8,128)S(1)} collective-permute-done((f32[8,128]{1,0:T(8,128)S(1)}, f32[8,128]{1,0:T(8,128)S(1)}, u32[]{:S(2)}, u32[]{:S(2)}) %collective-permute-start.5) | collective-permute-done | bytes 4128 | tf_op jit(solution)/shard_map/ppermute | solution.py:298
  51.4 3.5 %collective-permute-done.6 = f32[8,128]{1,0:T(8,128)S(1)} collective-permute-done((f32[8,128]{1,0:T(8,128)S(1)}, f32[8,128]{1,0:T(8,128)S(1)}, u32[]{:S(2)}, u32[]{:S(2)}) %collective-permute-start.6) | collective-permute-done | bytes 4128 | tf_op jit(solution)/shard_map/ppermute | solution.py:298
  54.9 1.5 %collective-permute-start.7 = (f32[8,128]{1,0:T(8,128)S(1)}, f32[8,128]{1,0:T(8,128)S(1)}, u32[]{:S(2)}, u32[]{:S(2)}) collective-permute-start(f32[8,128]{1,0:T(8,128)S(1)} %add.17), channel_id=1, source_target_pairs={{0,4},{4,0},{1,5},{5,1},{2,6},{6,2},{3,7},{7,3},{8,12},{12,8},{9,1... | collective-permute-start | bytes 12296 | tf_op jit(solution)/shard_map/ppermute | solution.py:298
  56.4 2.1 %collective-permute-done.7 = f32[8,128]{1,0:T(8,128)S(1)} collective-permute-done((f32[8,128]{1,0:T(8,128)S(1)}, f32[8,128]{1,0:T(8,128)S(1)}, u32[]{:S(2)}, u32[]{:S(2)}) %collective-permute-start.7) | collective-permute-done | bytes 4128 | tf_op jit(solution)/shard_map/ppermute | solution.py:298
  58.5 2.4 %collective-permute-start.8 = (f32[8,128]{1,0:T(8,128)S(1)}, f32[8,128]{1,0:T(8,128)S(1)}, u32[]{:S(2)}, u32[]{:S(2)}) collective-permute-start(f32[8,128]{1,0:T(8,128)S(1)} %add.18), channel_id=1, source_target_pairs={{0,8},{8,0},{16,24},{24,16},{1,9},{9,1},{17,25},{25,17},{2,10},{10... | collective-permute-start | bytes 12296 | tf_op jit(solution)/shard_map/ppermute | solution.py:298
  60.9 1.6 %collective-permute-done.8 = f32[8,128]{1,0:T(8,128)S(1)} collective-permute-done((f32[8,128]{1,0:T(8,128)S(1)}, f32[8,128]{1,0:T(8,128)S(1)}, u32[]{:S(2)}, u32[]{:S(2)}) %collective-permute-start.8) | collective-permute-done | bytes 4128 | tf_op jit(solution)/shard_map/ppermute | solution.py:298
  62.5 3.0 %collective-permute-start.9 = (f32[8,128]{1,0:T(8,128)S(1)}, f32[8,128]{1,0:T(8,128)S(1)}, u32[]{:S(2)}, u32[]{:S(2)}) collective-permute-start(f32[8,128]{1,0:T(8,128)S(1)} %add.19), channel_id=1, source_target_pairs={{0,16},{8,24},{16,0},{24,8},{1,17},{9,25},{17,1},{25,9},{2,18},{10... | collective-permute-start | bytes 12296 | tf_op jit(solution)/shard_map/ppermute | solution.py:298
  65.5 1.6 %collective-permute-done.9 = f32[8,128]{1,0:T(8,128)S(1)} collective-permute-done((f32[8,128]{1,0:T(8,128)S(1)}, f32[8,128]{1,0:T(8,128)S(1)}, u32[]{:S(2)}, u32[]{:S(2)}) %collective-permute-start.9) | collective-permute-done | bytes 4128 | tf_op jit(solution)/shard_map/ppermute | solution.py:298
  (24 shorter events, 1.3 us)
Async XLA Ops:
  0.6 0.8 %copy-start = (f32[16,8,128]{2,1,0:T(8,128)S(1)}, f32[16,8,128]{2,1,0:T(8,128)}, u32[]{:S(2)}) copy-start(f32[16,8,128]{2,1,0:T(8,128)} %vx_ref.1) | copy-start | bytes 196612
  1.5 0.8 %copy-start.1 = (f32[16,8,128]{2,1,0:T(8,128)S(1)}, f32[16,8,128]{2,1,0:T(8,128)}, u32[]{:S(2)}) copy-start(f32[16,8,128]{2,1,0:T(8,128)} %vz_ref.1) | copy-start | bytes 196612
  2.3 0.8 %copy-start.2 = (f32[16,8,128]{2,1,0:T(8,128)S(1)}, f32[16,8,128]{2,1,0:T(8,128)}, u32[]{:S(2)}) copy-start(f32[16,8,128]{2,1,0:T(8,128)} %vy_ref.1) | copy-start | bytes 196612
  3.2 0.8 %copy-start.3 = (f32[16,8,128]{2,1,0:T(8,128)S(1)}, f32[16,8,128]{2,1,0:T(8,128)}, u32[]{:S(2)}) copy-start(f32[16,8,128]{2,1,0:T(8,128)} %p_ref.1) | copy-start | bytes 196612
  4.0 0.8 %copy-start.4 = (s32[16,8,128]{2,1,0:T(8,128)S(1)}, s32[16,8,128]{2,1,0:T(8,128)}, u32[]{:S(2)}) copy-start(s32[16,8,128]{2,1,0:T(8,128)} %phase_ref.1) | copy-start | bytes 196612
  6.2 5.2 %collective-permute-start = (f32[16,8,128]{2,1,0:T(8,128)S(1)}, f32[16,8,128]{2,1,0:T(8,128)S(1)}, u32[]{:S(2)}, u32[]{:S(2)}) collective-permute-start(f32[16,8,128]{2,1,0:T(8,128)S(1)} %get-tuple-element.14), channel_id=1, source_target_pairs={{0,4},{4,0},{1,5},{5,1},{2,6},{6,2},{3,7},{7,3},{8,12},{12,8},{9,1... | collective-permute-start | bytes 196616 | tf_op jit(solution)/shard_map/ppermute | solution.py:321
  11.4 8.2 %collective-permute-start.2 = (f32[8,6,8,128]{3,2,1,0:T(8,128)S(1)}, f32[8,6,8,128]{3,2,1,0:T(8,128)S(1)}, u32[]{:S(2)}, u32[]{:S(2)}) collective-permute-start(f32[8,6,8,128]{3,2,1,0:T(8,128)S(1)} %pad_maximum_fusion.1), channel_id=1, source_target_pairs={{8,0},{16,8},{24,16},{9,1},{17,9},{25,17},{10,2},{18,10},{26,18},{... | collective-permute-start | bytes 589832 | tf_op jit(solution)/shard_map/ppermute | solution.py:289
  12.8 9.6 %copy-start.7 = (f32[4]{0:T(128)S(1)}, f32[4]{0:T(128)}, u32[]{:S(2)}) copy-start(f32[4]{0:T(128)} %param.14) | copy-start | bytes 52
  12.8 6.8 %collective-permute-start.1 = (f32[4,6,8,128]{3,2,1,0:T(8,128)S(1)}, f32[4,6,8,128]{3,2,1,0:T(8,128)S(1)}, u32[]{:S(2)}, u32[]{:S(2)}) collective-permute-start(f32[4,6,8,128]{3,2,1,0:T(8,128)S(1)} %pad_maximum_fusion.2), channel_id=1, source_target_pairs={{0,8},{8,16},{16,24},{1,9},{9,17},{17,25},{2,10},{10,18},{18,26},{... | collective-permute-start | bytes 294920 | tf_op jit(solution)/shard_map/ppermute | solution.py:289
  19.7 7.6 %copy-start.5 = (f32[4]{0:T(128)S(1)}, f32[4]{0:T(128)}, u32[]{:S(2)}) copy-start(f32[4]{0:T(128)} %scale_ref.1) | copy-start | bytes 52
  19.7 7.5 %copy-start.6 = (f32[4]{0:T(128)S(1)}, f32[4]{0:T(128)}, u32[]{:S(2)}) copy-start(f32[4]{0:T(128)} %rho_table_ref.1) | copy-start | bytes 52
  19.7 3.1 %collective-permute-start.4 = (f32[28,6,8,128]{3,2,1,0:T(8,128)S(1)}, f32[28,6,8,128]{3,2,1,0:T(8,128)S(1)}, u32[]{:S(2)}, u32[]{:S(2)}) collective-permute-start(f32[28,6,8,128]{3,2,1,0:T(8,128)S(1)} %pad_maximum_fusion.own_ref), channel_id=1, source_target_pairs={{0,1},{1,2},{2,3},{4,5},{5,6},{6,7},{8,9},{9,10},{10,11},{12,13},{... | collective-permute-start | bytes 2064392 | tf_op jit(solution)/shard_map/ppermute | solution.py:289
  21.0 6.2 %collective-permute-start.3 = (f32[28,6,8,128]{3,2,1,0:T(8,128)S(1)}, f32[28,6,8,128]{3,2,1,0:T(8,128)S(1)}, u32[]{:S(2)}, u32[]{:S(2)}) collective-permute-start(f32[28,6,8,128]{3,2,1,0:T(8,128)S(1)} %pad_maximum_fusion.own_ref), channel_id=1, source_target_pairs={{1,0},{2,1},{3,2},{5,4},{6,5},{7,6},{9,8},{10,9},{11,10},{13,12},{... | collective-permute-start | bytes 2064392 | tf_op jit(solution)/shard_map/ppermute | solution.py:289
  41.8 9.5 %collective-permute-start.5 = (f32[8,128]{1,0:T(8,128)S(1)}, f32[8,128]{1,0:T(8,128)S(1)}, u32[]{:S(2)}, u32[]{:S(2)}) collective-permute-start(f32[8,128]{1,0:T(8,128)S(1)} %get-tuple-element.19), channel_id=1, source_target_pairs={{0,1},{1,0},{2,3},{3,2},{4,5},{5,4},{6,7},{7,6},{8,9},{9,8},{10,11... | collective-permute-start | bytes 12296 | tf_op jit(solution)/shard_map/ppermute | solution.py:298
  51.3 3.6 %collective-permute-start.6 = (f32[8,128]{1,0:T(8,128)S(1)}, f32[8,128]{1,0:T(8,128)S(1)}, u32[]{:S(2)}, u32[]{:S(2)}) collective-permute-start(f32[8,128]{1,0:T(8,128)S(1)} %add.16), channel_id=1, source_target_pairs={{0,2},{1,3},{2,0},{3,1},{4,6},{5,7},{6,4},{7,5},{8,10},{9,11},{10,... | collective-permute-start | bytes 12296 | tf_op jit(solution)/shard_map/ppermute | solution.py:298
  54.9 3.6 %collective-permute-start.7 = (f32[8,128]{1,0:T(8,128)S(1)}, f32[8,128]{1,0:T(8,128)S(1)}, u32[]{:S(2)}, u32[]{:S(2)}) collective-permute-start(f32[8,128]{1,0:T(8,128)S(1)} %add.17), channel_id=1, source_target_pairs={{0,4},{4,0},{1,5},{5,1},{2,6},{6,2},{3,7},{7,3},{8,12},{12,8},{9,1... | collective-permute-start | bytes 12296 | tf_op jit(solution)/shard_map/ppermute | solution.py:298
  58.5 4.0 %collective-permute-start.8 = (f32[8,128]{1,0:T(8,128)S(1)}, f32[8,128]{1,0:T(8,128)S(1)}, u32[]{:S(2)}, u32[]{:S(2)}) collective-permute-start(f32[8,128]{1,0:T(8,128)S(1)} %add.18), channel_id=1, source_target_pairs={{0,8},{8,0},{16,24},{24,16},{1,9},{9,1},{17,25},{25,17},{2,10},{10... | collective-permute-start | bytes 12296 | tf_op jit(solution)/shard_map/ppermute | solution.py:298
  62.5 4.6 %collective-permute-start.9 = (f32[8,128]{1,0:T(8,128)S(1)}, f32[8,128]{1,0:T(8,128)S(1)}, u32[]{:S(2)}, u32[]{:S(2)}) collective-permute-start(f32[8,128]{1,0:T(8,128)S(1)} %add.19), channel_id=1, source_target_pairs={{0,16},{8,24},{16,0},{24,8},{1,17},{9,25},{17,1},{25,9},{2,18},{10... | collective-permute-start | bytes 12296 | tf_op jit(solution)/shard_map/ppermute | solution.py:298

commit v3 on v2

--- a/solution.py
+++ b/solution.py
@@ -289,17 +289,6 @@
     return lax.ppermute(a, axis, [(i, i + step) for i in range(count) if 0 <= i + step < count])
 
 
-def swap_sum(a, axis):
-    count = lax.axis_size(axis)
-    if count & (count - 1):
-        return lax.psum(a, axis)
-    bit = 1
-    while bit < count:
-        a = a + lax.ppermute(a, axis, [(i, i ^ bit) for i in range(count)])
-        bit *= 2
-    return a
-
-
 def local(vel_x, vel_y, vel_z, pressure, phase, visc_scale, power_n, density):
     bx, bz, by = pressure.shape
     f32 = jnp.float32
@@ -352,8 +341,9 @@
         compiler_params=pltpu.CompilerParams(vmem_limit_bytes=32 * 1024 * 1024),
     )(stack, above, below, visc_scale, power, density)
 
-    for axis in ("gz", "gy", "gx"):
-        total = swap_sum(total, axis)
+    devices = math.prod(counts)
+    total = jnp.broadcast_to(jnp.sum(total, axis=0, keepdims=True), (devices, by))
+    total = lax.all_to_all(total, ("gx", "gy", "gz"), 0, 0, tiled=True)
     p = pl.pallas_call(
         lambda *refs: final_kernel(*refs, cells=float(cells)),
         out_shape=block,

time: 68.3 us -> 64 us (0.937)
  blocking collectives: 0 us -> 21 us
  starting transfers between devices: 27.2 us -> 11.6 us
  waiting for transfers between devices: 19 us -> 9.3 us
    all_to_all x0 -> x1, blocking collectives: none -> 21 us  [local(): total = lax.all_to_all(total, ('gx', 'gy', 'gz'), 0, 0, tiled=True)]
    ppermute x5 -> x0, starting transfers between devices: 15.7 us -> none  [swap_sum(): a = a + lax.ppermute(a, axis, [(i, i ^ bit) for i in range(count)])]
    ppermute x5 -> x0, waiting for transfers between devices: 9.65 us -> none  [swap_sum(): a = a + lax.ppermute(a, axis, [(i, i ^ bit) for i in range(count)])]
  transfers between devices with their start and end apart: 10 -> 5, of which waited for: 9 -> 4; matrix products, arithmetic and copies ran while one was open for 0% -> 0% of each run, Pallas kernels for 0% -> 0%
where the time goes in v3:
time: 64 us; the launch traced here: 63.6 us
  blocking collectives  21 us (33%)
  Pallas kernels  16.6 us (26%)
  starting transfers between devices  11.6 us (18%)
  waiting for transfers between devices  9.3 us (15%)
  local copies, waits for them, and re-layouts  4.22 us (7%)
  between operations  0.75 us (1%)
    all_to_all x1, blocking collectives, local(): total = lax.all_to_all(total, ('gx', 'gy', 'gz'), 0, 0, tiled=True)  21 us
    pallas_call x1, Pallas kernels, local(): pl.pallas_call(main_kernel, out_shape=(block,) * 5 + (jax.ShapeDtypeStruc...  14.5 us
    ppermute x4, starting transfers between devices, shift(): lax.ppermute(a, axis, [(i, i + step) for i in range(count) if 0 <= i + st...  8.56 us
    ppermute x4, waiting for transfers between devices, shift(): lax.ppermute(a, axis, [(i, i + step) for i in range(count) if 0 <= i + st...  7.06 us
    unnamed x16, local copies, waits for them, and re-layouts  4.21 us
    ppermute x1, starting transfers between devices, local(): side = lax.ppermute(edge, 'gy', [(0, 1), (1, 0)])  3 us
    ppermute x1, waiting for transfers between devices, local(): side = lax.ppermute(edge, 'gy', [(0, 1), (1, 0)])  2.25 us
    pallas_call x1, Pallas kernels, local(): pl.pallas_call(pack_kernel, out_shape=(jax.ShapeDtypeStruct((bx, FIELDS,...  1.34 us
  transfers between devices with their start and end apart: 5, of which 4 were waited for; matrix products, arithmetic and copies ran while one was open for 0% of the time, Pallas kernels for 0%

profile of v3, /device:TPU:0, one launch (start us, length us, event | category | flops | bytes accessed | tf_op | source)
XLA Modules:
  0.0 63.6 jit_solution(12490257143767674703)
XLA Ops:
  0.6 0.0 copy-start
  0.6 0.8 %copy-done = f32[16,8,128]{2,1,0:T(8,128)S(1)} copy-done((f32[16,8,128]{2,1,0:T(8,128)S(1)}, f32[16,8,128]{2,1,0:T(8,128)}, u32[]{:S(2)}) %copy-start) | copy-done | bytes 65560
  1.5 0.8 %copy-done.1 = f32[16,8,128]{2,1,0:T(8,128)S(1)} copy-done((f32[16,8,128]{2,1,0:T(8,128)S(1)}, f32[16,8,128]{2,1,0:T(8,128)}, u32[]{:S(2)}) %copy-start.1) | copy-done | bytes 65560
  2.3 0.8 %copy-done.2 = f32[16,8,128]{2,1,0:T(8,128)S(1)} copy-done((f32[16,8,128]{2,1,0:T(8,128)S(1)}, f32[16,8,128]{2,1,0:T(8,128)}, u32[]{:S(2)}) %copy-start.2) | copy-done | bytes 65560
  3.2 0.8 %copy-done.3 = f32[16,8,128]{2,1,0:T(8,128)S(1)} copy-done((f32[16,8,128]{2,1,0:T(8,128)S(1)}, f32[16,8,128]{2,1,0:T(8,128)}, u32[]{:S(2)}) %copy-start.3) | copy-done | bytes 65560
  4.0 0.8 %copy-done.4 = s32[16,8,128]{2,1,0:T(8,128)S(1)} copy-done((s32[16,8,128]{2,1,0:T(8,128)S(1)}, s32[16,8,128]{2,1,0:T(8,128)}, u32[]{:S(2)}) %copy-start.4) | copy-done | bytes 65560
  4.8 1.3 %shard_map.119 = (f32[16,5,8,128]{3,2,1,0:T(8,128)S(1)}, f32[16,8,128]{2,1,0:T(8,128)S(1)}) custom-call(f32[16,8,128]{2,1,0:T(8,128)S(1)} %copy-done, f32[16,8,128]{2,1,0:T(8,128)S(1)} %copy-done.1, f32[16,8,128]{2,1,0:T(8,128)S(1)} %copy-done.2, f32[16,8,128]{2,1,0:T(8,128)S(1)} %copy-done.3, s32[16,8,128]{2,1,0:T(8,128)S(1)} %copy-done.4), custom_call_target="tpu_custom_call" | custom-call | tf_op jit(solution)/shard_map/pallas_call | solution.py:300
  6.2 3.0 %collective-permute-start = (f32[16,8,128]{2,1,0:T(8,128)S(1)}, f32[16,8,128]{2,1,0:T(8,128)S(1)}, u32[]{:S(2)}, u32[]{:S(2)}) collective-permute-start(f32[16,8,128]{2,1,0:T(8,128)S(1)} %get-tuple-element.14), channel_id=1, source_target_pairs={{0,4},{4,0},{1,5},{5,1},{2,6},{6,2},{3,7},{7,3},{8,12},{12,8},{9,1... | collective-permute-start | bytes 196616 | tf_op jit(solution)/shard_map/ppermute | solution.py:310
  9.2 2.2 %collective-permute-done = f32[16,8,128]{2,1,0:T(8,128)S(1)} collective-permute-done((f32[16,8,128]{2,1,0:T(8,128)S(1)}, f32[16,8,128]{2,1,0:T(8,128)S(1)}, u32[]{:S(2)}, u32[]{:S(2)}) %collective-permute-start) | collective-permute-done | bytes 65568 | tf_op jit(solution)/shard_map/ppermute | solution.py:310
  11.4 1.3 %collective-permute-start.2 = (f32[8,6,8,128]{3,2,1,0:T(8,128)S(1)}, f32[8,6,8,128]{3,2,1,0:T(8,128)S(1)}, u32[]{:S(2)}, u32[]{:S(2)}) collective-permute-start(f32[8,6,8,128]{3,2,1,0:T(8,128)S(1)} %pad_maximum_fusion.1), channel_id=1, source_target_pairs={{8,0},{16,8},{24,16},{9,1},{17,9},{25,17},{10,2},{18,10},{26,18},{... | collective-permute-start | bytes 589832 | tf_op jit(solution)/shard_map/ppermute | solution.py:289
  12.8 0.0 copy-start.7
  12.8 4.6 %collective-permute-start.1 = (f32[4,6,8,128]{3,2,1,0:T(8,128)S(1)}, f32[4,6,8,128]{3,2,1,0:T(8,128)S(1)}, u32[]{:S(2)}, u32[]{:S(2)}) collective-permute-start(f32[4,6,8,128]{3,2,1,0:T(8,128)S(1)} %pad_maximum_fusion.2), channel_id=1, source_target_pairs={{0,8},{8,16},{16,24},{1,9},{9,17},{17,25},{2,10},{10,18},{18,26},{... | collective-permute-start | bytes 294920 | tf_op jit(solution)/shard_map/ppermute | solution.py:289
  17.4 2.2 %collective-permute-done.1 = f32[4,6,8,128]{3,2,1,0:T(8,128)S(1)} collective-permute-done((f32[4,6,8,128]{3,2,1,0:T(8,128)S(1)}, f32[4,6,8,128]{3,2,1,0:T(8,128)S(1)}, u32[]{:S(2)}, u32[]{:S(2)}) %collective-permute-start.1) | collective-permute-done | bytes 98336 | tf_op jit(solution)/shard_map/ppermute | solution.py:289
  19.6 0.0 collective-permute-done.2
  19.7 0.0 copy-start.5
  19.7 0.0 copy-start.6
  19.7 1.3 %collective-permute-start.4 = (f32[28,6,8,128]{3,2,1,0:T(8,128)S(1)}, f32[28,6,8,128]{3,2,1,0:T(8,128)S(1)}, u32[]{:S(2)}, u32[]{:S(2)}) collective-permute-start(f32[28,6,8,128]{3,2,1,0:T(8,128)S(1)} %pad_maximum_fusion.own_ref), channel_id=1, source_target_pairs={{0,1},{1,2},{2,3},{4,5},{5,6},{6,7},{8,9},{9,10},{10,11},{12,13},{... | collective-permute-start | bytes 2064392 | tf_op jit(solution)/shard_map/ppermute | solution.py:289
  21.0 1.3 %collective-permute-start.3 = (f32[28,6,8,128]{3,2,1,0:T(8,128)S(1)}, f32[28,6,8,128]{3,2,1,0:T(8,128)S(1)}, u32[]{:S(2)}, u32[]{:S(2)}) collective-permute-start(f32[28,6,8,128]{3,2,1,0:T(8,128)S(1)} %pad_maximum_fusion.own_ref), channel_id=1, source_target_pairs={{1,0},{2,1},{3,2},{5,4},{6,5},{7,6},{9,8},{10,9},{11,10},{13,12},{... | collective-permute-start | bytes 2064392 | tf_op jit(solution)/shard_map/ppermute | solution.py:289
  22.3 0.0 copy-done.7
  22.4 0.4 collective-permute-done.4.below_ref
  22.7 4.5 %collective-permute-done.3.above_ref = f32[28,6,8,128]{3,2,1,0:T(8,128)S(1)} collective-permute-done((f32[28,6,8,128]{3,2,1,0:T(8,128)S(1)}, f32[28,6,8,128]{3,2,1,0:T(8,128)S(1)}, u32[]{:S(2)}, u32[]{:S(2)}) %collective-permute-start.3) | collective-permute-done | bytes 688160 | tf_op jit(solution)/shard_map/ppermute | solution.py:289
  27.2 14.5 %shard_map.120 = (f32[16,8,128]{2,1,0:T(8,128)}, f32[16,8,128]{2,1,0:T(8,128)}, f32[16,8,128]{2,1,0:T(8,128)}, f32[16,8,128]{2,1,0:T(8,128)S(1)}, f32[16,8,128]{2,1,0:T(8,128)}, /*index=5*/f32[8,128]{1,0:T(8,128)S(1)}) custom-call(f32[28,6,8,128]{3,2,1,0:T(8,128)S(1)} %pad_maximum_fusion.own_ref, f32[28,6,8,128]{3,2,1,0:T(8,128)S(1)} %collective-permute-done.3.above_ref, ...), custom_call_target="tpu_custom_call" | custom-call | tf_op jit(solution)/shard_map/pallas_call | solution.py:323
  41.8 21.0 %all_to_all.8 = f32[32,1,128]{2,1,0:T(1,128)S(1)} all-to-all(f32[32,1,128]{2,1,0:T(1,128)S(1)} %broadcast_in_dim.10), channel_id=1, replica_groups=mesh['gx'=4,'gy'=2,'gz'=4] {'gx','gy','gz'}, dimensions={0} | all-to-all | bytes 32768 | tf_op jit(solution)/shard_map/all_to_all | solution.py:346
  62.8 0.8 %shard_map.121 = f32[16,8,128]{2,1,0:T(8,128)} custom-call(f32[16,8,128]{2,1,0:T(8,128)S(1)} %get-tuple-element.18.refs_0_, f32[32,128]{1,0:T(8,128)S(1)} %bitcast.2), custom_call_target="tpu_custom_call" | custom-call | tf_op jit(solution)/shard_map/pallas_call | solution.py:347
  (12 shorter events, 0.1 us)
Async XLA Ops:
  0.6 0.8 %copy-start = (f32[16,8,128]{2,1,0:T(8,128)S(1)}, f32[16,8,128]{2,1,0:T(8,128)}, u32[]{:S(2)}) copy-start(f32[16,8,128]{2,1,0:T(8,128)} %vx_ref.1) | copy-start | bytes 196612
  1.5 0.8 %copy-start.1 = (f32[16,8,128]{2,1,0:T(8,128)S(1)}, f32[16,8,128]{2,1,0:T(8,128)}, u32[]{:S(2)}) copy-start(f32[16,8,128]{2,1,0:T(8,128)} %vz_ref.1) | copy-start | bytes 196612
  2.3 0.8 %copy-start.2 = (f32[16,8,128]{2,1,0:T(8,128)S(1)}, f32[16,8,128]{2,1,0:T(8,128)}, u32[]{:S(2)}) copy-start(f32[16,8,128]{2,1,0:T(8,128)} %vy_ref.1) | copy-start | bytes 196612
  3.2 0.8 %copy-start.3 = (f32[16,8,128]{2,1,0:T(8,128)S(1)}, f32[16,8,128]{2,1,0:T(8,128)}, u32[]{:S(2)}) copy-start(f32[16,8,128]{2,1,0:T(8,128)} %p_ref.1) | copy-start | bytes 196612
  4.0 0.8 %copy-start.4 = (s32[16,8,128]{2,1,0:T(8,128)S(1)}, s32[16,8,128]{2,1,0:T(8,128)}, u32[]{:S(2)}) copy-start(s32[16,8,128]{2,1,0:T(8,128)} %phase_ref.1) | copy-start | bytes 196612
  6.2 5.2 %collective-permute-start = (f32[16,8,128]{2,1,0:T(8,128)S(1)}, f32[16,8,128]{2,1,0:T(8,128)S(1)}, u32[]{:S(2)}, u32[]{:S(2)}) collective-permute-start(f32[16,8,128]{2,1,0:T(8,128)S(1)} %get-tuple-element.14), channel_id=1, source_target_pairs={{0,4},{4,0},{1,5},{5,1},{2,6},{6,2},{3,7},{7,3},{8,12},{12,8},{9,1... | collective-permute-start | bytes 196616 | tf_op jit(solution)/shard_map/ppermute | solution.py:310
  11.4 8.2 %collective-permute-start.2 = (f32[8,6,8,128]{3,2,1,0:T(8,128)S(1)}, f32[8,6,8,128]{3,2,1,0:T(8,128)S(1)}, u32[]{:S(2)}, u32[]{:S(2)}) collective-permute-start(f32[8,6,8,128]{3,2,1,0:T(8,128)S(1)} %pad_maximum_fusion.1), channel_id=1, source_target_pairs={{8,0},{16,8},{24,16},{9,1},{17,9},{25,17},{10,2},{18,10},{26,18},{... | collective-permute-start | bytes 589832 | tf_op jit(solution)/shard_map/ppermute | solution.py:289
  12.8 9.6 %copy-start.7 = (f32[4]{0:T(128)S(1)}, f32[4]{0:T(128)}, u32[]{:S(2)}) copy-start(f32[4]{0:T(128)} %param.14) | copy-start | bytes 52
  12.8 6.8 %collective-permute-start.1 = (f32[4,6,8,128]{3,2,1,0:T(8,128)S(1)}, f32[4,6,8,128]{3,2,1,0:T(8,128)S(1)}, u32[]{:S(2)}, u32[]{:S(2)}) collective-permute-start(f32[4,6,8,128]{3,2,1,0:T(8,128)S(1)} %pad_maximum_fusion.2), channel_id=1, source_target_pairs={{0,8},{8,16},{16,24},{1,9},{9,17},{17,25},{2,10},{10,18},{18,26},{... | collective-permute-start | bytes 294920 | tf_op jit(solution)/shard_map/ppermute | solution.py:289
  19.7 7.6 %copy-start.5 = (f32[4]{0:T(128)S(1)}, f32[4]{0:T(128)}, u32[]{:S(2)}) copy-start(f32[4]{0:T(128)} %scale_ref.1) | copy-start | bytes 52
  19.7 7.5 %copy-start.6 = (f32[4]{0:T(128)S(1)}, f32[4]{0:T(128)}, u32[]{:S(2)}) copy-start(f32[4]{0:T(128)} %rho_table_ref.1) | copy-start | bytes 52
  19.7 3.1 %collective-permute-start.4 = (f32[28,6,8,128]{3,2,1,0:T(8,128)S(1)}, f32[28,6,8,128]{3,2,1,0:T(8,128)S(1)}, u32[]{:S(2)}, u32[]{:S(2)}) collective-permute-start(f32[28,6,8,128]{3,2,1,0:T(8,128)S(1)} %pad_maximum_fusion.own_ref), channel_id=1, source_target_pairs={{0,1},{1,2},{2,3},{4,5},{5,6},{6,7},{8,9},{9,10},{10,11},{12,13},{... | collective-permute-start | bytes 2064392 | tf_op jit(solution)/shard_map/ppermute | solution.py:289
  21.0 6.2 %collective-permute-start.3 = (f32[28,6,8,128]{3,2,1,0:T(8,128)S(1)}, f32[28,6,8,128]{3,2,1,0:T(8,128)S(1)}, u32[]{:S(2)}, u32[]{:S(2)}) collective-permute-start(f32[28,6,8,128]{3,2,1,0:T(8,128)S(1)} %pad_maximum_fusion.own_ref), channel_id=1, source_target_pairs={{1,0},{2,1},{3,2},{5,4},{6,5},{7,6},{9,8},{10,9},{11,10},{13,12},{... | collective-permute-start | bytes 2064392 | tf_op jit(solution)/shard_map/ppermute | solution.py:289

commit v4 on v3

--- a/solution.py
+++ b/solution.py
@@ -44,41 +44,58 @@
     return 3 * (ITERS - k + 1) <= bz
 
 
-def pack_kernel(vx_ref, vz_ref, vy_ref, p_ref, phase_ref, stack_ref, edge_ref):
-    bx, bz, by = p_ref.shape
+def own_place(i, bx):
+    return lax.rem(i + (1 - lax.rem(lax.axis_index("gx"), 2)) * HIGH, bx)
+
+
+def pack_kernel(vx_hbm, vz_hbm, vy_hbm, p_hbm, phase_hbm, stack_ref, edge_ref, field_ref, phase_ref, sems):
+    bx, bz, by = phase_ref.shape
+    sources = (vx_hbm, vz_hbm, vy_hbm, p_hbm, phase_hbm)
+    targets = [field_ref.at[f] for f in range(FIELDS - 1)] + [phase_ref]
+    copies = [pltpu.make_async_copy(a, b, sems.at[f]) for f, (a, b) in enumerate(zip(sources, targets))]
+    for copy in copies:
+        copy.start()
     ix, iz, iy = lax.axis_index("gx"), lax.axis_index("gz"), lax.axis_index("gy")
-    lane = lax.broadcasted_iota(jnp.int32, (bz, by), 1)
-    row = lax.broadcasted_iota(jnp.int32, (bz, by), 0)
+    lane = lax.broadcasted_iota(jnp.int32, (1, bz, by), 2)
+    row = lax.broadcasted_iota(jnp.int32, (1, bz, by), 1)
     keep_z = (row > 0) | (iz > 0)
     keep_y = (lane > 0) | (iy > 0)
-
-    def plane(i, carry):
-        vx = vx_ref[i] * jnp.where((i > 0) | (ix > 0), 1.0, 0.0)
-        vz = jnp.where(keep_z, vz_ref[i], 0.0)
-        vy = jnp.where(keep_y, vy_ref[i], 0.0)
-        fields = (vx, vz, vy, p_ref[i], phase_ref[i].astype(jnp.float32))
-        edge = jnp.zeros((bz, by), jnp.float32)
-        for f, a in enumerate(fields):
-            stack_ref[i, f] = a
-            at = LANE_STEP * f
-            first = pltpu.roll(a, at, 1) if at else a
-            edge = jnp.where((lane >= at) & (lane < at + HIGH), first, edge)
-            last = pltpu.roll(a, at + LANE_STEP, 1)
-            edge = jnp.where((lane >= at + LANE_STEP - LOW) & (lane < at + LANE_STEP), last, edge)
-        edge_ref[i] = edge
+    for copy in copies:
+        copy.wait()
+
+    @pl.when(ix == 0)
+    def _():
+        field_ref[0, 0] = jnp.zeros((bz, by), jnp.float32)
+
+    count = 4
+
+    def planes(step, carry):
+        at = pl.ds(step * count, count)
+        to = pl.ds(own_place(step * count, bx), count)
+        vx, vz, vy, p = (field_ref[f, at] for f in range(FIELDS - 1))
+        vz = jnp.where(keep_z, vz, 0.0)
+        vy = jnp.where(keep_y, vy, 0.0)
+        edge = jnp.zeros((count, bz, by), jnp.float32)
+        for f, a in enumerate((vx, vz, vy, p, phase_ref[at].astype(jnp.float32))):
+            stack_ref[to, f] = a
+            base = LANE_STEP * f
+            first = pltpu.roll(a, base, 2) if base else a
+            edge = jnp.where((lane >= base) & (lane < base + HIGH), first, edge)
+            last = pltpu.roll(a, base + LANE_STEP, 2)
+            edge = jnp.where((lane >= base + LANE_STEP - LOW) & (lane < base + LANE_STEP), last, edge)
+        edge_ref[to] = edge
         return carry
 
-    lax.fori_loop(0, bx, plane, 0)
+    lax.fori_loop(0, bx // count, planes, 0)
 
 
 def main_kernel(
-    own_ref, above_ref, below_ref, scale_ref, power_ref, rho_table_ref,
+    own_ref, side_ref, face_0_ref, face_1_ref, corner_0_ref, corner_1_ref, scale_ref, power_ref, rho_table_ref,
     out_vx_ref, out_vz_ref, out_vy_ref, out_p_ref, out_eta_ref, sum_ref,
     va_ref, vb_ref, p_ref, pre_ref, power_field_ref, rho_ref, pre2_ref, power2_field_ref, rho2_ref,
     weight_ref, weight2_ref,
 ):
-    bz, by = own_ref.shape[2:]
-    bx = own_ref.shape[0] - LOW - HIGH
+    bx, _, bz, by = own_ref.shape
     lanes = 2 * by
     nx, nz, ny = lax.axis_size("gx"), lax.axis_size("gz"), lax.axis_size("gy")
     ix, iz, iy = lax.axis_index("gx"), lax.axis_index("gz"), lax.axis_index("gy")
@@ -87,47 +104,66 @@
     right = (lane < HIGH) & (iy < ny - 1)
     left = (lane >= by - LOW) & (iy > 0)
 
-    def unpack(i, carry):
-        x_in = (i + ix * bx >= LOW) & (i + ix * bx < LOW + nx * bx)
-        for t, (ref, z_in) in enumerate(((own_ref, None), (above_ref, iz < nz - 1), (below_ref, iz > 0))):
-            at = pl.ds(t * bz, bz)
-            ok = x_in if z_in is None else x_in & z_in
-            ok = jnp.where(ok, 1.0, 0.0)
-            edge = ref[i, FIELDS]
-            for f in range(FIELDS):
-                middle = ref[i, f]
-                shift = LANE_STEP * f
-                a = pltpu.roll(edge, (by - shift) % by, 1) if shift else edge
-                b = pltpu.roll(edge, (by - LANE_STEP - shift) % by, 1)
-                side = jnp.where(right, a, jnp.where(left, b, 0.0))
-                if f < 3:
-                    va_ref[f, i, at, 0:by] = middle
-                    va_ref[f, i, at, by:lanes] = side
-                elif f == 3:
-                    p_ref[i, at, 0:by] = middle
-                    p_ref[i, at, by:lanes] = side
-                else:
-                    for part, (ph, keep) in enumerate(((middle, None), (side, right | left))):
-                        to = pl.ds(part * by, by)
-                        values = []
-                        for table in (scale_ref, power_ref, rho_table_ref):
-                            value = table[0]
-                            for index in range(1, PHASES):
-                                value = jnp.where(ph == float(index), table[index], value)
-                            values.append(jnp.broadcast_to(value, (bz, by)))
-                        pre = values[0] * ok
-                        if keep is not None:
-                            pre = jnp.where(keep, pre, 0.0)
-                        pre_ref[i, at, to] = pre
-                        power_field_ref[i, at, to] = values[1]
-                        rho_ref[i, at, to] = values[2]
+    def unpack(ref, source, i, t, ok):
+        at = pl.ds(t * bz, bz)
+        ok = jnp.where(ok, 1.0, 0.0)
+        edge = ref[source, FIELDS]
+        for f in range(FIELDS):
+            middle = ref[source, f]
+            shift = LANE_STEP * f
+            a = pltpu.roll(edge, (by - shift) % by, 1) if shift else edge
+            b = pltpu.roll(edge, (by - LANE_STEP - shift) % by, 1)
+            side = jnp.where(right, a, jnp.where(left, b, 0.0))
+            if f < 3:
+                va_ref[f, i, at, 0:by] = middle
+                va_ref[f, i, at, by:lanes] = side
+            elif f == 3:
+                p_ref[i, at, 0:by] = middle
+                p_ref[i, at, by:lanes] = side
+            else:
+                for part, (ph, keep) in enumerate(((middle, None), (side, right | left))):
+                    to = pl.ds(part * by, by)
+                    values = []
+                    for table in (scale_ref, power_ref, rho_table_ref):
+                        value = table[0]
+                        for index in range(1, PHASES):
+                            value = jnp.where(ph == float(index), table[index], value)
+                        values.append(jnp.broadcast_to(value, (bz, by)))
+                    pre = values[0] * ok
+                    if keep is not None:
+                        pre = jnp.where(keep, pre, 0.0)
+                    pre_ref[i, at, to] = pre
+                    power_field_ref[i, at, to] = values[1]
+                    rho_ref[i, at, to] = values[2]
+
+    def unpack_planes(own, side, t, ok):
+        def own_plane(i, carry):
+            unpack(own, own_place(i, bx), LOW + i, t, ok)
+            return carry
+
+        def side_plane(i, carry):
+            unpack(side, i, lax.rem(LOW + bx + i, LOW + bx + HIGH), t, ok & jnp.where(i < HIGH, ix < nx - 1, ix > 0))
+            return carry
+
+        lax.fori_loop(0, bx, own_plane, 0)
+        lax.fori_loop(0, LOW + HIGH, side_plane, 0)
+
+    unpack_planes(own_ref, side_ref, 0, iz >= 0)
+    for parity in range(2):
+        @pl.when(lax.rem(iz, 2) == parity)
+        def _():
+            faces, corners = (face_0_ref, face_1_ref), (corner_0_ref, corner_1_ref)
+            unpack_planes(faces[parity], corners[parity], 1, iz < nz - 1)
+            unpack_planes(faces[1 - parity], corners[1 - parity], 2, iz > 0)
+
+    def merge(i, carry):
         row = lax.broadcasted_iota(jnp.int32, (bz, lanes), 0)
         for full, half in ((pre_ref, pre2_ref), (power_field_ref, power2_field_ref), (rho_ref, rho2_ref)):
             half[i, 0:bz] = full[i, 0:bz]
             half[i, bz : 2 * bz] = jnp.where(row < bz // 2, full[i, bz : 2 * bz], full[i, 2 * bz :])
         return carry
 
-    lax.fori_loop(0, bx + LOW + HIGH, unpack, 0)
+    lax.fori_loop(2, bx + LOW + HIGH - 4, merge, 0)
 
     for ref, high in ((weight_ref, 2 * bz), (weight2_ref, bz + bz // 2)):
         shape = ref.shape[1:]
@@ -284,46 +320,64 @@
     out_ref[...] = p_ref[...] - mean
 
 
-def shift(a, axis, step):
+def swap(a, axis, start):
     count = lax.axis_size(axis)
-    return lax.ppermute(a, axis, [(i, i + step) for i in range(count) if 0 <= i + step < count])
+    return lax.ppermute(a, axis, [(i, j) for k in range(start, count - 1, 2) for i, j in ((k, k + 1), (k + 1, k))])
+
+
+def exchange_sum(total, axes):
+    count = math.prod(lax.axis_size(a) for a in axes)
+    total = jnp.broadcast_to(jnp.sum(total, axis=0, keepdims=True), (count, total.shape[1]))
+    return lax.all_to_all(total, axes, 0, 0, tiled=True)
 
 
 def local(vel_x, vel_y, vel_z, pressure, phase, visc_scale, power_n, density):
     bx, bz, by = pressure.shape
+    assert bx == 2 * HIGH and bz == HIGH
     f32 = jnp.float32
-    counts = [lax.axis_size(a) for a in ("gx", "gz", "gy")]
-    cells = bx * bz * by * math.prod(counts)
+    ny = lax.axis_size("gy")
+    cells = bx * bz * by * math.prod(lax.axis_size(a) for a in ("gx", "gz", "gy"))
     deep = bx + LOW + HIGH
     block = jax.ShapeDtypeStruct((bx, bz, by), f32)
+    scratch = lambda *shape: pltpu.VMEM(shape, f32)
+    small = pltpu.CompilerParams(vmem_limit_bytes=4 * 1024 * 1024)
 
     stack, edge = pl.pallas_call(
         pack_kernel,
         out_shape=(jax.ShapeDtypeStruct((bx, FIELDS, bz, by), f32), block),
-        in_specs=[VMEM] * 5,
+        in_specs=[pl.BlockSpec(memory_space=pltpu.HBM)] * 5,
         out_specs=(VMEM, VMEM),
-        compiler_params=pltpu.CompilerParams(vmem_limit_bytes=4 * 1024 * 1024),
+        scratch_shapes=[
+            scratch(FIELDS - 1, bx, bz, by),
+            pltpu.VMEM((bx, bz, by), jnp.int32),
+            pltpu.SemaphoreType.DMA((FIELDS,)),
+        ],
+        compiler_params=small,
     )(vel_x, vel_z, vel_y, pressure, phase)
 
-    lane = lax.broadcasted_iota(jnp.int32, (bx, bz, by), 2)
-    if counts[2] == 2:
-        side = lax.ppermute(edge, "gy", [(0, 1), (1, 0)])
-    else:
-        side = jnp.where(lane % LANE_STEP < HIGH, shift(edge, "gy", -1), shift(edge, "gy", 1))
+    side = swap(edge, "gy", 0)
+    if ny > 2:
+        even = lax.rem(lax.axis_index("gy"), 2) == 0
+        other = swap(edge, "gy", 1)
+        lane = lax.broadcasted_iota(jnp.int32, (bx, bz, by), 2)
+        side = jnp.where((lane % LANE_STEP < HIGH) == even, side, other)
     stack = jnp.concatenate([stack, side[:, None]], axis=1)
-    low = shift(stack[bx - LOW :], "gx", 1)
-    high = shift(stack[:HIGH], "gx", -1)
-    stack = jnp.concatenate([low, stack, high], axis=0)
-    above = shift(stack, "gz", -1)
-    below = shift(stack, "gz", 1)
+
+    face_1 = swap(stack, "gz", 1)
+    x_0, x_1 = swap(stack[:HIGH], "gx", 0), swap(stack[HIGH:], "gx", 1)
+    face_0 = swap(stack, "gz", 0)
+    even = lax.rem(lax.axis_index("gx"), 2) == 0
+    low = jnp.where(even, x_1[HIGH - LOW :], x_0[HIGH - LOW :])
+    sides = jnp.concatenate([jnp.where(even, x_0, x_1), low], axis=0)
+    corner_1 = swap(sides, "gz", 1)
+    corner_0 = swap(sides, "gz", 0)
 
     power = (0.5 / math.log(2.0)) * (1.0 / power_n - 1.0)
-    scratch = lambda *shape: pltpu.VMEM(shape, f32)
     rows, lanes = 3 * bz, 2 * by
     vx, vz, vy, p, eta, total = pl.pallas_call(
         main_kernel,
         out_shape=(block,) * 5 + (jax.ShapeDtypeStruct((bz, by), f32),),
-        in_specs=[VMEM] * 3 + [SMEM] * 3,
+        in_specs=[VMEM] * 6 + [SMEM] * 3,
         out_specs=(VMEM,) * 6,
         scratch_shapes=[
             scratch(3, deep, rows, lanes),
@@ -339,17 +393,16 @@
             scratch(4, 2 * bz, lanes),
         ],
         compiler_params=pltpu.CompilerParams(vmem_limit_bytes=32 * 1024 * 1024),
-    )(stack, above, below, visc_scale, power, density)
-
-    devices = math.prod(counts)
-    total = jnp.broadcast_to(jnp.sum(total, axis=0, keepdims=True), (devices, by))
-    total = lax.all_to_all(total, ("gx", "gy", "gz"), 0, 0, tiled=True)
+    )(stack, sides, face_0, face_1, corner_0, corner_1, visc_scale, power, density)
+
+    total = exchange_sum(total, ("gy", "gz"))
+    total = exchange_sum(total, ("gx",))
     p = pl.pallas_call(
         lambda *refs: final_kernel(*refs, cells=float(cells)),
         out_shape=block,
         in_specs=[VMEM] * 2,
         out_specs=VMEM,
-        compiler_params=pltpu.CompilerParams(vmem_limit_bytes=4 * 1024 * 1024),
+        compiler_params=small,
     )(p, total)
     return (vx, vy, vz, p, eta)
 

time: 64 us -> 65.1 us (1.017)
  Pallas kernels: 16.6 us -> 20.2 us
  waiting for transfers between devices: 9.3 us -> 6.27 us
  starting transfers between devices: 11.6 us -> 13 us
  blocking collectives: 21 us -> 20 us
    pallas_call x1, Pallas kernels: 14.5 us -> 18.6 us  [local(): pl.pallas_call(main_kernel, out_shape=(block,) * 5 + (jax.ShapeDtypeStruc...]
    ppermute x5 -> x7, waiting for transfers between devices: 9.3 us -> 6.27 us  [swap(): lax.ppermute(a, axis, [(i, j) for k in range(start, count - 1, 2) for i,...]
    ppermute x5 -> x7, starting transfers between devices: 11.6 us -> 13 us  [swap(): lax.ppermute(a, axis, [(i, j) for k in range(start, count - 1, 2) for i,...]
    all_to_all x1 -> x2, blocking collectives: 21 us -> 20 us  [exchange_sum(): return lax.all_to_all(total, axes, 0, 0, tiled=True)]
  transfers between devices with their start and end apart: 5 -> 7, of which waited for: 4 -> 3; matrix products, arithmetic and copies ran while one was open for 0% -> 0% of each run, Pallas kernels for 0% -> 0%
where the time goes in v4:
time: 65.1 us; the launch traced here: 64.7 us
  Pallas kernels  20.2 us (31%)
  blocking collectives  20 us (31%)
  starting transfers between devices  13 us (20%)
  waiting for transfers between devices  6.27 us (10%)
  local copies, waits for them, and re-layouts  4.22 us (6%)
  between operations  0.77 us (1%)
    all_to_all x2, blocking collectives, exchange_sum(): return lax.all_to_all(total, axes, 0, 0, tiled=True)  20 us
    pallas_call x1, Pallas kernels, local(): pl.pallas_call(main_kernel, out_shape=(block,) * 5 + (jax.ShapeDtypeStruc...  18.6 us
    ppermute x7, starting transfers between devices, swap(): lax.ppermute(a, axis, [(i, j) for k in range(start, count - 1, 2) for i,...  13 us
    ppermute x7, waiting for transfers between devices, swap(): lax.ppermute(a, axis, [(i, j) for k in range(start, count - 1, 2) for i,...  6.27 us
    unnamed x16, local copies, waits for them, and re-layouts  4.21 us
  transfers between devices with their start and end apart: 7, of which 3 were waited for; matrix products, arithmetic and copies ran while one was open for 0% of the time, Pallas kernels for 0%

profile of v4, /device:TPU:0, one launch (start us, length us, event | category | flops | bytes accessed | tf_op | source)
XLA Modules:
  0.0 64.7 jit_solution(9751424265027573166)
XLA Ops:
  0.6 0.8 %copy-done = f32[16,8,128]{2,1,0:T(8,128)S(1)} copy-done((f32[16,8,128]{2,1,0:T(8,128)S(1)}, f32[16,8,128]{2,1,0:T(8,128)}, u32[]{:S(2)}) %copy-start) | copy-done | bytes 65560
  1.5 0.8 %copy-done.1 = f32[16,8,128]{2,1,0:T(8,128)S(1)} copy-done((f32[16,8,128]{2,1,0:T(8,128)S(1)}, f32[16,8,128]{2,1,0:T(8,128)}, u32[]{:S(2)}) %copy-start.1) | copy-done | bytes 65560
  2.3 0.8 %copy-done.2 = f32[16,8,128]{2,1,0:T(8,128)S(1)} copy-done((f32[16,8,128]{2,1,0:T(8,128)S(1)}, f32[16,8,128]{2,1,0:T(8,128)}, u32[]{:S(2)}) %copy-start.2) | copy-done | bytes 65560
  3.2 0.8 %copy-done.3 = f32[16,8,128]{2,1,0:T(8,128)S(1)} copy-done((f32[16,8,128]{2,1,0:T(8,128)S(1)}, f32[16,8,128]{2,1,0:T(8,128)}, u32[]{:S(2)}) %copy-start.3) | copy-done | bytes 65560
  4.0 0.8 %copy-done.4 = s32[16,8,128]{2,1,0:T(8,128)S(1)} copy-done((s32[16,8,128]{2,1,0:T(8,128)S(1)}, s32[16,8,128]{2,1,0:T(8,128)}, u32[]{:S(2)}) %copy-start.4) | copy-done | bytes 65560
  4.8 0.9 %shard_map.119 = (f32[16,5,8,128]{3,2,1,0:T(8,128)S(1)}, f32[16,8,128]{2,1,0:T(8,128)S(1)}) custom-call(f32[16,8,128]{2,1,0:T(8,128)S(1)} %copy-done, f32[16,8,128]{2,1,0:T(8,128)S(1)} %copy-done.1, f32[16,8,128]{2,1,0:T(8,128)S(1)} %copy-done.2, f32[16,8,128]{2,1,0:T(8,128)S(1)} %copy-done.3, s32[16,8,128]{2,1,0:T(8,128)S(1)} %copy-done.4), custom_call_target="tpu_custom_call" | custom-call | tf_op jit(solution)/shard_map/pallas_call | solution.py:345
  5.7 3.0 %collective-permute-start = (f32[16,8,128]{2,1,0:T(8,128)S(1)}, f32[16,8,128]{2,1,0:T(8,128)S(1)}, u32[]{:S(2)}, u32[]{:S(2)}) collective-permute-start(f32[16,8,128]{2,1,0:T(8,128)S(1)} %get-tuple-element.14), channel_id=1, source_target_pairs={{0,4},{4,0},{1,5},{5,1},{2,6},{6,2},{3,7},{7,3},{8,12},{12,8},{9,1... | collective-permute-start | bytes 196616 | tf_op jit(solution)/shard_map/ppermute | solution.py:325
  8.7 2.2 %collective-permute-done = f32[16,8,128]{2,1,0:T(8,128)S(1)} collective-permute-done((f32[16,8,128]{2,1,0:T(8,128)S(1)}, f32[16,8,128]{2,1,0:T(8,128)S(1)}, u32[]{:S(2)}, u32[]{:S(2)}) %collective-permute-start) | collective-permute-done | bytes 65568 | tf_op jit(solution)/shard_map/ppermute | solution.py:325
  11.0 0.7 %collective-permute-start.2 = (f32[8,6,8,128]{3,2,1,0:T(8,128)S(1)}, f32[8,6,8,128]{3,2,1,0:T(8,128)S(1)}, u32[]{:S(2)}, u32[]{:S(2)}) collective-permute-start(f32[8,6,8,128]{3,2,1,0:T(8,128)S(1)} %get-tuple-element.21), channel_id=1, source_target_pairs={{8,16},{16,8},{9,17},{17,9},{10,18},{18,10},{11,19},{19,11},{12,20... | collective-permute-start | bytes 589832 | tf_op jit(solution)/shard_map/ppermute | solution.py:325
  11.7 5.0 %collective-permute-start.1 = (f32[8,6,8,128]{3,2,1,0:T(8,128)S(1)}, f32[8,6,8,128]{3,2,1,0:T(8,128)S(1)}, u32[]{:S(2)}, u32[]{:S(2)}) collective-permute-start(f32[8,6,8,128]{3,2,1,0:T(8,128)S(1)} %get-tuple-element.22), channel_id=1, source_target_pairs={{0,8},{8,0},{16,24},{24,16},{1,9},{9,1},{17,25},{25,17},{2,10},{10... | collective-permute-start | bytes 589832 | tf_op jit(solution)/shard_map/ppermute | solution.py:325
  16.7 0.1 collective-permute-start.3
  16.8 0.7 %collective-permute-start.4 = (f32[16,6,8,128]{3,2,1,0:T(8,128)S(1)}, f32[16,6,8,128]{3,2,1,0:T(8,128)S(1)}, u32[]{:S(2)}, u32[]{:S(2)}) collective-permute-start(f32[16,6,8,128]{3,2,1,0:T(8,128)S(1)} %pad_maximum_fusion.own_ref), channel_id=1, source_target_pairs={{1,2},{2,1},{5,6},{6,5},{9,10},{10,9},{13,14},{14,13},{17,18},{18,... | collective-permute-start | bytes 1179656 | tf_op jit(solution)/shard_map/ppermute | solution.py:325
  17.5 0.0 collective-permute-done.2
  17.5 2.8 %collective-permute-done.1 = f32[8,6,8,128]{3,2,1,0:T(8,128)S(1)} collective-permute-done((f32[8,6,8,128]{3,2,1,0:T(8,128)S(1)}, f32[8,6,8,128]{3,2,1,0:T(8,128)S(1)}, u32[]{:S(2)}, u32[]{:S(2)}) %collective-permute-start.1) | collective-permute-done | bytes 196640 | tf_op jit(solution)/shard_map/ppermute | solution.py:325
  20.4 0.0 copy-start.7
  20.4 0.0 copy-start.5
  20.4 0.0 copy-start.6
  20.4 0.7 %collective-permute-start.6 = (f32[12,6,8,128]{3,2,1,0:T(8,128)S(1)}, f32[12,6,8,128]{3,2,1,0:T(8,128)S(1)}, u32[]{:S(2)}, u32[]{:S(2)}) collective-permute-start(f32[12,6,8,128]{3,2,1,0:T(8,128)S(1)} %pad_maximum_fusion.1.side_ref), channel_id=1, source_target_pairs={{1,2},{2,1},{5,6},{6,5},{9,10},{10,9},{13,14},{14,13},{17,18},{18,... | collective-permute-start | bytes 884744 | tf_op jit(solution)/shard_map/ppermute | solution.py:325
  21.1 2.9 %collective-permute-start.5 = (f32[12,6,8,128]{3,2,1,0:T(8,128)S(1)}, f32[12,6,8,128]{3,2,1,0:T(8,128)S(1)}, u32[]{:S(2)}, u32[]{:S(2)}) collective-permute-start(f32[12,6,8,128]{3,2,1,0:T(8,128)S(1)} %pad_maximum_fusion.1.side_ref), channel_id=1, source_target_pairs={{0,1},{1,0},{2,3},{3,2},{4,5},{5,4},{6,7},{7,6},{8,9},{9,8},{10,11... | collective-permute-start | bytes 884744 | tf_op jit(solution)/shard_map/ppermute | solution.py:325
  24.1 1.2 %collective-permute-done.5.corner_0_ref = f32[12,6,8,128]{3,2,1,0:T(8,128)S(1)} collective-permute-done((f32[12,6,8,128]{3,2,1,0:T(8,128)S(1)}, f32[12,6,8,128]{3,2,1,0:T(8,128)S(1)}, u32[]{:S(2)}, u32[]{:S(2)}) %collective-permute-start.5) | collective-permute-done | bytes 294944 | tf_op jit(solution)/shard_map/ppermute | solution.py:325
  25.3 18.6 %shard_map.120 = (f32[16,8,128]{2,1,0:T(8,128)}, f32[16,8,128]{2,1,0:T(8,128)}, f32[16,8,128]{2,1,0:T(8,128)}, f32[16,8,128]{2,1,0:T(8,128)S(1)}, f32[16,8,128]{2,1,0:T(8,128)}, /*index=5*/f32[8,128]{1,0:T(8,128)S(1)}) custom-call(f32[16,6,8,128]{3,2,1,0:T(8,128)S(1)} %pad_maximum_fusion.own_ref, f32[12,6,8,128]{3,2,1,0:T(8,128)S(1)} %pad_maximum_fusion.1.side_ref, ...), custom_call_target="tpu_custom_call" | custom-call | tf_op jit(solution)/shard_map/pallas_call | solution.py:377
  43.9 12.0 %all_to_all.14 = f32[8,1,128]{2,1,0:T(1,128)S(1)} all-to-all(f32[8,1,128]{2,1,0:T(1,128)S(1)} %broadcast_in_dim.7), channel_id=1, replica_groups=mesh['gx'=4,'gy'=2,'gz'=4] {'gy','gz'}, dimensions={0} | all-to-all | bytes 8192 | tf_op jit(solution)/shard_map/all_to_all | solution.py:331
  55.9 8.0 %all_to_all.15 = f32[4,1,128]{2,1,0:T(1,128)S(1)} all-to-all(f32[4,1,128]{2,1,0:T(1,128)S(1)} %broadcast_in_dim.8), channel_id=1, replica_groups=mesh['gx'=4,'gy'=2,'gz'=4] {'gx'}, dimensions={0} | all-to-all | bytes 4096 | tf_op jit(solution)/shard_map/all_to_all | solution.py:331
  63.9 0.8 %shard_map.121 = f32[16,8,128]{2,1,0:T(8,128)} custom-call(f32[16,8,128]{2,1,0:T(8,128)S(1)} %get-tuple-element.18.refs_0_, f32[4,128]{1,0:T(4,128)S(1)} %bitcast.3), custom_call_target="tpu_custom_call" | custom-call | tf_op jit(solution)/shard_map/pallas_call | solution.py:400
  (21 shorter events, 0.2 us)
Async XLA Ops:
  0.6 0.8 %copy-start = (f32[16,8,128]{2,1,0:T(8,128)S(1)}, f32[16,8,128]{2,1,0:T(8,128)}, u32[]{:S(2)}) copy-start(f32[16,8,128]{2,1,0:T(8,128)} %vx_hbm.1) | copy-start | bytes 196612
  1.5 0.8 %copy-start.1 = (f32[16,8,128]{2,1,0:T(8,128)S(1)}, f32[16,8,128]{2,1,0:T(8,128)}, u32[]{:S(2)}) copy-start(f32[16,8,128]{2,1,0:T(8,128)} %vz_hbm.1) | copy-start | bytes 196612
  2.3 0.8 %copy-start.2 = (f32[16,8,128]{2,1,0:T(8,128)S(1)}, f32[16,8,128]{2,1,0:T(8,128)}, u32[]{:S(2)}) copy-start(f32[16,8,128]{2,1,0:T(8,128)} %vy_hbm.1) | copy-start | bytes 196612
  3.2 0.8 %copy-start.3 = (f32[16,8,128]{2,1,0:T(8,128)S(1)}, f32[16,8,128]{2,1,0:T(8,128)}, u32[]{:S(2)}) copy-start(f32[16,8,128]{2,1,0:T(8,128)} %p_hbm.1) | copy-start | bytes 196612
  4.0 0.8 %copy-start.4 = (s32[16,8,128]{2,1,0:T(8,128)S(1)}, s32[16,8,128]{2,1,0:T(8,128)}, u32[]{:S(2)}) copy-start(s32[16,8,128]{2,1,0:T(8,128)} %phase_hbm.1) | copy-start | bytes 196612
  5.7 5.2 %collective-permute-start = (f32[16,8,128]{2,1,0:T(8,128)S(1)}, f32[16,8,128]{2,1,0:T(8,128)S(1)}, u32[]{:S(2)}, u32[]{:S(2)}) collective-permute-start(f32[16,8,128]{2,1,0:T(8,128)S(1)} %get-tuple-element.14), channel_id=1, source_target_pairs={{0,4},{4,0},{1,5},{5,1},{2,6},{6,2},{3,7},{7,3},{8,12},{12,8},{9,1... | collective-permute-start | bytes 196616 | tf_op jit(solution)/shard_map/ppermute | solution.py:325
  11.0 6.5 %collective-permute-start.2 = (f32[8,6,8,128]{3,2,1,0:T(8,128)S(1)}, f32[8,6,8,128]{3,2,1,0:T(8,128)S(1)}, u32[]{:S(2)}, u32[]{:S(2)}) collective-permute-start(f32[8,6,8,128]{3,2,1,0:T(8,128)S(1)} %get-tuple-element.21), channel_id=1, source_target_pairs={{8,16},{16,8},{9,17},{17,9},{10,18},{18,10},{11,19},{19,11},{12,20... | collective-permute-start | bytes 589832 | tf_op jit(solution)/shard_map/ppermute | solution.py:325
  11.7 8.6 %collective-permute-start.1 = (f32[8,6,8,128]{3,2,1,0:T(8,128)S(1)}, f32[8,6,8,128]{3,2,1,0:T(8,128)S(1)}, u32[]{:S(2)}, u32[]{:S(2)}) collective-permute-start(f32[8,6,8,128]{3,2,1,0:T(8,128)S(1)} %get-tuple-element.22), channel_id=1, source_target_pairs={{0,8},{8,0},{16,24},{24,16},{1,9},{9,1},{17,25},{25,17},{2,10},{10... | collective-permute-start | bytes 589832 | tf_op jit(solution)/shard_map/ppermute | solution.py:325
  16.7 7.4 %collective-permute-start.3 = (f32[16,6,8,128]{3,2,1,0:T(8,128)S(1)}, f32[16,6,8,128]{3,2,1,0:T(8,128)S(1)}, u32[]{:S(2)}, u32[]{:S(2)}) collective-permute-start(f32[16,6,8,128]{3,2,1,0:T(8,128)S(1)} %pad_maximum_fusion.own_ref), channel_id=1, source_target_pairs={{0,1},{1,0},{2,3},{3,2},{4,5},{5,4},{6,7},{7,6},{8,9},{9,8},{10,11... | collective-permute-start | bytes 1179656 | tf_op jit(solution)/shard_map/ppermute | solution.py:325
  16.8 7.3 %collective-permute-start.4 = (f32[16,6,8,128]{3,2,1,0:T(8,128)S(1)}, f32[16,6,8,128]{3,2,1,0:T(8,128)S(1)}, u32[]{:S(2)}, u32[]{:S(2)}) collective-permute-start(f32[16,6,8,128]{3,2,1,0:T(8,128)S(1)} %pad_maximum_fusion.own_ref), channel_id=1, source_target_pairs={{1,2},{2,1},{5,6},{6,5},{9,10},{10,9},{13,14},{14,13},{17,18},{18,... | collective-permute-start | bytes 1179656 | tf_op jit(solution)/shard_map/ppermute | solution.py:325
  20.4 3.7 %copy-start.7 = (f32[4]{0:T(128)S(1)}, f32[4]{0:T(128)}, u32[]{:S(2)}) copy-start(f32[4]{0:T(128)} %param.14) | copy-start | bytes 52
  20.4 4.9 %copy-start.5 = (f32[4]{0:T(128)S(1)}, f32[4]{0:T(128)}, u32[]{:S(2)}) copy-start(f32[4]{0:T(128)} %scale_ref.1) | copy-start | bytes 52
  20.4 4.8 %copy-start.6 = (f32[4]{0:T(128)S(1)}, f32[4]{0:T(128)}, u32[]{:S(2)}) copy-start(f32[4]{0:T(128)} %rho_table_ref.1) | copy-start | bytes 52
  20.4 3.6 %collective-permute-start.6 = (f32[12,6,8,128]{3,2,1,0:T(8,128)S(1)}, f32[12,6,8,128]{3,2,1,0:T(8,128)S(1)}, u32[]{:S(2)}, u32[]{:S(2)}) collective-permute-start(f32[12,6,8,128]{3,2,1,0:T(8,128)S(1)} %pad_maximum_fusion.1.side_ref), channel_id=1, source_target_pairs={{1,2},{2,1},{5,6},{6,5},{9,10},{10,9},{13,14},{14,13},{17,18},{18,... | collective-permute-start | bytes 884744 | tf_op jit(solution)/shard_map/ppermute | solution.py:325
  21.1 4.1 %collective-permute-start.5 = (f32[12,6,8,128]{3,2,1,0:T(8,128)S(1)}, f32[12,6,8,128]{3,2,1,0:T(8,128)S(1)}, u32[]{:S(2)}, u32[]{:S(2)}) collective-permute-start(f32[12,6,8,128]{3,2,1,0:T(8,128)S(1)} %pad_maximum_fusion.1.side_ref), channel_id=1, source_target_pairs={{0,1},{1,0},{2,3},{3,2},{4,5},{5,4},{6,7},{7,6},{8,9},{9,8},{10,11... | collective-permute-start | bytes 884744 | tf_op jit(solution)/shard_map/ppermute | solution.py:325

commit v5 on v4

v5 whole, which is shorter than its diff:
```python
import math

import jax
import jax.numpy as jnp
from jax import lax
from jax.experimental import pallas as pl
from jax.experimental.pallas import tpu as pltpu
from jax.sharding import PartitionSpec as P

ITERS = 4
PHASES = 4
LOW = ITERS
HIGH = 2 * ITERS
FIELDS = 5
LANE_STEP = 16
UNROLL = 3
GROUP = 4

VMEM = pl.BlockSpec(memory_space=pltpu.VMEM)
SMEM = pl.BlockSpec(memory_space=pltpu.SMEM)


def z_up(a):
    return pltpu.roll(a, a.shape[-2] - 1, a.ndim - 2)


def z_down(a):
    return pltpu.roll(a, 1, a.ndim - 2)


def y_up(a):
    return pltpu.roll(a, a.shape[-1] - 1, a.ndim - 1)


def y_down(a):
    return pltpu.roll(a, 1, a.ndim - 1)


def reciprocal(a):
    r = pl.reciprocal(a, approx=True)
    return r * (2.0 - a * r)


def merged(k, bz):
    return 3 * (ITERS - k + 1) <= bz


def edge_kernel(vx_hbm, vz_hbm, vy_hbm, p_hbm, phase_hbm, edge_hbm, field_ref, phase_ref, edge_ref, sems, out_sems):
    bx, bz, by = phase_ref.shape
    sources = (vx_hbm, vz_hbm, vy_hbm, p_hbm, phase_hbm)
    targets = [field_ref.at[f] for f in range(FIELDS - 1)] + [phase_ref]
    groups = bx // GROUP
    copies = []
    for g in range(groups):
        at = pl.ds(g * GROUP, GROUP)
        copies.append(
            [pltpu.make_async_copy(a.at[at], b.at[at], sems.at[g, f]) for f, (a, b) in enumerate(zip(sources, targets))]
        )
        for copy in copies[-1]:
            copy.start()
    ix, iz, iy = lax.axis_index("gx"), lax.axis_index("gz"), lax.axis_index("gy")
    lane = lax.broadcasted_iota(jnp.int32, (1, bz, by), 2)
    row = lax.broadcasted_iota(jnp.int32, (1, bz, by), 1)
    plane = lax.broadcasted_iota(jnp.int32, (GROUP, bz, by), 0)
    outs = []
    for g in range(groups):
        for copy in copies[g]:
            copy.wait()
        at = pl.ds(g * GROUP, GROUP)
        vx, vz, vy, p = (field_ref[f, at] for f in range(FIELDS - 1))
        if g == 0:
            vx = jnp.where((plane > 0) | (ix > 0), vx, 0.0)
        vz = jnp.where((row > 0) | (iz > 0), vz, 0.0)
        vy = jnp.where((lane > 0) | (iy > 0), vy, 0.0)
        edge = jnp.zeros((GROUP, bz, by), jnp.float32)
        for f, a in enumerate((vx, vz, vy, p, phase_ref[at].astype(jnp.float32))):
            base = LANE_STEP * f
            first = pltpu.roll(a, base, 2) if base else a
            edge = jnp.where((lane >= base) & (lane < base + HIGH), first, edge)
            last = pltpu.roll(a, base + LANE_STEP, 2)
            edge = jnp.where((lane >= base + LANE_STEP - LOW) & (lane < base + LANE_STEP), last, edge)
        edge_ref[at] = edge
        outs.append(pltpu.make_async_copy(edge_ref.at[at], edge_hbm.at[at], out_sems.at[g]))
        outs[-1].start()
    for copy in outs:
        copy.wait()


def unpack(block, ok, tables):
    count, _, bz, by = block.shape
    iy = lax.axis_index("gy")
    lane = lax.broadcasted_iota(jnp.int32, (1, bz, by), 2)
    right = (lane < HIGH) & (iy < lax.axis_size("gy") - 1)
    left = (lane >= by - LOW) & (iy > 0)
    ok = jnp.where(ok, 1.0, 0.0)
    edge = block[:, FIELDS]
    out = []
    for f in range(FIELDS):
        shift = LANE_STEP * f
        a = pltpu.roll(edge, (by - shift) % by, 2) if shift else edge
        b = pltpu.roll(edge, (by - LANE_STEP - shift) % by, 2)
        out.append([block[:, f], jnp.where(right, a, jnp.where(left, b, 0.0))])
    pair = out.pop()
    for number, table in enumerate(tables):
        values = []
        for part, ph in enumerate(pair):
            value = jnp.broadcast_to(table[0], ph.shape)
            for index in range(1, PHASES):
                value = jnp.where(ph == float(index), table[index], value)
            if number == 0:
                value = value * ok
                if part:
                    value = jnp.where(right | left, value, 0.0)
            values.append(value)
        out.append(values)
    return out


def unpack_planes(own_ref, side_ref, ok, tables, store):
    bx = own_ref.shape[0]
    ix, nx = lax.axis_index("gx"), lax.axis_size("gx")

    def group(g, carry):
        store(pl.ds(LOW + g * GROUP, GROUP), unpack(own_ref[pl.ds(g * GROUP, GROUP)], ok, tables))
        return carry

    lax.fori_loop(0, bx // GROUP, group, 0)
    for g in range((LOW + HIGH) // GROUP):
        at = g * GROUP
        high = at < HIGH
        values = unpack(side_ref[pl.ds(at, GROUP)], ok & (ix < nx - 1 if high else ix > 0), tables)
        store(pl.ds(LOW + bx + at if high else at - HIGH, GROUP), values)


def own_kernel(own_ref, side_ref, scale_ref, power_ref, rho_table_ref, v_ref, p_ref, pre_ref, power_field_ref, rho_ref):
    by = own_ref.shape[-1]
    refs = [v_ref.at[d] for d in range(3)] + [p_ref, pre_ref, power_field_ref, rho_ref]

    def store(planes, values):
        for ref, (own, beside) in zip(refs, values):
            ref[planes, :, 0:by] = own
            ref[planes, :, by : 2 * by] = beside

    unpack_planes(own_ref, side_ref, lax.axis_index("gz") >= 0, (scale_ref, power_ref, rho_table_ref), store)


def main_kernel(
    v_ref, p0_ref, pre_ref, power_field_ref, rho_ref,
    face_0_ref, face_1_ref, corner_0_ref, corner_1_ref, scale_ref, power_ref, rho_table_ref,
    out_vx_ref, out_vz_ref, out_vy_ref, out_p_ref, out_eta_ref, sum_ref,
    va_ref, vb_ref, p_ref, halo_ref, shared_ref, weight_ref, weight2_ref,
):
    bx, _, bz, by = face_0_ref.shape
    lanes = 2 * by
    nx, nz, ny = lax.axis_size("gx"), lax.axis_size("gz"), lax.axis_size("gy")
    ix, iz, iy = lax.axis_index("gx"), lax.axis_index("gz"), lax.axis_index("gy")
    tables = (scale_ref, power_ref, rho_table_ref)

    def store(t):
        def store_rows(planes, values):
            for n, pair in enumerate(values):
                for part, value in enumerate(pair):
                    halo_ref[n, planes, t * bz : (t + 1) * bz, part * by : (part + 1) * by] = value
                    if n >= 4:
                        half = bz // 2
                        rows = slice(t * half, (t + 1) * half)
                        shared_ref[n - 4, planes, rows, part * by : (part + 1) * by] = value[:, rows]

        return store_rows

    for parity in range(2):
        @pl.when(lax.rem(iz, 2) == parity)
        def _():
            faces, corners = (face_0_ref, face_1_ref), (corner_0_ref, corner_1_ref)
            unpack_planes(faces[parity], corners[parity], iz < nz - 1, tables, store(0))
            unpack_planes(faces[1 - parity], corners[1 - parity], iz > 0, tables, store(1))

    for ref, high in ((weight_ref, 2 * bz), (weight2_ref, bz + bz // 2)):
        shape = ref.shape[1:]
        r = lax.broadcasted_iota(jnp.int32, shape, 0)
        c = lax.broadcasted_iota(jnp.int32, shape, 1)
        zg = iz * bz + jnp.where(r < high, r, r - shape[0])
        yg = iy * by + jnp.where(c < by + HIGH, c, c - lanes)
        filled = (c < by + HIGH) | (c >= lanes - LOW)
        inside = filled & (zg >= 0) & (zg < nz * bz) & (yg >= 0) & (yg < ny * by)
        ref[0] = jnp.where(inside, 0.05, 0.0)
        ref[1] = jnp.where(inside & (zg > 0), 0.05, 0.0)
        ref[2] = jnp.where(inside & (yg > 0), 0.05, 0.0)
        ref[3] = jnp.where(inside, 0.0, 1.0)

    for k in range(1, ITERS + 1):
        old, new = (va_ref, vb_ref) if k % 2 else (vb_ref, va_ref)
        last = k == ITERS
        rows = 2 * bz if merged(k, bz) else 3 * bz
        own_constants = (pre_ref, power_field_ref, rho_ref)
        weight = weight2_ref if merged(k, bz) else weight_ref
        narrow = merged(k + 1, bz) and not merged(k, bz)
        all_rows = pl.ds(0, rows)

        def keep(value):
            if narrow:
                row = lax.broadcasted_iota(jnp.int32, (bz, lanes), 0)
                halo = jnp.where(row < bz // 2, value[..., bz : 2 * bz, :], value[..., 2 * bz :, :])
                return [(pl.ds(0, bz), value[..., 0:bz, :]), (pl.ds(bz, bz), halo)]
            return [(all_rows, value)]

        def store(d, j, count, value):
            for at, part in keep(value):
                new[d, pl.ds(j, count), at, :] = part

        def constant(n, planes):
            halo = shared_ref[n, planes] if merged(k, bz) else halo_ref[4 + n, planes]
            return jnp.concatenate([own_constants[n][planes], halo], axis=1)

        def load(d, j, count):
            planes = pl.ds(j, count)
            if k == 1:
                return jnp.concatenate([v_ref[d, planes], halo_ref[d, planes]], axis=1)
            return old[d, planes, all_rows, :]

        def cells(j, count):
            planes = pl.ds(j, count)
            vx1 = load(0, j, count + 1)
            vx = vx1[:count]
            vz, vy = load(1, j, count), load(2, j, count)
            if k == 1:
                p = jnp.concatenate([p0_ref[planes], halo_ref[3, planes]], axis=1)
            else:
                p = p_ref[planes, all_rows, :]
            rx = vx1[1:] - vx
            rz = z_up(vz) - vz
            ry = y_up(vy) - vy
            a = rx - ry
            b = ry - rz
            inv = (a * (a + b) + b * b) * (1.0 / 3.0) + 1.0
            eta = constant(0, planes) * jnp.exp2(constant(1, planes) * jnp.log(inv))
            quarter = 0.25 * eta
            div = rx + ry + rz
            p = p - quarter * (div + div)
            tx, tz, ty = eta * rx - p, eta * rz - p, eta * ry - p
            sz = quarter + z_down(quarter)
            sy = quarter + y_down(quarter)
            return vx, vz, vy, eta, p, quarter, tx, tz, ty, sz, sy

        def chunk(j, count, carry, start=False):
            planes = pl.ds(j, count)
            vx, vz, vy, eta, p, quarter, tx, tz, ty, sz, sy = cells(j, count)
            vz0, vy0 = load(1, j - 1, 1), load(2, j - 1, 1)
            quarter0, tx0, sz0, sy0, part_z0, part_y0, scale_z0, scale_y0 = carry
            join = lambda first, rest: jnp.concatenate([first, rest[:-1]], axis=0) if count > 1 else first
            bias = weight[3:4]
            sx = quarter + join(quarter0, quarter)
            exz = sz + join(sz0, sz)
            exy = sy + join(sy0, sy)
            ezy = sz + y_down(sz)
            fxz = exz * (vx - z_down(vx))
            fxy = exy * (vx - y_down(vx))
            low_vz, low_vy = join(vz0, vz), join(vy0, vy)
            gzx = exz * (vz - low_vz)
            hyx = exy * (vy - low_vy)
            gzy = ezy * (vz - y_down(vz))
            hyz = ezy * (vy - z_down(vy))
            res_x = (tx - join(tx0, tx)) + ((z_up(fxz) - fxz) + (y_up(fxy) - fxy))
            new_vx = vx + weight[0:1] * reciprocal(sx + bias) * res_x
            part_z = (tz - z_down(tz)) - constant(2, planes) + ((y_up(gzy) - gzy) - gzx)
            part_y = (ty - y_down(ty)) + ((z_up(hyz) - hyz) - hyx)
            scale_z = weight[1:2] * reciprocal(sz + bias)
            scale_y = weight[2:3] * reciprocal(sy + bias)
            new_vz = low_vz + join(scale_z0, scale_z) * (join(part_z0, part_z) + gzx)
            new_vy = low_vy + join(scale_y0, scale_y) * (join(part_y0, part_y) + hyx)
            if last:
                at = pl.ds(j - LOW, count)
                out_vx_ref[at] = new_vx[:, 0:bz, 0:by]
                out_p_ref[at] = p[:, 0:bz, 0:by]
                out_eta_ref[at] = eta[:, 0:bz, 0:by]
                sum_ref[...] += jnp.sum(p[:, 0:bz, 0:by], axis=0)
                if not start:
                    at = pl.ds(j - 1 - LOW, count)
                    out_vz_ref[at] = new_vz[:, 0:bz, 0:by]
                    out_vy_ref[at] = new_vy[:, 0:bz, 0:by]
            else:
                for at, part in keep(p):
                    p_ref[planes, at, :] = part
                store(0, j, count, new_vx)
                if not start:
                    store(1, j - 1, count, new_vz)
                    store(2, j - 1, count, new_vy)
            return tuple(a[-1:] for a in (quarter, tx, sz, sy, part_z, part_y, scale_z, scale_y))

        first, count = k, bx + LOW + HIGH - 3 * k
        if last:
            sum_ref[...] = jnp.zeros((bz, by), jnp.float32)
        _, _, _, _, p, quarter, tx, _, _, sz, sy = cells(first - 1, 1)
        if not last:
            for at, part in keep(p):
                p_ref[pl.ds(first - 1, 1), at, :] = part
        zero = jnp.zeros((1, rows, lanes), jnp.float32)
        carry = chunk(first, 1, (quarter, tx, sz, sy, zero, zero, zero, zero), start=True)
        steps, rest = divmod(count - 1, UNROLL)
        carry = lax.fori_loop(
            0, steps, lambda s, carry: chunk(first + 1 + s * UNROLL, UNROLL, carry), carry
        )
        if rest:
            carry = chunk(first + 1 + steps * UNROLL, rest, carry)
        j = first + count
        quarter0, tx0, sz0, sy0, part_z0, part_y0, scale_z0, scale_y0 = carry
        _, vz, vy, _, p, quarter, tx, _, _, sz, sy = cells(j, 1)
        vz0, vy0 = load(1, j - 1, 1), load(2, j - 1, 1)
        new_vz = vz0 + scale_z0 * (part_z0 + (sz + sz0) * (vz - vz0))
        new_vy = vy0 + scale_y0 * (part_y0 + (sy + sy0) * (vy - vy0))
        if last:
            out_vz_ref[pl.ds(j - 1 - LOW, 1)] = new_vz[:, 0:bz, 0:by]
            out_vy_ref[pl.ds(j - 1 - LOW, 1)] = new_vy[:, 0:bz, 0:by]
        else:
            for at, part in keep(p):
                p_ref[pl.ds(j, 1), at, :] = part
            store(1, j - 1, 1, new_vz)
            store(2, j - 1, 1, new_vy)

        if last:
            @pl.when(ix == 0)
            def _():
                out_vx_ref[0] = jnp.zeros((bz, by), jnp.float32)
        else:
            plane = jnp.zeros((3 * bz, lanes), jnp.float32)

            @pl.when(ix == 0)
            def _():
                for i in range(k, LOW):
                    for d in range(3):
                        new[d, i] = plane
                new[0, LOW] = plane

            @pl.when(ix == nx - 1)
            def _():
                for i in range(LOW + bx, first + count):
                    for d in range(3):
                        new[d, i] = plane


def final_kernel(p_ref, sum_ref, out_ref, *, cells):
    mean = jnp.sum(sum_ref[...]) * (1.0 / cells)
    out_ref[...] = p_ref[...] - mean


def swap(a, axis, start):
    count = lax.axis_size(axis)
    return lax.ppermute(a, axis, [(i, j) for k in range(start, count - 1, 2) for i, j in ((k, k + 1), (k + 1, k))])


def sum_everywhere(total):
    axes = ("gx", "gy", "gz")
    devices = math.prod(lax.axis_size(a) for a in axes)
    if devices & (devices - 1):
        return lax.psum(total, axes)
    bits = [1 << n for n in range(devices.bit_length() - 1)]
    stages = [bits[:1]] + [bits[n : n + 2] for n in range(1, len(bits), 2)]
    for stage in stages:
        masks = [stage[0]] if len(stage) == 1 else [stage[0], stage[1], stage[0] + stage[1]]
        parts = [lax.ppermute(total, axes, [(i, i ^ m) for i in range(devices)]) for m in masks]
        total = sum(parts, total)
    return total


def local(vel_x, vel_y, vel_z, pressure, phase, visc_scale, power_n, density):
    bx, bz, by = pressure.shape
    assert bx == 2 * HIGH and bz == HIGH
    f32 = jnp.float32
    ix, iz, iy = lax.axis_index("gx"), lax.axis_index("gz"), lax.axis_index("gy")
    ny = lax.axis_size("gy")
    cells = bx * bz * by * math.prod(lax.axis_size(a) for a in ("gx", "gz", "gy"))
    deep = bx + LOW + HIGH
    rows, lanes = 3 * bz, 2 * by
    shape = lambda *dims: jax.ShapeDtypeStruct(dims, f32)
    block = shape(bx, bz, by)
    scratch = lambda *dims: pltpu.VMEM(dims, f32)
    mebibyte = 1024 * 1024

    edge = pl.pallas_call(
        edge_kernel,
        out_shape=block,
        in_specs=[pl.BlockSpec(memory_space=pltpu.HBM)] * 5,
        out_specs=pl.BlockSpec(memory_space=pltpu.HBM),
        scratch_shapes=[
            scratch(FIELDS - 1, bx, bz, by),
            pltpu.VMEM((bx, bz, by), jnp.int32),
            scratch(bx, bz, by),
            pltpu.SemaphoreType.DMA((bx // GROUP, FIELDS)),
            pltpu.SemaphoreType.DMA((bx // GROUP,)),
        ],
        compiler_params=pltpu.CompilerParams(vmem_limit_bytes=58 * mebibyte),
    )(vel_x, vel_z, vel_y, pressure, phase)

    side = swap(edge, "gy", 0)
    if ny > 2:
        even = lax.rem(iy, 2) == 0
        other = swap(edge, "gy", 1)
        lane = lax.broadcasted_iota(jnp.int32, (bx, bz, by), 2)
        side = jnp.where((lane % LANE_STEP < HIGH) == even, side, other)
    clear = lambda v, axis, at: jnp.where((lax.broadcasted_iota(jnp.int32, v.shape, axis) == 0) & (at == 0), 0.0, v)
    fields = (clear(vel_x, 0, ix), clear(vel_z, 1, iz), clear(vel_y, 2, iy), pressure, phase.astype(f32))
    stack = jnp.concatenate([jnp.stack(fields, axis=1), side[:, None]], axis=1)

    even = lax.rem(ix, 2) == 0
    face_1 = swap(stack, "gz", 1)
    x_0 = swap(jnp.where(even, stack[HIGH:], stack[:HIGH]), "gx", 0)
    x_1 = swap(jnp.where(even, stack[:HIGH], stack[HIGH:]), "gx", 1)
    face_0 = swap(stack, "gz", 0)
    low = jnp.where(even, x_1[HIGH - LOW :], x_0[HIGH - LOW :])
    sides = jnp.concatenate([jnp.where(even, x_0, x_1), low], axis=0)
    corner_1 = swap(sides, "gz", 1)
    corner_0 = swap(sides, "gz", 0)

    tables = (visc_scale, (0.5 / math.log(2.0)) * (1.0 / power_n - 1.0), density)
    field = shape(deep, bz, lanes)
    own = pl.pallas_call(
        own_kernel,
        out_shape=(shape(3, deep, bz, lanes),) + (field,) * 4,
        in_specs=[VMEM] * 2 + [SMEM] * 3,
        out_specs=(VMEM,) * 5,
        compiler_params=pltpu.CompilerParams(vmem_limit_bytes=8 * mebibyte),
        cost_estimate=pl.CostEstimate(flops=deep * 30 * bz * lanes, bytes_accessed=12 * deep * bz * lanes * 4, transcendentals=0),
    )(stack, sides, *tables)
    vx, vz, vy, p, eta, total = pl.pallas_call(
        main_kernel,
        out_shape=(block,) * 5 + (shape(bz, by),),
        in_specs=[VMEM] * 9 + [SMEM] * 3,
        out_specs=(VMEM,) * 6,
        scratch_shapes=[
            scratch(3, deep, rows, lanes),
            scratch(3, deep, rows, lanes),
            scratch(deep, rows, lanes),
            scratch(7, deep, 2 * bz, lanes),
            scratch(3, deep, bz, lanes),
            scratch(4, rows, lanes),
            scratch(4, 2 * bz, lanes),
        ],
        compiler_params=pltpu.CompilerParams(vmem_limit_bytes=32 * mebibyte),
    )(*own, face_0, face_1, corner_0, corner_1, *tables)

    total = sum_everywhere(total)
    p = pl.pallas_call(
        lambda *refs: final_kernel(*refs, cells=float(cells)),
        out_shape=block,
        in_specs=[VMEM] * 2,
        out_specs=VMEM,
        compiler_params=pltpu.CompilerParams(vmem_limit_bytes=4 * mebibyte),
    )(p, total)
    return (vx, vy, vz, p, eta)


def solution(mesh):
    spec = P("gx", "gz", "gy")
    return jax.shard_map(
        local,
        mesh=mesh,
        in_specs=(spec,) * 5 + (P(),) * 3,
        out_specs=(spec,) * 5,
        check_vma=False,
    )
```

time: 65.1 us -> 55.6 us (0.85)
  blocking collectives: 20 us -> 0 us
  starting transfers between devices: 13 us -> 23.3 us
  waiting for transfers between devices: 6.27 us -> 10.5 us
  Pallas kernels: 20.2 us -> 17.2 us
  local copies, waits for them, and re-layouts: 4.22 us -> 3.17 us
    all_to_all x2 -> x0, blocking collectives: 20 us -> none  [exchange_sum(): return lax.all_to_all(total, axes, 0, 0, tiled=True)]
    ppermute x0 -> x7, starting transfers between devices: none -> 16.5 us  [sum_everywhere(): lax.ppermute(total, axes, [(i, i ^ m) for i in range(devices)])]
    ppermute x0 -> x7, waiting for transfers between devices: none -> 7.11 us  [sum_everywhere(): lax.ppermute(total, axes, [(i, i ^ m) for i in range(devices)])]
    ppermute x7, starting transfers between devices: 13 us -> 6.81 us  [swap(): lax.ppermute(a, axis, [(i, j) for k in range(start, count - 1, 2) for i,...]
    pallas_call x2 -> x3, Pallas kernels: 19.5 us -> 16.4 us  [the longest x1 13.3 us: local(): pl.pallas_call(main_kernel, out_shape=(block,) * 5 + (shape(bz, by),), in...]
    ppermute x7, waiting for transfers between devices: 6.27 us -> 3.36 us  [swap(): lax.ppermute(a, axis, [(i, j) for k in range(start, count - 1, 2) for i,...]
    unnamed x16 -> x17, local copies, waits for them, and re-layouts: 4.21 us -> 3.16 us
  transfers between devices with their start and end apart: 7 -> 14, of which waited for: 3 -> 7; matrix products, arithmetic and copies ran while one was open for 0% -> 0% of each run, Pallas kernels for 0% -> 2%
where the time goes in v5:
time: 55.6 us; the launch traced here: 55.3 us
  starting transfers between devices  23.3 us (42%)
  Pallas kernels  17.2 us (31%)
  waiting for transfers between devices  10.5 us (19%)
  local copies, waits for them, and re-layouts  3.17 us (6%)
  between operations  0.88 us (2%)
    ppermute x7, starting transfers between devices, sum_everywhere(): lax.ppermute(total, axes, [(i, i ^ m) for i in range(devices)])  16.5 us
    pallas_call x1, Pallas kernels, local(): pl.pallas_call(main_kernel, out_shape=(block,) * 5 + (shape(bz, by),), in...  13.3 us
    ppermute x7, waiting for transfers between devices, sum_everywhere(): lax.ppermute(total, axes, [(i, i ^ m) for i in range(devices)])  7.11 us
    ppermute x7, starting transfers between devices, swap(): lax.ppermute(a, axis, [(i, j) for k in range(start, count - 1, 2) for i,...  6.81 us
    ppermute x7, waiting for transfers between devices, swap(): lax.ppermute(a, axis, [(i, j) for k in range(start, count - 1, 2) for i,...  3.36 us
    unnamed x17, local copies, waits for them, and re-layouts  3.16 us
    pallas_call x1, Pallas kernels, local(): pl.pallas_call(edge_kernel, out_shape=block, in_specs=[pl.BlockSpec(memor...  2.08 us
  transfers between devices with their start and end apart: 14, of which 7 were waited for; matrix products, arithmetic and copies ran while one was open for 0% of the time, Pallas kernels for 2%

profile of v5, /device:TPU:0, one launch (start us, length us, event | category | flops | bytes accessed | tf_op | source)
XLA Modules:
  0.0 55.3 jit_solution(9232334225904148848)
XLA Ops:
  0.6 2.1 %shard_map.119 = f32[16,8,128]{2,1,0:T(8,128)} custom-call(f32[16,8,128]{2,1,0:T(8,128)} %vx_hbm.1, f32[16,8,128]{2,1,0:T(8,128)} %vz_hbm.1, f32[16,8,128]{2,1,0:T(8,128)} %vy_hbm.1, f32[16,8,128]{2,1,0:T(8,128)} %p_hbm.1, s32[16,8,128]{2,1,0:T(8,128)} %phase_hbm.1), custom_call_target="tpu_custom_call" | custom-call | tf_op jit(solution)/shard_map/pallas_call | solution.py:379
  2.7 3.0 %collective-permute-start = (f32[16,8,128]{2,1,0:T(8,128)}, f32[16,8,128]{2,1,0:T(8,128)S(1)}, u32[]{:S(2)}, u32[]{:S(2)}) collective-permute-start(f32[16,8,128]{2,1,0:T(8,128)} %shard_map.119), channel_id=1, source_target_pairs={{0,4},{4,0},{1,5},{5,1},{2,6},{6,2},{3,7},{7,3},{8,12},{12,8},{9,1... | collective-permute-start | bytes 196616 | tf_op jit(solution)/shard_map/ppermute | solution.py:348
  5.9 0.7 %copy-done.3 = f32[16,8,128]{2,1,0:T(8,128)S(1)} copy-done((f32[16,8,128]{2,1,0:T(8,128)S(1)}, f32[16,8,128]{2,1,0:T(8,128)}, u32[]{:S(2)}) %copy-start.3) | copy-done | bytes 65560
  6.7 0.8 %copy-done.4 = f32[16,8,128]{2,1,0:T(8,128)S(1)} copy-done((f32[16,8,128]{2,1,0:T(8,128)S(1)}, f32[16,8,128]{2,1,0:T(8,128)}, u32[]{:S(2)}) %copy-start.4) | copy-done | bytes 65560
  7.4 0.8 %copy-done.5 = f32[16,8,128]{2,1,0:T(8,128)S(1)} copy-done((f32[16,8,128]{2,1,0:T(8,128)S(1)}, f32[16,8,128]{2,1,0:T(8,128)}, u32[]{:S(2)}) %copy-start.5) | copy-done | bytes 65560
  8.3 0.8 %copy-done.6 = s32[16,8,128]{2,1,0:T(8,128)S(1)} copy-done((s32[16,8,128]{2,1,0:T(8,128)S(1)}, s32[16,8,128]{2,1,0:T(8,128)}, u32[]{:S(2)}) %copy-start.6) | copy-done | bytes 65560
  9.2 1.6 %collective-permute-start.1 = (f32[8,6,8,128]{3,2,1,0:T(8,128)S(1)}, f32[8,6,8,128]{3,2,1,0:T(8,128)S(1)}, u32[]{:S(2)}, u32[]{:S(2)}) collective-permute-start(f32[8,6,8,128]{3,2,1,0:T(8,128)S(1)} %get-tuple-element.28), channel_id=1, source_target_pairs={{0,8},{8,0},{16,24},{24,16},{1,9},{9,1},{17,25},{25,17},{2,10},{10... | collective-permute-start | bytes 589832 | tf_op jit(solution)/shard_map/ppermute | solution.py:348
  11.6 0.7 %collective-permute-start.4 = (f32[16,6,8,128]{3,2,1,0:T(8,128)S(1)}, f32[16,6,8,128]{3,2,1,0:T(8,128)S(1)}, u32[]{:S(2)}, u32[]{:S(2)}) collective-permute-start(f32[16,6,8,128]{3,2,1,0:T(8,128)S(1)} %bitcast_dynamic-update-slice_fusion.2.own_ref), channel_id=1, source_target_pairs={{1,2},{2,1},{5,6},{6,5},{9,10},{10,9},{13,14},{14,13},{17,18},{18,... | collective-permute-start | bytes 1179656 | tf_op jit(solution)/shard_map/ppermute | solution.py:348
  12.2 3.3 %collective-permute-done.1 = f32[8,6,8,128]{3,2,1,0:T(8,128)S(1)} collective-permute-done((f32[8,6,8,128]{3,2,1,0:T(8,128)S(1)}, f32[8,6,8,128]{3,2,1,0:T(8,128)S(1)}, u32[]{:S(2)}, u32[]{:S(2)}) %collective-permute-start.1) | collective-permute-done | bytes 196640 | tf_op jit(solution)/shard_map/ppermute | solution.py:348
  15.8 0.7 %collective-permute-start.6 = (f32[12,6,8,128]{3,2,1,0:T(8,128)S(1)}, f32[12,6,8,128]{3,2,1,0:T(8,128)S(1)}, u32[]{:S(2)}, u32[]{:S(2)}) collective-permute-start(f32[12,6,8,128]{3,2,1,0:T(8,128)S(1)} %pad_maximum_fusion.side_ref), channel_id=1, source_target_pairs={{1,2},{2,1},{5,6},{6,5},{9,10},{10,9},{13,14},{14,13},{17,18},{18,... | collective-permute-start | bytes 884744 | tf_op jit(solution)/shard_map/ppermute | solution.py:348
  16.5 1.0 %shard_map.120 = (f32[3,28,8,256]{3,2,1,0:T(8,128)S(1)}, f32[28,8,256]{2,1,0:T(8,128)S(1)}, f32[28,8,256]{2,1,0:T(8,128)S(1)}, f32[28,8,256]{2,1,0:T(8,128)S(1)}, f32[28,8,256]{2,1,0:T(8,128)S(1)}) custom-call(f32[16,6,8,128]{3,2,1,0:T(8,128)S(1)} %bitcast_dynamic-update-slice_fusion.2.own_ref, f32[12,6,8,128]{3,2,1,0:T(8,128)S(1)} %pad_maximum_fusion.side_ref, ...), custom_call_target="tpu_custom_call" | custom-call | flops 1720320 | bytes 2752512 | tf_op jit(solution)/shard_map/pallas_call | solution.py:416
  17.6 13.3 %shard_map.121 = (f32[16,8,128]{2,1,0:T(8,128)}, f32[16,8,128]{2,1,0:T(8,128)}, f32[16,8,128]{2,1,0:T(8,128)}, f32[16,8,128]{2,1,0:T(8,128)S(1)}, f32[16,8,128]{2,1,0:T(8,128)}, /*index=5*/f32[8,128]{1,0:T(8,128)S(1)}) custom-call(f32[3,28,8,256]{3,2,1,0:T(8,128)S(1)} %get-tuple-element.16.v_ref, f32[28,8,256]{2,1,0:T(8,128)S(1)} %get-tuple-element.17.p0_ref, ...), custom_call_target="tpu_custom_call" | custom-call | tf_op jit(solution)/shard_map/pallas_call | solution.py:424
  30.9 6.7 %collective-permute-start.7 = (f32[8,128]{1,0:T(8,128)S(1)}, f32[8,128]{1,0:T(8,128)S(1)}, u32[]{:S(2)}, u32[]{:S(2)}) collective-permute-start(f32[8,128]{1,0:T(8,128)S(1)} %get-tuple-element.25), channel_id=1, source_target_pairs={{0,1},{1,0},{2,3},{3,2},{4,5},{5,4},{6,7},{7,6},{8,9},{9,8},{10,11... | collective-permute-start | bytes 12296 | tf_op jit(solution)/shard_map/ppermute | solution.py:360
  37.6 0.8 %collective-permute-done.7 = f32[8,128]{1,0:T(8,128)S(1)} collective-permute-done((f32[8,128]{1,0:T(8,128)S(1)}, f32[8,128]{1,0:T(8,128)S(1)}, u32[]{:S(2)}, u32[]{:S(2)}) %collective-permute-start.7) | collective-permute-done | bytes 4128 | tf_op jit(solution)/shard_map/ppermute | solution.py:360
  38.4 1.9 %collective-permute-start.10 = (f32[8,128]{1,0:T(8,128)S(1)}, f32[8,128]{1,0:T(8,128)S(1)}, u32[]{:S(2)}, u32[]{:S(2)}) collective-permute-start(f32[8,128]{1,0:T(8,128)S(1)} %add.22), channel_id=1, source_target_pairs={{0,6},{1,7},{2,4},{3,5},{4,2},{5,3},{6,0},{7,1},{8,14},{9,15},{10,... | collective-permute-start | bytes 12296 | tf_op jit(solution)/shard_map/ppermute | solution.py:360
  40.3 1.0 %collective-permute-start.9 = (f32[8,128]{1,0:T(8,128)S(1)}, f32[8,128]{1,0:T(8,128)S(1)}, u32[]{:S(2)}, u32[]{:S(2)}) collective-permute-start(f32[8,128]{1,0:T(8,128)S(1)} %add.22), channel_id=1, source_target_pairs={{0,4},{1,5},{2,6},{3,7},{4,0},{5,1},{6,2},{7,3},{8,12},{9,13},{10,... | collective-permute-start | bytes 12296 | tf_op jit(solution)/shard_map/ppermute | solution.py:360
  41.9 1.0 %collective-permute-done.10 = f32[8,128]{1,0:T(8,128)S(1)} collective-permute-done((f32[8,128]{1,0:T(8,128)S(1)}, f32[8,128]{1,0:T(8,128)S(1)}, u32[]{:S(2)}, u32[]{:S(2)}) %collective-permute-start.10) | collective-permute-done | bytes 4128 | tf_op jit(solution)/shard_map/ppermute | solution.py:360
  42.9 1.0 %collective-permute-done.9 = f32[8,128]{1,0:T(8,128)S(1)} collective-permute-done((f32[8,128]{1,0:T(8,128)S(1)}, f32[8,128]{1,0:T(8,128)S(1)}, u32[]{:S(2)}, u32[]{:S(2)}) %collective-permute-start.9) | collective-permute-done | bytes 4128 | tf_op jit(solution)/shard_map/ppermute | solution.py:360
  43.9 1.0 %collective-permute-done.8 = f32[8,128]{1,0:T(8,128)S(1)} collective-permute-done((f32[8,128]{1,0:T(8,128)S(1)}, f32[8,128]{1,0:T(8,128)S(1)}, u32[]{:S(2)}, u32[]{:S(2)}) %collective-permute-start.8) | collective-permute-done | bytes 4128 | tf_op jit(solution)/shard_map/ppermute | solution.py:360
  44.9 3.6 %collective-permute-start.13 = (f32[8,128]{1,0:T(8,128)S(1)}, f32[8,128]{1,0:T(8,128)S(1)}, u32[]{:S(2)}, u32[]{:S(2)}) collective-permute-start(f32[8,128]{1,0:T(8,128)S(1)} %add_add_fusion.1), channel_id=1, source_target_pairs={{0,24},{1,25},{2,26},{3,27},{4,28},{5,29},{6,30},{7,31},{8,16},{9,... | collective-permute-start | bytes 12296 | tf_op jit(solution)/shard_map/ppermute | solution.py:360
  48.5 2.4 %collective-permute-start.12 = (f32[8,128]{1,0:T(8,128)S(1)}, f32[8,128]{1,0:T(8,128)S(1)}, u32[]{:S(2)}, u32[]{:S(2)}) collective-permute-start(f32[8,128]{1,0:T(8,128)S(1)} %add_add_fusion.1), channel_id=1, source_target_pairs={{0,16},{1,17},{2,18},{3,19},{4,20},{5,21},{6,22},{7,23},{8,24},{9,... | collective-permute-start | bytes 12296 | tf_op jit(solution)/shard_map/ppermute | solution.py:360
  51.2 1.8 %collective-permute-done.12 = f32[8,128]{1,0:T(8,128)S(1)} collective-permute-done((f32[8,128]{1,0:T(8,128)S(1)}, f32[8,128]{1,0:T(8,128)S(1)}, u32[]{:S(2)}, u32[]{:S(2)}) %collective-permute-start.12) | collective-permute-done | bytes 4128 | tf_op jit(solution)/shard_map/ppermute | solution.py:360
  53.0 1.5 %collective-permute-done.11 = f32[8,128]{1,0:T(8,128)S(1)} collective-permute-done((f32[8,128]{1,0:T(8,128)S(1)}, f32[8,128]{1,0:T(8,128)S(1)}, u32[]{:S(2)}, u32[]{:S(2)}) %collective-permute-start.11) | collective-permute-done | bytes 4128 | tf_op jit(solution)/shard_map/ppermute | solution.py:360
  54.5 0.8 %shard_map.122 = f32[16,8,128]{2,1,0:T(8,128)} custom-call(f32[16,8,128]{2,1,0:T(8,128)S(1)} %get-tuple-element.24.refs_0_, f32[8,128]{1,0:T(8,128)S(1)} %add_add_fusion.refs_1_), custom_call_target="tpu_custom_call" | custom-call | tf_op jit(solution)/shard_map/pallas_call | solution.py:442
  (41 shorter events, 2.1 us)
Async XLA Ops:
  0.6 5.1 %copy-start.2 = (f32[16,8,128]{2,1,0:T(8,128)S(1)}, f32[16,8,128]{2,1,0:T(8,128)}, u32[]{:S(2)}) copy-start(f32[16,8,128]{2,1,0:T(8,128)} %vx_hbm.1) | copy-start | bytes 196612
  2.7 6.4 %collective-permute-start = (f32[16,8,128]{2,1,0:T(8,128)}, f32[16,8,128]{2,1,0:T(8,128)S(1)}, u32[]{:S(2)}, u32[]{:S(2)}) collective-permute-start(f32[16,8,128]{2,1,0:T(8,128)} %shard_map.119), channel_id=1, source_target_pairs={{0,4},{4,0},{1,5},{5,1},{2,6},{6,2},{3,7},{7,3},{8,12},{12,8},{9,1... | collective-permute-start | bytes 196616 | tf_op jit(solution)/shard_map/ppermute | solution.py:348
  5.7 0.8 %copy-start.3 = (f32[16,8,128]{2,1,0:T(8,128)S(1)}, f32[16,8,128]{2,1,0:T(8,128)}, u32[]{:S(2)}) copy-start(f32[16,8,128]{2,1,0:T(8,128)} %vz_hbm.1) | copy-start | bytes 196612
  6.6 0.8 %copy-start.4 = (f32[16,8,128]{2,1,0:T(8,128)S(1)}, f32[16,8,128]{2,1,0:T(8,128)}, u32[]{:S(2)}) copy-start(f32[16,8,128]{2,1,0:T(8,128)} %vy_hbm.1) | copy-start | bytes 196612
  7.4 0.8 %copy-start.5 = (f32[16,8,128]{2,1,0:T(8,128)S(1)}, f32[16,8,128]{2,1,0:T(8,128)}, u32[]{:S(2)}) copy-start(f32[16,8,128]{2,1,0:T(8,128)} %p_hbm.1) | copy-start | bytes 196612
  8.3 0.8 %copy-start.6 = (s32[16,8,128]{2,1,0:T(8,128)S(1)}, s32[16,8,128]{2,1,0:T(8,128)}, u32[]{:S(2)}) copy-start(s32[16,8,128]{2,1,0:T(8,128)} %phase_hbm.1) | copy-start | bytes 196612
  9.2 6.4 %collective-permute-start.1 = (f32[8,6,8,128]{3,2,1,0:T(8,128)S(1)}, f32[8,6,8,128]{3,2,1,0:T(8,128)S(1)}, u32[]{:S(2)}, u32[]{:S(2)}) collective-permute-start(f32[8,6,8,128]{3,2,1,0:T(8,128)S(1)} %get-tuple-element.28), channel_id=1, source_target_pairs={{0,8},{8,0},{16,24},{24,16},{1,9},{9,1},{17,25},{25,17},{2,10},{10... | collective-permute-start | bytes 589832 | tf_op jit(solution)/shard_map/ppermute | solution.py:348
  10.8 4.8 %collective-permute-start.2 = (f32[8,6,8,128]{3,2,1,0:T(8,128)S(1)}, f32[8,6,8,128]{3,2,1,0:T(8,128)S(1)}, u32[]{:S(2)}, u32[]{:S(2)}) collective-permute-start(f32[8,6,8,128]{3,2,1,0:T(8,128)S(1)} %get-tuple-element.27), channel_id=1, source_target_pairs={{8,16},{16,8},{9,17},{17,9},{10,18},{18,10},{11,19},{19,11},{12,20... | collective-permute-start | bytes 589832 | tf_op jit(solution)/shard_map/ppermute | solution.py:348
  11.5 6.1 %collective-permute-start.3 = (f32[16,6,8,128]{3,2,1,0:T(8,128)S(1)}, f32[16,6,8,128]{3,2,1,0:T(8,128)S(1)}, u32[]{:S(2)}, u32[]{:S(2)}) collective-permute-start(f32[16,6,8,128]{3,2,1,0:T(8,128)S(1)} %bitcast_dynamic-update-slice_fusion.2.own_ref), channel_id=1, source_target_pairs={{0,1},{1,0},{2,3},{3,2},{4,5},{5,4},{6,7},{7,6},{8,9},{9,8},{10,11... | collective-permute-start | bytes 1179656 | tf_op jit(solution)/shard_map/ppermute | solution.py:348
  11.6 6.0 %collective-permute-start.4 = (f32[16,6,8,128]{3,2,1,0:T(8,128)S(1)}, f32[16,6,8,128]{3,2,1,0:T(8,128)S(1)}, u32[]{:S(2)}, u32[]{:S(2)}) collective-permute-start(f32[16,6,8,128]{3,2,1,0:T(8,128)S(1)} %bitcast_dynamic-update-slice_fusion.2.own_ref), channel_id=1, source_target_pairs={{1,2},{2,1},{5,6},{6,5},{9,10},{10,9},{13,14},{14,13},{17,18},{18,... | collective-permute-start | bytes 1179656 | tf_op jit(solution)/shard_map/ppermute | solution.py:348
  15.6 0.8 %copy-start.7 = (f32[4]{0:T(128)S(1)}, f32[4]{0:T(128)}, u32[]{:S(2)}) copy-start(f32[4]{0:T(128)} %param.14) | copy-start | bytes 52
  15.7 0.8 %copy-start = (f32[4]{0:T(128)S(1)}, f32[4]{0:T(128)}, u32[]{:S(2)}) copy-start(f32[4]{0:T(128)} %scale_ref.3) | copy-start | bytes 52
  15.7 0.8 %copy-start.1 = (f32[4]{0:T(128)S(1)}, f32[4]{0:T(128)}, u32[]{:S(2)}) copy-start(f32[4]{0:T(128)} %rho_table_ref.3) | copy-start | bytes 52
  15.7 1.9 %collective-permute-start.5 = (f32[12,6,8,128]{3,2,1,0:T(8,128)S(1)}, f32[12,6,8,128]{3,2,1,0:T(8,128)S(1)}, u32[]{:S(2)}, u32[]{:S(2)}) collective-permute-start(f32[12,6,8,128]{3,2,1,0:T(8,128)S(1)} %pad_maximum_fusion.side_ref), channel_id=1, source_target_pairs={{0,1},{1,0},{2,3},{3,2},{4,5},{5,4},{6,7},{7,6},{8,9},{9,8},{10,11... | collective-permute-start | bytes 884744 | tf_op jit(solution)/shard_map/ppermute | solution.py:348
  15.8 1.8 %collective-permute-start.6 = (f32[12,6,8,128]{3,2,1,0:T(8,128)S(1)}, f32[12,6,8,128]{3,2,1,0:T(8,128)S(1)}, u32[]{:S(2)}, u32[]{:S(2)}) collective-permute-start(f32[12,6,8,128]{3,2,1,0:T(8,128)S(1)} %pad_maximum_fusion.side_ref), channel_id=1, source_target_pairs={{1,2},{2,1},{5,6},{6,5},{9,10},{10,9},{13,14},{14,13},{17,18},{18,... | collective-permute-start | bytes 884744 | tf_op jit(solution)/shard_map/ppermute | solution.py:348
  30.9 7.5 %collective-permute-start.7 = (f32[8,128]{1,0:T(8,128)S(1)}, f32[8,128]{1,0:T(8,128)S(1)}, u32[]{:S(2)}, u32[]{:S(2)}) collective-permute-start(f32[8,128]{1,0:T(8,128)S(1)} %get-tuple-element.25), channel_id=1, source_target_pairs={{0,1},{1,0},{2,3},{3,2},{4,5},{5,4},{6,7},{7,6},{8,9},{9,8},{10,11... | collective-permute-start | bytes 12296 | tf_op jit(solution)/shard_map/ppermute | solution.py:360
  38.4 4.5 %collective-permute-start.10 = (f32[8,128]{1,0:T(8,128)S(1)}, f32[8,128]{1,0:T(8,128)S(1)}, u32[]{:S(2)}, u32[]{:S(2)}) collective-permute-start(f32[8,128]{1,0:T(8,128)S(1)} %add.22), channel_id=1, source_target_pairs={{0,6},{1,7},{2,4},{3,5},{4,2},{5,3},{6,0},{7,1},{8,14},{9,15},{10,... | collective-permute-start | bytes 12296 | tf_op jit(solution)/shard_map/ppermute | solution.py:360
  40.3 3.6 %collective-permute-start.9 = (f32[8,128]{1,0:T(8,128)S(1)}, f32[8,128]{1,0:T(8,128)S(1)}, u32[]{:S(2)}, u32[]{:S(2)}) collective-permute-start(f32[8,128]{1,0:T(8,128)S(1)} %add.22), channel_id=1, source_target_pairs={{0,4},{1,5},{2,6},{3,7},{4,0},{5,1},{6,2},{7,3},{8,12},{9,13},{10,... | collective-permute-start | bytes 12296 | tf_op jit(solution)/shard_map/ppermute | solution.py:360
  41.3 3.6 %collective-permute-start.8 = (f32[8,128]{1,0:T(8,128)S(1)}, f32[8,128]{1,0:T(8,128)S(1)}, u32[]{:S(2)}, u32[]{:S(2)}) collective-permute-start(f32[8,128]{1,0:T(8,128)S(1)} %add.22), channel_id=1, source_target_pairs={{0,2},{1,3},{2,0},{3,1},{4,6},{5,7},{6,4},{7,5},{8,10},{9,11},{10,... | collective-permute-start | bytes 12296 | tf_op jit(solution)/shard_map/ppermute | solution.py:360
  44.9 6.3 %collective-permute-start.13 = (f32[8,128]{1,0:T(8,128)S(1)}, f32[8,128]{1,0:T(8,128)S(1)}, u32[]{:S(2)}, u32[]{:S(2)}) collective-permute-start(f32[8,128]{1,0:T(8,128)S(1)} %add_add_fusion.1), channel_id=1, source_target_pairs={{0,24},{1,25},{2,26},{3,27},{4,28},{5,29},{6,30},{7,31},{8,16},{9,... | collective-permute-start | bytes 12296 | tf_op jit(solution)/shard_map/ppermute | solution.py:360
  48.5 4.5 %collective-permute-start.12 = (f32[8,128]{1,0:T(8,128)S(1)}, f32[8,128]{1,0:T(8,128)S(1)}, u32[]{:S(2)}, u32[]{:S(2)}) collective-permute-start(f32[8,128]{1,0:T(8,128)S(1)} %add_add_fusion.1), channel_id=1, source_target_pairs={{0,16},{1,17},{2,18},{3,19},{4,20},{5,21},{6,22},{7,23},{8,24},{9,... | collective-permute-start | bytes 12296 | tf_op jit(solution)/shard_map/ppermute | solution.py:360
  50.9 3.6 %collective-permute-start.11 = (f32[8,128]{1,0:T(8,128)S(1)}, f32[8,128]{1,0:T(8,128)S(1)}, u32[]{:S(2)}, u32[]{:S(2)}) collective-permute-start(f32[8,128]{1,0:T(8,128)S(1)} %add_add_fusion.1), channel_id=1, source_target_pairs={{0,8},{1,9},{2,10},{3,11},{4,12},{5,13},{6,14},{7,15},{8,0},{9,1},... | collective-permute-start | bytes 12296 | tf_op jit(solution)/shard_map/ppermute | solution.py:360

commit v6 on v5

--- a/solution.py
+++ b/solution.py
@@ -12,7 +12,7 @@
 LOW = ITERS
 HIGH = 2 * ITERS
 FIELDS = 5
-LANE_STEP = 16
+LANE_STEP = LOW + HIGH
 UNROLL = 3
 GROUP = 4
 
@@ -45,40 +45,50 @@
     return 3 * (ITERS - k + 1) <= bz
 
 
-def edge_kernel(vx_hbm, vz_hbm, vy_hbm, p_hbm, phase_hbm, edge_hbm, field_ref, phase_ref, edge_ref, sems, out_sems):
-    bx, bz, by = phase_ref.shape
-    sources = (vx_hbm, vz_hbm, vy_hbm, p_hbm, phase_hbm)
-    targets = [field_ref.at[f] for f in range(FIELDS - 1)] + [phase_ref]
-    groups = bx // GROUP
+def start_copies(sources, targets, sems):
     copies = []
-    for g in range(groups):
+    for g in range(sources[0].shape[0] // GROUP):
         at = pl.ds(g * GROUP, GROUP)
         copies.append(
             [pltpu.make_async_copy(a.at[at], b.at[at], sems.at[g, f]) for f, (a, b) in enumerate(zip(sources, targets))]
         )
         for copy in copies[-1]:
             copy.start()
+    return copies
+
+
+def clean_group(g, field_ref, phase_ref):
+    bx, bz, by = phase_ref.shape
     ix, iz, iy = lax.axis_index("gx"), lax.axis_index("gz"), lax.axis_index("gy")
+    plane, row, lane = (lax.broadcasted_iota(jnp.int32, (GROUP, bz, by), d) for d in range(3))
+    at = pl.ds(g * GROUP, GROUP)
+    vx, vz, vy, p = (field_ref[f, at] for f in range(FIELDS - 1))
+    if g == 0:
+        vx = jnp.where((plane > 0) | (ix > 0), vx, 0.0)
+    vz = jnp.where((row > 0) | (iz > 0), vz, 0.0)
+    vy = jnp.where((lane > 0) | (iy > 0), vy, 0.0)
+    return vx, vz, vy, p, phase_ref[at].astype(jnp.float32)
+
+
+def edge_kernel(vx_hbm, vz_hbm, vy_hbm, p_hbm, phase_hbm, edge_hbm, field_ref, phase_ref, edge_ref, sems, out_sems):
+    bx, bz, by = phase_ref.shape
+    targets = [field_ref.at[f] for f in range(FIELDS - 1)] + [phase_ref]
+    copies = start_copies((vx_hbm, vz_hbm, vy_hbm, p_hbm, phase_hbm), targets, sems)
     lane = lax.broadcasted_iota(jnp.int32, (1, bz, by), 2)
-    row = lax.broadcasted_iota(jnp.int32, (1, bz, by), 1)
-    plane = lax.broadcasted_iota(jnp.int32, (GROUP, bz, by), 0)
+    half = bx // GROUP // 2
     outs = []
-    for g in range(groups):
-        for copy in copies[g]:
-            copy.wait()
+    for g in range(half):
+        edge = jnp.zeros((GROUP, bz, by), jnp.float32)
+        for upper in range(2):
+            for copy in copies[g + upper * half]:
+                copy.wait()
+            for f, a in enumerate(clean_group(g + upper * half, field_ref, phase_ref)):
+                base = by // 2 * upper + LANE_STEP * f
+                first = pltpu.roll(a, base, 2) if base else a
+                edge = jnp.where((lane >= base) & (lane < base + HIGH), first, edge)
+                last = pltpu.roll(a, (base + LANE_STEP) % by, 2)
+                edge = jnp.where((lane >= base + HIGH) & (lane < base + LANE_STEP), last, edge)
         at = pl.ds(g * GROUP, GROUP)
-        vx, vz, vy, p = (field_ref[f, at] for f in range(FIELDS - 1))
-        if g == 0:
-            vx = jnp.where((plane > 0) | (ix > 0), vx, 0.0)
-        vz = jnp.where((row > 0) | (iz > 0), vz, 0.0)
-        vy = jnp.where((lane > 0) | (iy > 0), vy, 0.0)
-        edge = jnp.zeros((GROUP, bz, by), jnp.float32)
-        for f, a in enumerate((vx, vz, vy, p, phase_ref[at].astype(jnp.float32))):
-            base = LANE_STEP * f
-            first = pltpu.roll(a, base, 2) if base else a
-            edge = jnp.where((lane >= base) & (lane < base + HIGH), first, edge)
-            last = pltpu.roll(a, base + LANE_STEP, 2)
-            edge = jnp.where((lane >= base + LANE_STEP - LOW) & (lane < base + LANE_STEP), last, edge)
         edge_ref[at] = edge
         outs.append(pltpu.make_async_copy(edge_ref.at[at], edge_hbm.at[at], out_sems.at[g]))
         outs[-1].start()
@@ -86,7 +96,23 @@
         copy.wait()
 
 
-def unpack(block, ok, tables):
+def stack_kernel(vx_hbm, vz_hbm, vy_hbm, p_hbm, phase_hbm, stack_hbm, field_ref, phase_ref, stack_ref, sems, out_sems):
+    targets = [field_ref.at[f] for f in range(FIELDS - 1)] + [phase_ref]
+    copies = start_copies((vx_hbm, vz_hbm, vy_hbm, p_hbm, phase_hbm), targets, sems)
+    outs = []
+    for g in range(len(copies)):
+        for copy in copies[g]:
+            copy.wait()
+        at = pl.ds(g * GROUP, GROUP)
+        for f, a in enumerate(clean_group(g, field_ref, phase_ref)):
+            stack_ref[at, f] = a
+        outs.append(pltpu.make_async_copy(stack_ref.at[at], stack_hbm.at[at], out_sems.at[g]))
+        outs[-1].start()
+    for copy in outs:
+        copy.wait()
+
+
+def unpack(block, upper, ok, tables):
     count, _, bz, by = block.shape
     iy = lax.axis_index("gy")
     lane = lax.broadcasted_iota(jnp.int32, (1, bz, by), 2)
@@ -96,7 +122,7 @@
     edge = block[:, FIELDS]
     out = []
     for f in range(FIELDS):
-        shift = LANE_STEP * f
+        shift = by // 2 * upper + LANE_STEP * f
         a = pltpu.roll(edge, (by - shift) % by, 2) if shift else edge
         b = pltpu.roll(edge, (by - LANE_STEP - shift) % by, 2)
         out.append([block[:, f], jnp.where(right, a, jnp.where(left, b, 0.0))])
@@ -116,20 +142,24 @@
     return out
 
 
-def unpack_planes(own_ref, side_ref, ok, tables, store):
-    bx = own_ref.shape[0]
+def unpack_own(ref, ok, tables, store):
+    groups = ref.shape[0] // GROUP // 2
+    for upper in range(2):
+
+        def group(g, carry):
+            at = g * GROUP + upper * HIGH
+            store(pl.ds(LOW + at, GROUP), unpack(ref[pl.ds(at, GROUP)], upper, ok, tables))
+            return carry
+
+        lax.fori_loop(0, groups, group, 0)
+
+
+def unpack_sides(ref, bx, ok, tables, store):
     ix, nx = lax.axis_index("gx"), lax.axis_size("gx")
-
-    def group(g, carry):
-        store(pl.ds(LOW + g * GROUP, GROUP), unpack(own_ref[pl.ds(g * GROUP, GROUP)], ok, tables))
-        return carry
-
-    lax.fori_loop(0, bx // GROUP, group, 0)
-    for g in range((LOW + HIGH) // GROUP):
-        at = g * GROUP
-        high = at < HIGH
-        values = unpack(side_ref[pl.ds(at, GROUP)], ok & (ix < nx - 1 if high else ix > 0), tables)
-        store(pl.ds(LOW + bx + at if high else at - HIGH, GROUP), values)
+    for at in range(0, HIGH + LOW, GROUP):
+        low = at >= HIGH
+        values = unpack(ref[pl.ds(at, GROUP)], int(low), ok & (ix > 0 if low else ix < nx - 1), tables)
+        store(pl.ds(at - HIGH if low else LOW + bx + at, GROUP), values)
 
 
 def own_kernel(own_ref, side_ref, scale_ref, power_ref, rho_table_ref, v_ref, p_ref, pre_ref, power_field_ref, rho_ref):
@@ -141,39 +171,55 @@
             ref[planes, :, 0:by] = own
             ref[planes, :, by : 2 * by] = beside
 
-    unpack_planes(own_ref, side_ref, lax.axis_index("gz") >= 0, (scale_ref, power_ref, rho_table_ref), store)
+    tables = (scale_ref, power_ref, rho_table_ref)
+    unpack_own(own_ref, True, tables, store)
+    unpack_sides(side_ref, own_ref.shape[0], True, tables, store)
+
+
+def halo_store(halo_ref, shared_ref, t):
+    bz = shared_ref.shape[-2]
+    by = shared_ref.shape[-1] // 2
+    rows = slice(t * bz // 2, (t + 1) * bz // 2)
+
+    def store(planes, values):
+        for n, pair in enumerate(values):
+            for part, value in enumerate(pair):
+                at = slice(part * by, (part + 1) * by)
+                halo_ref[n, planes, t * bz : (t + 1) * bz, at] = value
+                if n >= 4:
+                    shared_ref[n - 4, planes, rows, at] = value[:, rows]
+
+    return store
+
+
+def face_kernel(face_0_ref, face_1_ref, scale_ref, power_ref, rho_table_ref, halo_ref, shared_ref):
+    iz, nz = lax.axis_index("gz"), lax.axis_size("gz")
+    tables = (scale_ref, power_ref, rho_table_ref)
+    for parity in range(2):
+        @pl.when(lax.rem(iz, 2) == parity)
+        def _():
+            faces = (face_0_ref, face_1_ref)
+            unpack_own(faces[parity], iz < nz - 1, tables, halo_store(halo_ref, shared_ref, 0))
+            unpack_own(faces[1 - parity], iz > 0, tables, halo_store(halo_ref, shared_ref, 1))
 
 
 def main_kernel(
-    v_ref, p0_ref, pre_ref, power_field_ref, rho_ref,
-    face_0_ref, face_1_ref, corner_0_ref, corner_1_ref, scale_ref, power_ref, rho_table_ref,
-    out_vx_ref, out_vz_ref, out_vy_ref, out_p_ref, out_eta_ref, sum_ref,
-    va_ref, vb_ref, p_ref, halo_ref, shared_ref, weight_ref, weight2_ref,
+    v_ref, p0_ref, pre_ref, power_field_ref, rho_ref, _halo, _shared,
+    corner_0_ref, corner_1_ref, scale_ref, power_ref, rho_table_ref,
+    out_vx_ref, out_vz_ref, out_vy_ref, out_p_ref, out_eta_ref, sum_ref, halo_ref, shared_ref,
+    va_ref, vb_ref, p_ref, weight_ref, weight2_ref,
 ):
-    bx, _, bz, by = face_0_ref.shape
+    bx, bz, by = out_p_ref.shape
     lanes = 2 * by
     nx, nz, ny = lax.axis_size("gx"), lax.axis_size("gz"), lax.axis_size("gy")
     ix, iz, iy = lax.axis_index("gx"), lax.axis_index("gz"), lax.axis_index("gy")
     tables = (scale_ref, power_ref, rho_table_ref)
-
-    def store(t):
-        def store_rows(planes, values):
-            for n, pair in enumerate(values):
-                for part, value in enumerate(pair):
-                    halo_ref[n, planes, t * bz : (t + 1) * bz, part * by : (part + 1) * by] = value
-                    if n >= 4:
-                        half = bz // 2
-                        rows = slice(t * half, (t + 1) * half)
-                        shared_ref[n - 4, planes, rows, part * by : (part + 1) * by] = value[:, rows]
-
-        return store_rows
-
     for parity in range(2):
         @pl.when(lax.rem(iz, 2) == parity)
         def _():
-            faces, corners = (face_0_ref, face_1_ref), (corner_0_ref, corner_1_ref)
-            unpack_planes(faces[parity], corners[parity], iz < nz - 1, tables, store(0))
-            unpack_planes(faces[1 - parity], corners[1 - parity], iz > 0, tables, store(1))
+            corners = (corner_0_ref, corner_1_ref)
+            unpack_sides(corners[parity], bx, iz < nz - 1, tables, halo_store(halo_ref, shared_ref, 0))
+            unpack_sides(corners[1 - parity], bx, iz > 0, tables, halo_store(halo_ref, shared_ref, 1))
 
     for ref, high in ((weight_ref, 2 * bz), (weight2_ref, bz + bz // 2)):
         shape = ref.shape[1:]
@@ -353,13 +399,14 @@
     devices = math.prod(lax.axis_size(a) for a in axes)
     if devices & (devices - 1):
         return lax.psum(total, axes)
-    bits = [1 << n for n in range(devices.bit_length() - 1)]
-    stages = [bits[:1]] + [bits[n : n + 2] for n in range(1, len(bits), 2)]
-    for stage in stages:
-        masks = [stage[0]] if len(stage) == 1 else [stage[0], stage[1], stage[0] + stage[1]]
-        parts = [lax.ppermute(total, axes, [(i, i ^ m) for i in range(devices)]) for m in masks]
-        total = sum(parts, total)
-    return total
+    odd = range(1, devices, 2)
+    first = lax.rem(lax.axis_index("gz"), 2) == 0
+    total = jnp.where(first, 0.0, total + lax.ppermute(total, axes, [(i ^ 1, i) for i in odd]))
+    bits = [1 << n for n in range(1, devices.bit_length() - 1)]
+    for stage in [bits[n : n + 2] for n in range(0, len(bits), 2)]:
+        masks = stage if len(stage) == 1 else [stage[0], stage[1], stage[0] + stage[1]]
+        total = sum([lax.ppermute(total, axes, [(i, i ^ m) for i in odd]) for m in masks], total)
+    return total + lax.ppermute(total, axes, [(i, i ^ 1) for i in odd])
 
 
 def local(vel_x, vel_y, vel_z, pressure, phase, visc_scale, power_n, density):
@@ -376,30 +423,35 @@
     scratch = lambda *dims: pltpu.VMEM(dims, f32)
     mebibyte = 1024 * 1024
 
-    edge = pl.pallas_call(
-        edge_kernel,
-        out_shape=block,
-        in_specs=[pl.BlockSpec(memory_space=pltpu.HBM)] * 5,
-        out_specs=pl.BlockSpec(memory_space=pltpu.HBM),
-        scratch_shapes=[
-            scratch(FIELDS - 1, bx, bz, by),
-            pltpu.VMEM((bx, bz, by), jnp.int32),
-            scratch(bx, bz, by),
-            pltpu.SemaphoreType.DMA((bx // GROUP, FIELDS)),
-            pltpu.SemaphoreType.DMA((bx // GROUP,)),
-        ],
-        compiler_params=pltpu.CompilerParams(vmem_limit_bytes=58 * mebibyte),
-    )(vel_x, vel_z, vel_y, pressure, phase)
-
+    hbm = pl.BlockSpec(memory_space=pltpu.HBM)
+
+    def packing(kernel, *dims):
+        groups = bx // GROUP
+        return pl.pallas_call(
+            kernel,
+            out_shape=shape(*dims),
+            in_specs=[hbm] * 5,
+            out_specs=hbm,
+            scratch_shapes=[
+                scratch(FIELDS - 1, bx, bz, by),
+                pltpu.VMEM((bx, bz, by), jnp.int32),
+                scratch(*dims),
+                pltpu.SemaphoreType.DMA((groups, FIELDS)),
+                pltpu.SemaphoreType.DMA((groups,)),
+            ],
+            compiler_params=pltpu.CompilerParams(vmem_limit_bytes=58 * mebibyte),
+            cost_estimate=pl.CostEstimate(flops=0, bytes_accessed=10 * bx * bz * by * 4, transcendentals=0),
+        )(vel_x, vel_z, vel_y, pressure, phase)
+
+    edge = packing(edge_kernel, bx // 2, bz, by)
     side = swap(edge, "gy", 0)
     if ny > 2:
         even = lax.rem(iy, 2) == 0
         other = swap(edge, "gy", 1)
-        lane = lax.broadcasted_iota(jnp.int32, (bx, bz, by), 2)
-        side = jnp.where((lane % LANE_STEP < HIGH) == even, side, other)
-    clear = lambda v, axis, at: jnp.where((lax.broadcasted_iota(jnp.int32, v.shape, axis) == 0) & (at == 0), 0.0, v)
-    fields = (clear(vel_x, 0, ix), clear(vel_z, 1, iz), clear(vel_y, 2, iy), pressure, phase.astype(f32))
-    stack = jnp.concatenate([jnp.stack(fields, axis=1), side[:, None]], axis=1)
+        lane = lax.broadcasted_iota(jnp.int32, side.shape, 2) % (by // 2) % LANE_STEP
+        side = jnp.where((lane < HIGH) == even, side, other)
+    fields = packing(stack_kernel, bx, FIELDS, bz, by)
+    stack = jnp.concatenate([fields, jnp.concatenate([side, side])[:, None]], axis=1)
 
     even = lax.rem(ix, 2) == 0
     face_1 = swap(stack, "gz", 1)
@@ -421,22 +473,29 @@
         compiler_params=pltpu.CompilerParams(vmem_limit_bytes=8 * mebibyte),
         cost_estimate=pl.CostEstimate(flops=deep * 30 * bz * lanes, bytes_accessed=12 * deep * bz * lanes * 4, transcendentals=0),
     )(stack, sides, *tables)
-    vx, vz, vy, p, eta, total = pl.pallas_call(
+    halo = pl.pallas_call(
+        face_kernel,
+        out_shape=(shape(7, deep, 2 * bz, lanes), shape(3, deep, bz, lanes)),
+        in_specs=[VMEM] * 2 + [SMEM] * 3,
+        out_specs=(VMEM,) * 2,
+        compiler_params=pltpu.CompilerParams(vmem_limit_bytes=8 * mebibyte),
+        cost_estimate=pl.CostEstimate(flops=deep * 30 * bz * lanes, bytes_accessed=24 * bx * bz * lanes * 4, transcendentals=0),
+    )(face_0, face_1, *tables)
+    vx, vz, vy, p, eta, total, _, _ = pl.pallas_call(
         main_kernel,
-        out_shape=(block,) * 5 + (shape(bz, by),),
+        out_shape=(block,) * 5 + (shape(bz, by),) + tuple(shape(*a.shape) for a in halo),
         in_specs=[VMEM] * 9 + [SMEM] * 3,
-        out_specs=(VMEM,) * 6,
+        out_specs=(VMEM,) * 8,
+        input_output_aliases={5: 6, 6: 7},
         scratch_shapes=[
             scratch(3, deep, rows, lanes),
             scratch(3, deep, rows, lanes),
             scratch(deep, rows, lanes),
-            scratch(7, deep, 2 * bz, lanes),
-            scratch(3, deep, bz, lanes),
             scratch(4, rows, lanes),
             scratch(4, 2 * bz, lanes),
         ],
         compiler_params=pltpu.CompilerParams(vmem_limit_bytes=32 * mebibyte),
-    )(*own, face_0, face_1, corner_0, corner_1, *tables)
+    )(*own, *halo, corner_0, corner_1, *tables)
 
     total = sum_everywhere(total)
     p = pl.pallas_call(

time: 55.6 us -> 67.2 us (1.21)
  waiting for transfers between devices: 10.5 us -> 19.6 us
  local copies, waits for them, and re-layouts: 3.17 us -> 0.01 us
  Pallas kernels: 17.2 us -> 19.6 us
  other arithmetic: 0.3 us -> 2.29 us
  starting transfers between devices: 23.3 us -> 24.2 us
    ppermute x7 -> x8, waiting for transfers between devices: 7.11 us -> 17.5 us  [the longest x1 16.6 us: sum_everywhere(): return total + lax.ppermute(total, axes, [(i, i ^ 1) for i in odd])]
    ppermute x7, starting transfers between devices: 6.81 us -> 13 us  [swap(): lax.ppermute(a, axis, [(i, j) for k in range(start, count - 1, 2) for i,...]
    ppermute x7 -> x8, starting transfers between devices: 16.5 us -> 11.1 us  [the longest x1 5.89 us: sum_everywhere(): lax.ppermute(total, axes, [(i ^ 1, i) for i in odd])]
    unnamed x17 -> x6, local copies, waits for them, and re-layouts: 3.16 us -> 0.01 us
    pallas_call x2 -> x4, Pallas kernels: 15.4 us -> 17.8 us  [the longest x1 12.6 us: local(): pl.pallas_call(main_kernel, out_shape=(block,) * 5 + (shape(bz, by),) + t...]
    ppermute x7, waiting for transfers between devices: 3.36 us -> 2.19 us  [swap(): lax.ppermute(a, axis, [(i, j) for k in range(start, count - 1, 2) for i,...]
    select_n x1, other arithmetic: 0.03 us -> 1.2 us  [local(): x_1 = swap(jnp.where(even, stack[:HIGH], stack[HIGH:]), 'gx', 1)]
    concatenate x0 -> x1, other arithmetic: none -> 1.01 us  [local(): jnp.concatenate([fields, jnp.concatenate([side, side])[:, None]], axis=1)]
  transfers between devices with their start and end apart: 14 -> 15, of which waited for: 7 -> 4; matrix products, arithmetic and copies ran while one was open for 0% -> 2% of each run, Pallas kernels for 2% -> 6%
where the time goes in v6:
time: 67.2 us; the launch traced here: 66.7 us
  starting transfers between devices  24.2 us (36%)
  Pallas kernels  19.6 us (29%)
  waiting for transfers between devices  19.6 us (29%)
  other arithmetic  2.29 us (3%)
  between operations  0.94 us (1%)
    ppermute x1, waiting for transfers between devices, sum_everywhere(): return total + lax.ppermute(total, axes, [(i, i ^ 1) for i in odd])  16.6 us
    ppermute x7, starting transfers between devices, swap(): lax.ppermute(a, axis, [(i, j) for k in range(start, count - 1, 2) for i,...  13 us
    pallas_call x1, Pallas kernels, local(): pl.pallas_call(main_kernel, out_shape=(block,) * 5 + (shape(bz, by),) + t...  12.6 us
    ppermute x1, starting transfers between devices, sum_everywhere(): lax.ppermute(total, axes, [(i ^ 1, i) for i in odd])  5.89 us
    ppermute x6, starting transfers between devices, sum_everywhere(): lax.ppermute(total, axes, [(i, i ^ m) for i in odd])  3.96 us
    pallas_call x2, Pallas kernels, packing(): pl.pallas_call(kernel, out_shape=shape(*dims), in_specs=[hbm] * 5, out_sp...  3.84 us
    ppermute x7, waiting for transfers between devices, swap(): lax.ppermute(a, axis, [(i, j) for k in range(start, count - 1, 2) for i,...  2.19 us
    pallas_call x1, Pallas kernels, local(): pl.pallas_call(face_kernel, out_shape=(shape(7, deep, 2 * bz, lanes), sha...  1.37 us
  transfers between devices with their start and end apart: 15, of which 4 were waited for; matrix products, arithmetic and copies ran while one was open for 2% of the time, Pallas kernels for 6%

profile of v6, /device:TPU:0, one launch (start us, length us, event | category | flops | bytes accessed | tf_op | source)
XLA Modules:
  0.0 66.7 jit_solution(16329846501603241614)
XLA Ops:
  0.7 2.1 %shard_map.120 = f32[8,8,128]{2,1,0:T(8,128)} custom-call(f32[16,8,128]{2,1,0:T(8,128)} %vx_hbm.3, f32[16,8,128]{2,1,0:T(8,128)} %vz_hbm.3, f32[16,8,128]{2,1,0:T(8,128)} %vy_hbm.3, f32[16,8,128]{2,1,0:T(8,128)} %p_hbm.3, s32[16,8,128]{2,1,0:T(8,128)} %phase_hbm.3), custom_call_target="tpu_custom_call" | custom-call | bytes 655360 | tf_op jit(solution)/shard_map/pallas_call | solution.py:430
  2.7 3.0 %collective-permute-start = (f32[8,8,128]{2,1,0:T(8,128)}, f32[8,8,128]{2,1,0:T(8,128)S(1)}, u32[]{:S(2)}, u32[]{:S(2)}) collective-permute-start(f32[8,8,128]{2,1,0:T(8,128)} %shard_map.120), channel_id=1, source_target_pairs={{0,4},{4,0},{1,5},{5,1},{2,6},{6,2},{3,7},{7,3},{8,12},{12,8},{9,1... | collective-permute-start | bytes 98312 | tf_op jit(solution)/shard_map/ppermute | solution.py:394
  5.7 1.8 %shard_map.119 = f32[16,5,8,128]{3,2,1,0:T(8,128)} custom-call(f32[16,8,128]{2,1,0:T(8,128)} %vx_hbm.3, f32[16,8,128]{2,1,0:T(8,128)} %vz_hbm.3, f32[16,8,128]{2,1,0:T(8,128)} %vy_hbm.3, f32[16,8,128]{2,1,0:T(8,128)} %p_hbm.3, s32[16,8,128]{2,1,0:T(8,128)} %phase_hbm.3), custom_call_target="tpu_custom_call" | custom-call | bytes 655360 | tf_op jit(solution)/shard_map/pallas_call | solution.py:430
  7.9 1.2 %broadcast_select_fusion.1 = (f32[8,6,8,128]{3,2,1,0:T(8,128)S(1)}, f32[8,6,8,128]{3,2,1,0:T(8,128)S(1)}) fusion(pred[]{:T(512)S(6)} %eq.6, f32[16,1,8,128]{3,2,1,0:T(8,128)S(1)} %maximum_bitcast_fusion, f32[16,5,8,128]{3,2,1,0:T(8,128)} %shard_map.119), kind=kLoop, calls=%fused_computation.10 | loop fusion | flops 294912 | bytes 786433 | tf_op jit(solution)/shard_map/jit(_where)/select_n | solution.py:459
  9.1 0.7 %collective-permute-start.2 = (f32[8,6,8,128]{3,2,1,0:T(8,128)S(1)}, f32[8,6,8,128]{3,2,1,0:T(8,128)S(1)}, u32[]{:S(2)}, u32[]{:S(2)}) collective-permute-start(f32[8,6,8,128]{3,2,1,0:T(8,128)S(1)} %get-tuple-element.31), channel_id=1, source_target_pairs={{8,16},{16,8},{9,17},{17,9},{10,18},{18,10},{11,19},{19,11},{12,20... | collective-permute-start | bytes 589832 | tf_op jit(solution)/shard_map/ppermute | solution.py:394
  9.7 5.0 %collective-permute-start.1 = (f32[8,6,8,128]{3,2,1,0:T(8,128)S(1)}, f32[8,6,8,128]{3,2,1,0:T(8,128)S(1)}, u32[]{:S(2)}, u32[]{:S(2)}) collective-permute-start(f32[8,6,8,128]{3,2,1,0:T(8,128)S(1)} %get-tuple-element.32), channel_id=1, source_target_pairs={{0,8},{8,0},{16,24},{24,16},{1,9},{9,1},{17,25},{25,17},{2,10},{10... | collective-permute-start | bytes 589832 | tf_op jit(solution)/shard_map/ppermute | solution.py:394
  14.7 1.0 %pad_maximum_fusion.own_ref = f32[16,6,8,128]{3,2,1,0:T(8,128)S(1)} fusion(f32[16,1,8,128]{3,2,1,0:T(8,128)S(1)} %maximum_bitcast_fusion, f32[16,5,8,128]{3,2,1,0:T(8,128)} %shard_map.119), kind=kLoop, calls=%fused_computation.2 | loop fusion | flops 98304 | bytes 786432 | tf_op jit(solution)/shard_map/concatenate | solution.py:454
  15.8 0.7 %collective-permute-start.4 = (f32[16,6,8,128]{3,2,1,0:T(8,128)S(1)}, f32[16,6,8,128]{3,2,1,0:T(8,128)S(1)}, u32[]{:S(2)}, u32[]{:S(2)}) collective-permute-start(f32[16,6,8,128]{3,2,1,0:T(8,128)S(1)} %pad_maximum_fusion.own_ref), channel_id=1, source_target_pairs={{1,2},{2,1},{5,6},{6,5},{9,10},{10,9},{13,14},{14,13},{17,18},{18,... | collective-permute-start | bytes 1179656 | tf_op jit(solution)/shard_map/ppermute | solution.py:394
  16.5 1.9 %collective-permute-done.1 = f32[8,6,8,128]{3,2,1,0:T(8,128)S(1)} collective-permute-done((f32[8,6,8,128]{3,2,1,0:T(8,128)S(1)}, f32[8,6,8,128]{3,2,1,0:T(8,128)S(1)}, u32[]{:S(2)}, u32[]{:S(2)}) %collective-permute-start.1) | collective-permute-done | bytes 196640 | tf_op jit(solution)/shard_map/ppermute | solution.py:394
  18.4 0.7 %collective-permute-start.6 = (f32[12,6,8,128]{3,2,1,0:T(8,128)S(1)}, f32[12,6,8,128]{3,2,1,0:T(8,128)S(1)}, u32[]{:S(2)}, u32[]{:S(2)}) collective-permute-start(f32[12,6,8,128]{3,2,1,0:T(8,128)S(1)} %pad_maximum_fusion.1.side_ref), channel_id=1, source_target_pairs={{1,2},{2,1},{5,6},{6,5},{9,10},{10,9},{13,14},{14,13},{17,18},{18,... | collective-permute-start | bytes 884744 | tf_op jit(solution)/shard_map/ppermute | solution.py:394
  19.1 2.9 %collective-permute-start.5 = (f32[12,6,8,128]{3,2,1,0:T(8,128)S(1)}, f32[12,6,8,128]{3,2,1,0:T(8,128)S(1)}, u32[]{:S(2)}, u32[]{:S(2)}) collective-permute-start(f32[12,6,8,128]{3,2,1,0:T(8,128)S(1)} %pad_maximum_fusion.1.side_ref), channel_id=1, source_target_pairs={{0,1},{1,0},{2,3},{3,2},{4,5},{5,4},{6,7},{7,6},{8,9},{9,8},{10,11... | collective-permute-start | bytes 884744 | tf_op jit(solution)/shard_map/ppermute | solution.py:394
  22.1 1.0 %shard_map.121 = (f32[3,28,8,256]{3,2,1,0:T(8,128)S(1)}, f32[28,8,256]{2,1,0:T(8,128)S(1)}, f32[28,8,256]{2,1,0:T(8,128)S(1)}, f32[28,8,256]{2,1,0:T(8,128)S(1)}, f32[28,8,256]{2,1,0:T(8,128)S(1)}) custom-call(f32[16,6,8,128]{3,2,1,0:T(8,128)S(1)} %pad_maximum_fusion.own_ref, f32[12,6,8,128]{3,2,1,0:T(8,128)S(1)} %pad_maximum_fusion.1.side_ref, ...), custom_call_target="tpu_custom_call" | custom-call | flops 1720320 | bytes 2752512 | tf_op jit(solution)/shard_map/pallas_call | solution.py:468
  23.1 1.4 %shard_map.122 = (f32[7,28,16,256]{3,2,1,0:T(8,128)S(1)}, f32[3,28,8,256]{3,2,1,0:T(8,128)S(1)}) custom-call(f32[16,6,8,128]{3,2,1,0:T(8,128)S(1)} %collective-permute-done.3.face_0_ref, f32[16,6,8,128]{3,2,1,0:T(8,128)S(1)} %collective-permute-done.4.face_1_ref, f32[4]{0:T(128)S(1)} %copy-done, f32[4]{0:T(128)S(1)} %add_multiply_fusion.power_ref, ...), custom_call_target="tpu_custom_call" | custom-call | flops 1720320 | bytes 3145728 | tf_op jit(solution)/shard_map/pallas_call | solution.py:476
  24.6 12.6 %shard_map.123 = (f32[16,8,128]{2,1,0:T(8,128)}, f32[16,8,128]{2,1,0:T(8,128)}, f32[16,8,128]{2,1,0:T(8,128)}, f32[16,8,128]{2,1,0:T(8,128)S(1)}, f32[16,8,128]{...) custom-call(f32[3,28,8,256]{3,2,1,0:T(8,128)S(1)} %get-tuple-element, ...), custom_call_target="tpu_custom_call", output_to_operand_aliasing={{6}: (5, {}), {7}: (6, {})} | custom-call | tf_op jit(solution)/shard_map/pallas_call | solution.py:484
  37.1 5.9 %collective-permute-start.7 = (f32[8,128]{1,0:T(8,128)S(1)}, f32[8,128]{1,0:T(8,128)S(1)}, u32[]{:S(2)}, u32[]{:S(2)}) collective-permute-start(f32[8,128]{1,0:T(8,128)S(1)} %get-tuple-element.29), channel_id=1, source_target_pairs={{0,1},{2,3},{4,5},{6,7},{8,9},{10,11},{12,13},{14,15},{16,17},{18,... | collective-permute-start | bytes 12296 | tf_op jit(solution)/shard_map/ppermute | solution.py:404
  43.1 0.8 %collective-permute-done.7 = f32[8,128]{1,0:T(8,128)S(1)} collective-permute-done((f32[8,128]{1,0:T(8,128)S(1)}, f32[8,128]{1,0:T(8,128)S(1)}, u32[]{:S(2)}, u32[]{:S(2)}) %collective-permute-start.7) | collective-permute-done | bytes 4128 | tf_op jit(solution)/shard_map/ppermute | solution.py:404
  44.5 0.7 collective-permute-start.9
  45.2 0.7 collective-permute-start.8
  45.9 0.7 collective-permute-start.13
  46.6 0.7 collective-permute-start.12
  47.2 0.7 collective-permute-start.11
  48.0 1.3 %collective-permute-start.14 = (f32[8,128]{1,0:T(8,128)S(1)}, f32[8,128]{1,0:T(8,128)S(1)}, u32[]{:S(2)}, u32[]{:S(2)}) collective-permute-start(f32[8,128]{1,0:T(8,128)S(1)} %add_add_fusion), channel_id=1, source_target_pairs={{1,0},{3,2},{5,4},{7,6},{9,8},{11,10},{13,12},{15,14},{17,16},{19,... | collective-permute-start | bytes 12296 | tf_op jit(solution)/shard_map/ppermute | solution.py:409
  49.3 16.6 %collective-permute-done.14 = f32[8,128]{1,0:T(8,128)S(1)} collective-permute-done((f32[8,128]{1,0:T(8,128)S(1)}, f32[8,128]{1,0:T(8,128)S(1)}, u32[]{:S(2)}, u32[]{:S(2)}) %collective-permute-start.14) | collective-permute-done | bytes 4128 | tf_op jit(solution)/shard_map/ppermute | solution.py:409
  65.9 0.8 %shard_map.124 = f32[16,8,128]{2,1,0:T(8,128)} custom-call(f32[16,8,128]{2,1,0:T(8,128)S(1)} %get-tuple-element.28.refs_0_, f32[8,128]{1,0:T(8,128)S(1)} %add.32.refs_1_), custom_call_target="tpu_custom_call" | custom-call | tf_op jit(solution)/shard_map/pallas_call | solution.py:501
  (29 shorter events, 1.2 us)
Async XLA Ops:
  0.6 21.4 %copy-start.2 = (f32[4]{0:T(128)S(1)}, f32[4]{0:T(128)}, u32[]{:S(2)}) copy-start(f32[4]{0:T(128)} %param.14) | copy-start | bytes 52
  0.6 21.4 %copy-start.1 = (f32[4]{0:T(128)S(1)}, f32[4]{0:T(128)}, u32[]{:S(2)}) copy-start(f32[4]{0:T(128)} %rho_table_ref.5) | copy-start | bytes 52
  0.7 21.4 %copy-start = (f32[4]{0:T(128)S(1)}, f32[4]{0:T(128)}, u32[]{:S(2)}) copy-start(f32[4]{0:T(128)} %scale_ref.5) | copy-start | bytes 52
  2.7 5.1 %collective-permute-start = (f32[8,8,128]{2,1,0:T(8,128)}, f32[8,8,128]{2,1,0:T(8,128)S(1)}, u32[]{:S(2)}, u32[]{:S(2)}) collective-permute-start(f32[8,8,128]{2,1,0:T(8,128)} %shard_map.120), channel_id=1, source_target_pairs={{0,4},{4,0},{1,5},{5,1},{2,6},{6,2},{3,7},{7,3},{8,12},{12,8},{9,1... | collective-permute-start | bytes 98312 | tf_op jit(solution)/shard_map/ppermute | solution.py:394
  9.1 7.4 %collective-permute-start.2 = (f32[8,6,8,128]{3,2,1,0:T(8,128)S(1)}, f32[8,6,8,128]{3,2,1,0:T(8,128)S(1)}, u32[]{:S(2)}, u32[]{:S(2)}) collective-permute-start(f32[8,6,8,128]{3,2,1,0:T(8,128)S(1)} %get-tuple-element.31), channel_id=1, source_target_pairs={{8,16},{16,8},{9,17},{17,9},{10,18},{18,10},{11,19},{19,11},{12,20... | collective-permute-start | bytes 589832 | tf_op jit(solution)/shard_map/ppermute | solution.py:394
  9.7 8.6 %collective-permute-start.1 = (f32[8,6,8,128]{3,2,1,0:T(8,128)S(1)}, f32[8,6,8,128]{3,2,1,0:T(8,128)S(1)}, u32[]{:S(2)}, u32[]{:S(2)}) collective-permute-start(f32[8,6,8,128]{3,2,1,0:T(8,128)S(1)} %get-tuple-element.32), channel_id=1, source_target_pairs={{0,8},{8,0},{16,24},{24,16},{1,9},{9,1},{17,25},{25,17},{2,10},{10... | collective-permute-start | bytes 589832 | tf_op jit(solution)/shard_map/ppermute | solution.py:394
  15.7 7.4 %collective-permute-start.3 = (f32[16,6,8,128]{3,2,1,0:T(8,128)S(1)}, f32[16,6,8,128]{3,2,1,0:T(8,128)S(1)}, u32[]{:S(2)}, u32[]{:S(2)}) collective-permute-start(f32[16,6,8,128]{3,2,1,0:T(8,128)S(1)} %pad_maximum_fusion.own_ref), channel_id=1, source_target_pairs={{0,1},{1,0},{2,3},{3,2},{4,5},{5,4},{6,7},{7,6},{8,9},{9,8},{10,11... | collective-permute-start | bytes 1179656 | tf_op jit(solution)/shard_map/ppermute | solution.py:394
  15.8 7.3 %collective-permute-start.4 = (f32[16,6,8,128]{3,2,1,0:T(8,128)S(1)}, f32[16,6,8,128]{3,2,1,0:T(8,128)S(1)}, u32[]{:S(2)}, u32[]{:S(2)}) collective-permute-start(f32[16,6,8,128]{3,2,1,0:T(8,128)S(1)} %pad_maximum_fusion.own_ref), channel_id=1, source_target_pairs={{1,2},{2,1},{5,6},{6,5},{9,10},{10,9},{13,14},{14,13},{17,18},{18,... | collective-permute-start | bytes 1179656 | tf_op jit(solution)/shard_map/ppermute | solution.py:394
  18.4 6.1 %collective-permute-start.6 = (f32[12,6,8,128]{3,2,1,0:T(8,128)S(1)}, f32[12,6,8,128]{3,2,1,0:T(8,128)S(1)}, u32[]{:S(2)}, u32[]{:S(2)}) collective-permute-start(f32[12,6,8,128]{3,2,1,0:T(8,128)S(1)} %pad_maximum_fusion.1.side_ref), channel_id=1, source_target_pairs={{1,2},{2,1},{5,6},{6,5},{9,10},{10,9},{13,14},{14,13},{17,18},{18,... | collective-permute-start | bytes 884744 | tf_op jit(solution)/shard_map/ppermute | solution.py:394
  19.1 5.4 %collective-permute-start.5 = (f32[12,6,8,128]{3,2,1,0:T(8,128)S(1)}, f32[12,6,8,128]{3,2,1,0:T(8,128)S(1)}, u32[]{:S(2)}, u32[]{:S(2)}) collective-permute-start(f32[12,6,8,128]{3,2,1,0:T(8,128)S(1)} %pad_maximum_fusion.1.side_ref), channel_id=1, source_target_pairs={{0,1},{1,0},{2,3},{3,2},{4,5},{5,4},{6,7},{7,6},{8,9},{9,8},{10,11... | collective-permute-start | bytes 884744 | tf_op jit(solution)/shard_map/ppermute | solution.py:394
  37.1 6.7 %collective-permute-start.7 = (f32[8,128]{1,0:T(8,128)S(1)}, f32[8,128]{1,0:T(8,128)S(1)}, u32[]{:S(2)}, u32[]{:S(2)}) collective-permute-start(f32[8,128]{1,0:T(8,128)S(1)} %get-tuple-element.29), channel_id=1, source_target_pairs={{0,1},{2,3},{4,5},{6,7},{8,9},{10,11},{12,13},{14,15},{16,17},{18,... | collective-permute-start | bytes 12296 | tf_op jit(solution)/shard_map/ppermute | solution.py:404
  43.9 2.0 %collective-permute-start.10 = (f32[8,128]{1,0:T(8,128)S(1)}, f32[8,128]{1,0:T(8,128)S(1)}, u32[]{:S(2)}, u32[]{:S(2)}) collective-permute-start(f32[8,128]{1,0:T(8,128)S(1)} %add_select_fusion), channel_id=1, source_target_pairs={{1,7},{3,5},{5,3},{7,1},{9,15},{11,13},{13,11},{15,9},{17,23},{19,... | collective-permute-start | bytes 12296 | tf_op jit(solution)/shard_map/ppermute | solution.py:408
  44.5 1.4 %collective-permute-start.9 = (f32[8,128]{1,0:T(8,128)S(1)}, f32[8,128]{1,0:T(8,128)S(1)}, u32[]{:S(2)}, u32[]{:S(2)}) collective-permute-start(f32[8,128]{1,0:T(8,128)S(1)} %add_select_fusion), channel_id=1, source_target_pairs={{1,5},{3,7},{5,1},{7,3},{9,13},{11,15},{13,9},{15,11},{17,21},{19,... | collective-permute-start | bytes 12296 | tf_op jit(solution)/shard_map/ppermute | solution.py:408
  45.2 0.7 %collective-permute-start.8 = (f32[8,128]{1,0:T(8,128)S(1)}, f32[8,128]{1,0:T(8,128)S(1)}, u32[]{:S(2)}, u32[]{:S(2)}) collective-permute-start(f32[8,128]{1,0:T(8,128)S(1)} %add_select_fusion), channel_id=1, source_target_pairs={{1,3},{3,1},{5,7},{7,5},{9,11},{11,9},{13,15},{15,13},{17,19},{19,... | collective-permute-start | bytes 12296 | tf_op jit(solution)/shard_map/ppermute | solution.py:408
  45.9 2.0 %collective-permute-start.13 = (f32[8,128]{1,0:T(8,128)S(1)}, f32[8,128]{1,0:T(8,128)S(1)}, u32[]{:S(2)}, u32[]{:S(2)}) collective-permute-start(f32[8,128]{1,0:T(8,128)S(1)} %add_add_fusion.1), channel_id=1, source_target_pairs={{1,25},{3,27},{5,29},{7,31},{9,17},{11,19},{13,21},{15,23},{17,9},... | collective-permute-start | bytes 12296 | tf_op jit(solution)/shard_map/ppermute | solution.py:408
  46.6 1.4 %collective-permute-start.12 = (f32[8,128]{1,0:T(8,128)S(1)}, f32[8,128]{1,0:T(8,128)S(1)}, u32[]{:S(2)}, u32[]{:S(2)}) collective-permute-start(f32[8,128]{1,0:T(8,128)S(1)} %add_add_fusion.1), channel_id=1, source_target_pairs={{1,17},{3,19},{5,21},{7,23},{9,25},{11,27},{13,29},{15,31},{17,1},... | collective-permute-start | bytes 12296 | tf_op jit(solution)/shard_map/ppermute | solution.py:408
  47.2 0.7 %collective-permute-start.11 = (f32[8,128]{1,0:T(8,128)S(1)}, f32[8,128]{1,0:T(8,128)S(1)}, u32[]{:S(2)}, u32[]{:S(2)}) collective-permute-start(f32[8,128]{1,0:T(8,128)S(1)} %add_add_fusion.1), channel_id=1, source_target_pairs={{1,9},{3,11},{5,13},{7,15},{9,1},{11,3},{13,5},{15,7},{17,25},{19,... | collective-permute-start | bytes 12296 | tf_op jit(solution)/shard_map/ppermute | solution.py:408
  48.0 17.9 %collective-permute-start.14 = (f32[8,128]{1,0:T(8,128)S(1)}, f32[8,128]{1,0:T(8,128)S(1)}, u32[]{:S(2)}, u32[]{:S(2)}) collective-permute-start(f32[8,128]{1,0:T(8,128)S(1)} %add_add_fusion), channel_id=1, source_target_pairs={{1,0},{3,2},{5,4},{7,6},{9,8},{11,10},{13,12},{15,14},{17,16},{19,... | collective-permute-start | bytes 12296 | tf_op jit(solution)/shard_map/ppermute | solution.py:409

commit v7 on v6

--- a/solution.py
+++ b/solution.py
@@ -70,56 +70,62 @@
     return vx, vz, vy, p, phase_ref[at].astype(jnp.float32)
 
 
-def edge_kernel(vx_hbm, vz_hbm, vy_hbm, p_hbm, phase_hbm, edge_hbm, field_ref, phase_ref, edge_ref, sems, out_sems):
+def pack_kernel(
+    vx_hbm, vz_hbm, vy_hbm, p_hbm, phase_hbm, edge_hbm, x_0_hbm, x_1_hbm, stack_hbm,
+    field_ref, phase_ref, edge_ref, stack_ref, sems, out_sems,
+):
     bx, bz, by = phase_ref.shape
     targets = [field_ref.at[f] for f in range(FIELDS - 1)] + [phase_ref]
     copies = start_copies((vx_hbm, vz_hbm, vy_hbm, p_hbm, phase_hbm), targets, sems)
     lane = lax.broadcasted_iota(jnp.int32, (1, bz, by), 2)
     half = bx // GROUP // 2
     outs = []
+
+    def out(source, target):
+        outs.append(pltpu.make_async_copy(source, target, out_sems.at[len(outs)]))
+        outs[-1].start()
+
     for g in range(half):
         edge = jnp.zeros((GROUP, bz, by), jnp.float32)
         for upper in range(2):
+            at = pl.ds((g + upper * half) * GROUP, GROUP)
             for copy in copies[g + upper * half]:
                 copy.wait()
             for f, a in enumerate(clean_group(g + upper * half, field_ref, phase_ref)):
+                stack_ref[at, f] = a
                 base = by // 2 * upper + LANE_STEP * f
                 first = pltpu.roll(a, base, 2) if base else a
                 edge = jnp.where((lane >= base) & (lane < base + HIGH), first, edge)
                 last = pltpu.roll(a, (base + LANE_STEP) % by, 2)
                 edge = jnp.where((lane >= base + HIGH) & (lane < base + LANE_STEP), last, edge)
+            out(stack_ref.at[at], stack_hbm.at[at])
         at = pl.ds(g * GROUP, GROUP)
         edge_ref[at] = edge
-        outs.append(pltpu.make_async_copy(edge_ref.at[at], edge_hbm.at[at], out_sems.at[g]))
-        outs[-1].start()
+        out(edge_ref.at[at], edge_hbm.at[at])
+    sem = out_sems.at[len(outs)], out_sems.at[len(outs) + 1]
+    lower, upper = stack_ref.at[pl.ds(0, HIGH)], stack_ref.at[pl.ds(HIGH, HIGH)]
+    for parity, (first, second) in enumerate(((upper, lower), (lower, upper))):
+        @pl.when(lax.rem(lax.axis_index("gx"), 2) == parity)
+        def _():
+            pair = pltpu.make_async_copy(first, x_0_hbm, sem[0]), pltpu.make_async_copy(second, x_1_hbm, sem[1])
+            for copy in pair:
+                copy.start()
+            for copy in pair:
+                copy.wait()
+
     for copy in outs:
         copy.wait()
 
 
-def stack_kernel(vx_hbm, vz_hbm, vy_hbm, p_hbm, phase_hbm, stack_hbm, field_ref, phase_ref, stack_ref, sems, out_sems):
-    targets = [field_ref.at[f] for f in range(FIELDS - 1)] + [phase_ref]
-    copies = start_copies((vx_hbm, vz_hbm, vy_hbm, p_hbm, phase_hbm), targets, sems)
-    outs = []
-    for g in range(len(copies)):
-        for copy in copies[g]:
-            copy.wait()
-        at = pl.ds(g * GROUP, GROUP)
-        for f, a in enumerate(clean_group(g, field_ref, phase_ref)):
-            stack_ref[at, f] = a
-        outs.append(pltpu.make_async_copy(stack_ref.at[at], stack_hbm.at[at], out_sems.at[g]))
-        outs[-1].start()
-    for copy in outs:
-        copy.wait()
-
-
-def unpack(block, upper, ok, tables):
-    count, _, bz, by = block.shape
+def unpack(ref, at, side, upper, ok, tables):
+    bz, by = ref.shape[-2:]
+    block = ref[pl.ds(at * FIELDS, GROUP * FIELDS)].reshape(GROUP, FIELDS, bz, by)
+    edge = ref[pl.ds(side, GROUP)]
     iy = lax.axis_index("gy")
     lane = lax.broadcasted_iota(jnp.int32, (1, bz, by), 2)
     right = (lane < HIGH) & (iy < lax.axis_size("gy") - 1)
     left = (lane >= by - LOW) & (iy > 0)
     ok = jnp.where(ok, 1.0, 0.0)
-    edge = block[:, FIELDS]
     out = []
     for f in range(FIELDS):
         shift = by // 2 * upper + LANE_STEP * f
@@ -143,22 +149,23 @@
 
 
 def unpack_own(ref, ok, tables, store):
-    groups = ref.shape[0] // GROUP // 2
+    bx = 2 * HIGH
     for upper in range(2):
 
         def group(g, carry):
             at = g * GROUP + upper * HIGH
-            store(pl.ds(LOW + at, GROUP), unpack(ref[pl.ds(at, GROUP)], upper, ok, tables))
+            store(pl.ds(LOW + at, GROUP), unpack(ref, at, bx * FIELDS + g * GROUP, upper, ok, tables))
             return carry
 
-        lax.fori_loop(0, groups, group, 0)
+        lax.fori_loop(0, HIGH // GROUP, group, 0)
 
 
 def unpack_sides(ref, bx, ok, tables, store):
     ix, nx = lax.axis_index("gx"), lax.axis_size("gx")
     for at in range(0, HIGH + LOW, GROUP):
         low = at >= HIGH
-        values = unpack(ref[pl.ds(at, GROUP)], int(low), ok & (ix > 0 if low else ix < nx - 1), tables)
+        side = (HIGH + LOW) * FIELDS + at
+        values = unpack(ref, at, side, int(low), ok & (ix > 0 if low else ix < nx - 1), tables)
         store(pl.ds(at - HIGH if low else LOW + bx + at, GROUP), values)
 
 
@@ -173,7 +180,7 @@
 
     tables = (scale_ref, power_ref, rho_table_ref)
     unpack_own(own_ref, True, tables, store)
-    unpack_sides(side_ref, own_ref.shape[0], True, tables, store)
+    unpack_sides(side_ref, 2 * HIGH, True, tables, store)
 
 
 def halo_store(halo_ref, shared_ref, t):
@@ -399,14 +406,11 @@
     devices = math.prod(lax.axis_size(a) for a in axes)
     if devices & (devices - 1):
         return lax.psum(total, axes)
-    odd = range(1, devices, 2)
-    first = lax.rem(lax.axis_index("gz"), 2) == 0
-    total = jnp.where(first, 0.0, total + lax.ppermute(total, axes, [(i ^ 1, i) for i in odd]))
-    bits = [1 << n for n in range(1, devices.bit_length() - 1)]
-    for stage in [bits[n : n + 2] for n in range(0, len(bits), 2)]:
+    bits = [1 << n for n in range(devices.bit_length() - 1)]
+    for stage in [bits[:1]] + [bits[n : n + 2] for n in range(1, len(bits), 2)]:
         masks = stage if len(stage) == 1 else [stage[0], stage[1], stage[0] + stage[1]]
-        total = sum([lax.ppermute(total, axes, [(i, i ^ m) for i in odd]) for m in masks], total)
-    return total + lax.ppermute(total, axes, [(i, i ^ 1) for i in odd])
+        total = sum([lax.ppermute(total, axes, [(i, i ^ m) for i in range(devices)]) for m in masks], total)
+    return total
 
 
 def local(vel_x, vel_y, vel_z, pressure, phase, visc_scale, power_n, density):
@@ -425,41 +429,45 @@
 
     hbm = pl.BlockSpec(memory_space=pltpu.HBM)
 
-    def packing(kernel, *dims):
-        groups = bx // GROUP
-        return pl.pallas_call(
-            kernel,
-            out_shape=shape(*dims),
-            in_specs=[hbm] * 5,
-            out_specs=hbm,
-            scratch_shapes=[
-                scratch(FIELDS - 1, bx, bz, by),
-                pltpu.VMEM((bx, bz, by), jnp.int32),
-                scratch(*dims),
-                pltpu.SemaphoreType.DMA((groups, FIELDS)),
-                pltpu.SemaphoreType.DMA((groups,)),
-            ],
-            compiler_params=pltpu.CompilerParams(vmem_limit_bytes=58 * mebibyte),
-            cost_estimate=pl.CostEstimate(flops=0, bytes_accessed=10 * bx * bz * by * 4, transcendentals=0),
-        )(vel_x, vel_z, vel_y, pressure, phase)
-
-    edge = packing(edge_kernel, bx // 2, bz, by)
+    groups = bx // GROUP
+    edge, half_0, half_1, stack = pl.pallas_call(
+        pack_kernel,
+        out_shape=(
+            shape(HIGH, bz, by),
+            shape(HIGH, FIELDS, bz, by),
+            shape(HIGH, FIELDS, bz, by),
+            shape(bx, FIELDS, bz, by),
+        ),
+        in_specs=[hbm] * 5,
+        out_specs=(hbm,) * 4,
+        scratch_shapes=[
+            scratch(FIELDS - 1, bx, bz, by),
+            pltpu.VMEM((bx, bz, by), jnp.int32),
+            scratch(HIGH, bz, by),
+            scratch(bx, FIELDS, bz, by),
+            pltpu.SemaphoreType.DMA((groups, FIELDS)),
+            pltpu.SemaphoreType.DMA((groups + groups // 2 + 2,)),
+        ],
+        compiler_params=pltpu.CompilerParams(vmem_limit_bytes=58 * mebibyte),
+        cost_estimate=pl.CostEstimate(flops=0, bytes_accessed=16 * bx * bz * by * 4, transcendentals=0),
+    )(vel_x, vel_z, vel_y, pressure, phase)
+
     side = swap(edge, "gy", 0)
+    x_0, x_1 = swap(half_0, "gx", 0), swap(half_1, "gx", 1)
     if ny > 2:
         even = lax.rem(iy, 2) == 0
         other = swap(edge, "gy", 1)
         lane = lax.broadcasted_iota(jnp.int32, side.shape, 2) % (by // 2) % LANE_STEP
         side = jnp.where((lane < HIGH) == even, side, other)
-    fields = packing(stack_kernel, bx, FIELDS, bz, by)
-    stack = jnp.concatenate([fields, jnp.concatenate([side, side])[:, None]], axis=1)
-
+    side_0, side_1 = swap(side, "gx", 0), swap(side, "gx", 1)
+
+    face = jnp.concatenate([stack.reshape(bx * FIELDS, bz, by), side])
+    face_1 = swap(face, "gz", 1)
+    face_0 = swap(face, "gz", 0)
     even = lax.rem(ix, 2) == 0
-    face_1 = swap(stack, "gz", 1)
-    x_0 = swap(jnp.where(even, stack[HIGH:], stack[:HIGH]), "gx", 0)
-    x_1 = swap(jnp.where(even, stack[:HIGH], stack[HIGH:]), "gx", 1)
-    face_0 = swap(stack, "gz", 0)
-    low = jnp.where(even, x_1[HIGH - LOW :], x_0[HIGH - LOW :])
-    sides = jnp.concatenate([jnp.where(even, x_0, x_1), low], axis=0)
+    choose = lambda a, b: (jnp.where(even, a, b), jnp.where(even, b, a)[HIGH - LOW :])
+    tiles = [a.reshape(-1, bz, by) for a in choose(x_0, x_1) + choose(side_0, side_1)]
+    sides = jnp.concatenate(tiles)
     corner_1 = swap(sides, "gz", 1)
     corner_0 = swap(sides, "gz", 0)
 
@@ -472,7 +480,7 @@
         out_specs=(VMEM,) * 5,
         compiler_params=pltpu.CompilerParams(vmem_limit_bytes=8 * mebibyte),
         cost_estimate=pl.CostEstimate(flops=deep * 30 * bz * lanes, bytes_accessed=12 * deep * bz * lanes * 4, transcendentals=0),
-    )(stack, sides, *tables)
+    )(face, sides, *tables)
     halo = pl.pallas_call(
         face_kernel,
         out_shape=(shape(7, deep, 2 * bz, lanes), shape(3, deep, bz, lanes)),

time: 67.2 us -> 56.3 us (0.84)
  waiting for transfers between devices: 19.6 us -> 7.44 us
  starting transfers between devices: 24.2 us -> 26.7 us
  Pallas kernels: 19.6 us -> 17.9 us
  local copies, waits for them, and re-layouts: 0.01 us -> 1.33 us
    ppermute x8 -> x7, waiting for transfers between devices: 17.5 us -> 7.41 us  [sum_everywhere(): lax.ppermute(total, axes, [(i, i ^ m) for i in range(devices)])]
    ppermute x7 -> x9, starting transfers between devices: 13 us -> 17.2 us  [swap(): lax.ppermute(a, axis, [(i, j) for k in range(start, count - 1, 2) for i,...]
    ppermute x7 -> x9, waiting for transfers between devices: 2.19 us -> 0.02 us  [swap(): lax.ppermute(a, axis, [(i, j) for k in range(start, count - 1, 2) for i,...]
    ppermute x8 -> x7, starting transfers between devices: 11.1 us -> 9.51 us  [sum_everywhere(): lax.ppermute(total, axes, [(i, i ^ m) for i in range(devices)])]
    pallas_call x2 -> x1, Pallas kernels: 3.84 us -> 2.24 us  [local(): pl.pallas_call(pack_kernel, out_shape=(shape(HIGH, bz, by), shape(HIGH, F...]
    unnamed x6 -> x8, local copies, waits for them, and re-layouts: 0.01 us -> 1.33 us
    select_n x4, other arithmetic: 1.23 us -> 0.04 us  [the longest x2 0.03 us: local(): jnp.where(even, a, b)]
  transfers between devices with their start and end apart: 15 -> 16, of which waited for: 4 -> 6; matrix products, arithmetic and copies ran while one was open for 2% -> 3% of each run, Pallas kernels for 6% -> 4%
where the time goes in v7:
time: 56.3 us; the launch traced here: 56 us
  starting transfers between devices  26.7 us (47%)
  Pallas kernels  17.9 us (32%)
  waiting for transfers between devices  7.44 us (13%)
  other arithmetic  1.73 us (3%)
  local copies, waits for them, and re-layouts  1.33 us (2%)
  between operations  0.84 us (1%)
    ppermute x9, starting transfers between devices, swap(): lax.ppermute(a, axis, [(i, j) for k in range(start, count - 1, 2) for i,...  17.2 us
    pallas_call x1, Pallas kernels, local(): pl.pallas_call(main_kernel, out_shape=(block,) * 5 + (shape(bz, by),) + t...  12.5 us
    ppermute x7, starting transfers between devices, sum_everywhere(): lax.ppermute(total, axes, [(i, i ^ m) for i in range(devices)])  9.51 us
    ppermute x7, waiting for transfers between devices, sum_everywhere(): lax.ppermute(total, axes, [(i, i ^ m) for i in range(devices)])  7.41 us
    pallas_call x1, Pallas kernels, local(): pl.pallas_call(pack_kernel, out_shape=(shape(HIGH, bz, by), shape(HIGH, F...  2.24 us
    pallas_call x1, Pallas kernels, local(): pl.pallas_call(face_kernel, out_shape=(shape(7, deep, 2 * bz, lanes), sha...  1.35 us
    unnamed x8, local copies, waits for them, and re-layouts  1.33 us
  transfers between devices with their start and end apart: 16, of which 6 were waited for; matrix products, arithmetic and copies ran while one was open for 3% of the time, Pallas kernels for 4%

profile of v7, /device:TPU:0, one launch (start us, length us, event | category | flops | bytes accessed | tf_op | source)
XLA Modules:
  0.0 56.0 jit_solution(385178832389205009)
XLA Ops:
  0.7 2.2 %shard_map.119 = (f32[8,8,128]{2,1,0:T(8,128)}, f32[8,5,8,128]{3,2,1,0:T(8,128)}, f32[8,5,8,128]{3,2,1,0:T(8,128)}, f32[16,5,8,128]{3,2,1,0:T(8,128)}) custom-call(f32[16,8,128]{2,1,0:T(8,128)} %vx_hbm.1, f32[16,8,128]{2,1,0:T(8,128)} %vz_hbm.1, f32[16,8,128]{2,1,0:T(8,128)} %vy_hbm.1, f32[16,8,128]{2,1,0:T(8,128)} %p_hbm.1, s32[16,8,128]{2,1,0:T(8,128)} %phase_hbm.1), custom_call_target="tpu_custom_call" | custom-call | bytes 1048576 | tf_op jit(solution)/shard_map/pallas_call | solution.py:433
  2.9 3.0 %collective-permute-start = (f32[8,8,128]{2,1,0:T(8,128)}, f32[8,8,128]{2,1,0:T(8,128)S(1)}, u32[]{:S(2)}, u32[]{:S(2)}) collective-permute-start(f32[8,8,128]{2,1,0:T(8,128)} %get-tuple-element.23), channel_id=1, source_target_pairs={{0,4},{4,0},{1,5},{5,1},{2,6},{6,2},{3,7},{7,3},{8,12},{12,8},{9,1... | collective-permute-start | bytes 98312 | tf_op jit(solution)/shard_map/ppermute | solution.py:401
  5.9 1.6 %collective-permute-start.1 = (f32[8,5,8,128]{3,2,1,0:T(8,128)}, f32[8,5,8,128]{3,2,1,0:T(8,128)S(1)}, u32[]{:S(2)}, u32[]{:S(2)}) collective-permute-start(f32[8,5,8,128]{3,2,1,0:T(8,128)} %get-tuple-element.24), channel_id=1, source_target_pairs={{0,8},{8,0},{16,24},{24,16},{1,9},{9,1},{17,25},{25,17},{2,10},{10... | collective-permute-start | bytes 491528 | tf_op jit(solution)/shard_map/ppermute | solution.py:401
  8.8 5.7 %collective-permute-start.3 = (f32[8,8,128]{2,1,0:T(8,128)S(1)}, f32[8,8,128]{2,1,0:T(8,128)S(1)}, u32[]{:S(2)}, u32[]{:S(2)}) collective-permute-start(f32[8,8,128]{2,1,0:T(8,128)S(1)} %collective-permute-done), channel_id=1, source_target_pairs={{0,8},{8,0},{16,24},{24,16},{1,9},{9,1},{17,25},{25,17},{2,10},{10... | collective-permute-start | bytes 98312 | tf_op jit(solution)/shard_map/ppermute | solution.py:401
  14.5 1.0 %pad_maximum_fusion.own_ref = f32[88,8,128]{2,1,0:T(8,128)S(1)} fusion(f32[8,8,128]{2,1,0:T(8,128)S(1)} %collective-permute-done, f32[80,8,128]{2,1,0:T(8,128)} %bitcast.4), kind=kLoop, calls=%fused_computation | loop fusion | flops 90112 | bytes 720896 | tf_op jit(solution)/shard_map/concatenate | solution.py:464
  15.5 0.7 %collective-permute-start.6 = (f32[88,8,128]{2,1,0:T(8,128)S(1)}, f32[88,8,128]{2,1,0:T(8,128)S(1)}, u32[]{:S(2)}, u32[]{:S(2)}) collective-permute-start(f32[88,8,128]{2,1,0:T(8,128)S(1)} %pad_maximum_fusion.own_ref), channel_id=1, source_target_pairs={{1,2},{2,1},{5,6},{6,5},{9,10},{10,9},{13,14},{14,13},{17,18},{18,... | collective-permute-start | bytes 1081352 | tf_op jit(solution)/shard_map/ppermute | solution.py:401
  16.3 2.9 %collective-permute-start.5 = (f32[88,8,128]{2,1,0:T(8,128)S(1)}, f32[88,8,128]{2,1,0:T(8,128)S(1)}, u32[]{:S(2)}, u32[]{:S(2)}) collective-permute-start(f32[88,8,128]{2,1,0:T(8,128)S(1)} %pad_maximum_fusion.own_ref), channel_id=1, source_target_pairs={{0,1},{1,0},{2,3},{3,2},{4,5},{5,4},{6,7},{7,6},{8,9},{9,8},{10,11... | collective-permute-start | bytes 1081352 | tf_op jit(solution)/shard_map/ppermute | solution.py:401
  19.3 0.7 %collective-permute-start.8 = (f32[72,8,128]{2,1,0:T(8,128)S(1)}, f32[72,8,128]{2,1,0:T(8,128)S(1)}, u32[]{:S(2)}, u32[]{:S(2)}) collective-permute-start(f32[72,8,128]{2,1,0:T(8,128)S(1)} %pad_maximum_fusion.1.side_ref), channel_id=1, source_target_pairs={{1,2},{2,1},{5,6},{6,5},{9,10},{10,9},{13,14},{14,13},{17,18},{18,... | collective-permute-start | bytes 884744 | tf_op jit(solution)/shard_map/ppermute | solution.py:401
  20.0 1.3 %collective-permute-start.7 = (f32[72,8,128]{2,1,0:T(8,128)S(1)}, f32[72,8,128]{2,1,0:T(8,128)S(1)}, u32[]{:S(2)}, u32[]{:S(2)}) collective-permute-start(f32[72,8,128]{2,1,0:T(8,128)S(1)} %pad_maximum_fusion.1.side_ref), channel_id=1, source_target_pairs={{0,1},{1,0},{2,3},{3,2},{4,5},{5,4},{6,7},{7,6},{8,9},{9,8},{10,11... | collective-permute-start | bytes 884744 | tf_op jit(solution)/shard_map/ppermute | solution.py:401
  23.3 1.0 %shard_map.120 = (f32[3,28,8,256]{3,2,1,0:T(8,128)S(1)}, f32[28,8,256]{2,1,0:T(8,128)S(1)}, f32[28,8,256]{2,1,0:T(8,128)S(1)}, f32[28,8,256]{2,1,0:T(8,128)S(1)}, f32[28,8,256]{2,1,0:T(8,128)S(1)}) custom-call(f32[88,8,128]{2,1,0:T(8,128)S(1)} %pad_maximum_fusion.own_ref, f32[72,8,128]{2,1,0:T(8,128)S(1)} %pad_maximum_fusion.1.side_ref, f32[4]{0:T(128)S(1)} %copy-done, ...), custom_call_target="tpu_custom_call" | custom-call | flops 1720320 | bytes 2752512 | tf_op jit(solution)/shard_map/pallas_call | solution.py:476
  24.4 1.3 %shard_map.121 = (f32[7,28,16,256]{3,2,1,0:T(8,128)S(1)}, f32[3,28,8,256]{3,2,1,0:T(8,128)S(1)}) custom-call(f32[88,8,128]{2,1,0:T(8,128)S(1)} %collective-permute-done.5.face_0_ref, f32[88,8,128]{2,1,0:T(8,128)S(1)} %collective-permute-done.6.face_1_ref, f32[4]{0:T(128)S(1)} %copy-done, f32[4]{0:T(128)S(1)} %add_multiply_fusion.power_ref, f32[4]{0:T(128)S(1)} %copy-done.2), custom_call_target="tpu_custom_call" | custom-call | flops 1720320 | bytes 3145728 | tf_op jit(solution)/shard_map/pallas_call | solution.py:484
  25.8 12.5 %shard_map.122 = (f32[16,8,128]{2,1,0:T(8,128)}, f32[16,8,128]{2,1,0:T(8,128)}, f32[16,8,128]{2,1,0:T(8,128)}, f32[16,8,128]{2,1,0:T(8,128)S(1)}, f32[16,8,128]{...) custom-call(f32[3,28,8,256]{3,2,1,0:T(8,128)S(1)} %get-tuple-element, ...), custom_call_target="tpu_custom_call", output_to_operand_aliasing={{6}: (5, {}), {7}: (6, {})} | custom-call | tf_op jit(solution)/shard_map/pallas_call | solution.py:492
  38.3 1.6 %collective-permute-start.9 = (f32[8,128]{1,0:T(8,128)S(1)}, f32[8,128]{1,0:T(8,128)S(1)}, u32[]{:S(2)}, u32[]{:S(2)}) collective-permute-start(f32[8,128]{1,0:T(8,128)S(1)} %get-tuple-element.37), channel_id=1, source_target_pairs={{0,1},{1,0},{2,3},{3,2},{4,5},{5,4},{6,7},{7,6},{8,9},{9,8},{10,11... | collective-permute-start | bytes 12296 | tf_op jit(solution)/shard_map/ppermute | solution.py:412
  39.9 0.8 %collective-permute-done.9 = f32[8,128]{1,0:T(8,128)S(1)} collective-permute-done((f32[8,128]{1,0:T(8,128)S(1)}, f32[8,128]{1,0:T(8,128)S(1)}, u32[]{:S(2)}, u32[]{:S(2)}) %collective-permute-start.9) | collective-permute-done | bytes 4128 | tf_op jit(solution)/shard_map/ppermute | solution.py:412
  40.7 2.0 %collective-permute-start.12 = (f32[8,128]{1,0:T(8,128)S(1)}, f32[8,128]{1,0:T(8,128)S(1)}, u32[]{:S(2)}, u32[]{:S(2)}) collective-permute-start(f32[8,128]{1,0:T(8,128)S(1)} %add.22), channel_id=1, source_target_pairs={{0,6},{1,7},{2,4},{3,5},{4,2},{5,3},{6,0},{7,1},{8,14},{9,15},{10,... | collective-permute-start | bytes 12296 | tf_op jit(solution)/shard_map/ppermute | solution.py:412
  42.7 1.4 %collective-permute-start.11 = (f32[8,128]{1,0:T(8,128)S(1)}, f32[8,128]{1,0:T(8,128)S(1)}, u32[]{:S(2)}, u32[]{:S(2)}) collective-permute-start(f32[8,128]{1,0:T(8,128)S(1)} %add.22), channel_id=1, source_target_pairs={{0,4},{1,5},{2,6},{3,7},{4,0},{5,1},{6,2},{7,3},{8,12},{9,13},{10,... | collective-permute-start | bytes 12296 | tf_op jit(solution)/shard_map/ppermute | solution.py:412
  44.2 1.0 %collective-permute-done.12 = f32[8,128]{1,0:T(8,128)S(1)} collective-permute-done((f32[8,128]{1,0:T(8,128)S(1)}, f32[8,128]{1,0:T(8,128)S(1)}, u32[]{:S(2)}, u32[]{:S(2)}) %collective-permute-start.12) | collective-permute-done | bytes 4128 | tf_op jit(solution)/shard_map/ppermute | solution.py:412
  45.3 1.1 %collective-permute-done.11 = f32[8,128]{1,0:T(8,128)S(1)} collective-permute-done((f32[8,128]{1,0:T(8,128)S(1)}, f32[8,128]{1,0:T(8,128)S(1)}, u32[]{:S(2)}, u32[]{:S(2)}) %collective-permute-start.11) | collective-permute-done | bytes 4128 | tf_op jit(solution)/shard_map/ppermute | solution.py:412
  46.3 1.4 %collective-permute-done.10 = f32[8,128]{1,0:T(8,128)S(1)} collective-permute-done((f32[8,128]{1,0:T(8,128)S(1)}, f32[8,128]{1,0:T(8,128)S(1)}, u32[]{:S(2)}, u32[]{:S(2)}) %collective-permute-start.10) | collective-permute-done | bytes 4128 | tf_op jit(solution)/shard_map/ppermute | solution.py:412
  47.8 2.9 %collective-permute-start.15 = (f32[8,128]{1,0:T(8,128)S(1)}, f32[8,128]{1,0:T(8,128)S(1)}, u32[]{:S(2)}, u32[]{:S(2)}) collective-permute-start(f32[8,128]{1,0:T(8,128)S(1)} %add_add_fusion.1), channel_id=1, source_target_pairs={{0,24},{1,25},{2,26},{3,27},{4,28},{5,29},{6,30},{7,31},{8,16},{9,... | collective-permute-start | bytes 12296 | tf_op jit(solution)/shard_map/ppermute | solution.py:412
  50.7 1.4 %collective-permute-start.13 = (f32[8,128]{1,0:T(8,128)S(1)}, f32[8,128]{1,0:T(8,128)S(1)}, u32[]{:S(2)}, u32[]{:S(2)}) collective-permute-start(f32[8,128]{1,0:T(8,128)S(1)} %add_add_fusion.1), channel_id=1, source_target_pairs={{0,8},{1,9},{2,10},{3,11},{4,12},{5,13},{6,14},{7,15},{8,0},{9,1},... | collective-permute-start | bytes 12296 | tf_op jit(solution)/shard_map/ppermute | solution.py:412
  52.2 1.0 %collective-permute-done.15 = f32[8,128]{1,0:T(8,128)S(1)} collective-permute-done((f32[8,128]{1,0:T(8,128)S(1)}, f32[8,128]{1,0:T(8,128)S(1)}, u32[]{:S(2)}, u32[]{:S(2)}) %collective-permute-start.15) | collective-permute-done | bytes 4128 | tf_op jit(solution)/shard_map/ppermute | solution.py:412
  53.2 2.0 %collective-permute-done.14 = f32[8,128]{1,0:T(8,128)S(1)} collective-permute-done((f32[8,128]{1,0:T(8,128)S(1)}, f32[8,128]{1,0:T(8,128)S(1)}, u32[]{:S(2)}, u32[]{:S(2)}) %collective-permute-start.14) | collective-permute-done | bytes 4128 | tf_op jit(solution)/shard_map/ppermute | solution.py:412
  55.2 0.8 %shard_map.123 = f32[16,8,128]{2,1,0:T(8,128)} custom-call(f32[16,8,128]{2,1,0:T(8,128)S(1)} %get-tuple-element.36.refs_0_, f32[8,128]{1,0:T(8,128)S(1)} %add_add_fusion.refs_1_), custom_call_target="tpu_custom_call" | custom-call | tf_op jit(solution)/shard_map/pallas_call | solution.py:509
  (31 shorter events, 3.5 us)
Async XLA Ops:
  0.6 25.1 %copy-start.3 = (f32[4]{0:T(128)S(1)}, f32[4]{0:T(128)}, u32[]{:S(2)}) copy-start(f32[4]{0:T(128)} %rho_table_ref.5) | copy-start | bytes 52
  0.6 25.1 %copy-start.1 = (f32[4]{0:T(128)S(1)}, f32[4]{0:T(128)}, u32[]{:S(2)}) copy-start(f32[4]{0:T(128)} %scale_ref.5) | copy-start | bytes 52
  2.9 5.3 %collective-permute-start = (f32[8,8,128]{2,1,0:T(8,128)}, f32[8,8,128]{2,1,0:T(8,128)S(1)}, u32[]{:S(2)}, u32[]{:S(2)}) collective-permute-start(f32[8,8,128]{2,1,0:T(8,128)} %get-tuple-element.23), channel_id=1, source_target_pairs={{0,4},{4,0},{1,5},{5,1},{2,6},{6,2},{3,7},{7,3},{8,12},{12,8},{9,1... | collective-permute-start | bytes 98312 | tf_op jit(solution)/shard_map/ppermute | solution.py:401
  5.9 13.3 %collective-permute-start.1 = (f32[8,5,8,128]{3,2,1,0:T(8,128)}, f32[8,5,8,128]{3,2,1,0:T(8,128)S(1)}, u32[]{:S(2)}, u32[]{:S(2)}) collective-permute-start(f32[8,5,8,128]{3,2,1,0:T(8,128)} %get-tuple-element.24), channel_id=1, source_target_pairs={{0,8},{8,0},{16,24},{24,16},{1,9},{9,1},{17,25},{25,17},{2,10},{10... | collective-permute-start | bytes 491528 | tf_op jit(solution)/shard_map/ppermute | solution.py:401
  7.5 11.7 %collective-permute-start.2 = (f32[8,5,8,128]{3,2,1,0:T(8,128)}, f32[8,5,8,128]{3,2,1,0:T(8,128)S(1)}, u32[]{:S(2)}, u32[]{:S(2)}) collective-permute-start(f32[8,5,8,128]{3,2,1,0:T(8,128)} %get-tuple-element.25), channel_id=1, source_target_pairs={{8,16},{16,8},{9,17},{17,9},{10,18},{18,10},{11,19},{19,11},{12,20... | collective-permute-start | bytes 491528 | tf_op jit(solution)/shard_map/ppermute | solution.py:401
  8.2 8.1 %collective-permute-start.4 = (f32[8,8,128]{2,1,0:T(8,128)S(1)}, f32[8,8,128]{2,1,0:T(8,128)S(1)}, u32[]{:S(2)}, u32[]{:S(2)}) collective-permute-start(f32[8,8,128]{2,1,0:T(8,128)S(1)} %collective-permute-done), channel_id=1, source_target_pairs={{8,16},{16,8},{9,17},{17,9},{10,18},{18,10},{11,19},{19,11},{12,20... | collective-permute-start | bytes 98312 | tf_op jit(solution)/shard_map/ppermute | solution.py:401
  8.8 10.3 %collective-permute-start.3 = (f32[8,8,128]{2,1,0:T(8,128)S(1)}, f32[8,8,128]{2,1,0:T(8,128)S(1)}, u32[]{:S(2)}, u32[]{:S(2)}) collective-permute-start(f32[8,8,128]{2,1,0:T(8,128)S(1)} %collective-permute-done), channel_id=1, source_target_pairs={{0,8},{8,0},{16,24},{24,16},{1,9},{9,1},{17,25},{25,17},{2,10},{10... | collective-permute-start | bytes 98312 | tf_op jit(solution)/shard_map/ppermute | solution.py:401
  15.5 8.8 %collective-permute-start.6 = (f32[88,8,128]{2,1,0:T(8,128)S(1)}, f32[88,8,128]{2,1,0:T(8,128)S(1)}, u32[]{:S(2)}, u32[]{:S(2)}) collective-permute-start(f32[88,8,128]{2,1,0:T(8,128)S(1)} %pad_maximum_fusion.own_ref), channel_id=1, source_target_pairs={{1,2},{2,1},{5,6},{6,5},{9,10},{10,9},{13,14},{14,13},{17,18},{18,... | collective-permute-start | bytes 1081352 | tf_op jit(solution)/shard_map/ppermute | solution.py:401
  16.3 8.1 %collective-permute-start.5 = (f32[88,8,128]{2,1,0:T(8,128)S(1)}, f32[88,8,128]{2,1,0:T(8,128)S(1)}, u32[]{:S(2)}, u32[]{:S(2)}) collective-permute-start(f32[88,8,128]{2,1,0:T(8,128)S(1)} %pad_maximum_fusion.own_ref), channel_id=1, source_target_pairs={{0,1},{1,0},{2,3},{3,2},{4,5},{5,4},{6,7},{7,6},{8,9},{9,8},{10,11... | collective-permute-start | bytes 1081352 | tf_op jit(solution)/shard_map/ppermute | solution.py:401
  19.3 6.4 %collective-permute-start.8 = (f32[72,8,128]{2,1,0:T(8,128)S(1)}, f32[72,8,128]{2,1,0:T(8,128)S(1)}, u32[]{:S(2)}, u32[]{:S(2)}) collective-permute-start(f32[72,8,128]{2,1,0:T(8,128)S(1)} %pad_maximum_fusion.1.side_ref), channel_id=1, source_target_pairs={{1,2},{2,1},{5,6},{6,5},{9,10},{10,9},{13,14},{14,13},{17,18},{18,... | collective-permute-start | bytes 884744 | tf_op jit(solution)/shard_map/ppermute | solution.py:401
  20.0 5.7 %collective-permute-start.7 = (f32[72,8,128]{2,1,0:T(8,128)S(1)}, f32[72,8,128]{2,1,0:T(8,128)S(1)}, u32[]{:S(2)}, u32[]{:S(2)}) collective-permute-start(f32[72,8,128]{2,1,0:T(8,128)S(1)} %pad_maximum_fusion.1.side_ref), channel_id=1, source_target_pairs={{0,1},{1,0},{2,3},{3,2},{4,5},{5,4},{6,7},{7,6},{8,9},{9,8},{10,11... | collective-permute-start | bytes 884744 | tf_op jit(solution)/shard_map/ppermute | solution.py:401
  22.0 0.7 %copy-start = (f32[4]{0:T(128)S(1)}, f32[4]{0:T(128)}, u32[]{:S(2)}) copy-start(f32[4]{0:T(128)} %scale_ref.5) | copy-start | bytes 52
  22.6 0.7 %copy-start.2 = (f32[4]{0:T(128)S(1)}, f32[4]{0:T(128)}, u32[]{:S(2)}) copy-start(f32[4]{0:T(128)} %rho_table_ref.5) | copy-start | bytes 52
  38.3 2.5 %collective-permute-start.9 = (f32[8,128]{1,0:T(8,128)S(1)}, f32[8,128]{1,0:T(8,128)S(1)}, u32[]{:S(2)}, u32[]{:S(2)}) collective-permute-start(f32[8,128]{1,0:T(8,128)S(1)} %get-tuple-element.37), channel_id=1, source_target_pairs={{0,1},{1,0},{2,3},{3,2},{4,5},{5,4},{6,7},{7,6},{8,9},{9,8},{10,11... | collective-permute-start | bytes 12296 | tf_op jit(solution)/shard_map/ppermute | solution.py:412
  40.7 4.5 %collective-permute-start.12 = (f32[8,128]{1,0:T(8,128)S(1)}, f32[8,128]{1,0:T(8,128)S(1)}, u32[]{:S(2)}, u32[]{:S(2)}) collective-permute-start(f32[8,128]{1,0:T(8,128)S(1)} %add.22), channel_id=1, source_target_pairs={{0,6},{1,7},{2,4},{3,5},{4,2},{5,3},{6,0},{7,1},{8,14},{9,15},{10,... | collective-permute-start | bytes 12296 | tf_op jit(solution)/shard_map/ppermute | solution.py:412
  42.7 3.6 %collective-permute-start.11 = (f32[8,128]{1,0:T(8,128)S(1)}, f32[8,128]{1,0:T(8,128)S(1)}, u32[]{:S(2)}, u32[]{:S(2)}) collective-permute-start(f32[8,128]{1,0:T(8,128)S(1)} %add.22), channel_id=1, source_target_pairs={{0,4},{1,5},{2,6},{3,7},{4,0},{5,1},{6,2},{7,3},{8,12},{9,13},{10,... | collective-permute-start | bytes 12296 | tf_op jit(solution)/shard_map/ppermute | solution.py:412
  44.2 3.6 %collective-permute-start.10 = (f32[8,128]{1,0:T(8,128)S(1)}, f32[8,128]{1,0:T(8,128)S(1)}, u32[]{:S(2)}, u32[]{:S(2)}) collective-permute-start(f32[8,128]{1,0:T(8,128)S(1)} %add.22), channel_id=1, source_target_pairs={{0,2},{1,3},{2,0},{3,1},{4,6},{5,7},{6,4},{7,5},{8,10},{9,11},{10,... | collective-permute-start | bytes 12296 | tf_op jit(solution)/shard_map/ppermute | solution.py:412
  47.8 5.4 %collective-permute-start.15 = (f32[8,128]{1,0:T(8,128)S(1)}, f32[8,128]{1,0:T(8,128)S(1)}, u32[]{:S(2)}, u32[]{:S(2)}) collective-permute-start(f32[8,128]{1,0:T(8,128)S(1)} %add_add_fusion.1), channel_id=1, source_target_pairs={{0,24},{1,25},{2,26},{3,27},{4,28},{5,29},{6,30},{7,31},{8,16},{9,... | collective-permute-start | bytes 12296 | tf_op jit(solution)/shard_map/ppermute | solution.py:412
  50.7 4.5 %collective-permute-start.14 = (f32[8,128]{1,0:T(8,128)S(1)}, f32[8,128]{1,0:T(8,128)S(1)}, u32[]{:S(2)}, u32[]{:S(2)}) collective-permute-start(f32[8,128]{1,0:T(8,128)S(1)} %add_add_fusion.1), channel_id=1, source_target_pairs={{0,16},{1,17},{2,18},{3,19},{4,20},{5,21},{6,22},{7,23},{8,24},{9,... | collective-permute-start | bytes 12296 | tf_op jit(solution)/shard_map/ppermute | solution.py:412
  50.7 4.5 %collective-permute-start.13 = (f32[8,128]{1,0:T(8,128)S(1)}, f32[8,128]{1,0:T(8,128)S(1)}, u32[]{:S(2)}, u32[]{:S(2)}) collective-permute-start(f32[8,128]{1,0:T(8,128)S(1)} %add_add_fusion.1), channel_id=1, source_target_pairs={{0,8},{1,9},{2,10},{3,11},{4,12},{5,13},{6,14},{7,15},{8,0},{9,1},... | collective-permute-start | bytes 12296 | tf_op jit(solution)/shard_map/ppermute | solution.py:412

commit v8 on v7

--- a/solution.py
+++ b/solution.py
@@ -70,6 +70,37 @@
     return vx, vz, vy, p, phase_ref[at].astype(jnp.float32)
 
 
+def add_edges(edge, fields, upper):
+    by = edge.shape[-1]
+    lane = lax.broadcasted_iota(jnp.int32, (1,) + edge.shape[1:], 2)
+    for f, a in enumerate(fields):
+        base = by // 2 * upper + LANE_STEP * f
+        first = pltpu.roll(a, base, 2) if base else a
+        edge = jnp.where((lane >= base) & (lane < base + HIGH), first, edge)
+        last = pltpu.roll(a, (base + LANE_STEP) % by, 2)
+        edge = jnp.where((lane >= base + HIGH) & (lane < base + LANE_STEP), last, edge)
+    return edge
+
+
+def sides_kernel(x_0_ref, x_1_ref, sides_ref, edge_ref):
+    bz, by = edge_ref.shape[1:]
+    for parity in range(2):
+        @pl.when(lax.rem(lax.axis_index("gx"), 2) == parity)
+        def _():
+            high, low = (x_0_ref, x_1_ref) if parity == 0 else (x_1_ref, x_0_ref)
+            for g in range(HIGH // GROUP):
+                edge = jnp.zeros((GROUP, bz, by), jnp.float32)
+                for upper, ref in enumerate((high, low)):
+                    at = g * GROUP
+                    if upper and at < HIGH - LOW:
+                        continue
+                    block = ref[pl.ds(at, GROUP)]
+                    to = HIGH + at - (HIGH - LOW) if upper else at
+                    sides_ref[pl.ds(to * FIELDS, GROUP * FIELDS)] = block.reshape(GROUP * FIELDS, bz, by)
+                    edge = add_edges(edge, [block[:, f] for f in range(FIELDS)], upper)
+                edge_ref[pl.ds(g * GROUP, GROUP)] = edge
+
+
 def pack_kernel(
     vx_hbm, vz_hbm, vy_hbm, p_hbm, phase_hbm, edge_hbm, x_0_hbm, x_1_hbm, stack_hbm,
     field_ref, phase_ref, edge_ref, stack_ref, sems, out_sems,
@@ -77,7 +108,6 @@
     bx, bz, by = phase_ref.shape
     targets = [field_ref.at[f] for f in range(FIELDS - 1)] + [phase_ref]
     copies = start_copies((vx_hbm, vz_hbm, vy_hbm, p_hbm, phase_hbm), targets, sems)
-    lane = lax.broadcasted_iota(jnp.int32, (1, bz, by), 2)
     half = bx // GROUP // 2
     outs = []
 
@@ -91,13 +121,10 @@
             at = pl.ds((g + upper * half) * GROUP, GROUP)
             for copy in copies[g + upper * half]:
                 copy.wait()
-            for f, a in enumerate(clean_group(g + upper * half, field_ref, phase_ref)):
+            fields = clean_group(g + upper * half, field_ref, phase_ref)
+            for f, a in enumerate(fields):
                 stack_ref[at, f] = a
-                base = by // 2 * upper + LANE_STEP * f
-                first = pltpu.roll(a, base, 2) if base else a
-                edge = jnp.where((lane >= base) & (lane < base + HIGH), first, edge)
-                last = pltpu.roll(a, (base + LANE_STEP) % by, 2)
-                edge = jnp.where((lane >= base + HIGH) & (lane < base + LANE_STEP), last, edge)
+            edge = add_edges(edge, fields, upper)
             out(stack_ref.at[at], stack_hbm.at[at])
         at = pl.ds(g * GROUP, GROUP)
         edge_ref[at] = edge
@@ -115,6 +142,10 @@
 
     for copy in outs:
         copy.wait()
+
+
+def read_tables(ref):
+    return [[ref[n, index] for index in range(PHASES)] for n in range(3)]
 
 
 def unpack(ref, at, side, upper, ok, tables):
@@ -164,12 +195,12 @@
     ix, nx = lax.axis_index("gx"), lax.axis_size("gx")
     for at in range(0, HIGH + LOW, GROUP):
         low = at >= HIGH
-        side = (HIGH + LOW) * FIELDS + at
+        side = (HIGH + LOW) * FIELDS + (at - LOW if low else at)
         values = unpack(ref, at, side, int(low), ok & (ix > 0 if low else ix < nx - 1), tables)
         store(pl.ds(at - HIGH if low else LOW + bx + at, GROUP), values)
 
 
-def own_kernel(own_ref, side_ref, scale_ref, power_ref, rho_table_ref, v_ref, p_ref, pre_ref, power_field_ref, rho_ref):
+def own_kernel(own_ref, side_ref, tables_ref, v_ref, p_ref, pre_ref, power_field_ref, rho_ref):
     by = own_ref.shape[-1]
     refs = [v_ref.at[d] for d in range(3)] + [p_ref, pre_ref, power_field_ref, rho_ref]
 
@@ -178,7 +209,7 @@
             ref[planes, :, 0:by] = own
             ref[planes, :, by : 2 * by] = beside
 
-    tables = (scale_ref, power_ref, rho_table_ref)
+    tables = read_tables(tables_ref)
     unpack_own(own_ref, True, tables, store)
     unpack_sides(side_ref, 2 * HIGH, True, tables, store)
 
@@ -199,9 +230,9 @@
     return store
 
 
-def face_kernel(face_0_ref, face_1_ref, scale_ref, power_ref, rho_table_ref, halo_ref, shared_ref):
+def face_kernel(face_0_ref, face_1_ref, tables_ref, halo_ref, shared_ref):
     iz, nz = lax.axis_index("gz"), lax.axis_size("gz")
-    tables = (scale_ref, power_ref, rho_table_ref)
+    tables = read_tables(tables_ref)
     for parity in range(2):
         @pl.when(lax.rem(iz, 2) == parity)
         def _():
@@ -212,7 +243,7 @@
 
 def main_kernel(
     v_ref, p0_ref, pre_ref, power_field_ref, rho_ref, _halo, _shared,
-    corner_0_ref, corner_1_ref, scale_ref, power_ref, rho_table_ref,
+    corner_0_ref, corner_1_ref, tables_ref,
     out_vx_ref, out_vz_ref, out_vy_ref, out_p_ref, out_eta_ref, sum_ref, halo_ref, shared_ref,
     va_ref, vb_ref, p_ref, weight_ref, weight2_ref,
 ):
@@ -220,7 +251,7 @@
     lanes = 2 * by
     nx, nz, ny = lax.axis_size("gx"), lax.axis_size("gz"), lax.axis_size("gy")
     ix, iz, iy = lax.axis_index("gx"), lax.axis_index("gz"), lax.axis_index("gy")
-    tables = (scale_ref, power_ref, rho_table_ref)
+    tables = read_tables(tables_ref)
     for parity in range(2):
         @pl.when(lax.rem(iz, 2) == parity)
         def _():
@@ -429,6 +460,7 @@
 
     hbm = pl.BlockSpec(memory_space=pltpu.HBM)
 
+    tables = jnp.stack([visc_scale, (0.5 / math.log(2.0)) * (1.0 / power_n - 1.0), density])
     groups = bx // GROUP
     edge, half_0, half_1, stack = pl.pallas_call(
         pack_kernel,
@@ -452,47 +484,50 @@
         cost_estimate=pl.CostEstimate(flops=0, bytes_accessed=16 * bx * bz * by * 4, transcendentals=0),
     )(vel_x, vel_z, vel_y, pressure, phase)
 
-    side = swap(edge, "gy", 0)
+    def edges_beside(edge):
+        side = swap(edge, "gy", 0)
+        if ny == 2:
+            return side
+        lane = lax.broadcasted_iota(jnp.int32, side.shape, 2) % (by // 2) % LANE_STEP
+        return jnp.where((lane < HIGH) == (lax.rem(iy, 2) == 0), side, swap(edge, "gy", 1))
+
+    side = edges_beside(edge)
     x_0, x_1 = swap(half_0, "gx", 0), swap(half_1, "gx", 1)
-    if ny > 2:
-        even = lax.rem(iy, 2) == 0
-        other = swap(edge, "gy", 1)
-        lane = lax.broadcasted_iota(jnp.int32, side.shape, 2) % (by // 2) % LANE_STEP
-        side = jnp.where((lane < HIGH) == even, side, other)
-    side_0, side_1 = swap(side, "gx", 0), swap(side, "gx", 1)
-
     face = jnp.concatenate([stack.reshape(bx * FIELDS, bz, by), side])
     face_1 = swap(face, "gz", 1)
     face_0 = swap(face, "gz", 0)
-    even = lax.rem(ix, 2) == 0
-    choose = lambda a, b: (jnp.where(even, a, b), jnp.where(even, b, a)[HIGH - LOW :])
-    tiles = [a.reshape(-1, bz, by) for a in choose(x_0, x_1) + choose(side_0, side_1)]
-    sides = jnp.concatenate(tiles)
+    sides, edge = pl.pallas_call(
+        sides_kernel,
+        out_shape=(shape((HIGH + LOW) * FIELDS, bz, by), shape(HIGH, bz, by)),
+        in_specs=[VMEM] * 2,
+        out_specs=(VMEM,) * 2,
+        compiler_params=pltpu.CompilerParams(vmem_limit_bytes=4 * mebibyte),
+    )(x_0, x_1)
+    sides = jnp.concatenate([sides, edges_beside(edge)])
     corner_1 = swap(sides, "gz", 1)
     corner_0 = swap(sides, "gz", 0)
 
-    tables = (visc_scale, (0.5 / math.log(2.0)) * (1.0 / power_n - 1.0), density)
     field = shape(deep, bz, lanes)
     own = pl.pallas_call(
         own_kernel,
         out_shape=(shape(3, deep, bz, lanes),) + (field,) * 4,
-        in_specs=[VMEM] * 2 + [SMEM] * 3,
+        in_specs=[VMEM] * 2 + [SMEM],
         out_specs=(VMEM,) * 5,
         compiler_params=pltpu.CompilerParams(vmem_limit_bytes=8 * mebibyte),
         cost_estimate=pl.CostEstimate(flops=deep * 30 * bz * lanes, bytes_accessed=12 * deep * bz * lanes * 4, transcendentals=0),
-    )(face, sides, *tables)
+    )(face, sides, tables)
     halo = pl.pallas_call(
         face_kernel,
         out_shape=(shape(7, deep, 2 * bz, lanes), shape(3, deep, bz, lanes)),
-        in_specs=[VMEM] * 2 + [SMEM] * 3,
+        in_specs=[VMEM] * 2 + [SMEM],
         out_specs=(VMEM,) * 2,
         compiler_params=pltpu.CompilerParams(vmem_limit_bytes=8 * mebibyte),
         cost_estimate=pl.CostEstimate(flops=deep * 30 * bz * lanes, bytes_accessed=24 * bx * bz * lanes * 4, transcendentals=0),
-    )(face_0, face_1, *tables)
+    )(face_0, face_1, tables)
     vx, vz, vy, p, eta, total, _, _ = pl.pallas_call(
         main_kernel,
         out_shape=(block,) * 5 + (shape(bz, by),) + tuple(shape(*a.shape) for a in halo),
-        in_specs=[VMEM] * 9 + [SMEM] * 3,
+        in_specs=[VMEM] * 9 + [SMEM],
         out_specs=(VMEM,) * 8,
         input_output_aliases={5: 6, 6: 7},
         scratch_shapes=[
@@ -503,7 +538,7 @@
             scratch(4, 2 * bz, lanes),
         ],
         compiler_params=pltpu.CompilerParams(vmem_limit_bytes=32 * mebibyte),
-    )(*own, *halo, corner_0, corner_1, *tables)
+    )(*own, *halo, corner_0, corner_1, tables)
 
     total = sum_everywhere(total)
     p = pl.pallas_call(

time: 56.3 us -> 56.7 us (level)
  waiting for transfers between devices: 7.44 us -> 12.4 us
  starting transfers between devices: 26.7 us -> 22.7 us
  local copies, waits for them, and re-layouts: 1.33 us -> 0.02 us
  other arithmetic: 1.73 us -> 2.35 us
    ppermute x9 -> x8, waiting for transfers between devices: 0.02 us -> 5.05 us  [swap(): lax.ppermute(a, axis, [(i, j) for k in range(start, count - 1, 2) for i,...]
    ppermute x9 -> x8, starting transfers between devices: 17.2 us -> 12.5 us  [swap(): lax.ppermute(a, axis, [(i, j) for k in range(start, count - 1, 2) for i,...]
    another operation x0 -> x2, other arithmetic: none -> 1.34 us  [local(): jnp.stack([visc_scale, 0.5 / math.log(2.0) * (1.0 / power_n - 1.0), densi...]
    unnamed x8 -> x1, local copies, waits for them, and re-layouts: 1.33 us -> 0.02 us
    ppermute x7, starting transfers between devices: 9.51 us -> 10.2 us  [sum_everywhere(): lax.ppermute(total, axes, [(i, i ^ m) for i in range(devices)])]
    mul x1 -> x0, other arithmetic: 0.66 us -> none  [local(): tables = (visc_scale, 0.5 / math.log(2.0) * (1.0 / power_n - 1.0), density)]
  transfers between devices with their start and end apart: 16 -> 15, of which waited for: 6 -> 8; matrix products, arithmetic and copies ran while one was open for 3% -> 4% of each run, Pallas kernels for 4% -> 5%
where the time goes in v8:
time: 56.7 us; the launch traced here: 56.4 us
  starting transfers between devices  22.7 us (40%)
  Pallas kernels  18.2 us (32%)
  waiting for transfers between devices  12.4 us (22%)
  other arithmetic  2.35 us (4%)
  between operations  0.74 us (1%)
    pallas_call x1, Pallas kernels, local(): pl.pallas_call(main_kernel, out_shape=(block,) * 5 + (shape(bz, by),) + t...  12.6 us
    ppermute x8, starting transfers between devices, swap(): lax.ppermute(a, axis, [(i, j) for k in range(start, count - 1, 2) for i,...  12.5 us
    ppermute x7, starting transfers between devices, sum_everywhere(): lax.ppermute(total, axes, [(i, i ^ m) for i in range(devices)])  10.2 us
    ppermute x7, waiting for transfers between devices, sum_everywhere(): lax.ppermute(total, axes, [(i, i ^ m) for i in range(devices)])  7.38 us
    ppermute x8, waiting for transfers between devices, swap(): lax.ppermute(a, axis, [(i, j) for k in range(start, count - 1, 2) for i,...  5.05 us
    pallas_call x1, Pallas kernels, local(): pl.pallas_call(pack_kernel, out_shape=(shape(HIGH, bz, by), shape(HIGH, F...  2.22 us
    pallas_call x1, Pallas kernels, local(): pl.pallas_call(face_kernel, out_shape=(shape(7, deep, 2 * bz, lanes), sha...  1.38 us
    another operation x2, other arithmetic, local(): jnp.stack([visc_scale, 0.5 / math.log(2.0) * (1.0 / power_n - 1.0), densi...  1.34 us
  transfers between devices with their start and end apart: 15, of which 8 were waited for; matrix products, arithmetic and copies ran while one was open for 4% of the time, Pallas kernels for 5%

profile of v8, /device:TPU:0, one launch (start us, length us, event | category | flops | bytes accessed | tf_op | source)
XLA Modules:
  0.0 56.4 jit_solution(2540738377923519474)
XLA Ops:
  0.6 2.2 %shard_map.119 = (f32[8,8,128]{2,1,0:T(8,128)}, f32[8,5,8,128]{3,2,1,0:T(8,128)}, f32[8,5,8,128]{3,2,1,0:T(8,128)}, f32[16,5,8,128]{3,2,1,0:T(8,128)}) custom-call(f32[16,8,128]{2,1,0:T(8,128)} %vx_hbm.1, f32[16,8,128]{2,1,0:T(8,128)} %vz_hbm.1, f32[16,8,128]{2,1,0:T(8,128)} %vy_hbm.1, f32[16,8,128]{2,1,0:T(8,128)} %p_hbm.1, s32[16,8,128]{2,1,0:T(8,128)} %phase_hbm.1), custom_call_target="tpu_custom_call" | custom-call | bytes 1048576 | tf_op jit(solution)/shard_map/pallas_call | solution.py:465
  2.9 3.1 %collective-permute-start.1 = (f32[8,5,8,128]{3,2,1,0:T(8,128)}, f32[8,5,8,128]{3,2,1,0:T(8,128)S(1)}, u32[]{:S(2)}, u32[]{:S(2)}) collective-permute-start(f32[8,5,8,128]{3,2,1,0:T(8,128)} %get-tuple-element.26), channel_id=1, source_target_pairs={{0,8},{8,0},{16,24},{24,16},{1,9},{9,1},{17,25},{25,17},{2,10},{10... | collective-permute-start | bytes 491528 | tf_op jit(solution)/shard_map/ppermute | solution.py:432
  6.6 1.6 %collective-permute-start = (f32[8,8,128]{2,1,0:T(8,128)}, f32[8,8,128]{2,1,0:T(8,128)S(1)}, u32[]{:S(2)}, u32[]{:S(2)}) collective-permute-start(f32[8,8,128]{2,1,0:T(8,128)} %get-tuple-element.25), channel_id=1, source_target_pairs={{0,4},{4,0},{1,5},{5,1},{2,6},{6,2},{3,7},{7,3},{8,12},{12,8},{9,1... | collective-permute-start | bytes 98312 | tf_op jit(solution)/shard_map/ppermute | solution.py:432
  8.2 2.6 %collective-permute-done = f32[8,8,128]{2,1,0:T(8,128)S(1)} collective-permute-done((f32[8,8,128]{2,1,0:T(8,128)}, f32[8,8,128]{2,1,0:T(8,128)S(1)}, u32[]{:S(2)}, u32[]{:S(2)}) %collective-permute-start) | collective-permute-done | bytes 32800 | tf_op jit(solution)/shard_map/ppermute | solution.py:432
  10.8 1.0 %pad_maximum_fusion.own_ref = f32[88,8,128]{2,1,0:T(8,128)S(1)} fusion(f32[8,8,128]{2,1,0:T(8,128)S(1)} %collective-permute-done, f32[80,8,128]{2,1,0:T(8,128)} %bitcast.5), kind=kLoop, calls=%fused_computation | loop fusion | flops 90112 | bytes 720896 | tf_op jit(solution)/shard_map/concatenate | solution.py:496
  11.8 0.7 %collective-permute-start.5 = (f32[88,8,128]{2,1,0:T(8,128)S(1)}, f32[88,8,128]{2,1,0:T(8,128)S(1)}, u32[]{:S(2)}, u32[]{:S(2)}) collective-permute-start(f32[88,8,128]{2,1,0:T(8,128)S(1)} %pad_maximum_fusion.own_ref), channel_id=1, source_target_pairs={{1,2},{2,1},{5,6},{6,5},{9,10},{10,9},{13,14},{14,13},{17,18},{18,... | collective-permute-start | bytes 1081352 | tf_op jit(solution)/shard_map/ppermute | solution.py:432
  12.5 2.9 %collective-permute-start.4 = (f32[88,8,128]{2,1,0:T(8,128)S(1)}, f32[88,8,128]{2,1,0:T(8,128)S(1)}, u32[]{:S(2)}, u32[]{:S(2)}) collective-permute-start(f32[88,8,128]{2,1,0:T(8,128)S(1)} %pad_maximum_fusion.own_ref), channel_id=1, source_target_pairs={{0,1},{1,0},{2,3},{3,2},{4,5},{5,4},{6,7},{7,6},{8,9},{9,8},{10,11... | collective-permute-start | bytes 1081352 | tf_op jit(solution)/shard_map/ppermute | solution.py:432
  15.6 1.6 %collective-permute-start.3 = (f32[8,8,128]{2,1,0:T(8,128)S(1)}, f32[8,8,128]{2,1,0:T(8,128)S(1)}, u32[]{:S(2)}, u32[]{:S(2)}) collective-permute-start(f32[8,8,128]{2,1,0:T(8,128)S(1)} %get-tuple-element.29), channel_id=1, source_target_pairs={{0,4},{4,0},{1,5},{5,1},{2,6},{6,2},{3,7},{7,3},{8,12},{12,8},{9,1... | collective-permute-start | bytes 98312 | tf_op jit(solution)/shard_map/ppermute | solution.py:432
  17.2 2.4 %collective-permute-done.3 = f32[8,8,128]{2,1,0:T(8,128)S(1)} collective-permute-done((f32[8,8,128]{2,1,0:T(8,128)S(1)}, f32[8,8,128]{2,1,0:T(8,128)S(1)}, u32[]{:S(2)}, u32[]{:S(2)}) %collective-permute-start.3) | collective-permute-done | bytes 32800 | tf_op jit(solution)/shard_map/ppermute | solution.py:432
  20.3 1.3 %collective-permute-start.6 = (f32[68,8,128]{2,1,0:T(8,128)S(1)}, f32[68,8,128]{2,1,0:T(8,128)S(1)}, u32[]{:S(2)}, u32[]{:S(2)}) collective-permute-start(f32[68,8,128]{2,1,0:T(8,128)S(1)} %constant_dynamic-update-slice_fusion.side_ref), channel_id=1, source_target_pairs={{0,1},{1,0},{2,3},{3,2},{4,5},{5,4},{6,7},{7,6},{8,9},{9,8},{10,11... | collective-permute-start | bytes 835592 | tf_op jit(solution)/shard_map/ppermute | solution.py:432
  22.3 0.7 %pad_maximum_fusion.1.tables_ref = f32[3,4]{1,0:T(4,128)S(1)} fusion(f32[1,4]{1,0:T(1,128)} %bitcast.6, f32[1,4]{1,0:T(1,128)S(1)} %multiply_bitcast_fusion, f32[1,4]{1,0:T(1,128)} %bitcast.7), kind=kLoop, calls=%fused_computation.5 | loop fusion | flops 24 | bytes 96 | tf_op jit(solution)/shard_map/stack | solution.py:463
  23.0 1.1 %shard_map.121 = (f32[3,28,8,256]{3,2,1,0:T(8,128)S(1)}, f32[28,8,256]{2,1,0:T(8,128)S(1)}, f32[28,8,256]{2,1,0:T(8,128)S(1)}, f32[28,8,256]{2,1,0:T(8,128)S(1)}, f32[28,8,256]{2,1,0:T(8,128)S(1)}) custom-call(f32[88,8,128]{2,1,0:T(8,128)S(1)} %pad_maximum_fusion.own_ref, f32[68,8,128]{2,1,0:T(8,128)S(1)} %constant_dynamic-update-slice_fusion.side_ref, ...), custom_call_target="tpu_custom_call" | custom-call | flops 1720320 | bytes 2752512 | tf_op jit(solution)/shard_map/pallas_call | solution.py:511
  24.1 1.4 %shard_map.122 = (f32[7,28,16,256]{3,2,1,0:T(8,128)S(1)}, f32[3,28,8,256]{3,2,1,0:T(8,128)S(1)}) custom-call(f32[88,8,128]{2,1,0:T(8,128)S(1)} %collective-permute-done.4.face_0_ref, f32[88,8,128]{2,1,0:T(8,128)S(1)} %collective-permute-done.5.face_1_ref, f32[3,4]{1,0:T(4,128)S(1)} %pad_maximum_fusion.1.tables_ref), custom_call_target="tpu_custom_call" | custom-call | flops 1720320 | bytes 3145728 | tf_op jit(solution)/shard_map/pallas_call | solution.py:519
  25.5 12.6 %shard_map.123 = (f32[16,8,128]{2,1,0:T(8,128)}, f32[16,8,128]{2,1,0:T(8,128)}, f32[16,8,128]{2,1,0:T(8,128)}, f32[16,8,128]{2,1,0:T(8,128)S(1)}, f32[16,8,128]{...) custom-call(f32[3,28,8,256]{3,2,1,0:T(8,128)S(1)} %get-tuple-element, ...), custom_call_target="tpu_custom_call", output_to_operand_aliasing={{6}: (5, {}), {7}: (6, {})} | custom-call | tf_op jit(solution)/shard_map/pallas_call | solution.py:527
  38.1 0.9 %collective-permute-start.8 = (f32[8,128]{1,0:T(8,128)S(1)}, f32[8,128]{1,0:T(8,128)S(1)}, u32[]{:S(2)}, u32[]{:S(2)}) collective-permute-start(f32[8,128]{1,0:T(8,128)S(1)} %get-tuple-element.41), channel_id=1, source_target_pairs={{0,1},{1,0},{2,3},{3,2},{4,5},{5,4},{6,7},{7,6},{8,9},{9,8},{10,11... | collective-permute-start | bytes 12296 | tf_op jit(solution)/shard_map/ppermute | solution.py:443
  39.0 0.8 %collective-permute-done.8 = f32[8,128]{1,0:T(8,128)S(1)} collective-permute-done((f32[8,128]{1,0:T(8,128)S(1)}, f32[8,128]{1,0:T(8,128)S(1)}, u32[]{:S(2)}, u32[]{:S(2)}) %collective-permute-start.8) | collective-permute-done | bytes 4128 | tf_op jit(solution)/shard_map/ppermute | solution.py:443
  39.8 2.3 %collective-permute-start.11 = (f32[8,128]{1,0:T(8,128)S(1)}, f32[8,128]{1,0:T(8,128)S(1)}, u32[]{:S(2)}, u32[]{:S(2)}) collective-permute-start(f32[8,128]{1,0:T(8,128)S(1)} %add.22), channel_id=1, source_target_pairs={{0,6},{1,7},{2,4},{3,5},{4,2},{5,3},{6,0},{7,1},{8,14},{9,15},{10,... | collective-permute-start | bytes 12296 | tf_op jit(solution)/shard_map/ppermute | solution.py:443
  43.3 1.0 %collective-permute-done.11 = f32[8,128]{1,0:T(8,128)S(1)} collective-permute-done((f32[8,128]{1,0:T(8,128)S(1)}, f32[8,128]{1,0:T(8,128)S(1)}, u32[]{:S(2)}, u32[]{:S(2)}) %collective-permute-start.11) | collective-permute-done | bytes 4128 | tf_op jit(solution)/shard_map/ppermute | solution.py:443
  44.3 1.4 %collective-permute-done.10 = f32[8,128]{1,0:T(8,128)S(1)} collective-permute-done((f32[8,128]{1,0:T(8,128)S(1)}, f32[8,128]{1,0:T(8,128)S(1)}, u32[]{:S(2)}, u32[]{:S(2)}) %collective-permute-start.10) | collective-permute-done | bytes 4128 | tf_op jit(solution)/shard_map/ppermute | solution.py:443
  46.2 2.5 %collective-permute-start.14 = (f32[8,128]{1,0:T(8,128)S(1)}, f32[8,128]{1,0:T(8,128)S(1)}, u32[]{:S(2)}, u32[]{:S(2)}) collective-permute-start(f32[8,128]{1,0:T(8,128)S(1)} %add_add_fusion.1), channel_id=1, source_target_pairs={{0,24},{1,25},{2,26},{3,27},{4,28},{5,29},{6,30},{7,31},{8,16},{9,... | collective-permute-start | bytes 12296 | tf_op jit(solution)/shard_map/ppermute | solution.py:443
  48.8 3.3 %collective-permute-start.13 = (f32[8,128]{1,0:T(8,128)S(1)}, f32[8,128]{1,0:T(8,128)S(1)}, u32[]{:S(2)}, u32[]{:S(2)}) collective-permute-start(f32[8,128]{1,0:T(8,128)S(1)} %add_add_fusion.1), channel_id=1, source_target_pairs={{0,16},{1,17},{2,18},{3,19},{4,20},{5,21},{6,22},{7,23},{8,24},{9,... | collective-permute-start | bytes 12296 | tf_op jit(solution)/shard_map/ppermute | solution.py:443
  52.1 1.6 %collective-permute-done.13 = f32[8,128]{1,0:T(8,128)S(1)} collective-permute-done((f32[8,128]{1,0:T(8,128)S(1)}, f32[8,128]{1,0:T(8,128)S(1)}, u32[]{:S(2)}, u32[]{:S(2)}) %collective-permute-start.13) | collective-permute-done | bytes 4128 | tf_op jit(solution)/shard_map/ppermute | solution.py:443
  53.7 2.0 %collective-permute-done.12 = f32[8,128]{1,0:T(8,128)S(1)} collective-permute-done((f32[8,128]{1,0:T(8,128)S(1)}, f32[8,128]{1,0:T(8,128)S(1)}, u32[]{:S(2)}, u32[]{:S(2)}) %collective-permute-start.12) | collective-permute-done | bytes 4128 | tf_op jit(solution)/shard_map/ppermute | solution.py:443
  55.7 0.8 %shard_map.124 = f32[16,8,128]{2,1,0:T(8,128)} custom-call(f32[16,8,128]{2,1,0:T(8,128)S(1)} %get-tuple-element.40.refs_0_, f32[8,128]{1,0:T(8,128)S(1)} %add_add_fusion.refs_1_), custom_call_target="tpu_custom_call" | custom-call | tf_op jit(solution)/shard_map/pallas_call | solution.py:544
  (20 shorter events, 3.9 us)
Async XLA Ops:
  2.9 12.6 %collective-permute-start.1 = (f32[8,5,8,128]{3,2,1,0:T(8,128)}, f32[8,5,8,128]{3,2,1,0:T(8,128)S(1)}, u32[]{:S(2)}, u32[]{:S(2)}) collective-permute-start(f32[8,5,8,128]{3,2,1,0:T(8,128)} %get-tuple-element.26), channel_id=1, source_target_pairs={{0,8},{8,0},{16,24},{24,16},{1,9},{9,1},{17,25},{25,17},{2,10},{10... | collective-permute-start | bytes 491528 | tf_op jit(solution)/shard_map/ppermute | solution.py:432
  6.0 9.5 %collective-permute-start.2 = (f32[8,5,8,128]{3,2,1,0:T(8,128)}, f32[8,5,8,128]{3,2,1,0:T(8,128)S(1)}, u32[]{:S(2)}, u32[]{:S(2)}) collective-permute-start(f32[8,5,8,128]{3,2,1,0:T(8,128)} %get-tuple-element.27), channel_id=1, source_target_pairs={{8,16},{16,8},{9,17},{17,9},{10,18},{18,10},{11,19},{19,11},{12,20... | collective-permute-start | bytes 491528 | tf_op jit(solution)/shard_map/ppermute | solution.py:432
  6.6 4.2 %collective-permute-start = (f32[8,8,128]{2,1,0:T(8,128)}, f32[8,8,128]{2,1,0:T(8,128)S(1)}, u32[]{:S(2)}, u32[]{:S(2)}) collective-permute-start(f32[8,8,128]{2,1,0:T(8,128)} %get-tuple-element.25), channel_id=1, source_target_pairs={{0,4},{4,0},{1,5},{5,1},{2,6},{6,2},{3,7},{7,3},{8,12},{12,8},{9,1... | collective-permute-start | bytes 98312 | tf_op jit(solution)/shard_map/ppermute | solution.py:432
  11.8 12.2 %collective-permute-start.5 = (f32[88,8,128]{2,1,0:T(8,128)S(1)}, f32[88,8,128]{2,1,0:T(8,128)S(1)}, u32[]{:S(2)}, u32[]{:S(2)}) collective-permute-start(f32[88,8,128]{2,1,0:T(8,128)S(1)} %pad_maximum_fusion.own_ref), channel_id=1, source_target_pairs={{1,2},{2,1},{5,6},{6,5},{9,10},{10,9},{13,14},{14,13},{17,18},{18,... | collective-permute-start | bytes 1081352 | tf_op jit(solution)/shard_map/ppermute | solution.py:432
  12.5 11.6 %collective-permute-start.4 = (f32[88,8,128]{2,1,0:T(8,128)S(1)}, f32[88,8,128]{2,1,0:T(8,128)S(1)}, u32[]{:S(2)}, u32[]{:S(2)}) collective-permute-start(f32[88,8,128]{2,1,0:T(8,128)S(1)} %pad_maximum_fusion.own_ref), channel_id=1, source_target_pairs={{0,1},{1,0},{2,3},{3,2},{4,5},{5,4},{6,7},{7,6},{8,9},{9,8},{10,11... | collective-permute-start | bytes 1081352 | tf_op jit(solution)/shard_map/ppermute | solution.py:432
  15.6 4.0 %collective-permute-start.3 = (f32[8,8,128]{2,1,0:T(8,128)S(1)}, f32[8,8,128]{2,1,0:T(8,128)S(1)}, u32[]{:S(2)}, u32[]{:S(2)}) collective-permute-start(f32[8,8,128]{2,1,0:T(8,128)S(1)} %get-tuple-element.29), channel_id=1, source_target_pairs={{0,4},{4,0},{1,5},{5,1},{2,6},{6,2},{3,7},{7,3},{8,12},{12,8},{9,1... | collective-permute-start | bytes 98312 | tf_op jit(solution)/shard_map/ppermute | solution.py:432
  19.6 5.8 %collective-permute-start.7 = (f32[68,8,128]{2,1,0:T(8,128)S(1)}, f32[68,8,128]{2,1,0:T(8,128)S(1)}, u32[]{:S(2)}, u32[]{:S(2)}) collective-permute-start(f32[68,8,128]{2,1,0:T(8,128)S(1)} %constant_dynamic-update-slice_fusion.side_ref), channel_id=1, source_target_pairs={{1,2},{2,1},{5,6},{6,5},{9,10},{10,9},{13,14},{14,13},{17,18},{18,... | collective-permute-start | bytes 835592 | tf_op jit(solution)/shard_map/ppermute | solution.py:432
  20.3 5.2 %collective-permute-start.6 = (f32[68,8,128]{2,1,0:T(8,128)S(1)}, f32[68,8,128]{2,1,0:T(8,128)S(1)}, u32[]{:S(2)}, u32[]{:S(2)}) collective-permute-start(f32[68,8,128]{2,1,0:T(8,128)S(1)} %constant_dynamic-update-slice_fusion.side_ref), channel_id=1, source_target_pairs={{0,1},{1,0},{2,3},{3,2},{4,5},{5,4},{6,7},{7,6},{8,9},{9,8},{10,11... | collective-permute-start | bytes 835592 | tf_op jit(solution)/shard_map/ppermute | solution.py:432
  38.1 1.7 %collective-permute-start.8 = (f32[8,128]{1,0:T(8,128)S(1)}, f32[8,128]{1,0:T(8,128)S(1)}, u32[]{:S(2)}, u32[]{:S(2)}) collective-permute-start(f32[8,128]{1,0:T(8,128)S(1)} %get-tuple-element.41), channel_id=1, source_target_pairs={{0,1},{1,0},{2,3},{3,2},{4,5},{5,4},{6,7},{7,6},{8,9},{9,8},{10,11... | collective-permute-start | bytes 12296 | tf_op jit(solution)/shard_map/ppermute | solution.py:443
  39.8 4.5 %collective-permute-start.11 = (f32[8,128]{1,0:T(8,128)S(1)}, f32[8,128]{1,0:T(8,128)S(1)}, u32[]{:S(2)}, u32[]{:S(2)}) collective-permute-start(f32[8,128]{1,0:T(8,128)S(1)} %add.22), channel_id=1, source_target_pairs={{0,6},{1,7},{2,4},{3,5},{4,2},{5,3},{6,0},{7,1},{8,14},{9,15},{10,... | collective-permute-start | bytes 12296 | tf_op jit(solution)/shard_map/ppermute | solution.py:443
  42.1 3.6 %collective-permute-start.10 = (f32[8,128]{1,0:T(8,128)S(1)}, f32[8,128]{1,0:T(8,128)S(1)}, u32[]{:S(2)}, u32[]{:S(2)}) collective-permute-start(f32[8,128]{1,0:T(8,128)S(1)} %add.22), channel_id=1, source_target_pairs={{0,4},{1,5},{2,6},{3,7},{4,0},{5,1},{6,2},{7,3},{8,12},{9,13},{10,... | collective-permute-start | bytes 12296 | tf_op jit(solution)/shard_map/ppermute | solution.py:443
  42.6 3.6 %collective-permute-start.9 = (f32[8,128]{1,0:T(8,128)S(1)}, f32[8,128]{1,0:T(8,128)S(1)}, u32[]{:S(2)}, u32[]{:S(2)}) collective-permute-start(f32[8,128]{1,0:T(8,128)S(1)} %add.22), channel_id=1, source_target_pairs={{0,2},{1,3},{2,0},{3,1},{4,6},{5,7},{6,4},{7,5},{8,10},{9,11},{10,... | collective-permute-start | bytes 12296 | tf_op jit(solution)/shard_map/ppermute | solution.py:443
  46.2 5.8 %collective-permute-start.14 = (f32[8,128]{1,0:T(8,128)S(1)}, f32[8,128]{1,0:T(8,128)S(1)}, u32[]{:S(2)}, u32[]{:S(2)}) collective-permute-start(f32[8,128]{1,0:T(8,128)S(1)} %add_add_fusion.1), channel_id=1, source_target_pairs={{0,24},{1,25},{2,26},{3,27},{4,28},{5,29},{6,30},{7,31},{8,16},{9,... | collective-permute-start | bytes 12296 | tf_op jit(solution)/shard_map/ppermute | solution.py:443
  48.8 4.9 %collective-permute-start.13 = (f32[8,128]{1,0:T(8,128)S(1)}, f32[8,128]{1,0:T(8,128)S(1)}, u32[]{:S(2)}, u32[]{:S(2)}) collective-permute-start(f32[8,128]{1,0:T(8,128)S(1)} %add_add_fusion.1), channel_id=1, source_target_pairs={{0,16},{1,17},{2,18},{3,19},{4,20},{5,21},{6,22},{7,23},{8,24},{9,... | collective-permute-start | bytes 12296 | tf_op jit(solution)/shard_map/ppermute | solution.py:443
  52.1 3.6 %collective-permute-start.12 = (f32[8,128]{1,0:T(8,128)S(1)}, f32[8,128]{1,0:T(8,128)S(1)}, u32[]{:S(2)}, u32[]{:S(2)}) collective-permute-start(f32[8,128]{1,0:T(8,128)S(1)} %add_add_fusion.1), channel_id=1, source_target_pairs={{0,8},{1,9},{2,10},{3,11},{4,12},{5,13},{6,14},{7,15},{8,0},{9,1},... | collective-permute-start | bytes 12296 | tf_op jit(solution)/shard_map/ppermute | solution.py:443

commit v9 on v8

--- a/solution.py
+++ b/solution.py
@@ -82,23 +82,37 @@
     return edge
 
 
-def sides_kernel(x_0_ref, x_1_ref, sides_ref, edge_ref):
+def high_and_low(x_0_ref, x_1_ref, body):
+    for parity, pair in enumerate(((x_0_ref, x_1_ref), (x_1_ref, x_0_ref))):
+        pl.when(lax.rem(lax.axis_index("gx"), 2) == parity)(lambda: body(*pair))
+
+
+def side_edge_kernel(x_0_ref, x_1_ref, own_edge_ref, edge_ref):
     bz, by = edge_ref.shape[1:]
-    for parity in range(2):
-        @pl.when(lax.rem(lax.axis_index("gx"), 2) == parity)
-        def _():
-            high, low = (x_0_ref, x_1_ref) if parity == 0 else (x_1_ref, x_0_ref)
-            for g in range(HIGH // GROUP):
-                edge = jnp.zeros((GROUP, bz, by), jnp.float32)
-                for upper, ref in enumerate((high, low)):
-                    at = g * GROUP
-                    if upper and at < HIGH - LOW:
-                        continue
+    edge_ref[0:HIGH] = own_edge_ref[...]
+
+    def body(high, low):
+        for at in range(0, HIGH, GROUP):
+            edge = jnp.zeros((GROUP, bz, by), jnp.float32)
+            for upper, ref in enumerate((high, low)):
+                if not upper or at >= HIGH - LOW:
                     block = ref[pl.ds(at, GROUP)]
-                    to = HIGH + at - (HIGH - LOW) if upper else at
-                    sides_ref[pl.ds(to * FIELDS, GROUP * FIELDS)] = block.reshape(GROUP * FIELDS, bz, by)
                     edge = add_edges(edge, [block[:, f] for f in range(FIELDS)], upper)
-                edge_ref[pl.ds(g * GROUP, GROUP)] = edge
+            edge_ref[pl.ds(HIGH + at, GROUP)] = edge
+
+    high_and_low(x_0_ref, x_1_ref, body)
+
+
+def sides_kernel(x_0_ref, x_1_ref, _edge_ref, sides_ref):
+    bz, by = sides_ref.shape[1:]
+
+    def body(high, low):
+        for at in range(0, HIGH, GROUP):
+            sides_ref[pl.ds(at * FIELDS, GROUP * FIELDS)] = high[pl.ds(at, GROUP)].reshape(-1, bz, by)
+        for at in range(HIGH - LOW, HIGH, GROUP):
+            sides_ref[pl.ds((at + LOW) * FIELDS, GROUP * FIELDS)] = low[pl.ds(at, GROUP)].reshape(-1, bz, by)
+
+    high_and_low(x_0_ref, x_1_ref, body)
 
 
 def pack_kernel(
@@ -145,105 +159,130 @@
 
 
 def read_tables(ref):
-    return [[ref[n, index] for index in range(PHASES)] for n in range(3)]
-
-
-def unpack(ref, at, side, upper, ok, tables):
+    return [[ref[n * PHASES + index] for index in range(PHASES)] for n in range(3)]
+
+
+def lookups(fields, ok, keep, tables):
+    *rest, phase = fields
+    for number, table in enumerate(tables):
+        value = jnp.broadcast_to(table[0], phase.shape)
+        for index in range(1, PHASES):
+            value = jnp.where(phase == float(index), table[index], value)
+        if number == 0:
+            value = value * jnp.where(ok, 1.0, 0.0)
+            if keep is not None:
+                value = jnp.where(keep, value, 0.0)
+        elif number == 1:
+            value = (0.5 / math.log(2.0)) * (reciprocal(value) - 1.0)
+        rest.append(value)
+    return rest
+
+
+def own_lanes(ref, at, ok, tables):
+    block = ref[pl.ds(at * FIELDS, GROUP * FIELDS)].reshape(GROUP, FIELDS, *ref.shape[-2:])
+    return lookups([block[:, f] for f in range(FIELDS)], ok, None, tables)
+
+
+def edge_lanes(ref, at, upper, ok, tables):
     bz, by = ref.shape[-2:]
-    block = ref[pl.ds(at * FIELDS, GROUP * FIELDS)].reshape(GROUP, FIELDS, bz, by)
-    edge = ref[pl.ds(side, GROUP)]
+    edge = ref[pl.ds(at, GROUP)]
     iy = lax.axis_index("gy")
     lane = lax.broadcasted_iota(jnp.int32, (1, bz, by), 2)
     right = (lane < HIGH) & (iy < lax.axis_size("gy") - 1)
     left = (lane >= by - LOW) & (iy > 0)
-    ok = jnp.where(ok, 1.0, 0.0)
-    out = []
+    fields = []
     for f in range(FIELDS):
         shift = by // 2 * upper + LANE_STEP * f
         a = pltpu.roll(edge, (by - shift) % by, 2) if shift else edge
         b = pltpu.roll(edge, (by - LANE_STEP - shift) % by, 2)
-        out.append([block[:, f], jnp.where(right, a, jnp.where(left, b, 0.0))])
-    pair = out.pop()
-    for number, table in enumerate(tables):
-        values = []
-        for part, ph in enumerate(pair):
-            value = jnp.broadcast_to(table[0], ph.shape)
-            for index in range(1, PHASES):
-                value = jnp.where(ph == float(index), table[index], value)
-            if number == 0:
-                value = value * ok
-                if part:
-                    value = jnp.where(right | left, value, 0.0)
-            values.append(value)
-        out.append(values)
-    return out
-
-
-def unpack_own(ref, ok, tables, store):
-    bx = 2 * HIGH
+        fields.append(jnp.where(right, a, jnp.where(left, b, 0.0)))
+    return lookups(fields, ok, right | left, tables)
+
+
+def unpack_block(ref, part, ok, tables, store):
     for upper in range(2):
 
         def group(g, carry):
             at = g * GROUP + upper * HIGH
-            store(pl.ds(LOW + at, GROUP), unpack(ref, at, bx * FIELDS + g * GROUP, upper, ok, tables))
+            values = edge_lanes(ref, g * GROUP, upper, ok, tables) if part else own_lanes(ref, at, ok, tables)
+            store(pl.ds(LOW + at, GROUP), part, values)
             return carry
 
         lax.fori_loop(0, HIGH // GROUP, group, 0)
 
 
-def unpack_sides(ref, bx, ok, tables, store):
+def unpack_sides(ref, part, ok, tables, store):
     ix, nx = lax.axis_index("gx"), lax.axis_size("gx")
     for at in range(0, HIGH + LOW, GROUP):
         low = at >= HIGH
-        side = (HIGH + LOW) * FIELDS + (at - LOW if low else at)
-        values = unpack(ref, at, side, int(low), ok & (ix > 0 if low else ix < nx - 1), tables)
-        store(pl.ds(at - HIGH if low else LOW + bx + at, GROUP), values)
-
-
-def own_kernel(own_ref, side_ref, tables_ref, v_ref, p_ref, pre_ref, power_field_ref, rho_ref):
-    by = own_ref.shape[-1]
-    refs = [v_ref.at[d] for d in range(3)] + [p_ref, pre_ref, power_field_ref, rho_ref]
-
-    def store(planes, values):
-        for ref, (own, beside) in zip(refs, values):
-            ref[planes, :, 0:by] = own
-            ref[planes, :, by : 2 * by] = beside
-
-    tables = read_tables(tables_ref)
-    unpack_own(own_ref, True, tables, store)
-    unpack_sides(side_ref, 2 * HIGH, True, tables, store)
+        here = ok & (ix > 0 if low else ix < nx - 1)
+        if part:
+            values = edge_lanes(ref, HIGH + (at - LOW if low else at), int(low), here, tables)
+        else:
+            values = own_lanes(ref, at, here, tables)
+        store(pl.ds(at - HIGH if low else LOW + 2 * HIGH + at, GROUP), part, values)
+
+
+def own_store(v_ref, *rest):
+    refs = [v_ref.at[d] for d in range(3)] + list(rest)
+
+    def store(planes, part, values):
+        by = values[0].shape[-1]
+        for ref, value in zip(refs, values):
+            ref[planes, :, part * by : (part + 1) * by] = value
+
+    return store
 
 
 def halo_store(halo_ref, shared_ref, t):
     bz = shared_ref.shape[-2]
-    by = shared_ref.shape[-1] // 2
     rows = slice(t * bz // 2, (t + 1) * bz // 2)
 
-    def store(planes, values):
-        for n, pair in enumerate(values):
-            for part, value in enumerate(pair):
-                at = slice(part * by, (part + 1) * by)
-                halo_ref[n, planes, t * bz : (t + 1) * bz, at] = value
-                if n >= 4:
-                    shared_ref[n - 4, planes, rows, at] = value[:, rows]
+    def store(planes, part, values):
+        by = values[0].shape[-1]
+        at = slice(part * by, (part + 1) * by)
+        for n, value in enumerate(values):
+            halo_ref[n, planes, t * bz : (t + 1) * bz, at] = value
+            if n >= 4:
+                shared_ref[n - 4, planes, rows, at] = value[:, rows]
 
     return store
 
 
-def face_kernel(face_0_ref, face_1_ref, tables_ref, halo_ref, shared_ref):
+def own_kernel(stack_in_ref, edge_in_ref, tables_ref, stack_ref, edge_ref, *refs):
+    edge_ref[...] = edge_in_ref[...]
+    stack_ref[...] = stack_in_ref[...]
+    unpack_block(stack_in_ref, 0, True, read_tables(tables_ref), own_store(*refs))
+
+
+def own_sides_kernel(sides_ref, edge_ref, tables_ref, *refs):
+    tables = read_tables(tables_ref)
+    refs = refs[len(refs) // 2 :]
+    unpack_sides(sides_ref, 0, True, tables, own_store(*refs))
+    unpack_block(edge_ref, 1, True, tables, own_store(*refs))
+    unpack_sides(edge_ref, 1, True, tables, own_store(*refs))
+
+
+def by_parity(body):
+    for parity in range(2):
+        pl.when(lax.rem(lax.axis_index("gz"), 2) == parity)(lambda: body(parity, 1 - parity))
+
+
+def halo_kernel(face_0_ref, face_1_ref, corner_0_ref, corner_1_ref, tables_ref, halo_ref, shared_ref):
     iz, nz = lax.axis_index("gz"), lax.axis_size("gz")
     tables = read_tables(tables_ref)
-    for parity in range(2):
-        @pl.when(lax.rem(iz, 2) == parity)
-        def _():
-            faces = (face_0_ref, face_1_ref)
-            unpack_own(faces[parity], iz < nz - 1, tables, halo_store(halo_ref, shared_ref, 0))
-            unpack_own(faces[1 - parity], iz > 0, tables, halo_store(halo_ref, shared_ref, 1))
+    faces, corners = (face_0_ref, face_1_ref), (corner_0_ref, corner_1_ref)
+
+    @by_parity
+    def _(above, below):
+        for t, (n, ok) in enumerate(((above, iz < nz - 1), (below, iz > 0))):
+            unpack_block(faces[n], 0, ok, tables, halo_store(halo_ref, shared_ref, t))
+            unpack_sides(corners[n], 0, ok, tables, halo_store(halo_ref, shared_ref, t))
 
 
 def main_kernel(
     v_ref, p0_ref, pre_ref, power_field_ref, rho_ref, _halo, _shared,
-    corner_0_ref, corner_1_ref, tables_ref,
+    edge_0_ref, edge_1_ref, tables_ref,
     out_vx_ref, out_vz_ref, out_vy_ref, out_p_ref, out_eta_ref, sum_ref, halo_ref, shared_ref,
     va_ref, vb_ref, p_ref, weight_ref, weight2_ref,
 ):
@@ -252,12 +291,14 @@
     nx, nz, ny = lax.axis_size("gx"), lax.axis_size("gz"), lax.axis_size("gy")
     ix, iz, iy = lax.axis_index("gx"), lax.axis_index("gz"), lax.axis_index("gy")
     tables = read_tables(tables_ref)
-    for parity in range(2):
-        @pl.when(lax.rem(iz, 2) == parity)
-        def _():
-            corners = (corner_0_ref, corner_1_ref)
-            unpack_sides(corners[parity], bx, iz < nz - 1, tables, halo_store(halo_ref, shared_ref, 0))
-            unpack_sides(corners[1 - parity], bx, iz > 0, tables, halo_store(halo_ref, shared_ref, 1))
+    tables = read_tables(tables_ref)
+    edges = (edge_0_ref, edge_1_ref)
+
+    @by_parity
+    def _(above, below):
+        for t, (n, ok) in enumerate(((above, iz < nz - 1), (below, iz > 0))):
+            unpack_block(edges[n], 1, ok, tables, halo_store(halo_ref, shared_ref, t))
+            unpack_sides(edges[n], 1, ok, tables, halo_store(halo_ref, shared_ref, t))
 
     for ref, high in ((weight_ref, 2 * bz), (weight2_ref, bz + bz // 2)):
         shape = ref.shape[1:]
@@ -460,7 +501,7 @@
 
     hbm = pl.BlockSpec(memory_space=pltpu.HBM)
 
-    tables = jnp.stack([visc_scale, (0.5 / math.log(2.0)) * (1.0 / power_n - 1.0), density])
+    tables = jnp.concatenate([visc_scale, power_n, density])
     groups = bx // GROUP
     edge, half_0, half_1, stack = pl.pallas_call(
         pack_kernel,
@@ -491,39 +532,54 @@
         lane = lax.broadcasted_iota(jnp.int32, side.shape, 2) % (by // 2) % LANE_STEP
         return jnp.where((lane < HIGH) == (lax.rem(iy, 2) == 0), side, swap(edge, "gy", 1))
 
-    side = edges_beside(edge)
     x_0, x_1 = swap(half_0, "gx", 0), swap(half_1, "gx", 1)
-    face = jnp.concatenate([stack.reshape(bx * FIELDS, bz, by), side])
-    face_1 = swap(face, "gz", 1)
-    face_0 = swap(face, "gz", 0)
-    sides, edge = pl.pallas_call(
+    stack = stack.reshape(bx * FIELDS, bz, by)
+    def unpacking(kernel, tiles, out_shape, *args, aliases={}):
+        return pl.pallas_call(
+            kernel,
+            out_shape=out_shape,
+            in_specs=[VMEM if a is not tables else SMEM for a in args],
+            out_specs=(VMEM,) * len(out_shape),
+            input_output_aliases=aliases,
+            compiler_params=pltpu.CompilerParams(vmem_limit_bytes=16 * mebibyte),
+            cost_estimate=pl.CostEstimate(
+                flops=tiles * 56000 * bz * by, bytes_accessed=tiles * 1400 * bz * by * 4, transcendentals=0
+            ),
+        )(*args)
+
+    small = pltpu.CompilerParams(vmem_limit_bytes=4 * mebibyte)
+    field = shape(deep, bz, lanes)
+    own_shape = (shape(3, deep, bz, lanes),) + (field,) * 4
+    stack, edge, *own = unpacking(
+        own_kernel, bx, (shape(*stack.shape), shape(*edge.shape)) + own_shape, stack, edge, tables
+    )
+    face_1 = swap(stack, "gz", 1)
+    face_0 = swap(stack, "gz", 0)
+    edge = pl.pallas_call(
+        side_edge_kernel,
+        out_shape=shape(2 * HIGH, bz, by),
+        in_specs=[VMEM] * 3,
+        out_specs=VMEM,
+        compiler_params=small,
+    )(x_0, x_1, edge)
+    sides = pl.pallas_call(
         sides_kernel,
-        out_shape=(shape((HIGH + LOW) * FIELDS, bz, by), shape(HIGH, bz, by)),
-        in_specs=[VMEM] * 2,
-        out_specs=(VMEM,) * 2,
-        compiler_params=pltpu.CompilerParams(vmem_limit_bytes=4 * mebibyte),
-    )(x_0, x_1)
-    sides = jnp.concatenate([sides, edges_beside(edge)])
+        out_shape=shape((HIGH + LOW) * FIELDS, bz, by),
+        in_specs=[VMEM] * 3,
+        out_specs=VMEM,
+        compiler_params=small,
+    )(x_0, x_1, edge)
+    edge = edges_beside(edge)
     corner_1 = swap(sides, "gz", 1)
     corner_0 = swap(sides, "gz", 0)
-
-    field = shape(deep, bz, lanes)
-    own = pl.pallas_call(
-        own_kernel,
-        out_shape=(shape(3, deep, bz, lanes),) + (field,) * 4,
-        in_specs=[VMEM] * 2 + [SMEM],
-        out_specs=(VMEM,) * 5,
-        compiler_params=pltpu.CompilerParams(vmem_limit_bytes=8 * mebibyte),
-        cost_estimate=pl.CostEstimate(flops=deep * 30 * bz * lanes, bytes_accessed=12 * deep * bz * lanes * 4, transcendentals=0),
-    )(face, sides, tables)
-    halo = pl.pallas_call(
-        face_kernel,
-        out_shape=(shape(7, deep, 2 * bz, lanes), shape(3, deep, bz, lanes)),
-        in_specs=[VMEM] * 2 + [SMEM],
-        out_specs=(VMEM,) * 2,
-        compiler_params=pltpu.CompilerParams(vmem_limit_bytes=8 * mebibyte),
-        cost_estimate=pl.CostEstimate(flops=deep * 30 * bz * lanes, bytes_accessed=24 * bx * bz * lanes * 4, transcendentals=0),
-    )(face_0, face_1, tables)
+    edge_1 = swap(edge, "gz", 1)
+    edge_0 = swap(edge, "gz", 0)
+
+    own = unpacking(
+        own_sides_kernel, 12 + deep, own_shape, sides, edge, tables, *own, aliases={n + 3: n for n in range(5)}
+    )
+    halo_shape = (shape(7, deep, 2 * bz, lanes), shape(3, deep, bz, lanes))
+    halo = unpacking(halo_kernel, 2 * deep, halo_shape, face_0, face_1, corner_0, corner_1, tables)
     vx, vz, vy, p, eta, total, _, _ = pl.pallas_call(
         main_kernel,
         out_shape=(block,) * 5 + (shape(bz, by),) + tuple(shape(*a.shape) for a in halo),
@@ -538,7 +594,7 @@
             scratch(4, 2 * bz, lanes),
         ],
         compiler_params=pltpu.CompilerParams(vmem_limit_bytes=32 * mebibyte),
-    )(*own, *halo, corner_0, corner_1, tables)
+    )(*own, *halo, edge_0, edge_1, tables)
 
     total = sum_everywhere(total)
     p = pl.pallas_call(

time: 56.7 us -> 54.3 us (0.958)
  waiting for transfers between devices: 12.4 us -> 7.86 us
  local copies, waits for them, and re-layouts: 0.02 us -> 1.73 us
  other arithmetic: 2.35 us -> 0.78 us
  starting transfers between devices: 22.7 us -> 23.7 us
  Pallas kernels: 18.2 us -> 19.1 us
    ppermute x8 -> x9, waiting for transfers between devices: 5.05 us -> 0.74 us  [swap(): lax.ppermute(a, axis, [(i, j) for k in range(start, count - 1, 2) for i,...]
    unnamed x1 -> x4, local copies, waits for them, and re-layouts: 0.02 us -> 1.73 us
    another operation x2 -> x0, other arithmetic: 1.34 us -> none  [local(): jnp.stack([visc_scale, 0.5 / math.log(2.0) * (1.0 / power_n - 1.0), densi...]
    ppermute x8 -> x9, starting transfers between devices: 12.5 us -> 13.7 us  [swap(): lax.ppermute(a, axis, [(i, j) for k in range(start, count - 1, 2) for i,...]
    pallas_call x1, Pallas kernels: 12.6 us -> 13.3 us  [local(): pl.pallas_call(main_kernel, out_shape=(block,) * 5 + (shape(bz, by),) + t...]
    pallas_call x3 -> x5, Pallas kernels: 2.62 us -> 2.84 us  [the longest x3 2.64 us: unpacking(): pl.pallas_call(kernel, out_shape=out_shape, in_specs=[VMEM if a is not ta...]
  transfers between devices with their start and end apart: 15 -> 16, of which waited for: 8 -> 7; matrix products, arithmetic and copies ran while one was open for 4% -> 1% of each run, Pallas kernels for 5% -> 5%
where the time goes in v9:
time: 54.3 us; the launch traced here: 53.9 us
  starting transfers between devices  23.7 us (44%)
  Pallas kernels  19.1 us (35%)
  waiting for transfers between devices  7.86 us (14%)
  local copies, waits for them, and re-layouts  1.73 us (3%)
  other arithmetic  0.78 us (1%)
  between operations  0.75 us (1%)
    ppermute x9, starting transfers between devices, swap(): lax.ppermute(a, axis, [(i, j) for k in range(start, count - 1, 2) for i,...  13.7 us
    pallas_call x1, Pallas kernels, local(): pl.pallas_call(main_kernel, out_shape=(block,) * 5 + (shape(bz, by),) + t...  13.3 us
    ppermute x7, starting transfers between devices, sum_everywhere(): lax.ppermute(total, axes, [(i, i ^ m) for i in range(devices)])  9.99 us
    ppermute x7, waiting for transfers between devices, sum_everywhere(): lax.ppermute(total, axes, [(i, i ^ m) for i in range(devices)])  7.11 us
    pallas_call x3, Pallas kernels, unpacking(): pl.pallas_call(kernel, out_shape=out_shape, in_specs=[VMEM if a is not ta...  2.64 us
    pallas_call x1, Pallas kernels, local(): pl.pallas_call(pack_kernel, out_shape=(shape(HIGH, bz, by), shape(HIGH, F...  2.22 us
    unnamed x4, local copies, waits for them, and re-layouts  1.73 us
  transfers between devices with their start and end apart: 16, of which 7 were waited for; matrix products, arithmetic and copies ran while one was open for 1% of the time, Pallas kernels for 5%

profile of v9, /device:TPU:0, one launch (start us, length us, event | category | flops | bytes accessed | tf_op | source)
XLA Modules:
  0.0 53.9 jit_solution(5701715833768527304)
XLA Ops:
  0.6 2.2 %shard_map.119 = (f32[8,8,128]{2,1,0:T(8,128)}, f32[8,5,8,128]{3,2,1,0:T(8,128)}, f32[8,5,8,128]{3,2,1,0:T(8,128)}, f32[16,5,8,128]{3,2,1,0:T(8,128)}) custom-call(f32[16,8,128]{2,1,0:T(8,128)} %vx_hbm.1, f32[16,8,128]{2,1,0:T(8,128)} %vz_hbm.1, f32[16,8,128]{2,1,0:T(8,128)} %vy_hbm.1, f32[16,8,128]{2,1,0:T(8,128)} %p_hbm.1, s32[16,8,128]{2,1,0:T(8,128)} %phase_hbm.1), custom_call_target="tpu_custom_call" | custom-call | bytes 1048576 | tf_op jit(solution)/shard_map/pallas_call | solution.py:506
  2.9 3.1 %collective-permute-start = (f32[8,5,8,128]{3,2,1,0:T(8,128)}, f32[8,5,8,128]{3,2,1,0:T(8,128)S(1)}, u32[]{:S(2)}, u32[]{:S(2)}) collective-permute-start(f32[8,5,8,128]{3,2,1,0:T(8,128)} %get-tuple-element.29), channel_id=1, source_target_pairs={{0,8},{8,0},{16,24},{24,16},{1,9},{9,1},{17,25},{25,17},{2,10},{10... | collective-permute-start | bytes 491528 | tf_op jit(solution)/shard_map/ppermute | solution.py:473
  6.6 0.8 %pad_maximum_fusion.tables_ref = f32[12]{0:T(128)S(1)} fusion(f32[4]{0:T(128)} %param.15, f32[4]{0:T(128)} %param.14, f32[4]{0:T(128)} %param.13), kind=kLoop, calls=%fused_computation.2 | loop fusion | flops 24 | bytes 96 | tf_op jit(solution)/shard_map/concatenate | solution.py:504
  7.4 1.0 %copy-done = f32[16,5,8,128]{3,2,1,0:T(8,128)S(1)} copy-done((f32[16,5,8,128]{3,2,1,0:T(8,128)S(1)}, f32[16,5,8,128]{3,2,1,0:T(8,128)}, u32[]{:S(2)}) %copy-start) | copy-done | bytes 327704
  8.4 0.8 %copy-done.1 = f32[8,8,128]{2,1,0:T(8,128)S(1)} copy-done((f32[8,8,128]{2,1,0:T(8,128)S(1)}, f32[8,8,128]{2,1,0:T(8,128)}, u32[]{:S(2)}) %copy-start.1) | copy-done | bytes 32792
  10.5 2.9 %collective-permute-start.3 = (f32[80,8,128]{2,1,0:T(8,128)S(1)}, f32[80,8,128]{2,1,0:T(8,128)S(1)}, u32[]{:S(2)}, u32[]{:S(2)}) collective-permute-start(f32[80,8,128]{2,1,0:T(8,128)S(1)} %get-tuple-element.44), channel_id=1, source_target_pairs={{0,1},{1,0},{2,3},{3,2},{4,5},{5,4},{6,7},{7,6},{8,9},{9,8},{10,11... | collective-permute-start | bytes 983048 | tf_op jit(solution)/shard_map/ppermute | solution.py:473
  13.6 1.6 %collective-permute-start.2 = (f32[16,8,128]{2,1,0:T(8,128)S(1)}, f32[16,8,128]{2,1,0:T(8,128)S(1)}, u32[]{:S(2)}, u32[]{:S(2)}) collective-permute-start(f32[16,8,128]{2,1,0:T(8,128)S(1)} %shard_map.121._edge_ref), channel_id=1, source_target_pairs={{0,4},{4,0},{1,5},{5,1},{2,6},{6,2},{3,7},{7,3},{8,12},{12,8},{9,1... | collective-permute-start | bytes 196616 | tf_op jit(solution)/shard_map/ppermute | solution.py:473
  15.9 1.3 %collective-permute-start.5 = (f32[60,8,128]{2,1,0:T(8,128)S(1)}, f32[60,8,128]{2,1,0:T(8,128)S(1)}, u32[]{:S(2)}, u32[]{:S(2)}) collective-permute-start(f32[60,8,128]{2,1,0:T(8,128)S(1)} %shard_map.122.sides_ref), channel_id=1, source_target_pairs={{0,1},{1,0},{2,3},{3,2},{4,5},{5,4},{6,7},{7,6},{8,9},{9,8},{10,11... | collective-permute-start | bytes 737288 | tf_op jit(solution)/shard_map/ppermute | solution.py:473
  17.2 0.7 %collective-permute-done.2.edge_ref = f32[16,8,128]{2,1,0:T(8,128)S(1)} collective-permute-done((f32[16,8,128]{2,1,0:T(8,128)S(1)}, f32[16,8,128]{2,1,0:T(8,128)S(1)}, u32[]{:S(2)}, u32[]{:S(2)}) %collective-permute-start.2) | collective-permute-done | bytes 65568 | tf_op jit(solution)/shard_map/ppermute | solution.py:473
  18.6 1.1 %shard_map.123 = (f32[3,28,8,256]{3,2,1,0:T(8,128)S(1)}, f32[28,8,256]{2,1,0:T(8,128)S(1)}, f32[28,8,256]{2,1,0:T(8,128)S(1)}, f32[28,8,256]{2,1,0:T(8,128)S(1)}, f32[28,8,256]{2,1,0:T(8,128)S(1)}) custom-call(f32[60,8,128]{2,1,0:T(8,128)S(1)} %shard_map.122.sides_ref, ...), custom_call_target="tpu_custom_call", output_to_operand_aliasing={{0}: (3, {}), {1}: (4, {}), {2}: (5, {}), {3}: (6, {}), {4}... | custom-call | flops 2293760000 | bytes 229376000 | tf_op jit(solution)/shard_map/pallas_call | solution.py:538
  19.7 2.1 %collective-permute-start.7 = (f32[16,8,128]{2,1,0:T(8,128)S(1)}, f32[16,8,128]{2,1,0:T(8,128)S(1)}, u32[]{:S(2)}, u32[]{:S(2)}) collective-permute-start(f32[16,8,128]{2,1,0:T(8,128)S(1)} %collective-permute-done.2.edge_ref), channel_id=1, source_target_pairs={{0,1},{1,0},{2,3},{3,2},{4,5},{5,4},{6,7},{7,6},{8,9},{9,8},{10,11... | collective-permute-start | bytes 196616 | tf_op jit(solution)/shard_map/ppermute | solution.py:473
  21.8 0.9 %shard_map.124 = (f32[7,28,16,256]{3,2,1,0:T(8,128)S(1)}, f32[3,28,8,256]{3,2,1,0:T(8,128)S(1)}) custom-call(f32[80,8,128]{2,1,0:T(8,128)S(1)} %collective-permute-done.3.face_0_ref, f32[80,8,128]{2,1,0:T(8,128)S(1)} %collective-permute-done.4.face_1_ref, f32[60,8,128]{2,1,0:T(8,128)S(1)} %collective-permute-done.5.corner_0_ref, ...), custom_call_target="tpu_custom_call" | custom-call | flops 3211264000 | bytes 321126400 | tf_op jit(solution)/shard_map/pallas_call | solution.py:538
  22.7 13.3 %shard_map.125 = (f32[16,8,128]{2,1,0:T(8,128)}, f32[16,8,128]{2,1,0:T(8,128)}, f32[16,8,128]{2,1,0:T(8,128)}, f32[16,8,128]{2,1,0:T(8,128)S(1)}, f32[16,8,128]{...) custom-call(f32[3,28,8,256]{3,2,1,0:T(8,128)S(1)} %get-tuple-element, ...), custom_call_target="tpu_custom_call", output_to_operand_aliasing={{6}: (5, {}), {7}: (6, {})} | custom-call | tf_op jit(solution)/shard_map/pallas_call | solution.py:583
  36.7 0.8 %collective-permute-done.9 = f32[8,128]{1,0:T(8,128)S(1)} collective-permute-done((f32[8,128]{1,0:T(8,128)S(1)}, f32[8,128]{1,0:T(8,128)S(1)}, u32[]{:S(2)}, u32[]{:S(2)}) %collective-permute-start.9) | collective-permute-done | bytes 4128 | tf_op jit(solution)/shard_map/ppermute | solution.py:484
  37.5 1.5 %collective-permute-start.12 = (f32[8,128]{1,0:T(8,128)S(1)}, f32[8,128]{1,0:T(8,128)S(1)}, u32[]{:S(2)}, u32[]{:S(2)}) collective-permute-start(f32[8,128]{1,0:T(8,128)S(1)} %add.21), channel_id=1, source_target_pairs={{0,6},{1,7},{2,4},{3,5},{4,2},{5,3},{6,0},{7,1},{8,14},{9,15},{10,... | collective-permute-start | bytes 12296 | tf_op jit(solution)/shard_map/ppermute | solution.py:484
  39.1 1.0 %collective-permute-start.11 = (f32[8,128]{1,0:T(8,128)S(1)}, f32[8,128]{1,0:T(8,128)S(1)}, u32[]{:S(2)}, u32[]{:S(2)}) collective-permute-start(f32[8,128]{1,0:T(8,128)S(1)} %add.21), channel_id=1, source_target_pairs={{0,4},{1,5},{2,6},{3,7},{4,0},{5,1},{6,2},{7,3},{8,12},{9,13},{10,... | collective-permute-start | bytes 12296 | tf_op jit(solution)/shard_map/ppermute | solution.py:484
  40.1 0.9 %collective-permute-start.10 = (f32[8,128]{1,0:T(8,128)S(1)}, f32[8,128]{1,0:T(8,128)S(1)}, u32[]{:S(2)}, u32[]{:S(2)}) collective-permute-start(f32[8,128]{1,0:T(8,128)S(1)} %add.21), channel_id=1, source_target_pairs={{0,2},{1,3},{2,0},{3,1},{4,6},{5,7},{6,4},{7,5},{8,10},{9,11},{10,... | collective-permute-start | bytes 12296 | tf_op jit(solution)/shard_map/ppermute | solution.py:484
  41.0 1.0 %collective-permute-done.12 = f32[8,128]{1,0:T(8,128)S(1)} collective-permute-done((f32[8,128]{1,0:T(8,128)S(1)}, f32[8,128]{1,0:T(8,128)S(1)}, u32[]{:S(2)}, u32[]{:S(2)}) %collective-permute-start.12) | collective-permute-done | bytes 4128 | tf_op jit(solution)/shard_map/ppermute | solution.py:484
  42.7 1.0 %collective-permute-done.10 = f32[8,128]{1,0:T(8,128)S(1)} collective-permute-done((f32[8,128]{1,0:T(8,128)S(1)}, f32[8,128]{1,0:T(8,128)S(1)}, u32[]{:S(2)}, u32[]{:S(2)}) %collective-permute-start.10) | collective-permute-done | bytes 4128 | tf_op jit(solution)/shard_map/ppermute | solution.py:484
  43.7 2.5 %collective-permute-start.15 = (f32[8,128]{1,0:T(8,128)S(1)}, f32[8,128]{1,0:T(8,128)S(1)}, u32[]{:S(2)}, u32[]{:S(2)}) collective-permute-start(f32[8,128]{1,0:T(8,128)S(1)} %add_add_fusion.1), channel_id=1, source_target_pairs={{0,24},{1,25},{2,26},{3,27},{4,28},{5,29},{6,30},{7,31},{8,16},{9,... | collective-permute-start | bytes 12296 | tf_op jit(solution)/shard_map/ppermute | solution.py:484
  46.2 3.3 %collective-permute-start.14 = (f32[8,128]{1,0:T(8,128)S(1)}, f32[8,128]{1,0:T(8,128)S(1)}, u32[]{:S(2)}, u32[]{:S(2)}) collective-permute-start(f32[8,128]{1,0:T(8,128)S(1)} %add_add_fusion.1), channel_id=1, source_target_pairs={{0,16},{1,17},{2,18},{3,19},{4,20},{5,21},{6,22},{7,23},{8,24},{9,... | collective-permute-start | bytes 12296 | tf_op jit(solution)/shard_map/ppermute | solution.py:484
  49.6 1.6 %collective-permute-done.14 = f32[8,128]{1,0:T(8,128)S(1)} collective-permute-done((f32[8,128]{1,0:T(8,128)S(1)}, f32[8,128]{1,0:T(8,128)S(1)}, u32[]{:S(2)}, u32[]{:S(2)}) %collective-permute-start.14) | collective-permute-done | bytes 4128 | tf_op jit(solution)/shard_map/ppermute | solution.py:484
  51.2 2.0 %collective-permute-done.13 = f32[8,128]{1,0:T(8,128)S(1)} collective-permute-done((f32[8,128]{1,0:T(8,128)S(1)}, f32[8,128]{1,0:T(8,128)S(1)}, u32[]{:S(2)}, u32[]{:S(2)}) %collective-permute-start.13) | collective-permute-done | bytes 4128 | tf_op jit(solution)/shard_map/ppermute | solution.py:484
  53.2 0.8 %shard_map.126 = f32[16,8,128]{2,1,0:T(8,128)} custom-call(f32[16,8,128]{2,1,0:T(8,128)S(1)} %get-tuple-element.50.refs_0_, f32[8,128]{1,0:T(8,128)S(1)} %add_add_fusion.refs_1_), custom_call_target="tpu_custom_call" | custom-call | tf_op jit(solution)/shard_map/pallas_call | solution.py:600
  (24 shorter events, 4.9 us)
Async XLA Ops:
  2.9 10.5 %collective-permute-start = (f32[8,5,8,128]{3,2,1,0:T(8,128)}, f32[8,5,8,128]{3,2,1,0:T(8,128)S(1)}, u32[]{:S(2)}, u32[]{:S(2)}) collective-permute-start(f32[8,5,8,128]{3,2,1,0:T(8,128)} %get-tuple-element.29), channel_id=1, source_target_pairs={{0,8},{8,0},{16,24},{24,16},{1,9},{9,1},{17,25},{25,17},{2,10},{10... | collective-permute-start | bytes 491528 | tf_op jit(solution)/shard_map/ppermute | solution.py:473
  6.0 7.5 %collective-permute-start.1 = (f32[8,5,8,128]{3,2,1,0:T(8,128)}, f32[8,5,8,128]{3,2,1,0:T(8,128)S(1)}, u32[]{:S(2)}, u32[]{:S(2)}) collective-permute-start(f32[8,5,8,128]{3,2,1,0:T(8,128)} %get-tuple-element.30), channel_id=1, source_target_pairs={{8,16},{16,8},{9,17},{17,9},{10,18},{18,10},{11,19},{19,11},{12,20... | collective-permute-start | bytes 491528 | tf_op jit(solution)/shard_map/ppermute | solution.py:473
  7.4 1.0 %copy-start = (f32[16,5,8,128]{3,2,1,0:T(8,128)S(1)}, f32[16,5,8,128]{3,2,1,0:T(8,128)}, u32[]{:S(2)}) copy-start(f32[16,5,8,128]{3,2,1,0:T(8,128)} %get-tuple-element.31) | copy-start | bytes 983044
  8.4 0.8 %copy-start.1 = (f32[8,8,128]{2,1,0:T(8,128)S(1)}, f32[8,8,128]{2,1,0:T(8,128)}, u32[]{:S(2)}) copy-start(f32[8,8,128]{2,1,0:T(8,128)} %get-tuple-element.32.edge_in_ref) | copy-start | bytes 98308
  9.8 9.9 %collective-permute-start.4 = (f32[80,8,128]{2,1,0:T(8,128)S(1)}, f32[80,8,128]{2,1,0:T(8,128)S(1)}, u32[]{:S(2)}, u32[]{:S(2)}) collective-permute-start(f32[80,8,128]{2,1,0:T(8,128)S(1)} %get-tuple-element.44), channel_id=1, source_target_pairs={{1,2},{2,1},{5,6},{6,5},{9,10},{10,9},{13,14},{14,13},{17,18},{18,... | collective-permute-start | bytes 983048 | tf_op jit(solution)/shard_map/ppermute | solution.py:473
  10.5 11.3 %collective-permute-start.3 = (f32[80,8,128]{2,1,0:T(8,128)S(1)}, f32[80,8,128]{2,1,0:T(8,128)S(1)}, u32[]{:S(2)}, u32[]{:S(2)}) collective-permute-start(f32[80,8,128]{2,1,0:T(8,128)S(1)} %get-tuple-element.44), channel_id=1, source_target_pairs={{0,1},{1,0},{2,3},{3,2},{4,5},{5,4},{6,7},{7,6},{8,9},{9,8},{10,11... | collective-permute-start | bytes 983048 | tf_op jit(solution)/shard_map/ppermute | solution.py:473
  13.6 4.3 %collective-permute-start.2 = (f32[16,8,128]{2,1,0:T(8,128)S(1)}, f32[16,8,128]{2,1,0:T(8,128)S(1)}, u32[]{:S(2)}, u32[]{:S(2)}) collective-permute-start(f32[16,8,128]{2,1,0:T(8,128)S(1)} %shard_map.121._edge_ref), channel_id=1, source_target_pairs={{0,4},{4,0},{1,5},{5,1},{2,6},{6,2},{3,7},{7,3},{8,12},{12,8},{9,1... | collective-permute-start | bytes 196616 | tf_op jit(solution)/shard_map/ppermute | solution.py:473
  15.2 6.6 %collective-permute-start.6 = (f32[60,8,128]{2,1,0:T(8,128)S(1)}, f32[60,8,128]{2,1,0:T(8,128)S(1)}, u32[]{:S(2)}, u32[]{:S(2)}) collective-permute-start(f32[60,8,128]{2,1,0:T(8,128)S(1)} %shard_map.122.sides_ref), channel_id=1, source_target_pairs={{1,2},{2,1},{5,6},{6,5},{9,10},{10,9},{13,14},{14,13},{17,18},{18,... | collective-permute-start | bytes 737288 | tf_op jit(solution)/shard_map/ppermute | solution.py:473
  15.9 5.9 %collective-permute-start.5 = (f32[60,8,128]{2,1,0:T(8,128)S(1)}, f32[60,8,128]{2,1,0:T(8,128)S(1)}, u32[]{:S(2)}, u32[]{:S(2)}) collective-permute-start(f32[60,8,128]{2,1,0:T(8,128)S(1)} %shard_map.122.sides_ref), channel_id=1, source_target_pairs={{0,1},{1,0},{2,3},{3,2},{4,5},{5,4},{6,7},{7,6},{8,9},{9,8},{10,11... | collective-permute-start | bytes 737288 | tf_op jit(solution)/shard_map/ppermute | solution.py:473
  17.9 4.8 %collective-permute-start.8 = (f32[16,8,128]{2,1,0:T(8,128)S(1)}, f32[16,8,128]{2,1,0:T(8,128)S(1)}, u32[]{:S(2)}, u32[]{:S(2)}) collective-permute-start(f32[16,8,128]{2,1,0:T(8,128)S(1)} %collective-permute-done.2.edge_ref), channel_id=1, source_target_pairs={{1,2},{2,1},{5,6},{6,5},{9,10},{10,9},{13,14},{14,13},{17,18},{18,... | collective-permute-start | bytes 196616 | tf_op jit(solution)/shard_map/ppermute | solution.py:473
  19.7 3.0 %collective-permute-start.7 = (f32[16,8,128]{2,1,0:T(8,128)S(1)}, f32[16,8,128]{2,1,0:T(8,128)S(1)}, u32[]{:S(2)}, u32[]{:S(2)}) collective-permute-start(f32[16,8,128]{2,1,0:T(8,128)S(1)} %collective-permute-done.2.edge_ref), channel_id=1, source_target_pairs={{0,1},{1,0},{2,3},{3,2},{4,5},{5,4},{6,7},{7,6},{8,9},{9,8},{10,11... | collective-permute-start | bytes 196616 | tf_op jit(solution)/shard_map/ppermute | solution.py:473
  36.0 1.5 %collective-permute-start.9 = (f32[8,128]{1,0:T(8,128)S(1)}, f32[8,128]{1,0:T(8,128)S(1)}, u32[]{:S(2)}, u32[]{:S(2)}) collective-permute-start(f32[8,128]{1,0:T(8,128)S(1)} %get-tuple-element.51), channel_id=1, source_target_pairs={{0,1},{1,0},{2,3},{3,2},{4,5},{5,4},{6,7},{7,6},{8,9},{9,8},{10,11... | collective-permute-start | bytes 12296 | tf_op jit(solution)/shard_map/ppermute | solution.py:484
  37.5 4.5 %collective-permute-start.12 = (f32[8,128]{1,0:T(8,128)S(1)}, f32[8,128]{1,0:T(8,128)S(1)}, u32[]{:S(2)}, u32[]{:S(2)}) collective-permute-start(f32[8,128]{1,0:T(8,128)S(1)} %add.21), channel_id=1, source_target_pairs={{0,6},{1,7},{2,4},{3,5},{4,2},{5,3},{6,0},{7,1},{8,14},{9,15},{10,... | collective-permute-start | bytes 12296 | tf_op jit(solution)/shard_map/ppermute | solution.py:484
  39.1 3.6 %collective-permute-start.11 = (f32[8,128]{1,0:T(8,128)S(1)}, f32[8,128]{1,0:T(8,128)S(1)}, u32[]{:S(2)}, u32[]{:S(2)}) collective-permute-start(f32[8,128]{1,0:T(8,128)S(1)} %add.21), channel_id=1, source_target_pairs={{0,4},{1,5},{2,6},{3,7},{4,0},{5,1},{6,2},{7,3},{8,12},{9,13},{10,... | collective-permute-start | bytes 12296 | tf_op jit(solution)/shard_map/ppermute | solution.py:484
  40.1 3.6 %collective-permute-start.10 = (f32[8,128]{1,0:T(8,128)S(1)}, f32[8,128]{1,0:T(8,128)S(1)}, u32[]{:S(2)}, u32[]{:S(2)}) collective-permute-start(f32[8,128]{1,0:T(8,128)S(1)} %add.21), channel_id=1, source_target_pairs={{0,2},{1,3},{2,0},{3,1},{4,6},{5,7},{6,4},{7,5},{8,10},{9,11},{10,... | collective-permute-start | bytes 12296 | tf_op jit(solution)/shard_map/ppermute | solution.py:484
  43.7 5.8 %collective-permute-start.15 = (f32[8,128]{1,0:T(8,128)S(1)}, f32[8,128]{1,0:T(8,128)S(1)}, u32[]{:S(2)}, u32[]{:S(2)}) collective-permute-start(f32[8,128]{1,0:T(8,128)S(1)} %add_add_fusion.1), channel_id=1, source_target_pairs={{0,24},{1,25},{2,26},{3,27},{4,28},{5,29},{6,30},{7,31},{8,16},{9,... | collective-permute-start | bytes 12296 | tf_op jit(solution)/shard_map/ppermute | solution.py:484
  46.2 4.9 %collective-permute-start.14 = (f32[8,128]{1,0:T(8,128)S(1)}, f32[8,128]{1,0:T(8,128)S(1)}, u32[]{:S(2)}, u32[]{:S(2)}) collective-permute-start(f32[8,128]{1,0:T(8,128)S(1)} %add_add_fusion.1), channel_id=1, source_target_pairs={{0,16},{1,17},{2,18},{3,19},{4,20},{5,21},{6,22},{7,23},{8,24},{9,... | collective-permute-start | bytes 12296 | tf_op jit(solution)/shard_map/ppermute | solution.py:484
  49.6 3.6 %collective-permute-start.13 = (f32[8,128]{1,0:T(8,128)S(1)}, f32[8,128]{1,0:T(8,128)S(1)}, u32[]{:S(2)}, u32[]{:S(2)}) collective-permute-start(f32[8,128]{1,0:T(8,128)S(1)} %add_add_fusion.1), channel_id=1, source_target_pairs={{0,8},{1,9},{2,10},{3,11},{4,12},{5,13},{6,14},{7,15},{8,0},{9,1},... | collective-permute-start | bytes 12296 | tf_op jit(solution)/shard_map/ppermute | solution.py:484

commit v10 on v9

v10 whole, which is shorter than its diff:
```python
import math

import jax
import jax.numpy as jnp
from jax import lax
from jax.experimental import pallas as pl
from jax.experimental.pallas import tpu as pltpu
from jax.sharding import PartitionSpec as P

ITERS = 4
PHASES = 4
FIELDS = 5
DEPTH = ITERS
LANE_STEP = 2 * DEPTH + 1
UNROLL = 4
GROUP = 4

VMEM = pl.BlockSpec(memory_space=pltpu.VMEM)
SMEM = pl.BlockSpec(memory_space=pltpu.SMEM)
HBM = pl.BlockSpec(memory_space=pltpu.HBM)


def z_up(a):
    return pltpu.roll(a, a.shape[-2] - 1, a.ndim - 2)


def z_down(a):
    return pltpu.roll(a, 1, a.ndim - 2)


def y_up(a):
    return pltpu.roll(a, a.shape[-1] - 1, a.ndim - 1)


def y_down(a):
    return pltpu.roll(a, 1, a.ndim - 1)


def reciprocal(a):
    r = pl.reciprocal(a, approx=True)
    return r * (2.0 - a * r)


def iota(shape, axis):
    return lax.broadcasted_iota(jnp.int32, shape, axis)


def odd(axis):
    return lax.rem(lax.axis_index(axis), 2) == 1


def by_parity(axis, pair, body):
    pl.when(jnp.logical_not(odd(axis)))(lambda: body(pair[0], pair[1]))
    pl.when(odd(axis))(lambda: body(pair[1], pair[0]))


def start_copies(sources, targets, sems):
    copies = []
    for g in range(sources[0].shape[0] // GROUP):
        at = pl.ds(g * GROUP, GROUP)
        copies.append(
            [pltpu.make_async_copy(a.at[at], b.at[at], sems.at[g, f]) for f, (a, b) in enumerate(zip(sources, targets))]
        )
        for copy in copies[-1]:
            copy.start()
    return copies


def clean_group(g, field_ref, phase_ref):
    bx, bz, by = phase_ref.shape
    ix, iz, iy = lax.axis_index("gx"), lax.axis_index("gz"), lax.axis_index("gy")
    plane, row, lane = (iota((GROUP, bz, by), d) for d in range(3))
    at = pl.ds(g * GROUP, GROUP)
    vx, vz, vy, p = (field_ref[f, at] for f in range(FIELDS - 1))
    if g == 0:
        vx = jnp.where((plane > 0) | (ix > 0), vx, 0.0)
    vz = jnp.where((row > 0) | (iz > 0), vz, 0.0)
    vy = jnp.where((lane > 0) | (iy > 0), vy, 0.0)
    return vx, vz, vy, p, phase_ref[at].astype(jnp.float32)


def add_edge(edge, a, base):
    by = edge.shape[-1]
    lane = iota((1,) * (edge.ndim - 1) + (by,), edge.ndim - 1)
    first = pltpu.roll(a, base, a.ndim - 1) if base else a
    edge = jnp.where((lane >= base) & (lane <= base + DEPTH), first, edge)
    last = pltpu.roll(a, (base + LANE_STEP) % by, a.ndim - 1)
    return jnp.where((lane > base + DEPTH) & (lane < base + LANE_STEP), last, edge)


def add_edges(edge, fields, upper):
    for f, a in enumerate(fields):
        edge = add_edge(edge, a, edge.shape[-1] // 2 * upper + LANE_STEP * f)
    return edge


def beside(edge, f, upper):
    by = edge.shape[-1]
    iy = lax.axis_index("gy")
    lane = iota((1,) * (edge.ndim - 1) + (by,), edge.ndim - 1)
    right = (lane <= DEPTH) & (iy < lax.axis_size("gy") - 1)
    left = (lane >= by - DEPTH) & (iy > 0)
    shift = by // 2 * upper + LANE_STEP * f
    a = pltpu.roll(edge, by - shift, edge.ndim - 1) if shift else edge
    b = pltpu.roll(edge, (by - LANE_STEP - shift) % by, edge.ndim - 1)
    return jnp.where(right, a, jnp.where(left, b, 0.0))


def pack_kernel(
    vx_hbm, vz_hbm, vy_hbm, p_hbm, phase_hbm, edge_hbm, x_0_hbm, x_1_hbm, stack_hbm,
    field_ref, phase_ref, edge_ref, stack_ref, sems, out_sems,
):
    bx, bz, by = phase_ref.shape
    targets = [field_ref.at[f] for f in range(FIELDS - 1)] + [phase_ref]
    copies = start_copies((vx_hbm, vz_hbm, vy_hbm, p_hbm, phase_hbm), targets, sems)
    half = bx // GROUP // 2
    outs = []

    def out(source, target):
        outs.append(pltpu.make_async_copy(source, target, out_sems.at[len(outs)]))
        outs[-1].start()

    for g in range(half):
        edge = jnp.zeros((GROUP, bz, by), jnp.float32)
        for upper in range(2):
            at = (g + upper * half) * GROUP
            for copy in copies[g + upper * half]:
                copy.wait()
            fields = clean_group(g + upper * half, field_ref, phase_ref)
            for f, a in enumerate(fields):
                for i in range(GROUP):
                    stack_ref[(at + i) * FIELDS + f] = a[i]
            edge = add_edges(edge, fields, upper)
            at = pl.ds(at * FIELDS, GROUP * FIELDS)
            out(stack_ref.at[at], stack_hbm.at[at])
        at = pl.ds(g * GROUP, GROUP)
        edge_ref[at] = edge
        out(edge_ref.at[at], edge_hbm.at[at])
    count = x_0_hbm.shape[0]
    down, up = stack_ref.at[pl.ds(0, count)], stack_ref.at[pl.ds(bx * FIELDS - count, count)]
    sem = out_sems.at[len(outs)], out_sems.at[len(outs) + 1]

    def send(to_above, to_below):
        pair = pltpu.make_async_copy(up, to_above, sem[0]), pltpu.make_async_copy(down, to_below, sem[1])
        for copy in pair:
            copy.start()
        for copy in pair:
            copy.wait()

    by_parity("gx", (x_0_hbm, x_1_hbm), send)
    for copy in outs:
        copy.wait()


def side_edge_kernel(x_0_ref, x_1_ref, own_edge_ref, edge_ref):
    bz, by = edge_ref.shape[1:]
    own = own_edge_ref.shape[0]
    edge_ref[0:own] = own_edge_ref[...]

    def body(above, below):
        edge = jnp.zeros((DEPTH, bz, by), jnp.float32)
        for upper, (ref, at) in enumerate(((above, 0), (below, 1))):
            block = ref[pl.ds(at, DEPTH * FIELDS)].reshape(DEPTH, FIELDS, bz, by)
            edge = add_edges(edge, [block[:, f] for f in range(FIELDS)], upper)
        edge_ref[own:] = edge
        edge_ref[own] = add_edge(edge[0], above[DEPTH * FIELDS], FIELDS * LANE_STEP)

    by_parity("gx", (x_0_ref, x_1_ref), body)


def half_rows(tiles, swap):
    down = odd("gz") if swap == 0 else jnp.logical_not(odd("gz"))
    half = tiles.shape[-2] // 2
    return jnp.where(down, tiles[..., :half, :], tiles[..., half:, :])


def store_next_rows(refs, at, tiles):
    half = tiles.shape[-2] // 2
    for ref in refs:
        for i in range(tiles.shape[0]):
            ref[at + i // half, i % half : i % half + 1, :] = tiles[i, half : half + 1, :]


def sides_kernel(x_0_ref, x_1_ref, _edge_ref, sides_ref, z_0_ref, z_1_ref):
    count = DEPTH * FIELDS
    bz, by = sides_ref.shape[1:]

    def body(above, below):
        sides_ref[0:count] = above[0:count]
        sides_ref[count : 2 * count] = below[1 : count + 1]
        sides_ref[2 * count] = above[count]

    by_parity("gx", (x_0_ref, x_1_ref), body)
    tiles = sides_ref[...]
    for swap, ref in enumerate((z_0_ref, z_1_ref)):
        ref[0 : 2 * count + 1] = half_rows(tiles, swap)
    vz = tiles[0 : 2 * count].reshape(2 * DEPTH, FIELDS, bz, by)[:, 1]
    store_next_rows((z_0_ref, z_1_ref), 2 * count + 1, vz)


def edge_rows_kernel(edge_ref, z_0_ref, z_1_ref):
    tiles = edge_ref[...]
    for swap, ref in enumerate((z_0_ref, z_1_ref)):
        ref[0 : tiles.shape[0]] = half_rows(tiles, swap)
    store_next_rows((z_0_ref, z_1_ref), tiles.shape[0], tiles)


def lookups(fields, ok, keep, table_ref):
    *rest, phase = fields
    for number in range(3):
        table = [table_ref[number * PHASES + index] for index in range(PHASES)]
        value = jnp.broadcast_to(table[0], phase.shape)
        for index in range(1, PHASES):
            value = jnp.where(phase == float(index), table[index], value)
        if number == 0:
            value = value * jnp.where(ok, 1.0, 0.0)
            if keep is not None:
                value = jnp.where(keep, value, 0.0)
        elif number == 1:
            value = (0.5 / math.log(2.0)) * (reciprocal(value) - 1.0)
        rest.append(value)
    return rest


def own_lanes(block, ok, tables):
    block = block.reshape(-1, FIELDS, *block.shape[-2:])
    return lookups([block[:, f] for f in range(FIELDS)], ok, None, tables)


def edge_lanes(edge, upper, ok, tables):
    by = edge.shape[-1]
    iy = lax.axis_index("gy")
    lane = iota((1, 1, by), 2)
    keep = ((lane <= DEPTH) & (iy < lax.axis_size("gy") - 1)) | ((lane >= by - DEPTH) & (iy > 0))
    return lookups([beside(edge, f, upper) for f in range(FIELDS)], ok, keep, tables)


def store_to(refs):
    def store(planes, part, values):
        by = values[0].shape[-1]
        for ref, value in zip(refs, values):
            ref[planes, :, part * by : (part + 1) * by] = value

    return store


def unpack_own(load, bx, ok, tables, store):
    def group(g, carry):
        at = g * GROUP
        store(pl.ds(DEPTH + at, GROUP), 0, own_lanes(load(at * FIELDS, GROUP * FIELDS), ok, tables))
        return carry

    lax.fori_loop(0, bx // GROUP, group, 0)


def unpack_own_edges(load, bx, ok, tables, store):
    half = bx // 2
    for upper in range(2):

        def group(g, carry):
            at = g * GROUP
            values = edge_lanes(load(at, GROUP), upper, ok, tables)
            store(pl.ds(DEPTH + upper * half + at, GROUP), 1, values)
            return carry

        lax.fori_loop(0, half // GROUP, group, 0)


def side_places(bx):
    ix = lax.axis_index("gx")
    return (pl.ds(DEPTH + bx, DEPTH), ix < lax.axis_size("gx") - 1), (pl.ds(0, DEPTH), ix > 0)


def unpack_sides(load, bx, ok, tables, store, vx_ref):
    count = DEPTH * FIELDS
    for n, (planes, inside) in enumerate(side_places(bx)):
        store(planes, 0, own_lanes(load(n * count, count), ok & inside, tables))
    vx = load(2 * count, 1)
    vx_ref[pl.ds(bx + 2 * DEPTH, 1), :, 0 : vx.shape[-1]] = vx


def unpack_side_edges(load, bx, ok, tables, store, vx_ref):
    half = bx // 2
    edge = load(half, DEPTH)
    for upper, (planes, inside) in enumerate(side_places(bx)):
        store(planes, 1, edge_lanes(edge, upper, ok & inside, tables))
    by = edge.shape[-1]
    vx_ref[pl.ds(bx + 2 * DEPTH, 1), :, by : 2 * by] = beside(edge[0:1], FIELDS, 0)


def own_kernel(stack_ref, edge_in_ref, tables_ref, z_0_ref, z_1_ref, edge_ref, v_ref, *rest):
    edge_ref[...] = edge_in_ref[...]
    count = stack_ref.shape[0]
    bx = count // FIELDS
    size = GROUP * FIELDS

    def group(g, carry):
        at = pl.ds(g * size, size)
        tiles = stack_ref[at]
        for swap, ref in enumerate((z_0_ref, z_1_ref)):
            ref[at] = half_rows(tiles, swap)
        return carry

    lax.fori_loop(0, bx // GROUP, group, 0)
    for g in range(bx // GROUP):
        vz = stack_ref[pl.ds(g * size, size)].reshape(GROUP, FIELDS, *stack_ref.shape[1:])[:, 1]
        store_next_rows((z_0_ref, z_1_ref), count + g * GROUP // (stack_ref.shape[1] // 2), vz)
    store = store_to([v_ref.at[d] for d in range(3)] + list(rest))
    unpack_own(lambda at, n: stack_ref[pl.ds(at, n)], bx, True, tables_ref, store)


def own_sides_kernel(sides_ref, edge_ref, tables_ref, *refs):
    v_ref, *rest = refs[len(refs) // 2 :]
    bx = v_ref.shape[1] - 2 * DEPTH - 1
    store = store_to([v_ref.at[d] for d in range(3)] + list(rest))
    unpack_sides(lambda at, n: sides_ref[pl.ds(at, n)], bx, True, tables_ref, store, v_ref.at[0])
    load = lambda at, n: edge_ref[pl.ds(at, n)]
    unpack_own_edges(load, bx, True, tables_ref, store)
    unpack_side_edges(load, bx, True, tables_ref, store, v_ref.at[0])


def rows_in_grid(bz):
    iz = lax.axis_index("gz")
    row = iota((1, bz, 1), 1)
    return ((row < bz // 2) & (iz < lax.axis_size("gz") - 1)) | ((row >= bz // 2) & (iz > 0))


def load_both(above, below):
    return lambda at, n: jnp.concatenate([above[pl.ds(at, n)], below[pl.ds(at, n)]], axis=1)


def halo_kernel(face_0_ref, face_1_ref, corner_0_ref, corner_1_ref, tables_ref, halo_ref, next_ref):
    half, by = face_0_ref.shape[1:]
    bz = 2 * half
    bx = halo_ref.shape[1] - 2 * DEPTH - 1
    ok = rows_in_grid(bz)
    store = store_to([halo_ref.at[n] for n in range(7)])

    def faces(above, below):
        unpack_own(load_both(above, below), bx, ok, tables_ref, store)
        for i in range(bx):
            n = i % half
            next_ref[DEPTH + i, half - 1 : half, 0:by] = above[bx * FIELDS + i // half, n : n + 1, :]

    def corners(above, below):
        unpack_sides(load_both(above, below), bx, ok, tables_ref, store, halo_ref.at[0])
        for i in range(2 * DEPTH):
            n = i % half
            to = DEPTH + bx + i if i < DEPTH else i - DEPTH
            next_ref[to, half - 1 : half, 0:by] = above[2 * DEPTH * FIELDS + 1 + i // half, n : n + 1, :]

    by_parity("gz", (face_0_ref, face_1_ref), faces)
    by_parity("gz", (corner_0_ref, corner_1_ref), corners)


def unpack_halo_edges(edge_0_ref, edge_1_ref, tables_ref, halo_ref, next_ref):
    half, by = edge_0_ref.shape[1:]
    bx = halo_ref.shape[1] - 2 * DEPTH - 1
    ok = rows_in_grid(2 * half)
    store = store_to([halo_ref.at[n] for n in range(7)])
    tiles = bx // 2 + DEPTH

    def body(above, below):
        load = load_both(above, below)
        unpack_own_edges(load, bx, ok, tables_ref, store)
        unpack_side_edges(load, bx, ok, tables_ref, store, halo_ref.at[0])
        for n in range(tiles // half):
            rows = above[tiles + n]
            for upper in range(2):
                values = beside(rows, 1, upper)
                for i in range(half):
                    tile = n * half + i
                    if tile < bx // 2:
                        to = DEPTH + upper * (bx // 2) + tile
                    else:
                        to = tile - bx // 2 + (0 if upper else DEPTH + bx)
                    next_ref[to, half - 1 : half, by : 2 * by] = values[i : i + 1]

    by_parity("gz", (edge_0_ref, edge_1_ref), body)


def main_kernel(
    v_ref, p0_ref, pre_ref, power_field_ref, rho_ref, _halo, _next, edge_0_ref, edge_1_ref, tables_ref,
    out_vx_ref, out_vz_ref, out_vy_ref, out_p_ref, out_eta_ref, sum_ref, halo_ref, next_ref,
    va_ref, vb_ref, p_ref, weight_ref,
):
    bx, bz, by = out_p_ref.shape
    rows, lanes = 2 * bz, 2 * by
    nx, nz, ny = lax.axis_size("gx"), lax.axis_size("gz"), lax.axis_size("gy")
    ix, iz, iy = lax.axis_index("gx"), lax.axis_index("gz"), lax.axis_index("gy")
    unpack_halo_edges(edge_0_ref, edge_1_ref, tables_ref, halo_ref, next_ref)

    shape = (rows, lanes)
    r, c = iota(shape, 0), iota(shape, 1)
    zg = iz * bz + jnp.where(r < bz + bz // 2, r, r - rows)
    yg = iy * by + jnp.where(c <= by + DEPTH, c, c - lanes)
    filled = (c <= by + DEPTH) | (c >= lanes - DEPTH)
    inside = filled & (zg >= 0) & (zg < nz * bz) & (yg >= 0) & (yg < ny * by)
    weight_ref[0] = jnp.where(inside, 0.05, 0.0)
    weight_ref[1] = jnp.where(inside & (zg > 0), 0.05, 0.0)
    weight_ref[2] = jnp.where(inside & (yg > 0), 0.05, 0.0)
    weight_ref[3] = jnp.where(inside, 0.0, 1.0)

    def with_halo(own, n, planes):
        return jnp.concatenate([own[planes], halo_ref[n, planes]], axis=1)

    for k in range(1, ITERS + 1):
        old, new = (va_ref, vb_ref) if k % 2 else (vb_ref, va_ref)
        last = k == ITERS

        def load(d, j, count):
            planes = pl.ds(j, count)
            return with_halo(v_ref.at[d], d, planes) if k == 1 else old[d, planes]

        def cells(j, count):
            planes = pl.ds(j, count)
            vx1 = load(0, j, count + 1)
            vx = vx1[:count]
            vz, vy = load(1, j, count), load(2, j, count)
            p = with_halo(p0_ref, 3, planes) if k == 1 else p_ref[planes]
            up = z_up(vz)
            if k == 1:
                after = next_ref[planes]
                after = jnp.concatenate([after, after], axis=1)
                up = jnp.where(iota((1, rows, lanes), 1) == bz + bz // 2 - 1, after, up)
            rx = vx1[1:] - vx
            rz = up - vz
            ry = y_up(vy) - vy
            a = rx - ry
            b = ry - rz
            inv = (a * (a + b) + b * b) * (1.0 / 3.0) + 1.0
            eta = with_halo(pre_ref, 4, planes) * jnp.exp2(with_halo(power_field_ref, 5, planes) * jnp.log(inv))
            quarter = 0.25 * eta
            div = rx + ry + rz
            p = p - quarter * (div + div)
            tx, tz, ty = eta * rx - p, eta * rz - p, eta * ry - p
            sz = quarter + z_down(quarter)
            sy = quarter + y_down(quarter)
            return vx, vz, vy, eta, p, quarter, tx, tz, ty, sz, sy

        def chunk(j, count, carry, start=False):
            planes = pl.ds(j, count)
            vx, vz, vy, eta, p, quarter, tx, tz, ty, sz, sy = cells(j, count)
            vz0, vy0 = load(1, j - 1, 1), load(2, j - 1, 1)
            quarter0, tx0, sz0, sy0, part_z0, part_y0, scale_z0, scale_y0 = carry
            join = lambda first, rest: jnp.concatenate([first, rest[:-1]], axis=0) if count > 1 else first
            bias = weight_ref[3:4]
            sx = quarter + join(quarter0, quarter)
            exz = sz + join(sz0, sz)
            exy = sy + join(sy0, sy)
            ezy = sz + y_down(sz)
            fxz = exz * (vx - z_down(vx))
            fxy = exy * (vx - y_down(vx))
            low_vz, low_vy = join(vz0, vz), join(vy0, vy)
            gzx = exz * (vz - low_vz)
            hyx = exy * (vy - low_vy)
            gzy = ezy * (vz - y_down(vz))
            hyz = ezy * (vy - z_down(vy))
            res_x = (tx - join(tx0, tx)) + ((z_up(fxz) - fxz) + (y_up(fxy) - fxy))
            new_vx = vx + weight_ref[0:1] * reciprocal(sx + bias) * res_x
            part_z = (tz - z_down(tz)) - with_halo(rho_ref, 6, planes) + ((y_up(gzy) - gzy) - gzx)
            part_y = (ty - y_down(ty)) + ((z_up(hyz) - hyz) - hyx)
            scale_z = weight_ref[1:2] * reciprocal(sz + bias)
            scale_y = weight_ref[2:3] * reciprocal(sy + bias)
            new_vz = low_vz + join(scale_z0, scale_z) * (join(part_z0, part_z) + gzx)
            new_vy = low_vy + join(scale_y0, scale_y) * (join(part_y0, part_y) + hyx)
            if last:
                at = pl.ds(j - DEPTH, count)
                out_vx_ref[at] = new_vx[:, 0:bz, 0:by]
                out_p_ref[at] = p[:, 0:bz, 0:by]
                out_eta_ref[at] = eta[:, 0:bz, 0:by]
                sum_ref[...] += jnp.sum(p[:, 0:bz, 0:by], axis=0)
                if not start:
                    at = pl.ds(j - 1 - DEPTH, count)
                    out_vz_ref[at] = new_vz[:, 0:bz, 0:by]
                    out_vy_ref[at] = new_vy[:, 0:bz, 0:by]
            else:
                p_ref[planes] = p
                new[0, planes] = new_vx
                if not start:
                    new[1, pl.ds(j - 1, count)] = new_vz
                    new[2, pl.ds(j - 1, count)] = new_vy
            return tuple(a[-1:] for a in (quarter, tx, sz, sy, part_z, part_y, scale_z, scale_y))

        first, end = k, bx + 2 * DEPTH - k
        if last:
            sum_ref[...] = jnp.zeros((bz, by), jnp.float32)
        _, _, _, _, p, quarter, tx, _, _, sz, sy = cells(first - 1, 1)
        if not last:
            p_ref[pl.ds(first - 1, 1)] = p
        zero = jnp.zeros((1, rows, lanes), jnp.float32)
        carry = chunk(first, 1, (quarter, tx, sz, sy, zero, zero, zero, zero), start=True)
        steps, rest = divmod((end - 1 if last else end) - first, UNROLL)
        carry = lax.fori_loop(
            0, steps, lambda s, carry: chunk(first + 1 + s * UNROLL, UNROLL, carry), carry
        )
        if rest:
            carry = chunk(first + 1 + steps * UNROLL, rest, carry)
        if last:
            quarter0, tx0, sz0, sy0, part_z0, part_y0, scale_z0, scale_y0 = carry
            _, vz, vy, _, _, _, _, _, _, sz, sy = cells(end, 1)
            vz0, vy0 = load(1, end - 1, 1), load(2, end - 1, 1)
            new_vz = vz0 + scale_z0 * (part_z0 + (sz + sz0) * (vz - vz0))
            new_vy = vy0 + scale_y0 * (part_y0 + (sy + sy0) * (vy - vy0))
            out_vz_ref[pl.ds(end - 1 - DEPTH, 1)] = new_vz[:, 0:bz, 0:by]
            out_vy_ref[pl.ds(end - 1 - DEPTH, 1)] = new_vy[:, 0:bz, 0:by]

            @pl.when(ix == 0)
            def _():
                out_vx_ref[0] = jnp.zeros((bz, by), jnp.float32)
        else:
            plane = jnp.zeros((rows, lanes), jnp.float32)

            @pl.when(ix == 0)
            def _():
                for i in range(first, DEPTH):
                    for d in range(3):
                        new[d, i] = plane
                new[0, DEPTH] = plane

            @pl.when(ix == nx - 1)
            def _():
                for i in range(DEPTH + bx, end + 1):
                    for d in range(3):
                        new[d, i] = plane


def final_kernel(p_ref, sum_ref, out_ref, *, cells):
    mean = jnp.sum(sum_ref[...]) * (1.0 / cells)
    out_ref[...] = p_ref[...] - mean


def swap(a, axis, start):
    count = lax.axis_size(axis)
    return lax.ppermute(a, axis, [(i, j) for k in range(start, count - 1, 2) for i, j in ((k, k + 1), (k + 1, k))])


def sum_everywhere(total):
    axes = ("gx", "gy", "gz")
    devices = math.prod(lax.axis_size(a) for a in axes)
    if devices & (devices - 1):
        return lax.psum(total, axes)
    bits = [1 << n for n in range(devices.bit_length() - 1)]
    for stage in [bits[:1]] + [bits[n : n + 2] for n in range(1, len(bits), 2)]:
        masks = stage if len(stage) == 1 else [stage[0], stage[1], stage[0] + stage[1]]
        total = sum([lax.ppermute(total, axes, [(i, i ^ m) for i in range(devices)]) for m in masks], total)
    return total


def local(vel_x, vel_y, vel_z, pressure, phase, visc_scale, power_n, density):
    bx, bz, by = pressure.shape
    assert bx % (2 * GROUP) == 0 and bz == 2 * DEPTH and DEPTH == GROUP
    f32 = jnp.float32
    iy, ny = lax.axis_index("gy"), lax.axis_size("gy")
    cells = bx * bz * by * math.prod(lax.axis_size(a) for a in ("gx", "gz", "gy"))
    deep = bx + 2 * DEPTH + 1
    rows, lanes = 2 * bz, 2 * by
    shape = lambda *dims: jax.ShapeDtypeStruct(dims, f32)
    block = shape(bx, bz, by)
    scratch = lambda *dims: pltpu.VMEM(dims, f32)
    limit = lambda mebibytes: pltpu.CompilerParams(vmem_limit_bytes=mebibytes * 1024 * 1024)
    tables = jnp.concatenate([visc_scale, power_n, density])

    groups = bx // GROUP
    sent = shape(DEPTH * FIELDS + 1, bz, by)
    edge, x_0, x_1, stack = pl.pallas_call(
        pack_kernel,
        out_shape=(shape(bx // 2, bz, by), sent, sent, shape(bx * FIELDS, bz, by)),
        in_specs=[HBM] * 5,
        out_specs=(HBM,) * 4,
        scratch_shapes=[
            scratch(FIELDS - 1, bx, bz, by),
            pltpu.VMEM((bx, bz, by), jnp.int32),
            scratch(bx // 2, bz, by),
            scratch(bx * FIELDS, bz, by),
            pltpu.SemaphoreType.DMA((groups, FIELDS)),
            pltpu.SemaphoreType.DMA((groups + groups // 2 + 2,)),
        ],
        compiler_params=limit(58),
    )(vel_x, vel_z, vel_y, pressure, phase)

    def edges_beside(edge):
        side = swap(edge, "gy", 0)
        if ny == 2:
            return side
        lane = iota(side.shape, 2) % (by // 2) % LANE_STEP
        return jnp.where((lane <= DEPTH) == (lax.rem(iy, 2) == 0), side, swap(edge, "gy", 1))

    estimate = lambda size: pl.CostEstimate(
        flops=4 * size * bz * by, bytes_accessed=size * bz * by * 4, transcendentals=0
    )
    long = estimate(100000)

    def unpacking(kernel, tiles, out_shape, *args, aliases={}):
        return pl.pallas_call(
            kernel,
            out_shape=out_shape,
            in_specs=[VMEM if a is not tables else SMEM for a in args],
            out_specs=(VMEM,) * len(out_shape),
            input_output_aliases=aliases,
            compiler_params=limit(16),
            cost_estimate=estimate(13 * tiles),
        )(*args)

    field = shape(deep, bz, lanes)
    own_shape = (shape(3, deep, bz, lanes),) + (field,) * 4
    half = lambda tiles, planes: shape(tiles + planes // (bz // 2), bz // 2, by)
    x_0, x_1 = swap(x_0, "gx", 0), swap(x_1, "gx", 1)
    face = half(bx * FIELDS, bx)
    z_0, z_1, edge, *own = unpacking(own_kernel, bx, (face, face, shape(*edge.shape)) + own_shape, stack, edge, tables)
    face_1, face_0 = swap(z_1, "gz", 1), swap(z_0, "gz", 0)

    tiles = bx // 2 + DEPTH
    edge = pl.pallas_call(
        side_edge_kernel,
        out_shape=shape(tiles, bz, by),
        in_specs=[VMEM] * 3,
        out_specs=VMEM,
        compiler_params=limit(4),
    )(x_0, x_1, edge)
    corner = half(2 * DEPTH * FIELDS + 1, 2 * DEPTH)
    sides, z_0, z_1 = pl.pallas_call(
        sides_kernel,
        out_shape=(shape(2 * DEPTH * FIELDS + 1, bz, by), corner, corner),
        in_specs=[VMEM] * 3,
        out_specs=(VMEM,) * 3,
        compiler_params=limit(4),
    )(x_0, x_1, edge)
    edge = edges_beside(edge)
    corner_1, corner_0 = swap(z_1, "gz", 1), swap(z_0, "gz", 0)
    z_0, z_1 = pl.pallas_call(
        edge_rows_kernel,
        out_shape=(half(tiles, tiles),) * 2,
        in_specs=[VMEM],
        out_specs=(VMEM,) * 2,
        compiler_params=limit(4),
        cost_estimate=long,
    )(edge)
    edge_1, edge_0 = swap(z_1, "gz", 1), swap(z_0, "gz", 0)

    own = unpacking(
        own_sides_kernel, 2 * deep, own_shape, sides, edge, tables, *own, aliases={n + 3: n for n in range(5)}
    )
    halo = unpacking(
        halo_kernel, deep, (shape(7, deep, bz, lanes), field), face_0, face_1, corner_0, corner_1, tables
    )
    vx, vz, vy, p, eta, total, _, _ = pl.pallas_call(
        main_kernel,
        out_shape=(block,) * 5 + (shape(bz, by),) + tuple(shape(*a.shape) for a in halo),
        in_specs=[VMEM] * 9 + [SMEM],
        out_specs=(VMEM,) * 8,
        input_output_aliases={5: 6, 6: 7},
        scratch_shapes=[
            scratch(3, deep, rows, lanes),
            scratch(3, deep, rows, lanes),
            scratch(deep, rows, lanes),
            scratch(4, rows, lanes),
        ],
        compiler_params=limit(32),
    )(*own, *halo, edge_0, edge_1, tables)

    total = sum_everywhere(total)
    p = pl.pallas_call(
        lambda *refs: final_kernel(*refs, cells=float(cells)),
        out_shape=block,
        in_specs=[VMEM] * 2,
        out_specs=VMEM,
        compiler_params=limit(4),
    )(p, total)
    return (vx, vy, vz, p, eta)


def solution(mesh):
    spec = P("gx", "gz", "gy")
    return jax.shard_map(
        local,
        mesh=mesh,
        in_specs=(spec,) * 5 + (P(),) * 3,
        out_specs=(spec,) * 5,
        check_vma=False,
    )
```

time: 54.3 us -> 50.1 us (0.923)
  Pallas kernels: 19.1 us -> 15.1 us
  waiting for transfers between devices: 7.86 us -> 7.14 us
    pallas_call x1, Pallas kernels: 13.3 us -> 9.42 us  [local(): pl.pallas_call(main_kernel, out_shape=(block,) * 5 + (shape(bz, by),) + t...]
    ppermute x7, starting transfers between devices: 9.99 us -> 12 us  [sum_everywhere(): lax.ppermute(total, axes, [(i, i ^ m) for i in range(devices)])]
    ppermute x9, starting transfers between devices: 13.7 us -> 12.2 us  [swap(): lax.ppermute(a, axis, [(i, j) for k in range(start, count - 1, 2) for i,...]
    ppermute x9, waiting for transfers between devices: 0.74 us -> 0.02 us  [swap(): lax.ppermute(a, axis, [(i, j) for k in range(start, count - 1, 2) for i,...]
    pallas_call x3 -> x4, Pallas kernels: 2.43 us -> 2.4 us  [the longest x1 2.18 us: local(): pl.pallas_call(pack_kernel, out_shape=(shape(bx // 2, bz, by), sent, sent...]
  transfers between devices with their start and end apart: 16 -> 16, of which waited for: 7 -> 6; matrix products, arithmetic and copies ran while one was open for 1% -> 2% of each run, Pallas kernels for 5% -> 6%
where the time goes in v10:
time: 50.1 us; the launch traced here: 49.8 us
  starting transfers between devices  24.2 us (48%)
  Pallas kernels  15.1 us (30%)
  waiting for transfers between devices  7.14 us (14%)
  local copies, waits for them, and re-layouts  1.73 us (3%)
  between operations  0.8 us (2%)
  other arithmetic  0.78 us (2%)
    ppermute x9, starting transfers between devices, swap(): lax.ppermute(a, axis, [(i, j) for k in range(start, count - 1, 2) for i,...  12.2 us
    ppermute x7, starting transfers between devices, sum_everywhere(): lax.ppermute(total, axes, [(i, i ^ m) for i in range(devices)])  12 us
    pallas_call x1, Pallas kernels, local(): pl.pallas_call(main_kernel, out_shape=(block,) * 5 + (shape(bz, by),) + t...  9.42 us
    ppermute x7, waiting for transfers between devices, sum_everywhere(): lax.ppermute(total, axes, [(i, i ^ m) for i in range(devices)])  7.11 us
    pallas_call x3, Pallas kernels, unpacking(): pl.pallas_call(kernel, out_shape=out_shape, in_specs=[VMEM if a is not ta...  2.53 us
    pallas_call x1, Pallas kernels, local(): pl.pallas_call(pack_kernel, out_shape=(shape(bx // 2, bz, by), sent, sent...  2.18 us
    unnamed x4, local copies, waits for them, and re-layouts  1.73 us
  transfers between devices with their start and end apart: 16, of which 6 were waited for; matrix products, arithmetic and copies ran while one was open for 2% of the time, Pallas kernels for 6%

profile of v10, /device:TPU:0, one launch (start us, length us, event | category | flops | bytes accessed | tf_op | source)
XLA Modules:
  0.0 49.8 jit_solution(10451268371560977905)
XLA Ops:
  0.6 2.2 %shard_map.119 = (f32[8,8,128]{2,1,0:T(8,128)}, f32[21,8,128]{2,1,0:T(8,128)}, f32[21,8,128]{2,1,0:T(8,128)}, f32[80,8,128]{2,1,0:T(8,128)}) custom-call(f32[16,8,128]{2,1,0:T(8,128)} %vx_hbm.1, f32[16,8,128]{2,1,0:T(8,128)} %vz_hbm.1, f32[16,8,128]{2,1,0:T(8,128)} %vy_hbm.1, f32[16,8,128]{2,1,0:T(8,128)} %p_hbm.1, s32[16,8,128]{2,1,0:T(8,128)} %phase_hbm.1), custom_call_target="tpu_custom_call" | custom-call | tf_op jit(solution)/shard_map/pallas_call | solution.py:566
  2.8 3.1 %collective-permute-start = (f32[21,8,128]{2,1,0:T(8,128)}, f32[21,8,128]{2,1,0:T(8,128)S(1)}, u32[]{:S(2)}, u32[]{:S(2)}) collective-permute-start(f32[21,8,128]{2,1,0:T(8,128)} %get-tuple-element.35), channel_id=1, source_target_pairs={{0,8},{8,0},{16,24},{24,16},{1,9},{9,1},{17,25},{25,17},{2,10},{10... | collective-permute-start | bytes 258056 | tf_op jit(solution)/shard_map/ppermute | solution.py:535
  6.5 0.8 %pad_maximum_fusion.tables_ref = f32[12]{0:T(128)S(1)} fusion(f32[4]{0:T(128)} %param.15, f32[4]{0:T(128)} %param.14, f32[4]{0:T(128)} %param.13), kind=kLoop, calls=%fused_computation.2 | loop fusion | flops 24 | bytes 96 | tf_op jit(solution)/shard_map/concatenate | solution.py:562
  7.3 1.0 %copy-done = f32[80,8,128]{2,1,0:T(8,128)S(1)} copy-done((f32[80,8,128]{2,1,0:T(8,128)S(1)}, f32[80,8,128]{2,1,0:T(8,128)}, u32[]{:S(2)}) %copy-start) | copy-done | bytes 327704
  8.3 0.8 %copy-done.1 = f32[8,8,128]{2,1,0:T(8,128)S(1)} copy-done((f32[8,8,128]{2,1,0:T(8,128)S(1)}, f32[8,8,128]{2,1,0:T(8,128)}, u32[]{:S(2)}) %copy-start.1) | copy-done | bytes 32792
  9.0 0.7 %shard_map.120 = (f32[84,4,128]{2,1,0:T(4,128)S(1)}, f32[84,4,128]{2,1,0:T(4,128)S(1)}, f32[8,8,128]{2,1,0:T(8,128)S(1)}, f32[3,25,8,256]{3,2,1,0:T(8,128)S(1)},...) custom-call(f32[80,8,128]{2,1,0:T(8,128)S(1)} %copy-done, ...), custom_call_target="tpu_custom_call" | custom-call | flops 851968 | bytes 851968 | tf_op jit(solution)/shard_map/pallas_call | solution.py:595
  10.7 1.6 %collective-permute-start.2 = (f32[12,8,128]{2,1,0:T(8,128)S(1)}, f32[12,8,128]{2,1,0:T(8,128)S(1)}, u32[]{:S(2)}, u32[]{:S(2)}) collective-permute-start(f32[12,8,128]{2,1,0:T(8,128)S(1)} %shard_map.121._edge_ref), channel_id=1, source_target_pairs={{0,4},{4,0},{1,5},{5,1},{2,6},{6,2},{3,7},{7,3},{8,12},{12,8},{9,1... | collective-permute-start | bytes 147464 | tf_op jit(solution)/shard_map/ppermute | solution.py:535
  12.4 2.7 %collective-permute-start.5 = (f32[43,4,128]{2,1,0:T(4,128)S(1)}, f32[43,4,128]{2,1,0:T(4,128)S(1)}, u32[]{:S(2)}, u32[]{:S(2)}) collective-permute-start(f32[43,4,128]{2,1,0:T(4,128)S(1)} %get-tuple-element.53), channel_id=1, source_target_pairs={{0,1},{1,0},{2,3},{3,2},{4,5},{5,4},{6,7},{7,6},{8,9},{9,8},{10,11... | collective-permute-start | bytes 264200 | tf_op jit(solution)/shard_map/ppermute | solution.py:535
  15.7 2.2 %collective-permute-start.7 = (f32[15,4,128]{2,1,0:T(4,128)S(1)}, f32[15,4,128]{2,1,0:T(4,128)S(1)}, u32[]{:S(2)}, u32[]{:S(2)}) collective-permute-start(f32[15,4,128]{2,1,0:T(4,128)S(1)} %get-tuple-element.57), channel_id=1, source_target_pairs={{0,1},{1,0},{2,3},{3,2},{4,5},{5,4},{6,7},{7,6},{8,9},{9,8},{10,11... | collective-permute-start | bytes 92168 | tf_op jit(solution)/shard_map/ppermute | solution.py:535
  18.6 1.1 %shard_map.123 = (f32[3,25,8,256]{3,2,1,0:T(8,128)S(1)}, f32[25,8,256]{2,1,0:T(8,128)S(1)}, f32[25,8,256]{2,1,0:T(8,128)S(1)}, f32[25,8,256]{2,1,0:T(8,128)S(1)}, f32[25,8,256]{2,1,0:T(8,128)S(1)}) custom-call(f32[41,8,128]{2,1,0:T(8,128)S(1)} %get-tuple-element.40.sides_ref, ...), custom_call_target="tpu_custom_call", output_to_operand_aliasing={{0}: (3, {}), {1}: (4, {}), {2}: (5, {}), {3}: (6, {}), {4}... | custom-call | flops 2662400 | bytes 2662400 | tf_op jit(solution)/shard_map/pallas_call | solution.py:595
  20.4 9.4 %shard_map.126 = (f32[16,8,128]{2,1,0:T(8,128)}, f32[16,8,128]{2,1,0:T(8,128)}, f32[16,8,128]{2,1,0:T(8,128)}, f32[16,8,128]{2,1,0:T(8,128)S(1)}, f32[16,8,128]{...) custom-call(f32[3,25,8,256]{3,2,1,0:T(8,128)S(1)} %get-tuple-element, ...), custom_call_target="tpu_custom_call", output_to_operand_aliasing={{6}: (5, {}), {7}: (6, {})} | custom-call | tf_op jit(solution)/shard_map/pallas_call | solution.py:647
  29.8 2.7 %collective-permute-start.9 = (f32[8,128]{1,0:T(8,128)S(1)}, f32[8,128]{1,0:T(8,128)S(1)}, u32[]{:S(2)}, u32[]{:S(2)}) collective-permute-start(f32[8,128]{1,0:T(8,128)S(1)} %get-tuple-element.63), channel_id=1, source_target_pairs={{0,1},{1,0},{2,3},{3,2},{4,5},{5,4},{6,7},{7,6},{8,9},{9,8},{10,11... | collective-permute-start | bytes 12296 | tf_op jit(solution)/shard_map/ppermute | solution.py:546
  32.6 0.8 %collective-permute-done.9 = f32[8,128]{1,0:T(8,128)S(1)} collective-permute-done((f32[8,128]{1,0:T(8,128)S(1)}, f32[8,128]{1,0:T(8,128)S(1)}, u32[]{:S(2)}, u32[]{:S(2)}) %collective-permute-start.9) | collective-permute-done | bytes 4128 | tf_op jit(solution)/shard_map/ppermute | solution.py:546
  33.4 1.7 %collective-permute-start.12 = (f32[8,128]{1,0:T(8,128)S(1)}, f32[8,128]{1,0:T(8,128)S(1)}, u32[]{:S(2)}, u32[]{:S(2)}) collective-permute-start(f32[8,128]{1,0:T(8,128)S(1)} %add.21), channel_id=1, source_target_pairs={{0,6},{1,7},{2,4},{3,5},{4,2},{5,3},{6,0},{7,1},{8,14},{9,15},{10,... | collective-permute-start | bytes 12296 | tf_op jit(solution)/shard_map/ppermute | solution.py:546
  35.1 0.9 %collective-permute-start.11 = (f32[8,128]{1,0:T(8,128)S(1)}, f32[8,128]{1,0:T(8,128)S(1)}, u32[]{:S(2)}, u32[]{:S(2)}) collective-permute-start(f32[8,128]{1,0:T(8,128)S(1)} %add.21), channel_id=1, source_target_pairs={{0,4},{1,5},{2,6},{3,7},{4,0},{5,1},{6,2},{7,3},{8,12},{9,13},{10,... | collective-permute-start | bytes 12296 | tf_op jit(solution)/shard_map/ppermute | solution.py:546
  36.0 0.9 %collective-permute-start.10 = (f32[8,128]{1,0:T(8,128)S(1)}, f32[8,128]{1,0:T(8,128)S(1)}, u32[]{:S(2)}, u32[]{:S(2)}) collective-permute-start(f32[8,128]{1,0:T(8,128)S(1)} %add.21), channel_id=1, source_target_pairs={{0,2},{1,3},{2,0},{3,1},{4,6},{5,7},{6,4},{7,5},{8,10},{9,11},{10,... | collective-permute-start | bytes 12296 | tf_op jit(solution)/shard_map/ppermute | solution.py:546
  36.9 1.0 %collective-permute-done.12 = f32[8,128]{1,0:T(8,128)S(1)} collective-permute-done((f32[8,128]{1,0:T(8,128)S(1)}, f32[8,128]{1,0:T(8,128)S(1)}, u32[]{:S(2)}, u32[]{:S(2)}) %collective-permute-start.12) | collective-permute-done | bytes 4128 | tf_op jit(solution)/shard_map/ppermute | solution.py:546
  37.9 0.8 %collective-permute-done.11 = f32[8,128]{1,0:T(8,128)S(1)} collective-permute-done((f32[8,128]{1,0:T(8,128)S(1)}, f32[8,128]{1,0:T(8,128)S(1)}, u32[]{:S(2)}, u32[]{:S(2)}) %collective-permute-start.11) | collective-permute-done | bytes 4128 | tf_op jit(solution)/shard_map/ppermute | solution.py:546
  38.7 0.9 %collective-permute-done.10 = f32[8,128]{1,0:T(8,128)S(1)} collective-permute-done((f32[8,128]{1,0:T(8,128)S(1)}, f32[8,128]{1,0:T(8,128)S(1)}, u32[]{:S(2)}, u32[]{:S(2)}) %collective-permute-start.10) | collective-permute-done | bytes 4128 | tf_op jit(solution)/shard_map/ppermute | solution.py:546
  39.6 2.5 %collective-permute-start.15 = (f32[8,128]{1,0:T(8,128)S(1)}, f32[8,128]{1,0:T(8,128)S(1)}, u32[]{:S(2)}, u32[]{:S(2)}) collective-permute-start(f32[8,128]{1,0:T(8,128)S(1)} %add_add_fusion.1), channel_id=1, source_target_pairs={{0,24},{1,25},{2,26},{3,27},{4,28},{5,29},{6,30},{7,31},{8,16},{9,... | collective-permute-start | bytes 12296 | tf_op jit(solution)/shard_map/ppermute | solution.py:546
  42.1 3.3 %collective-permute-start.14 = (f32[8,128]{1,0:T(8,128)S(1)}, f32[8,128]{1,0:T(8,128)S(1)}, u32[]{:S(2)}, u32[]{:S(2)}) collective-permute-start(f32[8,128]{1,0:T(8,128)S(1)} %add_add_fusion.1), channel_id=1, source_target_pairs={{0,16},{1,17},{2,18},{3,19},{4,20},{5,21},{6,22},{7,23},{8,24},{9,... | collective-permute-start | bytes 12296 | tf_op jit(solution)/shard_map/ppermute | solution.py:546
  45.4 1.6 %collective-permute-done.14 = f32[8,128]{1,0:T(8,128)S(1)} collective-permute-done((f32[8,128]{1,0:T(8,128)S(1)}, f32[8,128]{1,0:T(8,128)S(1)}, u32[]{:S(2)}, u32[]{:S(2)}) %collective-permute-start.14) | collective-permute-done | bytes 4128 | tf_op jit(solution)/shard_map/ppermute | solution.py:546
  47.0 2.0 %collective-permute-done.13 = f32[8,128]{1,0:T(8,128)S(1)} collective-permute-done((f32[8,128]{1,0:T(8,128)S(1)}, f32[8,128]{1,0:T(8,128)S(1)}, u32[]{:S(2)}, u32[]{:S(2)}) %collective-permute-start.13) | collective-permute-done | bytes 4128 | tf_op jit(solution)/shard_map/ppermute | solution.py:546
  49.0 0.8 %shard_map.127 = f32[16,8,128]{2,1,0:T(8,128)} custom-call(f32[16,8,128]{2,1,0:T(8,128)S(1)} %get-tuple-element.62.refs_0_, f32[8,128]{1,0:T(8,128)S(1)} %add_add_fusion.refs_1_), custom_call_target="tpu_custom_call" | custom-call | tf_op jit(solution)/shard_map/pallas_call | solution.py:663
  (25 shorter events, 3.7 us)
Async XLA Ops:
  2.8 7.7 %collective-permute-start = (f32[21,8,128]{2,1,0:T(8,128)}, f32[21,8,128]{2,1,0:T(8,128)S(1)}, u32[]{:S(2)}, u32[]{:S(2)}) collective-permute-start(f32[21,8,128]{2,1,0:T(8,128)} %get-tuple-element.35), channel_id=1, source_target_pairs={{0,8},{8,0},{16,24},{24,16},{1,9},{9,1},{17,25},{25,17},{2,10},{10... | collective-permute-start | bytes 258056 | tf_op jit(solution)/shard_map/ppermute | solution.py:535
  5.9 4.7 %collective-permute-start.1 = (f32[21,8,128]{2,1,0:T(8,128)}, f32[21,8,128]{2,1,0:T(8,128)S(1)}, u32[]{:S(2)}, u32[]{:S(2)}) collective-permute-start(f32[21,8,128]{2,1,0:T(8,128)} %get-tuple-element.36), channel_id=1, source_target_pairs={{8,16},{16,8},{9,17},{17,9},{10,18},{18,10},{11,19},{19,11},{12,20... | collective-permute-start | bytes 258056 | tf_op jit(solution)/shard_map/ppermute | solution.py:535
  7.3 1.0 %copy-start = (f32[80,8,128]{2,1,0:T(8,128)S(1)}, f32[80,8,128]{2,1,0:T(8,128)}, u32[]{:S(2)}) copy-start(f32[80,8,128]{2,1,0:T(8,128)} %get-tuple-element.37.stack_ref) | copy-start | bytes 983044
  8.3 0.8 %copy-start.1 = (f32[8,8,128]{2,1,0:T(8,128)S(1)}, f32[8,8,128]{2,1,0:T(8,128)}, u32[]{:S(2)}) copy-start(f32[8,8,128]{2,1,0:T(8,128)} %get-tuple-element.38.edge_in_ref) | copy-start | bytes 98308
  9.8 8.1 %collective-permute-start.3 = (f32[84,4,128]{2,1,0:T(4,128)S(1)}, f32[84,4,128]{2,1,0:T(4,128)S(1)}, u32[]{:S(2)}, u32[]{:S(2)}) collective-permute-start(f32[84,4,128]{2,1,0:T(4,128)S(1)} %get-tuple-element.51), channel_id=1, source_target_pairs={{0,1},{1,0},{2,3},{3,2},{4,5},{5,4},{6,7},{7,6},{8,9},{9,8},{10,11... | collective-permute-start | bytes 516104 | tf_op jit(solution)/shard_map/ppermute | solution.py:535
  9.9 9.8 %collective-permute-start.4 = (f32[84,4,128]{2,1,0:T(4,128)S(1)}, f32[84,4,128]{2,1,0:T(4,128)S(1)}, u32[]{:S(2)}, u32[]{:S(2)}) collective-permute-start(f32[84,4,128]{2,1,0:T(4,128)S(1)} %get-tuple-element.52), channel_id=1, source_target_pairs={{1,2},{2,1},{5,6},{6,5},{9,10},{10,9},{13,14},{14,13},{17,18},{18,... | collective-permute-start | bytes 516104 | tf_op jit(solution)/shard_map/ppermute | solution.py:535
  10.7 4.9 %collective-permute-start.2 = (f32[12,8,128]{2,1,0:T(8,128)S(1)}, f32[12,8,128]{2,1,0:T(8,128)S(1)}, u32[]{:S(2)}, u32[]{:S(2)}) collective-permute-start(f32[12,8,128]{2,1,0:T(8,128)S(1)} %shard_map.121._edge_ref), channel_id=1, source_target_pairs={{0,4},{4,0},{1,5},{5,1},{2,6},{6,2},{3,7},{7,3},{8,12},{12,8},{9,1... | collective-permute-start | bytes 147464 | tf_op jit(solution)/shard_map/ppermute | solution.py:535
  12.4 7.3 %collective-permute-start.5 = (f32[43,4,128]{2,1,0:T(4,128)S(1)}, f32[43,4,128]{2,1,0:T(4,128)S(1)}, u32[]{:S(2)}, u32[]{:S(2)}) collective-permute-start(f32[43,4,128]{2,1,0:T(4,128)S(1)} %get-tuple-element.53), channel_id=1, source_target_pairs={{0,1},{1,0},{2,3},{3,2},{4,5},{5,4},{6,7},{7,6},{8,9},{9,8},{10,11... | collective-permute-start | bytes 264200 | tf_op jit(solution)/shard_map/ppermute | solution.py:535
  15.0 4.7 %collective-permute-start.6 = (f32[43,4,128]{2,1,0:T(4,128)S(1)}, f32[43,4,128]{2,1,0:T(4,128)S(1)}, u32[]{:S(2)}, u32[]{:S(2)}) collective-permute-start(f32[43,4,128]{2,1,0:T(4,128)S(1)} %get-tuple-element.54), channel_id=1, source_target_pairs={{1,2},{2,1},{5,6},{6,5},{9,10},{10,9},{13,14},{14,13},{17,18},{18,... | collective-permute-start | bytes 264200 | tf_op jit(solution)/shard_map/ppermute | solution.py:535
  15.7 4.7 %collective-permute-start.7 = (f32[15,4,128]{2,1,0:T(4,128)S(1)}, f32[15,4,128]{2,1,0:T(4,128)S(1)}, u32[]{:S(2)}, u32[]{:S(2)}) collective-permute-start(f32[15,4,128]{2,1,0:T(4,128)S(1)} %get-tuple-element.57), channel_id=1, source_target_pairs={{0,1},{1,0},{2,3},{3,2},{4,5},{5,4},{6,7},{7,6},{8,9},{9,8},{10,11... | collective-permute-start | bytes 92168 | tf_op jit(solution)/shard_map/ppermute | solution.py:535
  17.9 2.5 %collective-permute-start.8 = (f32[15,4,128]{2,1,0:T(4,128)S(1)}, f32[15,4,128]{2,1,0:T(4,128)S(1)}, u32[]{:S(2)}, u32[]{:S(2)}) collective-permute-start(f32[15,4,128]{2,1,0:T(4,128)S(1)} %get-tuple-element.58), channel_id=1, source_target_pairs={{1,2},{2,1},{5,6},{6,5},{9,10},{10,9},{13,14},{14,13},{17,18},{18,... | collective-permute-start | bytes 92168 | tf_op jit(solution)/shard_map/ppermute | solution.py:535
  29.8 3.5 %collective-permute-start.9 = (f32[8,128]{1,0:T(8,128)S(1)}, f32[8,128]{1,0:T(8,128)S(1)}, u32[]{:S(2)}, u32[]{:S(2)}) collective-permute-start(f32[8,128]{1,0:T(8,128)S(1)} %get-tuple-element.63), channel_id=1, source_target_pairs={{0,1},{1,0},{2,3},{3,2},{4,5},{5,4},{6,7},{7,6},{8,9},{9,8},{10,11... | collective-permute-start | bytes 12296 | tf_op jit(solution)/shard_map/ppermute | solution.py:546
  33.4 4.5 %collective-permute-start.12 = (f32[8,128]{1,0:T(8,128)S(1)}, f32[8,128]{1,0:T(8,128)S(1)}, u32[]{:S(2)}, u32[]{:S(2)}) collective-permute-start(f32[8,128]{1,0:T(8,128)S(1)} %add.21), channel_id=1, source_target_pairs={{0,6},{1,7},{2,4},{3,5},{4,2},{5,3},{6,0},{7,1},{8,14},{9,15},{10,... | collective-permute-start | bytes 12296 | tf_op jit(solution)/shard_map/ppermute | solution.py:546
  35.1 3.6 %collective-permute-start.11 = (f32[8,128]{1,0:T(8,128)S(1)}, f32[8,128]{1,0:T(8,128)S(1)}, u32[]{:S(2)}, u32[]{:S(2)}) collective-permute-start(f32[8,128]{1,0:T(8,128)S(1)} %add.21), channel_id=1, source_target_pairs={{0,4},{1,5},{2,6},{3,7},{4,0},{5,1},{6,2},{7,3},{8,12},{9,13},{10,... | collective-permute-start | bytes 12296 | tf_op jit(solution)/shard_map/ppermute | solution.py:546
  36.0 3.6 %collective-permute-start.10 = (f32[8,128]{1,0:T(8,128)S(1)}, f32[8,128]{1,0:T(8,128)S(1)}, u32[]{:S(2)}, u32[]{:S(2)}) collective-permute-start(f32[8,128]{1,0:T(8,128)S(1)} %add.21), channel_id=1, source_target_pairs={{0,2},{1,3},{2,0},{3,1},{4,6},{5,7},{6,4},{7,5},{8,10},{9,11},{10,... | collective-permute-start | bytes 12296 | tf_op jit(solution)/shard_map/ppermute | solution.py:546
  39.6 5.8 %collective-permute-start.15 = (f32[8,128]{1,0:T(8,128)S(1)}, f32[8,128]{1,0:T(8,128)S(1)}, u32[]{:S(2)}, u32[]{:S(2)}) collective-permute-start(f32[8,128]{1,0:T(8,128)S(1)} %add_add_fusion.1), channel_id=1, source_target_pairs={{0,24},{1,25},{2,26},{3,27},{4,28},{5,29},{6,30},{7,31},{8,16},{9,... | collective-permute-start | bytes 12296 | tf_op jit(solution)/shard_map/ppermute | solution.py:546
  42.1 5.0 %collective-permute-start.14 = (f32[8,128]{1,0:T(8,128)S(1)}, f32[8,128]{1,0:T(8,128)S(1)}, u32[]{:S(2)}, u32[]{:S(2)}) collective-permute-start(f32[8,128]{1,0:T(8,128)S(1)} %add_add_fusion.1), channel_id=1, source_target_pairs={{0,16},{1,17},{2,18},{3,19},{4,20},{5,21},{6,22},{7,23},{8,24},{9,... | collective-permute-start | bytes 12296 | tf_op jit(solution)/shard_map/ppermute | solution.py:546
  45.4 3.6 %collective-permute-start.13 = (f32[8,128]{1,0:T(8,128)S(1)}, f32[8,128]{1,0:T(8,128)S(1)}, u32[]{:S(2)}, u32[]{:S(2)}) collective-permute-start(f32[8,128]{1,0:T(8,128)S(1)} %add_add_fusion.1), channel_id=1, source_target_pairs={{0,8},{1,9},{2,10},{3,11},{4,12},{5,13},{6,14},{7,15},{8,0},{9,1},... | collective-permute-start | bytes 12296 | tf_op jit(solution)/shard_map/ppermute | solution.py:546

commit v11 on v10

--- a/solution.py
+++ b/solution.py
@@ -107,7 +107,7 @@
 
 
 def pack_kernel(
-    vx_hbm, vz_hbm, vy_hbm, p_hbm, phase_hbm, edge_hbm, x_0_hbm, x_1_hbm, stack_hbm,
+    vx_hbm, vz_hbm, vy_hbm, p_hbm, phase_hbm, scale_ref, power_ref, rho_ref, edge_hbm, x_0_hbm, x_1_hbm, stack_hbm,
     field_ref, phase_ref, edge_ref, stack_ref, sems, out_sems,
 ):
     bx, bz, by = phase_ref.shape
@@ -136,6 +136,17 @@
         at = pl.ds(g * GROUP, GROUP)
         edge_ref[at] = edge
         out(edge_ref.at[at], edge_hbm.at[at])
+        stack_ref[pl.ds(bx * FIELDS + g * GROUP, GROUP)] = edge
+    count = bx * FIELDS + bx // 2
+    row = iota((bz, by), 0)
+    entries = [ref[index] for ref in (scale_ref, power_ref, rho_ref) for index in range(PHASES)]
+    for n in range(2):
+        tile = jnp.zeros((bz, by), jnp.float32)
+        for r, entry in enumerate(entries[n * bz : (n + 1) * bz]):
+            tile = jnp.where(row == r, entry, tile)
+        stack_ref[count + n] = tile
+    at = pl.ds(bx * FIELDS, count + 2 - bx * FIELDS)
+    out(stack_ref.at[at], stack_hbm.at[at])
     count = x_0_hbm.shape[0]
     down, up = stack_ref.at[pl.ds(0, count)], stack_ref.at[pl.ds(bx * FIELDS - count, count)]
     sem = out_sems.at[len(outs)], out_sems.at[len(outs) + 1]
@@ -181,7 +192,7 @@
             ref[at + i // half, i % half : i % half + 1, :] = tiles[i, half : half + 1, :]
 
 
-def sides_kernel(x_0_ref, x_1_ref, _edge_ref, sides_ref, z_0_ref, z_1_ref):
+def sides_kernel(x_0_ref, x_1_ref, edge_ref, sides_ref, z_0_ref, z_1_ref):
     count = DEPTH * FIELDS
     bz, by = sides_ref.shape[1:]
 
@@ -192,23 +203,21 @@
 
     by_parity("gx", (x_0_ref, x_1_ref), body)
     tiles = sides_ref[...]
-    for swap, ref in enumerate((z_0_ref, z_1_ref)):
-        ref[0 : 2 * count + 1] = half_rows(tiles, swap)
     vz = tiles[0 : 2 * count].reshape(2 * DEPTH, FIELDS, bz, by)[:, 1]
-    store_next_rows((z_0_ref, z_1_ref), 2 * count + 1, vz)
-
-
-def edge_rows_kernel(edge_ref, z_0_ref, z_1_ref):
-    tiles = edge_ref[...]
-    for swap, ref in enumerate((z_0_ref, z_1_ref)):
-        ref[0 : tiles.shape[0]] = half_rows(tiles, swap)
-    store_next_rows((z_0_ref, z_1_ref), tiles.shape[0], tiles)
+    at = 0
+    for whole, after in ((tiles, vz), (edge_ref[...], edge_ref[...])):
+        for swap, ref in enumerate((z_0_ref, z_1_ref)):
+            ref[at : at + whole.shape[0]] = half_rows(whole, swap)
+        at += whole.shape[0]
+        store_next_rows((z_0_ref, z_1_ref), at, after)
+        at += after.shape[0] // (bz // 2)
 
 
 def lookups(fields, ok, keep, table_ref):
     *rest, phase = fields
     for number in range(3):
-        table = [table_ref[number * PHASES + index] for index in range(PHASES)]
+        rows = [divmod(number * PHASES + index, table_ref.shape[1]) for index in range(PHASES)]
+        table = [table_ref[n, r : r + 1, :] for n, r in rows]
         value = jnp.broadcast_to(table[0], phase.shape)
         for index in range(1, PHASES):
             value = jnp.where(phase == float(index), table[index], value)
@@ -288,10 +297,11 @@
     vx_ref[pl.ds(bx + 2 * DEPTH, 1), :, by : 2 * by] = beside(edge[0:1], FIELDS, 0)
 
 
-def own_kernel(stack_ref, edge_in_ref, tables_ref, z_0_ref, z_1_ref, edge_ref, v_ref, *rest):
-    edge_ref[...] = edge_in_ref[...]
-    count = stack_ref.shape[0]
-    bx = count // FIELDS
+def own_kernel(stack_ref, z_0_ref, z_1_ref, edge_ref, tables_ref, v_ref, *rest):
+    bx = v_ref.shape[1] - 2 * DEPTH - 1
+    count = bx * FIELDS
+    edge_ref[...] = stack_ref[count : count + bx // 2]
+    tables_ref[...] = stack_ref[count + bx // 2 :]
     size = GROUP * FIELDS
 
     def group(g, carry):
@@ -329,43 +339,40 @@
     return lambda at, n: jnp.concatenate([above[pl.ds(at, n)], below[pl.ds(at, n)]], axis=1)
 
 
-def halo_kernel(face_0_ref, face_1_ref, corner_0_ref, corner_1_ref, tables_ref, halo_ref, next_ref):
+def halo_kernel(face_0_ref, face_1_ref, tables_ref, halo_ref, next_ref):
     half, by = face_0_ref.shape[1:]
-    bz = 2 * half
     bx = halo_ref.shape[1] - 2 * DEPTH - 1
-    ok = rows_in_grid(bz)
     store = store_to([halo_ref.at[n] for n in range(7)])
 
-    def faces(above, below):
-        unpack_own(load_both(above, below), bx, ok, tables_ref, store)
+    def body(above, below):
+        unpack_own(load_both(above, below), bx, rows_in_grid(2 * half), tables_ref, store)
         for i in range(bx):
             n = i % half
             next_ref[DEPTH + i, half - 1 : half, 0:by] = above[bx * FIELDS + i // half, n : n + 1, :]
 
-    def corners(above, below):
+    by_parity("gz", (face_0_ref, face_1_ref), body)
+
+
+def unpack_corners(corner_0_ref, corner_1_ref, tables_ref, halo_ref, next_ref):
+    half, by = corner_0_ref.shape[1:]
+    bx = halo_ref.shape[1] - 2 * DEPTH - 1
+    ok = rows_in_grid(2 * half)
+    store = store_to([halo_ref.at[n] for n in range(7)])
+    fields = 2 * DEPTH * FIELDS + 1
+    edges = fields + 2 * DEPTH // half
+    tiles = bx // 2 + DEPTH
+
+    def body(above, below):
         unpack_sides(load_both(above, below), bx, ok, tables_ref, store, halo_ref.at[0])
         for i in range(2 * DEPTH):
             n = i % half
             to = DEPTH + bx + i if i < DEPTH else i - DEPTH
-            next_ref[to, half - 1 : half, 0:by] = above[2 * DEPTH * FIELDS + 1 + i // half, n : n + 1, :]
-
-    by_parity("gz", (face_0_ref, face_1_ref), faces)
-    by_parity("gz", (corner_0_ref, corner_1_ref), corners)
-
-
-def unpack_halo_edges(edge_0_ref, edge_1_ref, tables_ref, halo_ref, next_ref):
-    half, by = edge_0_ref.shape[1:]
-    bx = halo_ref.shape[1] - 2 * DEPTH - 1
-    ok = rows_in_grid(2 * half)
-    store = store_to([halo_ref.at[n] for n in range(7)])
-    tiles = bx // 2 + DEPTH
-
-    def body(above, below):
-        load = load_both(above, below)
+            next_ref[to, half - 1 : half, 0:by] = above[fields + i // half, n : n + 1, :]
+        load = load_both(above.at[pl.ds(edges, tiles)], below.at[pl.ds(edges, tiles)])
         unpack_own_edges(load, bx, ok, tables_ref, store)
         unpack_side_edges(load, bx, ok, tables_ref, store, halo_ref.at[0])
         for n in range(tiles // half):
-            rows = above[tiles + n]
+            rows = above[edges + tiles + n]
             for upper in range(2):
                 values = beside(rows, 1, upper)
                 for i in range(half):
@@ -376,11 +383,11 @@
                         to = tile - bx // 2 + (0 if upper else DEPTH + bx)
                     next_ref[to, half - 1 : half, by : 2 * by] = values[i : i + 1]
 
-    by_parity("gz", (edge_0_ref, edge_1_ref), body)
+    by_parity("gz", (corner_0_ref, corner_1_ref), body)
 
 
 def main_kernel(
-    v_ref, p0_ref, pre_ref, power_field_ref, rho_ref, _halo, _next, edge_0_ref, edge_1_ref, tables_ref,
+    v_ref, p0_ref, pre_ref, power_field_ref, rho_ref, _halo, _next, corner_0_ref, corner_1_ref, tables_ref,
     out_vx_ref, out_vz_ref, out_vy_ref, out_p_ref, out_eta_ref, sum_ref, halo_ref, next_ref,
     va_ref, vb_ref, p_ref, weight_ref,
 ):
@@ -388,7 +395,7 @@
     rows, lanes = 2 * bz, 2 * by
     nx, nz, ny = lax.axis_size("gx"), lax.axis_size("gz"), lax.axis_size("gy")
     ix, iz, iy = lax.axis_index("gx"), lax.axis_index("gz"), lax.axis_index("gy")
-    unpack_halo_edges(edge_0_ref, edge_1_ref, tables_ref, halo_ref, next_ref)
+    unpack_corners(corner_0_ref, corner_1_ref, tables_ref, halo_ref, next_ref)
 
     shape = (rows, lanes)
     r, c = iota(shape, 0), iota(shape, 1)
@@ -559,25 +566,24 @@
     block = shape(bx, bz, by)
     scratch = lambda *dims: pltpu.VMEM(dims, f32)
     limit = lambda mebibytes: pltpu.CompilerParams(vmem_limit_bytes=mebibytes * 1024 * 1024)
-    tables = jnp.concatenate([visc_scale, power_n, density])
-
     groups = bx // GROUP
+    stacked = bx * FIELDS + bx // 2 + 2
     sent = shape(DEPTH * FIELDS + 1, bz, by)
     edge, x_0, x_1, stack = pl.pallas_call(
         pack_kernel,
-        out_shape=(shape(bx // 2, bz, by), sent, sent, shape(bx * FIELDS, bz, by)),
-        in_specs=[HBM] * 5,
+        out_shape=(shape(bx // 2, bz, by), sent, sent, shape(stacked, bz, by)),
+        in_specs=[HBM] * 5 + [SMEM] * 3,
         out_specs=(HBM,) * 4,
         scratch_shapes=[
             scratch(FIELDS - 1, bx, bz, by),
             pltpu.VMEM((bx, bz, by), jnp.int32),
             scratch(bx // 2, bz, by),
-            scratch(bx * FIELDS, bz, by),
+            scratch(stacked, bz, by),
             pltpu.SemaphoreType.DMA((groups, FIELDS)),
-            pltpu.SemaphoreType.DMA((groups + groups // 2 + 2,)),
+            pltpu.SemaphoreType.DMA((groups + groups // 2 + 3,)),
         ],
         compiler_params=limit(58),
-    )(vel_x, vel_z, vel_y, pressure, phase)
+    )(vel_x, vel_z, vel_y, pressure, phase, visc_scale, power_n, density)
 
     def edges_beside(edge):
         side = swap(edge, "gy", 0)
@@ -589,13 +595,12 @@
     estimate = lambda size: pl.CostEstimate(
         flops=4 * size * bz * by, bytes_accessed=size * bz * by * 4, transcendentals=0
     )
-    long = estimate(100000)
 
     def unpacking(kernel, tiles, out_shape, *args, aliases={}):
         return pl.pallas_call(
             kernel,
             out_shape=out_shape,
-            in_specs=[VMEM if a is not tables else SMEM for a in args],
+            in_specs=[VMEM] * len(args),
             out_specs=(VMEM,) * len(out_shape),
             input_output_aliases=aliases,
             compiler_params=limit(16),
@@ -607,7 +612,8 @@
     half = lambda tiles, planes: shape(tiles + planes // (bz // 2), bz // 2, by)
     x_0, x_1 = swap(x_0, "gx", 0), swap(x_1, "gx", 1)
     face = half(bx * FIELDS, bx)
-    z_0, z_1, edge, *own = unpacking(own_kernel, bx, (face, face, shape(*edge.shape)) + own_shape, stack, edge, tables)
+    extra = (shape(bx // 2, bz, by), shape(2, bz, by))
+    z_0, z_1, edge, tables, *own = unpacking(own_kernel, bx, (face, face) + extra + own_shape, stack)
     face_1, face_0 = swap(z_1, "gz", 1), swap(z_0, "gz", 0)
 
     tiles = bx // 2 + DEPTH
@@ -618,7 +624,8 @@
         out_specs=VMEM,
         compiler_params=limit(4),
     )(x_0, x_1, edge)
-    corner = half(2 * DEPTH * FIELDS + 1, 2 * DEPTH)
+    edge = edges_beside(edge)
+    corner = half(2 * DEPTH * FIELDS + 1 + tiles, 2 * DEPTH + tiles)
     sides, z_0, z_1 = pl.pallas_call(
         sides_kernel,
         out_shape=(shape(2 * DEPTH * FIELDS + 1, bz, by), corner, corner),
@@ -626,28 +633,16 @@
         out_specs=(VMEM,) * 3,
         compiler_params=limit(4),
     )(x_0, x_1, edge)
-    edge = edges_beside(edge)
     corner_1, corner_0 = swap(z_1, "gz", 1), swap(z_0, "gz", 0)
-    z_0, z_1 = pl.pallas_call(
-        edge_rows_kernel,
-        out_shape=(half(tiles, tiles),) * 2,
-        in_specs=[VMEM],
-        out_specs=(VMEM,) * 2,
-        compiler_params=limit(4),
-        cost_estimate=long,
-    )(edge)
-    edge_1, edge_0 = swap(z_1, "gz", 1), swap(z_0, "gz", 0)
 
     own = unpacking(
         own_sides_kernel, 2 * deep, own_shape, sides, edge, tables, *own, aliases={n + 3: n for n in range(5)}
     )
-    halo = unpacking(
-        halo_kernel, deep, (shape(7, deep, bz, lanes), field), face_0, face_1, corner_0, corner_1, tables
-    )
+    halo = unpacking(halo_kernel, deep, (shape(7, deep, bz, lanes), field), face_0, face_1, tables)
     vx, vz, vy, p, eta, total, _, _ = pl.pallas_call(
         main_kernel,
         out_shape=(block,) * 5 + (shape(bz, by),) + tuple(shape(*a.shape) for a in halo),
-        in_specs=[VMEM] * 9 + [SMEM],
+        in_specs=[VMEM] * 10,
         out_specs=(VMEM,) * 8,
         input_output_aliases={5: 6, 6: 7},
         scratch_shapes=[
@@ -657,7 +652,7 @@
             scratch(4, rows, lanes),
         ],
         compiler_params=limit(32),
-    )(*own, *halo, edge_0, edge_1, tables)
+    )(*own, *halo, corner_0, corner_1, tables)
 
     total = sum_everywhere(total)
     p = pl.pallas_call(

time: 50.1 us -> 48.8 us (0.974)
  waiting for transfers between devices: 7.14 us -> 10.3 us
  Pallas kernels: 15.1 us -> 13.6 us
  starting transfers between devices: 24.2 us -> 22.8 us
  other arithmetic: 0.78 us -> 0.01 us
  local copies, waits for them, and re-layouts: 1.73 us -> 0.98 us
    ppermute x9 -> x7, starting transfers between devices: 12.2 us -> 8.76 us  [swap(): lax.ppermute(a, axis, [(i, j) for k in range(start, count - 1, 2) for i,...]
    ppermute x9 -> x7, waiting for transfers between devices: 0.02 us -> 2.36 us  [swap(): lax.ppermute(a, axis, [(i, j) for k in range(start, count - 1, 2) for i,...]
    ppermute x7, starting transfers between devices: 12 us -> 14.1 us  [sum_everywhere(): lax.ppermute(total, axes, [(i, i ^ m) for i in range(devices)])]
    pallas_call x4 -> x3, Pallas kernels: 2.55 us -> 0.86 us  [unpacking(): pl.pallas_call(kernel, out_shape=out_shape, in_specs=[VMEM] * len(args),...]
    ppermute x7, waiting for transfers between devices: 7.11 us -> 7.97 us  [sum_everywhere(): lax.ppermute(total, axes, [(i, i ^ m) for i in range(devices)])]
    concatenate x1 -> x0, other arithmetic: 0.77 us -> none  [local(): tables = jnp.concatenate([visc_scale, power_n, density])]
    unnamed x4 -> x2, local copies, waits for them, and re-layouts: 1.73 us -> 0.98 us
    pallas_call x1, Pallas kernels: 2.18 us -> 2.87 us  [local(): pl.pallas_call(pack_kernel, out_shape=(shape(bx // 2, bz, by), sent, sent...]
  transfers between devices with their start and end apart: 16 -> 14, of which waited for: 6 -> 8; matrix products, arithmetic and copies ran while one was open for 2% -> 0% of each run, Pallas kernels for 6% -> 2%
where the time goes in v11:
time: 48.8 us; the launch traced here: 48.5 us
  starting transfers between devices  22.8 us (47%)
  Pallas kernels  13.6 us (28%)
  waiting for transfers between devices  10.3 us (21%)
  local copies, waits for them, and re-layouts  0.98 us (2%)
  between operations  0.76 us (2%)
    ppermute x7, starting transfers between devices, sum_everywhere(): lax.ppermute(total, axes, [(i, i ^ m) for i in range(devices)])  14.1 us
    pallas_call x1, Pallas kernels, local(): pl.pallas_call(main_kernel, out_shape=(block,) * 5 + (shape(bz, by),) + t...  8.86 us
    ppermute x7, starting transfers between devices, swap(): lax.ppermute(a, axis, [(i, j) for k in range(start, count - 1, 2) for i,...  8.76 us
    ppermute x7, waiting for transfers between devices, sum_everywhere(): lax.ppermute(total, axes, [(i, i ^ m) for i in range(devices)])  7.97 us
    pallas_call x1, Pallas kernels, local(): pl.pallas_call(pack_kernel, out_shape=(shape(bx // 2, bz, by), sent, sent...  2.87 us
    ppermute x7, waiting for transfers between devices, swap(): lax.ppermute(a, axis, [(i, j) for k in range(start, count - 1, 2) for i,...  2.36 us
    unnamed x2, local copies, waits for them, and re-layouts  0.98 us
  transfers between devices with their start and end apart: 14, of which 8 were waited for; matrix products, arithmetic and copies ran while one was open for 0% of the time, Pallas kernels for 2%

profile of v11, /device:TPU:0, one launch (start us, length us, event | category | flops | bytes accessed | tf_op | source)
XLA Modules:
  0.0 48.5 jit_solution(10680918681450520402)
XLA Ops:
  0.6 2.9 %shard_map.119 = (f32[8,8,128]{2,1,0:T(8,128)}, f32[21,8,128]{2,1,0:T(8,128)}, f32[21,8,128]{2,1,0:T(8,128)}, f32[90,8,128]{2,1,0:T(8,128)}) custom-call(f32[16,8,128]{2,1,0:T(8,128)} %vx_hbm.1, f32[16,8,128]{2,1,0:T(8,128)} %vz_hbm.1, f32[16,8,128]{2,1,0:T(8,128)} %vy_hbm.1, f32[16,8,128]{2,1,0:T(8,128)} %p_hbm.1, s32[16,8,128]{2,1,0:T(8,128)} %phase_hbm.1, ...), custom_call_target="tpu_custom_call" | custom-call | tf_op jit(solution)/shard_map/pallas_call | solution.py:572
  3.5 3.1 %collective-permute-start = (f32[21,8,128]{2,1,0:T(8,128)}, f32[21,8,128]{2,1,0:T(8,128)S(1)}, u32[]{:S(2)}, u32[]{:S(2)}) collective-permute-start(f32[21,8,128]{2,1,0:T(8,128)} %get-tuple-element.33), channel_id=1, source_target_pairs={{0,8},{8,0},{16,24},{24,16},{1,9},{9,1},{17,25},{25,17},{2,10},{10... | collective-permute-start | bytes 258056 | tf_op jit(solution)/shard_map/ppermute | solution.py:542
  6.6 0.7 %collective-permute-start.1 = (f32[21,8,128]{2,1,0:T(8,128)}, f32[21,8,128]{2,1,0:T(8,128)S(1)}, u32[]{:S(2)}, u32[]{:S(2)}) collective-permute-start(f32[21,8,128]{2,1,0:T(8,128)} %get-tuple-element.34), channel_id=1, source_target_pairs={{8,16},{16,8},{9,17},{17,9},{10,18},{18,10},{11,19},{19,11},{12,20... | collective-permute-start | bytes 258056 | tf_op jit(solution)/shard_map/ppermute | solution.py:542
  7.3 1.0 %copy-done = f32[90,8,128]{2,1,0:T(8,128)S(1)} copy-done((f32[90,8,128]{2,1,0:T(8,128)S(1)}, f32[90,8,128]{2,1,0:T(8,128)}, u32[]{:S(2)}) %copy-start) | copy-done | bytes 368664
  8.2 0.2 shard_map.120
  8.5 0.7 %collective-permute-start.4 = (f32[84,4,128]{2,1,0:T(4,128)S(1)}, f32[84,4,128]{2,1,0:T(4,128)S(1)}, u32[]{:S(2)}, u32[]{:S(2)}) collective-permute-start(f32[84,4,128]{2,1,0:T(4,128)S(1)} %get-tuple-element.50), channel_id=1, source_target_pairs={{1,2},{2,1},{5,6},{6,5},{9,10},{10,9},{13,14},{14,13},{17,18},{18,... | collective-permute-start | bytes 516104 | tf_op jit(solution)/shard_map/ppermute | solution.py:542
  9.5 1.9 %collective-permute-start.2 = (f32[12,8,128]{2,1,0:T(8,128)S(1)}, f32[12,8,128]{2,1,0:T(8,128)S(1)}, u32[]{:S(2)}, u32[]{:S(2)}) collective-permute-start(f32[12,8,128]{2,1,0:T(8,128)S(1)} %shard_map.121), channel_id=1, source_target_pairs={{0,4},{4,0},{1,5},{5,1},{2,6},{6,2},{3,7},{7,3},{8,12},{12,8},{9,1... | collective-permute-start | bytes 147464 | tf_op jit(solution)/shard_map/ppermute | solution.py:542
  11.4 2.2 %collective-permute-done.2.edge_ref = f32[12,8,128]{2,1,0:T(8,128)S(1)} collective-permute-done((f32[12,8,128]{2,1,0:T(8,128)S(1)}, f32[12,8,128]{2,1,0:T(8,128)S(1)}, u32[]{:S(2)}, u32[]{:S(2)}) %collective-permute-start.2) | collective-permute-done | bytes 49184 | tf_op jit(solution)/shard_map/ppermute | solution.py:542
  13.7 1.7 %collective-permute-start.5 = (f32[58,4,128]{2,1,0:T(4,128)S(1)}, f32[58,4,128]{2,1,0:T(4,128)S(1)}, u32[]{:S(2)}, u32[]{:S(2)}) collective-permute-start(f32[58,4,128]{2,1,0:T(4,128)S(1)} %get-tuple-element.53), channel_id=1, source_target_pairs={{0,1},{1,0},{2,3},{3,2},{4,5},{5,4},{6,7},{7,6},{8,9},{9,8},{10,11... | collective-permute-start | bytes 356360 | tf_op jit(solution)/shard_map/ppermute | solution.py:542
  15.4 0.7 %collective-permute-start.6 = (f32[58,4,128]{2,1,0:T(4,128)S(1)}, f32[58,4,128]{2,1,0:T(4,128)S(1)}, u32[]{:S(2)}, u32[]{:S(2)}) collective-permute-start(f32[58,4,128]{2,1,0:T(4,128)S(1)} %get-tuple-element.54), channel_id=1, source_target_pairs={{1,2},{2,1},{5,6},{6,5},{9,10},{10,9},{13,14},{14,13},{17,18},{18,... | collective-permute-start | bytes 356360 | tf_op jit(solution)/shard_map/ppermute | solution.py:542
  16.1 0.5 %shard_map.123 = (f32[3,25,8,256]{3,2,1,0:T(8,128)S(1)}, f32[25,8,256]{2,1,0:T(8,128)S(1)}, f32[25,8,256]{2,1,0:T(8,128)S(1)}, f32[25,8,256]{2,1,0:T(8,128)S(1)}, f32[25,8,256]{2,1,0:T(8,128)S(1)}) custom-call(f32[41,8,128]{2,1,0:T(8,128)S(1)} %get-tuple-element.37.sides_ref, ...), custom_call_target="tpu_custom_call", output_to_operand_aliasing={{0}: (3, {}), {1}: (4, {}), {2}: (5, {}), {3}: (6, {}), {4}... | custom-call | flops 2662400 | bytes 2662400 | tf_op jit(solution)/shard_map/pallas_call | solution.py:600
  16.8 8.9 %shard_map.125 = (f32[16,8,128]{2,1,0:T(8,128)}, f32[16,8,128]{2,1,0:T(8,128)}, f32[16,8,128]{2,1,0:T(8,128)}, f32[16,8,128]{2,1,0:T(8,128)S(1)}, f32[16,8,128]{...) custom-call(f32[3,25,8,256]{3,2,1,0:T(8,128)S(1)} %get-tuple-element, ...), custom_call_target="tpu_custom_call", output_to_operand_aliasing={{6}: (5, {}), {7}: (6, {})} | custom-call | tf_op jit(solution)/shard_map/pallas_call | solution.py:642
  25.6 4.8 %collective-permute-start.7 = (f32[8,128]{1,0:T(8,128)S(1)}, f32[8,128]{1,0:T(8,128)S(1)}, u32[]{:S(2)}, u32[]{:S(2)}) collective-permute-start(f32[8,128]{1,0:T(8,128)S(1)} %get-tuple-element.59), channel_id=1, source_target_pairs={{0,1},{1,0},{2,3},{3,2},{4,5},{5,4},{6,7},{7,6},{8,9},{9,8},{10,11... | collective-permute-start | bytes 12296 | tf_op jit(solution)/shard_map/ppermute | solution.py:553
  30.4 0.8 %collective-permute-done.7 = f32[8,128]{1,0:T(8,128)S(1)} collective-permute-done((f32[8,128]{1,0:T(8,128)S(1)}, f32[8,128]{1,0:T(8,128)S(1)}, u32[]{:S(2)}, u32[]{:S(2)}) %collective-permute-start.7) | collective-permute-done | bytes 4128 | tf_op jit(solution)/shard_map/ppermute | solution.py:553
  31.2 2.9 %collective-permute-start.10 = (f32[8,128]{1,0:T(8,128)S(1)}, f32[8,128]{1,0:T(8,128)S(1)}, u32[]{:S(2)}, u32[]{:S(2)}) collective-permute-start(f32[8,128]{1,0:T(8,128)S(1)} %add.21), channel_id=1, source_target_pairs={{0,6},{1,7},{2,4},{3,5},{4,2},{5,3},{6,0},{7,1},{8,14},{9,15},{10,... | collective-permute-start | bytes 12296 | tf_op jit(solution)/shard_map/ppermute | solution.py:553
  34.1 0.5 %collective-permute-start.9 = (f32[8,128]{1,0:T(8,128)S(1)}, f32[8,128]{1,0:T(8,128)S(1)}, u32[]{:S(2)}, u32[]{:S(2)}) collective-permute-start(f32[8,128]{1,0:T(8,128)S(1)} %add.21), channel_id=1, source_target_pairs={{0,4},{1,5},{2,6},{3,7},{4,0},{5,1},{6,2},{7,3},{8,12},{9,13},{10,... | collective-permute-start | bytes 12296 | tf_op jit(solution)/shard_map/ppermute | solution.py:553
  34.7 1.0 %collective-permute-done.10 = f32[8,128]{1,0:T(8,128)S(1)} collective-permute-done((f32[8,128]{1,0:T(8,128)S(1)}, f32[8,128]{1,0:T(8,128)S(1)}, u32[]{:S(2)}, u32[]{:S(2)}) %collective-permute-start.10) | collective-permute-done | bytes 4128 | tf_op jit(solution)/shard_map/ppermute | solution.py:553
  35.8 2.0 %collective-permute-done.9 = f32[8,128]{1,0:T(8,128)S(1)} collective-permute-done((f32[8,128]{1,0:T(8,128)S(1)}, f32[8,128]{1,0:T(8,128)S(1)}, u32[]{:S(2)}, u32[]{:S(2)}) %collective-permute-start.9) | collective-permute-done | bytes 4128 | tf_op jit(solution)/shard_map/ppermute | solution.py:553
  37.7 0.5 %collective-permute-done.8 = f32[8,128]{1,0:T(8,128)S(1)} collective-permute-done((f32[8,128]{1,0:T(8,128)S(1)}, f32[8,128]{1,0:T(8,128)S(1)}, u32[]{:S(2)}, u32[]{:S(2)}) %collective-permute-start.8) | collective-permute-done | bytes 4128 | tf_op jit(solution)/shard_map/ppermute | solution.py:553
  38.3 2.5 %collective-permute-start.13 = (f32[8,128]{1,0:T(8,128)S(1)}, f32[8,128]{1,0:T(8,128)S(1)}, u32[]{:S(2)}, u32[]{:S(2)}) collective-permute-start(f32[8,128]{1,0:T(8,128)S(1)} %add_add_fusion.1), channel_id=1, source_target_pairs={{0,24},{1,25},{2,26},{3,27},{4,28},{5,29},{6,30},{7,31},{8,16},{9,... | collective-permute-start | bytes 12296 | tf_op jit(solution)/shard_map/ppermute | solution.py:553
  40.8 3.3 %collective-permute-start.12 = (f32[8,128]{1,0:T(8,128)S(1)}, f32[8,128]{1,0:T(8,128)S(1)}, u32[]{:S(2)}, u32[]{:S(2)}) collective-permute-start(f32[8,128]{1,0:T(8,128)S(1)} %add_add_fusion.1), channel_id=1, source_target_pairs={{0,16},{1,17},{2,18},{3,19},{4,20},{5,21},{6,22},{7,23},{8,24},{9,... | collective-permute-start | bytes 12296 | tf_op jit(solution)/shard_map/ppermute | solution.py:553
  44.1 1.6 %collective-permute-done.12 = f32[8,128]{1,0:T(8,128)S(1)} collective-permute-done((f32[8,128]{1,0:T(8,128)S(1)}, f32[8,128]{1,0:T(8,128)S(1)}, u32[]{:S(2)}, u32[]{:S(2)}) %collective-permute-start.12) | collective-permute-done | bytes 4128 | tf_op jit(solution)/shard_map/ppermute | solution.py:553
  45.7 2.0 %collective-permute-done.11 = f32[8,128]{1,0:T(8,128)S(1)} collective-permute-done((f32[8,128]{1,0:T(8,128)S(1)}, f32[8,128]{1,0:T(8,128)S(1)}, u32[]{:S(2)}, u32[]{:S(2)}) %collective-permute-start.11) | collective-permute-done | bytes 4128 | tf_op jit(solution)/shard_map/ppermute | solution.py:553
  47.7 0.8 %shard_map.126 = f32[16,8,128]{2,1,0:T(8,128)} custom-call(f32[16,8,128]{2,1,0:T(8,128)S(1)} %get-tuple-element.58.refs_0_, f32[8,128]{1,0:T(8,128)S(1)} %add_add_fusion.refs_1_), custom_call_target="tpu_custom_call" | custom-call | tf_op jit(solution)/shard_map/pallas_call | solution.py:658
  (17 shorter events, 0.7 us)
Async XLA Ops:
  3.5 5.8 %collective-permute-start = (f32[21,8,128]{2,1,0:T(8,128)}, f32[21,8,128]{2,1,0:T(8,128)S(1)}, u32[]{:S(2)}, u32[]{:S(2)}) collective-permute-start(f32[21,8,128]{2,1,0:T(8,128)} %get-tuple-element.33), channel_id=1, source_target_pairs={{0,8},{8,0},{16,24},{24,16},{1,9},{9,1},{17,25},{25,17},{2,10},{10... | collective-permute-start | bytes 258056 | tf_op jit(solution)/shard_map/ppermute | solution.py:542
  6.6 2.7 %collective-permute-start.1 = (f32[21,8,128]{2,1,0:T(8,128)}, f32[21,8,128]{2,1,0:T(8,128)S(1)}, u32[]{:S(2)}, u32[]{:S(2)}) collective-permute-start(f32[21,8,128]{2,1,0:T(8,128)} %get-tuple-element.34), channel_id=1, source_target_pairs={{8,16},{16,8},{9,17},{17,9},{10,18},{18,10},{11,19},{19,11},{12,20... | collective-permute-start | bytes 258056 | tf_op jit(solution)/shard_map/ppermute | solution.py:542
  7.3 1.0 %copy-start = (f32[90,8,128]{2,1,0:T(8,128)S(1)}, f32[90,8,128]{2,1,0:T(8,128)}, u32[]{:S(2)}) copy-start(f32[90,8,128]{2,1,0:T(8,128)} %get-tuple-element.35.stack_ref) | copy-start | bytes 1105924
  8.4 8.1 %collective-permute-start.3 = (f32[84,4,128]{2,1,0:T(4,128)S(1)}, f32[84,4,128]{2,1,0:T(4,128)S(1)}, u32[]{:S(2)}, u32[]{:S(2)}) collective-permute-start(f32[84,4,128]{2,1,0:T(4,128)S(1)} %get-tuple-element.49), channel_id=1, source_target_pairs={{0,1},{1,0},{2,3},{3,2},{4,5},{5,4},{6,7},{7,6},{8,9},{9,8},{10,11... | collective-permute-start | bytes 516104 | tf_op jit(solution)/shard_map/ppermute | solution.py:542
  8.5 8.1 %collective-permute-start.4 = (f32[84,4,128]{2,1,0:T(4,128)S(1)}, f32[84,4,128]{2,1,0:T(4,128)S(1)}, u32[]{:S(2)}, u32[]{:S(2)}) collective-permute-start(f32[84,4,128]{2,1,0:T(4,128)S(1)} %get-tuple-element.50), channel_id=1, source_target_pairs={{1,2},{2,1},{5,6},{6,5},{9,10},{10,9},{13,14},{14,13},{17,18},{18,... | collective-permute-start | bytes 516104 | tf_op jit(solution)/shard_map/ppermute | solution.py:542
  9.5 4.2 %collective-permute-start.2 = (f32[12,8,128]{2,1,0:T(8,128)S(1)}, f32[12,8,128]{2,1,0:T(8,128)S(1)}, u32[]{:S(2)}, u32[]{:S(2)}) collective-permute-start(f32[12,8,128]{2,1,0:T(8,128)S(1)} %shard_map.121), channel_id=1, source_target_pairs={{0,4},{4,0},{1,5},{5,1},{2,6},{6,2},{3,7},{7,3},{8,12},{12,8},{9,1... | collective-permute-start | bytes 147464 | tf_op jit(solution)/shard_map/ppermute | solution.py:542
  13.7 3.1 %collective-permute-start.5 = (f32[58,4,128]{2,1,0:T(4,128)S(1)}, f32[58,4,128]{2,1,0:T(4,128)S(1)}, u32[]{:S(2)}, u32[]{:S(2)}) collective-permute-start(f32[58,4,128]{2,1,0:T(4,128)S(1)} %get-tuple-element.53), channel_id=1, source_target_pairs={{0,1},{1,0},{2,3},{3,2},{4,5},{5,4},{6,7},{7,6},{8,9},{9,8},{10,11... | collective-permute-start | bytes 356360 | tf_op jit(solution)/shard_map/ppermute | solution.py:542
  15.4 1.4 %collective-permute-start.6 = (f32[58,4,128]{2,1,0:T(4,128)S(1)}, f32[58,4,128]{2,1,0:T(4,128)S(1)}, u32[]{:S(2)}, u32[]{:S(2)}) collective-permute-start(f32[58,4,128]{2,1,0:T(4,128)S(1)} %get-tuple-element.54), channel_id=1, source_target_pairs={{1,2},{2,1},{5,6},{6,5},{9,10},{10,9},{13,14},{14,13},{17,18},{18,... | collective-permute-start | bytes 356360 | tf_op jit(solution)/shard_map/ppermute | solution.py:542
  25.6 5.6 %collective-permute-start.7 = (f32[8,128]{1,0:T(8,128)S(1)}, f32[8,128]{1,0:T(8,128)S(1)}, u32[]{:S(2)}, u32[]{:S(2)}) collective-permute-start(f32[8,128]{1,0:T(8,128)S(1)} %get-tuple-element.59), channel_id=1, source_target_pairs={{0,1},{1,0},{2,3},{3,2},{4,5},{5,4},{6,7},{7,6},{8,9},{9,8},{10,11... | collective-permute-start | bytes 12296 | tf_op jit(solution)/shard_map/ppermute | solution.py:553
  31.2 4.5 %collective-permute-start.10 = (f32[8,128]{1,0:T(8,128)S(1)}, f32[8,128]{1,0:T(8,128)S(1)}, u32[]{:S(2)}, u32[]{:S(2)}) collective-permute-start(f32[8,128]{1,0:T(8,128)S(1)} %add.21), channel_id=1, source_target_pairs={{0,6},{1,7},{2,4},{3,5},{4,2},{5,3},{6,0},{7,1},{8,14},{9,15},{10,... | collective-permute-start | bytes 12296 | tf_op jit(solution)/shard_map/ppermute | solution.py:553
  34.1 3.6 %collective-permute-start.9 = (f32[8,128]{1,0:T(8,128)S(1)}, f32[8,128]{1,0:T(8,128)S(1)}, u32[]{:S(2)}, u32[]{:S(2)}) collective-permute-start(f32[8,128]{1,0:T(8,128)S(1)} %add.21), channel_id=1, source_target_pairs={{0,4},{1,5},{2,6},{3,7},{4,0},{5,1},{6,2},{7,3},{8,12},{9,13},{10,... | collective-permute-start | bytes 12296 | tf_op jit(solution)/shard_map/ppermute | solution.py:553
  34.7 3.6 %collective-permute-start.8 = (f32[8,128]{1,0:T(8,128)S(1)}, f32[8,128]{1,0:T(8,128)S(1)}, u32[]{:S(2)}, u32[]{:S(2)}) collective-permute-start(f32[8,128]{1,0:T(8,128)S(1)} %add.21), channel_id=1, source_target_pairs={{0,2},{1,3},{2,0},{3,1},{4,6},{5,7},{6,4},{7,5},{8,10},{9,11},{10,... | collective-permute-start | bytes 12296 | tf_op jit(solution)/shard_map/ppermute | solution.py:553
  38.3 5.8 %collective-permute-start.13 = (f32[8,128]{1,0:T(8,128)S(1)}, f32[8,128]{1,0:T(8,128)S(1)}, u32[]{:S(2)}, u32[]{:S(2)}) collective-permute-start(f32[8,128]{1,0:T(8,128)S(1)} %add_add_fusion.1), channel_id=1, source_target_pairs={{0,24},{1,25},{2,26},{3,27},{4,28},{5,29},{6,30},{7,31},{8,16},{9,... | collective-permute-start | bytes 12296 | tf_op jit(solution)/shard_map/ppermute | solution.py:553
  40.8 5.0 %collective-permute-start.12 = (f32[8,128]{1,0:T(8,128)S(1)}, f32[8,128]{1,0:T(8,128)S(1)}, u32[]{:S(2)}, u32[]{:S(2)}) collective-permute-start(f32[8,128]{1,0:T(8,128)S(1)} %add_add_fusion.1), channel_id=1, source_target_pairs={{0,16},{1,17},{2,18},{3,19},{4,20},{5,21},{6,22},{7,23},{8,24},{9,... | collective-permute-start | bytes 12296 | tf_op jit(solution)/shard_map/ppermute | solution.py:553
  44.1 3.6 %collective-permute-start.11 = (f32[8,128]{1,0:T(8,128)S(1)}, f32[8,128]{1,0:T(8,128)S(1)}, u32[]{:S(2)}, u32[]{:S(2)}) collective-permute-start(f32[8,128]{1,0:T(8,128)S(1)} %add_add_fusion.1), channel_id=1, source_target_pairs={{0,8},{1,9},{2,10},{3,11},{4,12},{5,13},{6,14},{7,15},{8,0},{9,1},... | collective-permute-start | bytes 12296 | tf_op jit(solution)/shard_map/ppermute | solution.py:553

commit v12 on v11

--- a/solution.py
+++ b/solution.py
@@ -542,18 +542,6 @@
     return lax.ppermute(a, axis, [(i, j) for k in range(start, count - 1, 2) for i, j in ((k, k + 1), (k + 1, k))])
 
 
-def sum_everywhere(total):
-    axes = ("gx", "gy", "gz")
-    devices = math.prod(lax.axis_size(a) for a in axes)
-    if devices & (devices - 1):
-        return lax.psum(total, axes)
-    bits = [1 << n for n in range(devices.bit_length() - 1)]
-    for stage in [bits[:1]] + [bits[n : n + 2] for n in range(1, len(bits), 2)]:
-        masks = stage if len(stage) == 1 else [stage[0], stage[1], stage[0] + stage[1]]
-        total = sum([lax.ppermute(total, axes, [(i, i ^ m) for i in range(devices)]) for m in masks], total)
-    return total
-
-
 def local(vel_x, vel_y, vel_z, pressure, phase, visc_scale, power_n, density):
     bx, bz, by = pressure.shape
     assert bx % (2 * GROUP) == 0 and bz == 2 * DEPTH and DEPTH == GROUP
@@ -654,7 +642,7 @@
         compiler_params=limit(32),
     )(*own, *halo, corner_0, corner_1, tables)
 
-    total = sum_everywhere(total)
+    total = lax.all_gather(jnp.sum(total, axis=0, keepdims=True), ("gx", "gy", "gz"), axis=0, tiled=True)
     p = pl.pallas_call(
         lambda *refs: final_kernel(*refs, cells=float(cells)),
         out_shape=block,

time: 48.8 us -> 72 us (1.48)
  blocking collectives: 0 us -> 45.3 us
  starting transfers between devices: 22.8 us -> 8.76 us
  waiting for transfers between devices: 10.3 us -> 2.36 us
    all_gather x0 -> x1, blocking collectives: none -> 45.3 us  [local(): lax.all_gather(jnp.sum(total, axis=0, keepdims=True), ('gx', 'gy', 'gz'),...]
    ppermute x7 -> x0, starting transfers between devices: 14.1 us -> none  [sum_everywhere(): lax.ppermute(total, axes, [(i, i ^ m) for i in range(devices)])]
    ppermute x7 -> x0, waiting for transfers between devices: 7.97 us -> none  [sum_everywhere(): lax.ppermute(total, axes, [(i, i ^ m) for i in range(devices)])]
  transfers between devices with their start and end apart: 14 -> 7, of which waited for: 8 -> 2; matrix products, arithmetic and copies ran while one was open for 0% -> 0% of each run, Pallas kernels for 2% -> 1%
where the time goes in v12:
time: 72 us; the launch traced here: 71.8 us
  blocking collectives  45.3 us (63%)
  Pallas kernels  13.5 us (19%)
  starting transfers between devices  8.76 us (12%)
  waiting for transfers between devices  2.36 us (3%)
  local copies, waits for them, and re-layouts  0.98 us (1%)
  between operations  0.75 us (1%)
    all_gather x1, blocking collectives, local(): lax.all_gather(jnp.sum(total, axis=0, keepdims=True), ('gx', 'gy', 'gz'),...  45.3 us
    pallas_call x1, Pallas kernels, local(): pl.pallas_call(main_kernel, out_shape=(block,) * 5 + (shape(bz, by),) + t...  8.86 us
    ppermute x7, starting transfers between devices, swap(): lax.ppermute(a, axis, [(i, j) for k in range(start, count - 1, 2) for i,...  8.76 us
    pallas_call x1, Pallas kernels, local(): pl.pallas_call(pack_kernel, out_shape=(shape(bx // 2, bz, by), sent, sent...  2.87 us
    ppermute x7, waiting for transfers between devices, swap(): lax.ppermute(a, axis, [(i, j) for k in range(start, count - 1, 2) for i,...  2.36 us
  transfers between devices with their start and end apart: 7, of which 2 were waited for; matrix products, arithmetic and copies ran while one was open for 0% of the time, Pallas kernels for 1%

profile of v12, /device:TPU:0, one launch (start us, length us, event | category | flops | bytes accessed | tf_op | source)
XLA Modules:
  0.0 71.8 jit_solution(16115627121478410854)
XLA Ops:
  0.6 2.9 %shard_map.119 = (f32[8,8,128]{2,1,0:T(8,128)}, f32[21,8,128]{2,1,0:T(8,128)}, f32[21,8,128]{2,1,0:T(8,128)}, f32[90,8,128]{2,1,0:T(8,128)}) custom-call(f32[16,8,128]{2,1,0:T(8,128)} %vx_hbm.1, f32[16,8,128]{2,1,0:T(8,128)} %vz_hbm.1, f32[16,8,128]{2,1,0:T(8,128)} %vy_hbm.1, f32[16,8,128]{2,1,0:T(8,128)} %p_hbm.1, s32[16,8,128]{2,1,0:T(8,128)} %phase_hbm.1, ...), custom_call_target="tpu_custom_call" | custom-call | tf_op jit(solution)/shard_map/pallas_call | solution.py:560
  3.5 3.1 %collective-permute-start = (f32[21,8,128]{2,1,0:T(8,128)}, f32[21,8,128]{2,1,0:T(8,128)S(1)}, u32[]{:S(2)}, u32[]{:S(2)}) collective-permute-start(f32[21,8,128]{2,1,0:T(8,128)} %get-tuple-element.33), channel_id=1, source_target_pairs={{0,8},{8,0},{16,24},{24,16},{1,9},{9,1},{17,25},{25,17},{2,10},{10... | collective-permute-start | bytes 258056 | tf_op jit(solution)/shard_map/ppermute | solution.py:542
  6.6 0.7 collective-permute-start.1
  7.3 1.0 %copy-done = f32[90,8,128]{2,1,0:T(8,128)S(1)} copy-done((f32[90,8,128]{2,1,0:T(8,128)S(1)}, f32[90,8,128]{2,1,0:T(8,128)}, u32[]{:S(2)}) %copy-start) | copy-done | bytes 368664
  8.2 0.2 shard_map.120
  8.4 0.1 collective-permute-start.3
  8.5 0.7 collective-permute-start.4
  9.2 0.1 collective-permute-done.x_0_ref
  9.3 0.0 collective-permute-done.1.x_1_ref
  9.3 0.1 shard_map.121
  9.5 1.9 %collective-permute-start.2 = (f32[12,8,128]{2,1,0:T(8,128)S(1)}, f32[12,8,128]{2,1,0:T(8,128)S(1)}, u32[]{:S(2)}, u32[]{:S(2)}) collective-permute-start(f32[12,8,128]{2,1,0:T(8,128)S(1)} %shard_map.121), channel_id=1, source_target_pairs={{0,4},{4,0},{1,5},{5,1},{2,6},{6,2},{3,7},{7,3},{8,12},{12,8},{9,1... | collective-permute-start | bytes 147464 | tf_op jit(solution)/shard_map/ppermute | solution.py:542
  11.4 2.2 %collective-permute-done.2.edge_ref = f32[12,8,128]{2,1,0:T(8,128)S(1)} collective-permute-done((f32[12,8,128]{2,1,0:T(8,128)S(1)}, f32[12,8,128]{2,1,0:T(8,128)S(1)}, u32[]{:S(2)}, u32[]{:S(2)}) %collective-permute-start.2) | collective-permute-done | bytes 49184 | tf_op jit(solution)/shard_map/ppermute | solution.py:542
  13.6 0.1 shard_map.122
  13.7 1.7 %collective-permute-start.5 = (f32[58,4,128]{2,1,0:T(4,128)S(1)}, f32[58,4,128]{2,1,0:T(4,128)S(1)}, u32[]{:S(2)}, u32[]{:S(2)}) collective-permute-start(f32[58,4,128]{2,1,0:T(4,128)S(1)} %get-tuple-element.53), channel_id=1, source_target_pairs={{0,1},{1,0},{2,3},{3,2},{4,5},{5,4},{6,7},{7,6},{8,9},{9,8},{10,11... | collective-permute-start | bytes 356360 | tf_op jit(solution)/shard_map/ppermute | solution.py:542
  15.4 0.7 collective-permute-start.6
  16.1 0.5 shard_map.123
  16.6 0.0 collective-permute-done.3.face_0_ref
  16.6 0.0 collective-permute-done.4.face_1_ref
  16.6 0.2 shard_map.124
  16.8 0.0 collective-permute-done.5.corner_0_ref
  16.8 0.0 collective-permute-done.6.corner_1_ref
  16.8 8.9 %shard_map.125 = (f32[16,8,128]{2,1,0:T(8,128)}, f32[16,8,128]{2,1,0:T(8,128)}, f32[16,8,128]{2,1,0:T(8,128)}, f32[16,8,128]{2,1,0:T(8,128)S(1)}, f32[16,8,128]{...) custom-call(f32[3,25,8,256]{3,2,1,0:T(8,128)S(1)} %get-tuple-element, ...), custom_call_target="tpu_custom_call", output_to_operand_aliasing={{6}: (5, {}), {7}: (6, {})} | custom-call | tf_op jit(solution)/shard_map/pallas_call | solution.py:630
  25.7 45.3 %all-gather.1 = f32[32,1,128]{2,1,0:T(1,128)S(1)} all-gather(f32[1,1,128]{2,1,0:T(1,128)S(1)} %bitcast.3), channel_id=2, replica_groups=mesh['gx'=4,'gy'=2,'gz'=4] {'gx','gy','gz'}, dimensions={0}, use_global_device_ids=true | all-gather | bytes 16896 | tf_op jit(solution)/shard_map/all_gather | solution.py:645
  71.0 0.8 %shard_map.126 = f32[16,8,128]{2,1,0:T(8,128)} custom-call(f32[16,8,128]{2,1,0:T(8,128)S(1)} %get-tuple-element.58.refs_0_, f32[32,128]{1,0:T(8,128)S(1)} %bitcast.2), custom_call_target="tpu_custom_call" | custom-call | tf_op jit(solution)/shard_map/pallas_call | solution.py:646
  (2 shorter events, 0.0 us)
Async XLA Ops:
  3.5 5.8 %collective-permute-start = (f32[21,8,128]{2,1,0:T(8,128)}, f32[21,8,128]{2,1,0:T(8,128)S(1)}, u32[]{:S(2)}, u32[]{:S(2)}) collective-permute-start(f32[21,8,128]{2,1,0:T(8,128)} %get-tuple-element.33), channel_id=1, source_target_pairs={{0,8},{8,0},{16,24},{24,16},{1,9},{9,1},{17,25},{25,17},{2,10},{10... | collective-permute-start | bytes 258056 | tf_op jit(solution)/shard_map/ppermute | solution.py:542
  6.6 2.7 %collective-permute-start.1 = (f32[21,8,128]{2,1,0:T(8,128)}, f32[21,8,128]{2,1,0:T(8,128)S(1)}, u32[]{:S(2)}, u32[]{:S(2)}) collective-permute-start(f32[21,8,128]{2,1,0:T(8,128)} %get-tuple-element.34), channel_id=1, source_target_pairs={{8,16},{16,8},{9,17},{17,9},{10,18},{18,10},{11,19},{19,11},{12,20... | collective-permute-start | bytes 258056 | tf_op jit(solution)/shard_map/ppermute | solution.py:542
  7.3 1.0 %copy-start = (f32[90,8,128]{2,1,0:T(8,128)S(1)}, f32[90,8,128]{2,1,0:T(8,128)}, u32[]{:S(2)}) copy-start(f32[90,8,128]{2,1,0:T(8,128)} %get-tuple-element.35.stack_ref) | copy-start | bytes 1105924
  8.4 8.1 %collective-permute-start.3 = (f32[84,4,128]{2,1,0:T(4,128)S(1)}, f32[84,4,128]{2,1,0:T(4,128)S(1)}, u32[]{:S(2)}, u32[]{:S(2)}) collective-permute-start(f32[84,4,128]{2,1,0:T(4,128)S(1)} %get-tuple-element.49), channel_id=1, source_target_pairs={{0,1},{1,0},{2,3},{3,2},{4,5},{5,4},{6,7},{7,6},{8,9},{9,8},{10,11... | collective-permute-start | bytes 516104 | tf_op jit(solution)/shard_map/ppermute | solution.py:542
  8.5 8.1 %collective-permute-start.4 = (f32[84,4,128]{2,1,0:T(4,128)S(1)}, f32[84,4,128]{2,1,0:T(4,128)S(1)}, u32[]{:S(2)}, u32[]{:S(2)}) collective-permute-start(f32[84,4,128]{2,1,0:T(4,128)S(1)} %get-tuple-element.50), channel_id=1, source_target_pairs={{1,2},{2,1},{5,6},{6,5},{9,10},{10,9},{13,14},{14,13},{17,18},{18,... | collective-permute-start | bytes 516104 | tf_op jit(solution)/shard_map/ppermute | solution.py:542
  9.5 4.2 %collective-permute-start.2 = (f32[12,8,128]{2,1,0:T(8,128)S(1)}, f32[12,8,128]{2,1,0:T(8,128)S(1)}, u32[]{:S(2)}, u32[]{:S(2)}) collective-permute-start(f32[12,8,128]{2,1,0:T(8,128)S(1)} %shard_map.121), channel_id=1, source_target_pairs={{0,4},{4,0},{1,5},{5,1},{2,6},{6,2},{3,7},{7,3},{8,12},{12,8},{9,1... | collective-permute-start | bytes 147464 | tf_op jit(solution)/shard_map/ppermute | solution.py:542
  13.7 3.1 %collective-permute-start.5 = (f32[58,4,128]{2,1,0:T(4,128)S(1)}, f32[58,4,128]{2,1,0:T(4,128)S(1)}, u32[]{:S(2)}, u32[]{:S(2)}) collective-permute-start(f32[58,4,128]{2,1,0:T(4,128)S(1)} %get-tuple-element.53), channel_id=1, source_target_pairs={{0,1},{1,0},{2,3},{3,2},{4,5},{5,4},{6,7},{7,6},{8,9},{9,8},{10,11... | collective-permute-start | bytes 356360 | tf_op jit(solution)/shard_map/ppermute | solution.py:542
  15.4 1.4 %collective-permute-start.6 = (f32[58,4,128]{2,1,0:T(4,128)S(1)}, f32[58,4,128]{2,1,0:T(4,128)S(1)}, u32[]{:S(2)}, u32[]{:S(2)}) collective-permute-start(f32[58,4,128]{2,1,0:T(4,128)S(1)} %get-tuple-element.54), channel_id=1, source_target_pairs={{1,2},{2,1},{5,6},{6,5},{9,10},{10,9},{13,14},{14,13},{17,18},{18,... | collective-permute-start | bytes 356360 | tf_op jit(solution)/shard_map/ppermute | solution.py:542

commit v13 on v10

--- a/solution.py
+++ b/solution.py
@@ -16,7 +16,6 @@
 GROUP = 4
 
 VMEM = pl.BlockSpec(memory_space=pltpu.VMEM)
-SMEM = pl.BlockSpec(memory_space=pltpu.SMEM)
 HBM = pl.BlockSpec(memory_space=pltpu.HBM)
 
 
@@ -107,12 +106,17 @@
 
 
 def pack_kernel(
-    vx_hbm, vz_hbm, vy_hbm, p_hbm, phase_hbm, edge_hbm, x_0_hbm, x_1_hbm, stack_hbm,
-    field_ref, phase_ref, edge_ref, stack_ref, sems, out_sems,
+    vx_hbm, vz_hbm, vy_hbm, p_hbm, phase_hbm, scale_hbm, power_hbm, rho_hbm, edge_hbm, x_0_hbm, x_1_hbm, stack_hbm,
+    field_ref, phase_ref, edge_ref, stack_ref, scale_ref, power_ref, rho_ref, sems, out_sems, table_sems,
 ):
     bx, bz, by = phase_ref.shape
     targets = [field_ref.at[f] for f in range(FIELDS - 1)] + [phase_ref]
     copies = start_copies((vx_hbm, vz_hbm, vy_hbm, p_hbm, phase_hbm), targets, sems)
+    table_refs = (scale_ref, power_ref, rho_ref)
+    pairs = zip((scale_hbm, power_hbm, rho_hbm), table_refs)
+    table_copies = [pltpu.make_async_copy(a, b, table_sems.at[n]) for n, (a, b) in enumerate(pairs)]
+    for copy in table_copies:
+        copy.start()
     half = bx // GROUP // 2
     outs = []
 
@@ -136,6 +140,19 @@
         at = pl.ds(g * GROUP, GROUP)
         edge_ref[at] = edge
         out(edge_ref.at[at], edge_hbm.at[at])
+        stack_ref[pl.ds(bx * FIELDS + g * GROUP, GROUP)] = edge
+    count = bx * FIELDS + bx // 2
+    row = iota((bz, by), 0)
+    for copy in table_copies:
+        copy.wait()
+    entries = [ref[index] for ref in table_refs for index in range(PHASES)]
+    for n in range(2):
+        tile = jnp.zeros((bz, by), jnp.float32)
+        for r, entry in enumerate(entries[n * bz : (n + 1) * bz]):
+            tile = jnp.where(row == r, entry, tile)
+        stack_ref[count + n] = tile
+    at = pl.ds(bx * FIELDS, count + 2 - bx * FIELDS)
+    out(stack_ref.at[at], stack_hbm.at[at])
     count = x_0_hbm.shape[0]
     down, up = stack_ref.at[pl.ds(0, count)], stack_ref.at[pl.ds(bx * FIELDS - count, count)]
     sem = out_sems.at[len(outs)], out_sems.at[len(outs) + 1]
@@ -208,7 +225,8 @@
 def lookups(fields, ok, keep, table_ref):
     *rest, phase = fields
     for number in range(3):
-        table = [table_ref[number * PHASES + index] for index in range(PHASES)]
+        rows = [divmod(number * PHASES + index, table_ref.shape[1]) for index in range(PHASES)]
+        table = [table_ref[n, r : r + 1, :] for n, r in rows]
         value = jnp.broadcast_to(table[0], phase.shape)
         for index in range(1, PHASES):
             value = jnp.where(phase == float(index), table[index], value)
@@ -288,10 +306,11 @@
     vx_ref[pl.ds(bx + 2 * DEPTH, 1), :, by : 2 * by] = beside(edge[0:1], FIELDS, 0)
 
 
-def own_kernel(stack_ref, edge_in_ref, tables_ref, z_0_ref, z_1_ref, edge_ref, v_ref, *rest):
-    edge_ref[...] = edge_in_ref[...]
-    count = stack_ref.shape[0]
-    bx = count // FIELDS
+def own_kernel(stack_ref, z_0_ref, z_1_ref, edge_ref, tables_ref, v_ref, *rest):
+    bx = v_ref.shape[1] - 2 * DEPTH - 1
+    count = bx * FIELDS
+    edge_ref[...] = stack_ref[count : count + bx // 2]
+    tables_ref[...] = stack_ref[count + bx // 2 :]
     size = GROUP * FIELDS
 
     def group(g, carry):
@@ -538,13 +557,10 @@
 def sum_everywhere(total):
     axes = ("gx", "gy", "gz")
     devices = math.prod(lax.axis_size(a) for a in axes)
-    if devices & (devices - 1):
-        return lax.psum(total, axes)
-    bits = [1 << n for n in range(devices.bit_length() - 1)]
-    for stage in [bits[:1]] + [bits[n : n + 2] for n in range(1, len(bits), 2)]:
-        masks = stage if len(stage) == 1 else [stage[0], stage[1], stage[0] + stage[1]]
-        total = sum([lax.ppermute(total, axes, [(i, i ^ m) for i in range(devices)]) for m in masks], total)
-    return total
+    total = total + lax.ppermute(total, axes, [(i, i ^ 1) for i in range(devices)])
+    total = jnp.broadcast_to(jnp.sum(total, axis=0, keepdims=True), (devices // 2, total.shape[1]))
+    groups = [list(range(n, devices, 2)) for n in range(2)]
+    return lax.all_to_all(total, axes, 0, 0, tiled=True, axis_index_groups=groups)
 
 
 def local(vel_x, vel_y, vel_z, pressure, phase, visc_scale, power_n, density):
@@ -559,25 +575,28 @@
     block = shape(bx, bz, by)
     scratch = lambda *dims: pltpu.VMEM(dims, f32)
     limit = lambda mebibytes: pltpu.CompilerParams(vmem_limit_bytes=mebibytes * 1024 * 1024)
-    tables = jnp.concatenate([visc_scale, power_n, density])
-
     groups = bx // GROUP
+    stacked = bx * FIELDS + bx // 2 + 2
     sent = shape(DEPTH * FIELDS + 1, bz, by)
     edge, x_0, x_1, stack = pl.pallas_call(
         pack_kernel,
-        out_shape=(shape(bx // 2, bz, by), sent, sent, shape(bx * FIELDS, bz, by)),
-        in_specs=[HBM] * 5,
+        out_shape=(shape(bx // 2, bz, by), sent, sent, shape(stacked, bz, by)),
+        in_specs=[HBM] * 8,
         out_specs=(HBM,) * 4,
         scratch_shapes=[
             scratch(FIELDS - 1, bx, bz, by),
             pltpu.VMEM((bx, bz, by), jnp.int32),
             scratch(bx // 2, bz, by),
-            scratch(bx * FIELDS, bz, by),
+            scratch(stacked, bz, by),
+            pltpu.SMEM((PHASES,), f32),
+            pltpu.SMEM((PHASES,), f32),
+            pltpu.SMEM((PHASES,), f32),
             pltpu.SemaphoreType.DMA((groups, FIELDS)),
-            pltpu.SemaphoreType.DMA((groups + groups // 2 + 2,)),
+            pltpu.SemaphoreType.DMA((groups + groups // 2 + 3,)),
+            pltpu.SemaphoreType.DMA((3,)),
         ],
         compiler_params=limit(58),
-    )(vel_x, vel_z, vel_y, pressure, phase)
+    )(vel_x, vel_z, vel_y, pressure, phase, visc_scale, power_n, density)
 
     def edges_beside(edge):
         side = swap(edge, "gy", 0)
@@ -589,13 +608,12 @@
     estimate = lambda size: pl.CostEstimate(
         flops=4 * size * bz * by, bytes_accessed=size * bz * by * 4, transcendentals=0
     )
-    long = estimate(100000)
 
     def unpacking(kernel, tiles, out_shape, *args, aliases={}):
         return pl.pallas_call(
             kernel,
             out_shape=out_shape,
-            in_specs=[VMEM if a is not tables else SMEM for a in args],
+            in_specs=[VMEM] * len(args),
             out_specs=(VMEM,) * len(out_shape),
             input_output_aliases=aliases,
             compiler_params=limit(16),
@@ -607,7 +625,8 @@
     half = lambda tiles, planes: shape(tiles + planes // (bz // 2), bz // 2, by)
     x_0, x_1 = swap(x_0, "gx", 0), swap(x_1, "gx", 1)
     face = half(bx * FIELDS, bx)
-    z_0, z_1, edge, *own = unpacking(own_kernel, bx, (face, face, shape(*edge.shape)) + own_shape, stack, edge, tables)
+    extra = (shape(bx // 2, bz, by), shape(2, bz, by))
+    z_0, z_1, edge, tables, *own = unpacking(own_kernel, bx, (face, face) + extra + own_shape, stack)
     face_1, face_0 = swap(z_1, "gz", 1), swap(z_0, "gz", 0)
 
     tiles = bx // 2 + DEPTH
@@ -634,7 +653,7 @@
         in_specs=[VMEM],
         out_specs=(VMEM,) * 2,
         compiler_params=limit(4),
-        cost_estimate=long,
+        cost_estimate=estimate(100000),
     )(edge)
     edge_1, edge_0 = swap(z_1, "gz", 1), swap(z_0, "gz", 0)
 
@@ -647,7 +666,7 @@
     vx, vz, vy, p, eta, total, _, _ = pl.pallas_call(
         main_kernel,
         out_shape=(block,) * 5 + (shape(bz, by),) + tuple(shape(*a.shape) for a in halo),
-        in_specs=[VMEM] * 9 + [SMEM],
+        in_specs=[VMEM] * 10,
         out_specs=(VMEM,) * 8,
         input_output_aliases={5: 6, 6: 7},
         scratch_shapes=[

time: 50.1 us -> 46.2 us (0.922)
  blocking collectives: 0 us -> 14.2 us
  starting transfers between devices: 24.2 us -> 15.9 us
  waiting for transfers between devices: 7.14 us -> 0.98 us
  Pallas kernels: 15.1 us -> 12.9 us
  other arithmetic: 0.78 us -> 0.02 us
  local copies, waits for them, and re-layouts: 1.73 us -> 0.99 us
    all_to_all x0 -> x1, blocking collectives: none -> 14.2 us  [sum_everywhere(): lax.all_to_all(total, axes, 0, 0, tiled=True, axis_index_groups=groups)]
    ppermute x7 -> x1, starting transfers between devices: 12 us -> 3.78 us  [sum_everywhere(): lax.ppermute(total, axes, [(i, i ^ 1) for i in range(devices)])]
    ppermute x7 -> x1, waiting for transfers between devices: 7.11 us -> 0.82 us  [sum_everywhere(): lax.ppermute(total, axes, [(i, i ^ 1) for i in range(devices)])]
    pallas_call x3, Pallas kernels: 2.53 us -> 0.9 us  [unpacking(): pl.pallas_call(kernel, out_shape=out_shape, in_specs=[VMEM] * len(args),...]
    concatenate x1 -> x0, other arithmetic: 0.77 us -> none  [local(): tables = jnp.concatenate([visc_scale, power_n, density])]
    unnamed x4 -> x2, local copies, waits for them, and re-layouts: 1.73 us -> 0.98 us
    pallas_call x1, Pallas kernels: 9.42 us -> 8.82 us  [local(): pl.pallas_call(main_kernel, out_shape=(block,) * 5 + (shape(bz, by),) + t...]
  transfers between devices with their start and end apart: 16 -> 10, of which waited for: 6 -> 2; matrix products, arithmetic and copies ran while one was open for 2% -> 0% of each run, Pallas kernels for 6% -> 2%
where the time goes in v13:
time: 46.2 us; the launch traced here: 45.8 us
  starting transfers between devices  15.9 us (34%)
  blocking collectives  14.2 us (31%)
  Pallas kernels  12.9 us (28%)
  local copies, waits for them, and re-layouts  0.99 us (2%)
  waiting for transfers between devices  0.98 us (2%)
  between operations  0.79 us (2%)
    all_to_all x1, blocking collectives, sum_everywhere(): lax.all_to_all(total, axes, 0, 0, tiled=True, axis_index_groups=groups)  14.2 us
    ppermute x9, starting transfers between devices, swap(): lax.ppermute(a, axis, [(i, j) for k in range(start, count - 1, 2) for i,...  12.1 us
    pallas_call x1, Pallas kernels, local(): pl.pallas_call(main_kernel, out_shape=(block,) * 5 + (shape(bz, by),) + t...  8.82 us
    ppermute x1, starting transfers between devices, sum_everywhere(): lax.ppermute(total, axes, [(i, i ^ 1) for i in range(devices)])  3.78 us
    pallas_call x1, Pallas kernels, local(): pl.pallas_call(pack_kernel, out_shape=(shape(bx // 2, bz, by), sent, sent...  2.24 us
    unnamed x2, local copies, waits for them, and re-layouts  0.98 us
  transfers between devices with their start and end apart: 10, of which 2 were waited for; matrix products, arithmetic and copies ran while one was open for 0% of the time, Pallas kernels for 2%

profile of v13, /device:TPU:0, one launch (start us, length us, event | category | flops | bytes accessed | tf_op | source)
XLA Modules:
  0.0 45.8 jit_solution(12779408590125059911)
XLA Ops:
  0.6 2.2 %shard_map.119 = (f32[8,8,128]{2,1,0:T(8,128)}, f32[21,8,128]{2,1,0:T(8,128)}, f32[21,8,128]{2,1,0:T(8,128)}, f32[90,8,128]{2,1,0:T(8,128)}) custom-call(f32[16,8,128]{2,1,0:T(8,128)} %vx_hbm.1, f32[16,8,128]{2,1,0:T(8,128)} %vz_hbm.1, f32[16,8,128]{2,1,0:T(8,128)} %vy_hbm.1, f32[16,8,128]{2,1,0:T(8,128)} %p_hbm.1, s32[16,8,128]{2,1,0:T(8,128)} %phase_hbm.1, ...), custom_call_target="tpu_custom_call" | custom-call | tf_op jit(solution)/shard_map/pallas_call | solution.py:581
  2.9 3.1 %collective-permute-start = (f32[21,8,128]{2,1,0:T(8,128)}, f32[21,8,128]{2,1,0:T(8,128)S(1)}, u32[]{:S(2)}, u32[]{:S(2)}) collective-permute-start(f32[21,8,128]{2,1,0:T(8,128)} %get-tuple-element.35), channel_id=1, source_target_pairs={{0,8},{8,0},{16,24},{24,16},{1,9},{9,1},{17,25},{25,17},{2,10},{10... | collective-permute-start | bytes 258056 | tf_op jit(solution)/shard_map/ppermute | solution.py:554
  6.0 0.7 %collective-permute-start.1 = (f32[21,8,128]{2,1,0:T(8,128)}, f32[21,8,128]{2,1,0:T(8,128)S(1)}, u32[]{:S(2)}, u32[]{:S(2)}) collective-permute-start(f32[21,8,128]{2,1,0:T(8,128)} %get-tuple-element.36), channel_id=1, source_target_pairs={{8,16},{16,8},{9,17},{17,9},{10,18},{18,10},{11,19},{19,11},{12,20... | collective-permute-start | bytes 258056 | tf_op jit(solution)/shard_map/ppermute | solution.py:554
  6.6 1.0 %copy-done = f32[90,8,128]{2,1,0:T(8,128)S(1)} copy-done((f32[90,8,128]{2,1,0:T(8,128)S(1)}, f32[90,8,128]{2,1,0:T(8,128)}, u32[]{:S(2)}) %copy-start) | copy-done | bytes 368664
  7.6 0.2 shard_map.120
  7.8 0.1 collective-permute-start.3
  7.9 0.7 %collective-permute-start.4 = (f32[84,4,128]{2,1,0:T(4,128)S(1)}, f32[84,4,128]{2,1,0:T(4,128)S(1)}, u32[]{:S(2)}, u32[]{:S(2)}) collective-permute-start(f32[84,4,128]{2,1,0:T(4,128)S(1)} %get-tuple-element.52), channel_id=1, source_target_pairs={{1,2},{2,1},{5,6},{6,5},{9,10},{10,9},{13,14},{14,13},{17,18},{18,... | collective-permute-start | bytes 516104 | tf_op jit(solution)/shard_map/ppermute | solution.py:554
  8.6 0.1 collective-permute-done.x_0_ref
  8.7 0.1 shard_map.121._edge_ref
  8.9 1.9 %collective-permute-start.2 = (f32[12,8,128]{2,1,0:T(8,128)S(1)}, f32[12,8,128]{2,1,0:T(8,128)S(1)}, u32[]{:S(2)}, u32[]{:S(2)}) collective-permute-start(f32[12,8,128]{2,1,0:T(8,128)S(1)} %shard_map.121._edge_ref), channel_id=1, source_target_pairs={{0,4},{4,0},{1,5},{5,1},{2,6},{6,2},{3,7},{7,3},{8,12},{12,8},{9,1... | collective-permute-start | bytes 147464 | tf_op jit(solution)/shard_map/ppermute | solution.py:554
  10.9 2.2 %collective-permute-start.5 = (f32[43,4,128]{2,1,0:T(4,128)S(1)}, f32[43,4,128]{2,1,0:T(4,128)S(1)}, u32[]{:S(2)}, u32[]{:S(2)}) collective-permute-start(f32[43,4,128]{2,1,0:T(4,128)S(1)} %get-tuple-element.53), channel_id=1, source_target_pairs={{0,1},{1,0},{2,3},{3,2},{4,5},{5,4},{6,7},{7,6},{8,9},{9,8},{10,11... | collective-permute-start | bytes 264200 | tf_op jit(solution)/shard_map/ppermute | solution.py:554
  13.0 0.7 %collective-permute-start.6 = (f32[43,4,128]{2,1,0:T(4,128)S(1)}, f32[43,4,128]{2,1,0:T(4,128)S(1)}, u32[]{:S(2)}, u32[]{:S(2)}) collective-permute-start(f32[43,4,128]{2,1,0:T(4,128)S(1)} %get-tuple-element.54), channel_id=1, source_target_pairs={{1,2},{2,1},{5,6},{6,5},{9,10},{10,9},{13,14},{14,13},{17,18},{18,... | collective-permute-start | bytes 264200 | tf_op jit(solution)/shard_map/ppermute | solution.py:554
  13.7 0.0 collective-permute-done.2.edge_ref
  13.7 2.2 %collective-permute-start.7 = (f32[15,4,128]{2,1,0:T(4,128)S(1)}, f32[15,4,128]{2,1,0:T(4,128)S(1)}, u32[]{:S(2)}, u32[]{:S(2)}) collective-permute-start(f32[15,4,128]{2,1,0:T(4,128)S(1)} %get-tuple-element.57), channel_id=1, source_target_pairs={{0,1},{1,0},{2,3},{3,2},{4,5},{5,4},{6,7},{7,6},{8,9},{9,8},{10,11... | collective-permute-start | bytes 92168 | tf_op jit(solution)/shard_map/ppermute | solution.py:554
  15.9 0.7 %collective-permute-start.8 = (f32[15,4,128]{2,1,0:T(4,128)S(1)}, f32[15,4,128]{2,1,0:T(4,128)S(1)}, u32[]{:S(2)}, u32[]{:S(2)}) collective-permute-start(f32[15,4,128]{2,1,0:T(4,128)S(1)} %get-tuple-element.58), channel_id=1, source_target_pairs={{1,2},{2,1},{5,6},{6,5},{9,10},{10,9},{13,14},{14,13},{17,18},{18,... | collective-permute-start | bytes 92168 | tf_op jit(solution)/shard_map/ppermute | solution.py:554
  16.6 0.5 %shard_map.123 = (f32[3,25,8,256]{3,2,1,0:T(8,128)S(1)}, f32[25,8,256]{2,1,0:T(8,128)S(1)}, f32[25,8,256]{2,1,0:T(8,128)S(1)}, f32[25,8,256]{2,1,0:T(8,128)S(1)}, f32[25,8,256]{2,1,0:T(8,128)S(1)}) custom-call(f32[41,8,128]{2,1,0:T(8,128)S(1)} %get-tuple-element.39.sides_ref, ...), custom_call_target="tpu_custom_call", output_to_operand_aliasing={{0}: (3, {}), {1}: (4, {}), {2}: (5, {}), {3}: (6, {}), {4}... | custom-call | flops 2662400 | bytes 2662400 | tf_op jit(solution)/shard_map/pallas_call | solution.py:613
  17.1 0.0 collective-permute-done.6.corner_1_ref
  17.2 0.2 shard_map.124
  17.4 0.0 collective-permute-done.8.edge_1_ref
  17.4 8.8 %shard_map.126 = (f32[16,8,128]{2,1,0:T(8,128)}, f32[16,8,128]{2,1,0:T(8,128)}, f32[16,8,128]{2,1,0:T(8,128)}, f32[16,8,128]{2,1,0:T(8,128)S(1)}, f32[16,8,128]{...) custom-call(f32[3,25,8,256]{3,2,1,0:T(8,128)S(1)} %get-tuple-element, ...), custom_call_target="tpu_custom_call", output_to_operand_aliasing={{6}: (5, {}), {7}: (6, {})} | custom-call | tf_op jit(solution)/shard_map/pallas_call | solution.py:666
  26.2 3.8 %collective-permute-start.9 = (f32[8,128]{1,0:T(8,128)S(1)}, f32[8,128]{1,0:T(8,128)S(1)}, u32[]{:S(2)}, u32[]{:S(2)}) collective-permute-start(f32[8,128]{1,0:T(8,128)S(1)} %get-tuple-element.63), channel_id=1, source_target_pairs={{0,1},{1,0},{2,3},{3,2},{4,5},{5,4},{6,7},{7,6},{8,9},{9,8},{10,11... | collective-permute-start | bytes 12296 | tf_op jit(solution)/shard_map/ppermute | solution.py:560
  30.0 0.8 %collective-permute-done.9 = f32[8,128]{1,0:T(8,128)S(1)} collective-permute-done((f32[8,128]{1,0:T(8,128)S(1)}, f32[8,128]{1,0:T(8,128)S(1)}, u32[]{:S(2)}, u32[]{:S(2)}) %collective-permute-start.9) | collective-permute-done | bytes 4128 | tf_op jit(solution)/shard_map/ppermute | solution.py:560
  30.8 14.2 %all_to_all.8 = f32[16,1,128]{2,1,0:T(1,128)S(1)} all-to-all(f32[16,1,128]{2,1,0:T(1,128)S(1)} %broadcast_in_dim.2), channel_id=1, replica_groups={{0,2,4,6,8,10,12,14,16,18,20,22,24,26,28,30},{1,3,5,7,9,11,13,15,17,19,..., dimensions={0} | all-to-all | bytes 16384 | tf_op jit(solution)/shard_map/all_to_all | solution.py:563
  45.1 0.8 %shard_map.127 = f32[16,8,128]{2,1,0:T(8,128)} custom-call(f32[16,8,128]{2,1,0:T(8,128)S(1)} %get-tuple-element.62.refs_0_, f32[16,128]{1,0:T(8,128)S(1)} %bitcast.1), custom_call_target="tpu_custom_call" | custom-call | tf_op jit(solution)/shard_map/pallas_call | solution.py:682
  (10 shorter events, 0.1 us)
Async XLA Ops:
  2.9 5.8 %collective-permute-start = (f32[21,8,128]{2,1,0:T(8,128)}, f32[21,8,128]{2,1,0:T(8,128)S(1)}, u32[]{:S(2)}, u32[]{:S(2)}) collective-permute-start(f32[21,8,128]{2,1,0:T(8,128)} %get-tuple-element.35), channel_id=1, source_target_pairs={{0,8},{8,0},{16,24},{24,16},{1,9},{9,1},{17,25},{25,17},{2,10},{10... | collective-permute-start | bytes 258056 | tf_op jit(solution)/shard_map/ppermute | solution.py:554
  6.0 2.7 %collective-permute-start.1 = (f32[21,8,128]{2,1,0:T(8,128)}, f32[21,8,128]{2,1,0:T(8,128)S(1)}, u32[]{:S(2)}, u32[]{:S(2)}) collective-permute-start(f32[21,8,128]{2,1,0:T(8,128)} %get-tuple-element.36), channel_id=1, source_target_pairs={{8,16},{16,8},{9,17},{17,9},{10,18},{18,10},{11,19},{19,11},{12,20... | collective-permute-start | bytes 258056 | tf_op jit(solution)/shard_map/ppermute | solution.py:554
  6.6 1.0 %copy-start = (f32[90,8,128]{2,1,0:T(8,128)S(1)}, f32[90,8,128]{2,1,0:T(8,128)}, u32[]{:S(2)}) copy-start(f32[90,8,128]{2,1,0:T(8,128)} %get-tuple-element.37.stack_ref) | copy-start | bytes 1105924
  7.8 8.1 %collective-permute-start.3 = (f32[84,4,128]{2,1,0:T(4,128)S(1)}, f32[84,4,128]{2,1,0:T(4,128)S(1)}, u32[]{:S(2)}, u32[]{:S(2)}) collective-permute-start(f32[84,4,128]{2,1,0:T(4,128)S(1)} %get-tuple-element.51), channel_id=1, source_target_pairs={{0,1},{1,0},{2,3},{3,2},{4,5},{5,4},{6,7},{7,6},{8,9},{9,8},{10,11... | collective-permute-start | bytes 516104 | tf_op jit(solution)/shard_map/ppermute | solution.py:554
  7.9 9.2 %collective-permute-start.4 = (f32[84,4,128]{2,1,0:T(4,128)S(1)}, f32[84,4,128]{2,1,0:T(4,128)S(1)}, u32[]{:S(2)}, u32[]{:S(2)}) collective-permute-start(f32[84,4,128]{2,1,0:T(4,128)S(1)} %get-tuple-element.52), channel_id=1, source_target_pairs={{1,2},{2,1},{5,6},{6,5},{9,10},{10,9},{13,14},{14,13},{17,18},{18,... | collective-permute-start | bytes 516104 | tf_op jit(solution)/shard_map/ppermute | solution.py:554
  8.9 4.8 %collective-permute-start.2 = (f32[12,8,128]{2,1,0:T(8,128)S(1)}, f32[12,8,128]{2,1,0:T(8,128)S(1)}, u32[]{:S(2)}, u32[]{:S(2)}) collective-permute-start(f32[12,8,128]{2,1,0:T(8,128)S(1)} %shard_map.121._edge_ref), channel_id=1, source_target_pairs={{0,4},{4,0},{1,5},{5,1},{2,6},{6,2},{3,7},{7,3},{8,12},{12,8},{9,1... | collective-permute-start | bytes 147464 | tf_op jit(solution)/shard_map/ppermute | solution.py:554
  10.9 6.3 %collective-permute-start.5 = (f32[43,4,128]{2,1,0:T(4,128)S(1)}, f32[43,4,128]{2,1,0:T(4,128)S(1)}, u32[]{:S(2)}, u32[]{:S(2)}) collective-permute-start(f32[43,4,128]{2,1,0:T(4,128)S(1)} %get-tuple-element.53), channel_id=1, source_target_pairs={{0,1},{1,0},{2,3},{3,2},{4,5},{5,4},{6,7},{7,6},{8,9},{9,8},{10,11... | collective-permute-start | bytes 264200 | tf_op jit(solution)/shard_map/ppermute | solution.py:554
  13.0 4.1 %collective-permute-start.6 = (f32[43,4,128]{2,1,0:T(4,128)S(1)}, f32[43,4,128]{2,1,0:T(4,128)S(1)}, u32[]{:S(2)}, u32[]{:S(2)}) collective-permute-start(f32[43,4,128]{2,1,0:T(4,128)S(1)} %get-tuple-element.54), channel_id=1, source_target_pairs={{1,2},{2,1},{5,6},{6,5},{9,10},{10,9},{13,14},{14,13},{17,18},{18,... | collective-permute-start | bytes 264200 | tf_op jit(solution)/shard_map/ppermute | solution.py:554
  13.7 3.6 %collective-permute-start.7 = (f32[15,4,128]{2,1,0:T(4,128)S(1)}, f32[15,4,128]{2,1,0:T(4,128)S(1)}, u32[]{:S(2)}, u32[]{:S(2)}) collective-permute-start(f32[15,4,128]{2,1,0:T(4,128)S(1)} %get-tuple-element.57), channel_id=1, source_target_pairs={{0,1},{1,0},{2,3},{3,2},{4,5},{5,4},{6,7},{7,6},{8,9},{9,8},{10,11... | collective-permute-start | bytes 92168 | tf_op jit(solution)/shard_map/ppermute | solution.py:554
  15.9 1.4 %collective-permute-start.8 = (f32[15,4,128]{2,1,0:T(4,128)S(1)}, f32[15,4,128]{2,1,0:T(4,128)S(1)}, u32[]{:S(2)}, u32[]{:S(2)}) collective-permute-start(f32[15,4,128]{2,1,0:T(4,128)S(1)} %get-tuple-element.58), channel_id=1, source_target_pairs={{1,2},{2,1},{5,6},{6,5},{9,10},{10,9},{13,14},{14,13},{17,18},{18,... | collective-permute-start | bytes 92168 | tf_op jit(solution)/shard_map/ppermute | solution.py:554
  26.2 4.6 %collective-permute-start.9 = (f32[8,128]{1,0:T(8,128)S(1)}, f32[8,128]{1,0:T(8,128)S(1)}, u32[]{:S(2)}, u32[]{:S(2)}) collective-permute-start(f32[8,128]{1,0:T(8,128)S(1)} %get-tuple-element.63), channel_id=1, source_target_pairs={{0,1},{1,0},{2,3},{3,2},{4,5},{5,4},{6,7},{7,6},{8,9},{9,8},{10,11... | collective-permute-start | bytes 12296 | tf_op jit(solution)/shard_map/ppermute | solution.py:560

commit v14 on v13

--- a/solution.py
+++ b/solution.py
@@ -169,7 +169,7 @@
         copy.wait()
 
 
-def side_edge_kernel(x_0_ref, x_1_ref, own_edge_ref, edge_ref):
+def side_edge_kernel(x_1_ref, x_0_ref, own_edge_ref, edge_ref):
     bz, by = edge_ref.shape[1:]
     own = own_edge_ref.shape[0]
     edge_ref[0:own] = own_edge_ref[...]
@@ -198,7 +198,7 @@
             ref[at + i // half, i % half : i % half + 1, :] = tiles[i, half : half + 1, :]
 
 
-def sides_kernel(x_0_ref, x_1_ref, _edge_ref, sides_ref, z_0_ref, z_1_ref):
+def sides_kernel(x_1_ref, x_0_ref, _edge_ref, sides_ref, z_0_ref, z_1_ref):
     count = DEPTH * FIELDS
     bz, by = sides_ref.shape[1:]
 
@@ -457,72 +457,73 @@
             sy = quarter + y_down(quarter)
             return vx, vz, vy, eta, p, quarter, tx, tz, ty, sz, sy
 
-        def chunk(j, count, carry, start=False):
+        def chunk(j, count, carry=None, final=False):
+            if carry is None:
+                below = cells(j - 1, count + 1)
+                if not last:
+                    p_ref[pl.ds(j - 1, 1)] = below[4][:1]
+                vx, vz, vy, eta, p, quarter, tx, tz, ty, sz, sy = (a[1:] for a in below)
+                join = lambda n, a: below[n][:-1]
+            else:
+                vx, vz, vy, eta, p, quarter, tx, tz, ty, sz, sy = cells(j, count)
+                first = {1: load(1, j - 1, 1), 2: load(2, j - 1, 1), 5: carry[0], 6: carry[1], 9: carry[2], 10: carry[3]}
+                join = lambda n, a: jnp.concatenate([first[n], a[:-1]], axis=0)
             planes = pl.ds(j, count)
-            vx, vz, vy, eta, p, quarter, tx, tz, ty, sz, sy = cells(j, count)
-            vz0, vy0 = load(1, j - 1, 1), load(2, j - 1, 1)
-            quarter0, tx0, sz0, sy0, part_z0, part_y0, scale_z0, scale_y0 = carry
-            join = lambda first, rest: jnp.concatenate([first, rest[:-1]], axis=0) if count > 1 else first
             bias = weight_ref[3:4]
-            sx = quarter + join(quarter0, quarter)
-            exz = sz + join(sz0, sz)
-            exy = sy + join(sy0, sy)
+            sx = quarter + join(5, quarter)
+            exz = sz + join(9, sz)
+            exy = sy + join(10, sy)
             ezy = sz + y_down(sz)
             fxz = exz * (vx - z_down(vx))
             fxy = exy * (vx - y_down(vx))
-            low_vz, low_vy = join(vz0, vz), join(vy0, vy)
+            low_vz, low_vy = join(1, vz), join(2, vy)
             gzx = exz * (vz - low_vz)
             hyx = exy * (vy - low_vy)
             gzy = ezy * (vz - y_down(vz))
             hyz = ezy * (vy - z_down(vy))
-            res_x = (tx - join(tx0, tx)) + ((z_up(fxz) - fxz) + (y_up(fxy) - fxy))
+            res_x = (tx - join(6, tx)) + ((z_up(fxz) - fxz) + (y_up(fxy) - fxy))
             new_vx = vx + weight_ref[0:1] * reciprocal(sx + bias) * res_x
             part_z = (tz - z_down(tz)) - with_halo(rho_ref, 6, planes) + ((y_up(gzy) - gzy) - gzx)
             part_y = (ty - y_down(ty)) + ((z_up(hyz) - hyz) - hyx)
             scale_z = weight_ref[1:2] * reciprocal(sz + bias)
             scale_y = weight_ref[2:3] * reciprocal(sy + bias)
-            new_vz = low_vz + join(scale_z0, scale_z) * (join(part_z0, part_z) + gzx)
-            new_vy = low_vy + join(scale_y0, scale_y) * (join(part_y0, part_y) + hyx)
+
+            def lower(n, a):
+                return a[:-1] if carry is None else jnp.concatenate([carry[n], a[:-1]], axis=0)
+
+            skip = 1 if carry is None else 0
+            new_vz = low_vz[skip:] + lower(6, scale_z) * (lower(4, part_z) + gzx[skip:])
+            new_vy = low_vy[skip:] + lower(7, scale_y) * (lower(5, part_y) + hyx[skip:])
+            at = pl.ds(j - 1 + skip - (DEPTH if last else 0), count - skip)
             if last:
-                at = pl.ds(j - DEPTH, count)
-                out_vx_ref[at] = new_vx[:, 0:bz, 0:by]
-                out_p_ref[at] = p[:, 0:bz, 0:by]
-                out_eta_ref[at] = eta[:, 0:bz, 0:by]
-                sum_ref[...] += jnp.sum(p[:, 0:bz, 0:by], axis=0)
-                if not start:
-                    at = pl.ds(j - 1 - DEPTH, count)
-                    out_vz_ref[at] = new_vz[:, 0:bz, 0:by]
-                    out_vy_ref[at] = new_vy[:, 0:bz, 0:by]
+                own = count - 1 if final else count
+                here = pl.ds(j - DEPTH, own)
+                out_vx_ref[here] = new_vx[:own, 0:bz, 0:by]
+                out_p_ref[here] = p[:own, 0:bz, 0:by]
+                out_eta_ref[here] = eta[:own, 0:bz, 0:by]
+                sum_ref[...] += jnp.sum(p[:own, 0:bz, 0:by], axis=0)
+                out_vz_ref[at] = new_vz[:, 0:bz, 0:by]
+                out_vy_ref[at] = new_vy[:, 0:bz, 0:by]
             else:
                 p_ref[planes] = p
                 new[0, planes] = new_vx
-                if not start:
-                    new[1, pl.ds(j - 1, count)] = new_vz
-                    new[2, pl.ds(j - 1, count)] = new_vy
+                new[1, at] = new_vz
+                new[2, at] = new_vy
             return tuple(a[-1:] for a in (quarter, tx, sz, sy, part_z, part_y, scale_z, scale_y))
 
         first, end = k, bx + 2 * DEPTH - k
         if last:
             sum_ref[...] = jnp.zeros((bz, by), jnp.float32)
-        _, _, _, _, p, quarter, tx, _, _, sz, sy = cells(first - 1, 1)
-        if not last:
-            p_ref[pl.ds(first - 1, 1)] = p
-        zero = jnp.zeros((1, rows, lanes), jnp.float32)
-        carry = chunk(first, 1, (quarter, tx, sz, sy, zero, zero, zero, zero), start=True)
-        steps, rest = divmod((end - 1 if last else end) - first, UNROLL)
+        count = end - first + 1
+        steps = (count - 2) // UNROLL
+        start = count - steps * UNROLL
+        carry = chunk(first, start)
+        loops = steps - 1 if last else steps
         carry = lax.fori_loop(
-            0, steps, lambda s, carry: chunk(first + 1 + s * UNROLL, UNROLL, carry), carry
+            0, loops, lambda s, carry: chunk(first + start + s * UNROLL, UNROLL, carry), carry
         )
-        if rest:
-            carry = chunk(first + 1 + steps * UNROLL, rest, carry)
         if last:
-            quarter0, tx0, sz0, sy0, part_z0, part_y0, scale_z0, scale_y0 = carry
-            _, vz, vy, _, _, _, _, _, _, sz, sy = cells(end, 1)
-            vz0, vy0 = load(1, end - 1, 1), load(2, end - 1, 1)
-            new_vz = vz0 + scale_z0 * (part_z0 + (sz + sz0) * (vz - vz0))
-            new_vy = vy0 + scale_y0 * (part_y0 + (sy + sy0) * (vy - vy0))
-            out_vz_ref[pl.ds(end - 1 - DEPTH, 1)] = new_vz[:, 0:bz, 0:by]
-            out_vy_ref[pl.ds(end - 1 - DEPTH, 1)] = new_vy[:, 0:bz, 0:by]
+            chunk(end + 1 - UNROLL, UNROLL, carry, final=True)
 
             @pl.when(ix == 0)
             def _():
@@ -623,7 +624,7 @@
     field = shape(deep, bz, lanes)
     own_shape = (shape(3, deep, bz, lanes),) + (field,) * 4
     half = lambda tiles, planes: shape(tiles + planes // (bz // 2), bz // 2, by)
-    x_0, x_1 = swap(x_0, "gx", 0), swap(x_1, "gx", 1)
+    x_1, x_0 = swap(x_1, "gx", 1), swap(x_0, "gx", 0)
     face = half(bx * FIELDS, bx)
     extra = (shape(bx // 2, bz, by), shape(2, bz, by))
     z_0, z_1, edge, tables, *own = unpacking(own_kernel, bx, (face, face) + extra + own_shape, stack)
@@ -636,7 +637,7 @@
         in_specs=[VMEM] * 3,
         out_specs=VMEM,
         compiler_params=limit(4),
-    )(x_0, x_1, edge)
+    )(x_1, x_0, edge)
     corner = half(2 * DEPTH * FIELDS + 1, 2 * DEPTH)
     sides, z_0, z_1 = pl.pallas_call(
         sides_kernel,
@@ -644,7 +645,7 @@
         in_specs=[VMEM] * 3,
         out_specs=(VMEM,) * 3,
         compiler_params=limit(4),
-    )(x_0, x_1, edge)
+    )(x_1, x_0, edge)
     edge = edges_beside(edge)
     corner_1, corner_0 = swap(z_1, "gz", 1), swap(z_0, "gz", 0)
     z_0, z_1 = pl.pallas_call(

time: 46.2 us -> 44.8 us (0.970)
  blocking collectives: 14.2 us -> 10.9 us
  starting transfers between devices: 15.9 us -> 18.1 us
  Pallas kernels: 12.9 us -> 12.1 us
  waiting for transfers between devices: 0.98 us -> 1.57 us
    all_to_all x1, blocking collectives: 14.2 us -> 10.9 us  [sum_everywhere(): lax.all_to_all(total, axes, 0, 0, tiled=True, axis_index_groups=groups)]
    ppermute x9, starting transfers between devices: 12.1 us -> 14.3 us  [swap(): lax.ppermute(a, axis, [(i, j) for k in range(start, count - 1, 2) for i,...]
    pallas_call x1, Pallas kernels: 8.82 us -> 7.97 us  [local(): pl.pallas_call(main_kernel, out_shape=(block,) * 5 + (shape(bz, by),) + t...]
    ppermute x9, waiting for transfers between devices: 0.16 us -> 0.74 us  [swap(): lax.ppermute(a, axis, [(i, j) for k in range(start, count - 1, 2) for i,...]
where the time goes in v14:
time: 44.8 us; the launch traced here: 44.5 us
  starting transfers between devices  18.1 us (40%)
  Pallas kernels  12.1 us (27%)
  blocking collectives  10.9 us (24%)
  waiting for transfers between devices  1.57 us (4%)
  local copies, waits for them, and re-layouts  1 us (2%)
  between operations  0.79 us (2%)
    ppermute x9, starting transfers between devices, swap(): lax.ppermute(a, axis, [(i, j) for k in range(start, count - 1, 2) for i,...  14.3 us
    all_to_all x1, blocking collectives, sum_everywhere(): lax.all_to_all(total, axes, 0, 0, tiled=True, axis_index_groups=groups)  10.9 us
    pallas_call x1, Pallas kernels, local(): pl.pallas_call(main_kernel, out_shape=(block,) * 5 + (shape(bz, by),) + t...  7.97 us
    ppermute x1, starting transfers between devices, sum_everywhere(): lax.ppermute(total, axes, [(i, i ^ 1) for i in range(devices)])  3.78 us
    pallas_call x1, Pallas kernels, local(): pl.pallas_call(pack_kernel, out_shape=(shape(bx // 2, bz, by), sent, sent...  2.24 us
    unnamed x2, local copies, waits for them, and re-layouts  0.99 us
    pallas_call x3, Pallas kernels, unpacking(): pl.pallas_call(kernel, out_shape=out_shape, in_specs=[VMEM] * len(args),...  0.9 us
  transfers between devices with their start and end apart: 10, of which 2 were waited for; matrix products, arithmetic and copies ran while one was open for 0% of the time, Pallas kernels for 2%

profile of v14, /device:TPU:0, one launch (start us, length us, event | category | flops | bytes accessed | tf_op | source)
XLA Modules:
  0.0 44.5 jit_solution(9353972805706163446)
XLA Ops:
  0.6 2.2 %shard_map.119 = (f32[8,8,128]{2,1,0:T(8,128)}, f32[21,8,128]{2,1,0:T(8,128)}, f32[21,8,128]{2,1,0:T(8,128)}, f32[90,8,128]{2,1,0:T(8,128)}) custom-call(f32[16,8,128]{2,1,0:T(8,128)} %vx_hbm.1, f32[16,8,128]{2,1,0:T(8,128)} %vz_hbm.1, f32[16,8,128]{2,1,0:T(8,128)} %vy_hbm.1, f32[16,8,128]{2,1,0:T(8,128)} %p_hbm.1, s32[16,8,128]{2,1,0:T(8,128)} %phase_hbm.1, ...), custom_call_target="tpu_custom_call" | custom-call | tf_op jit(solution)/shard_map/pallas_call | solution.py:582
  2.9 0.7 %collective-permute-start = (f32[21,8,128]{2,1,0:T(8,128)}, f32[21,8,128]{2,1,0:T(8,128)S(1)}, u32[]{:S(2)}, u32[]{:S(2)}) collective-permute-start(f32[21,8,128]{2,1,0:T(8,128)} %get-tuple-element.35), channel_id=1, source_target_pairs={{8,16},{16,8},{9,17},{17,9},{10,18},{18,10},{11,19},{19,11},{12,20... | collective-permute-start | bytes 258056 | tf_op jit(solution)/shard_map/ppermute | solution.py:555
  3.6 5.9 %collective-permute-start.1 = (f32[21,8,128]{2,1,0:T(8,128)}, f32[21,8,128]{2,1,0:T(8,128)S(1)}, u32[]{:S(2)}, u32[]{:S(2)}) collective-permute-start(f32[21,8,128]{2,1,0:T(8,128)} %get-tuple-element.36), channel_id=1, source_target_pairs={{0,8},{8,0},{16,24},{24,16},{1,9},{9,1},{17,25},{25,17},{2,10},{10... | collective-permute-start | bytes 258056 | tf_op jit(solution)/shard_map/ppermute | solution.py:555
  9.5 1.0 %copy-done = f32[90,8,128]{2,1,0:T(8,128)S(1)} copy-done((f32[90,8,128]{2,1,0:T(8,128)S(1)}, f32[90,8,128]{2,1,0:T(8,128)}, u32[]{:S(2)}) %copy-start) | copy-done | bytes 368664
  10.4 0.2 shard_map.120
  10.6 0.1 collective-permute-start.3
  10.7 0.7 %collective-permute-start.4 = (f32[84,4,128]{2,1,0:T(4,128)S(1)}, f32[84,4,128]{2,1,0:T(4,128)S(1)}, u32[]{:S(2)}, u32[]{:S(2)}) collective-permute-start(f32[84,4,128]{2,1,0:T(4,128)S(1)} %get-tuple-element.52), channel_id=1, source_target_pairs={{1,2},{2,1},{5,6},{6,5},{9,10},{10,9},{13,14},{14,13},{17,18},{18,... | collective-permute-start | bytes 516104 | tf_op jit(solution)/shard_map/ppermute | solution.py:555
  11.4 0.0 collective-permute-done.x_1_ref
  11.4 0.7 %collective-permute-done.1.x_0_ref = f32[21,8,128]{2,1,0:T(8,128)S(1)} collective-permute-done((f32[21,8,128]{2,1,0:T(8,128)}, f32[21,8,128]{2,1,0:T(8,128)S(1)}, u32[]{:S(2)}, u32[]{:S(2)}) %collective-permute-start.1) | collective-permute-done | bytes 86048 | tf_op jit(solution)/shard_map/ppermute | solution.py:555
  12.1 0.1 shard_map.121._edge_ref
  12.3 1.6 %collective-permute-start.2 = (f32[12,8,128]{2,1,0:T(8,128)S(1)}, f32[12,8,128]{2,1,0:T(8,128)S(1)}, u32[]{:S(2)}, u32[]{:S(2)}) collective-permute-start(f32[12,8,128]{2,1,0:T(8,128)S(1)} %shard_map.121._edge_ref), channel_id=1, source_target_pairs={{0,4},{4,0},{1,5},{5,1},{2,6},{6,2},{3,7},{7,3},{8,12},{12,8},{9,1... | collective-permute-start | bytes 147464 | tf_op jit(solution)/shard_map/ppermute | solution.py:555
  13.9 2.0 %collective-permute-start.5 = (f32[43,4,128]{2,1,0:T(4,128)S(1)}, f32[43,4,128]{2,1,0:T(4,128)S(1)}, u32[]{:S(2)}, u32[]{:S(2)}) collective-permute-start(f32[43,4,128]{2,1,0:T(4,128)S(1)} %get-tuple-element.53), channel_id=1, source_target_pairs={{0,1},{1,0},{2,3},{3,2},{4,5},{5,4},{6,7},{7,6},{8,9},{9,8},{10,11... | collective-permute-start | bytes 264200 | tf_op jit(solution)/shard_map/ppermute | solution.py:555
  15.9 0.7 %collective-permute-start.6 = (f32[43,4,128]{2,1,0:T(4,128)S(1)}, f32[43,4,128]{2,1,0:T(4,128)S(1)}, u32[]{:S(2)}, u32[]{:S(2)}) collective-permute-start(f32[43,4,128]{2,1,0:T(4,128)S(1)} %get-tuple-element.54), channel_id=1, source_target_pairs={{1,2},{2,1},{5,6},{6,5},{9,10},{10,9},{13,14},{14,13},{17,18},{18,... | collective-permute-start | bytes 264200 | tf_op jit(solution)/shard_map/ppermute | solution.py:555
  16.6 2.2 %collective-permute-start.7 = (f32[15,4,128]{2,1,0:T(4,128)S(1)}, f32[15,4,128]{2,1,0:T(4,128)S(1)}, u32[]{:S(2)}, u32[]{:S(2)}) collective-permute-start(f32[15,4,128]{2,1,0:T(4,128)S(1)} %get-tuple-element.57), channel_id=1, source_target_pairs={{0,1},{1,0},{2,3},{3,2},{4,5},{5,4},{6,7},{7,6},{8,9},{9,8},{10,11... | collective-permute-start | bytes 92168 | tf_op jit(solution)/shard_map/ppermute | solution.py:555
  18.8 0.0 collective-permute-done.3.face_0_ref
  18.8 0.7 %collective-permute-start.8 = (f32[15,4,128]{2,1,0:T(4,128)S(1)}, f32[15,4,128]{2,1,0:T(4,128)S(1)}, u32[]{:S(2)}, u32[]{:S(2)}) collective-permute-start(f32[15,4,128]{2,1,0:T(4,128)S(1)} %get-tuple-element.58), channel_id=1, source_target_pairs={{1,2},{2,1},{5,6},{6,5},{9,10},{10,9},{13,14},{14,13},{17,18},{18,... | collective-permute-start | bytes 92168 | tf_op jit(solution)/shard_map/ppermute | solution.py:555
  19.4 0.5 %shard_map.123 = (f32[3,25,8,256]{3,2,1,0:T(8,128)S(1)}, f32[25,8,256]{2,1,0:T(8,128)S(1)}, f32[25,8,256]{2,1,0:T(8,128)S(1)}, f32[25,8,256]{2,1,0:T(8,128)S(1)}, f32[25,8,256]{2,1,0:T(8,128)S(1)}) custom-call(f32[41,8,128]{2,1,0:T(8,128)S(1)} %get-tuple-element.39.sides_ref, ...), custom_call_target="tpu_custom_call", output_to_operand_aliasing={{0}: (3, {}), {1}: (4, {}), {2}: (5, {}), {3}: (6, {}), {4}... | custom-call | flops 2662400 | bytes 2662400 | tf_op jit(solution)/shard_map/pallas_call | solution.py:614
  20.0 0.0 collective-permute-done.4.face_1_ref
  20.0 0.2 shard_map.124
  20.2 8.0 %shard_map.126 = (f32[16,8,128]{2,1,0:T(8,128)}, f32[16,8,128]{2,1,0:T(8,128)}, f32[16,8,128]{2,1,0:T(8,128)}, f32[16,8,128]{2,1,0:T(8,128)S(1)}, f32[16,8,128]{...) custom-call(f32[3,25,8,256]{3,2,1,0:T(8,128)S(1)} %get-tuple-element, ...), custom_call_target="tpu_custom_call", output_to_operand_aliasing={{6}: (5, {}), {7}: (6, {})} | custom-call | tf_op jit(solution)/shard_map/pallas_call | solution.py:667
  28.2 3.8 %collective-permute-start.9 = (f32[8,128]{1,0:T(8,128)S(1)}, f32[8,128]{1,0:T(8,128)S(1)}, u32[]{:S(2)}, u32[]{:S(2)}) collective-permute-start(f32[8,128]{1,0:T(8,128)S(1)} %get-tuple-element.63), channel_id=1, source_target_pairs={{0,1},{1,0},{2,3},{3,2},{4,5},{5,4},{6,7},{7,6},{8,9},{9,8},{10,11... | collective-permute-start | bytes 12296 | tf_op jit(solution)/shard_map/ppermute | solution.py:561
  32.0 0.8 %collective-permute-done.9 = f32[8,128]{1,0:T(8,128)S(1)} collective-permute-done((f32[8,128]{1,0:T(8,128)S(1)}, f32[8,128]{1,0:T(8,128)S(1)}, u32[]{:S(2)}, u32[]{:S(2)}) %collective-permute-start.9) | collective-permute-done | bytes 4128 | tf_op jit(solution)/shard_map/ppermute | solution.py:561
  32.8 10.9 %all_to_all.8 = f32[16,1,128]{2,1,0:T(1,128)S(1)} all-to-all(f32[16,1,128]{2,1,0:T(1,128)S(1)} %broadcast_in_dim.2), channel_id=1, replica_groups={{0,2,4,6,8,10,12,14,16,18,20,22,24,26,28,30},{1,3,5,7,9,11,13,15,17,19,..., dimensions={0} | all-to-all | bytes 16384 | tf_op jit(solution)/shard_map/all_to_all | solution.py:564
  43.7 0.8 %shard_map.127 = f32[16,8,128]{2,1,0:T(8,128)} custom-call(f32[16,8,128]{2,1,0:T(8,128)S(1)} %get-tuple-element.62.refs_0_, f32[16,128]{1,0:T(8,128)S(1)} %bitcast.1), custom_call_target="tpu_custom_call" | custom-call | tf_op jit(solution)/shard_map/pallas_call | solution.py:683
  (10 shorter events, 0.1 us)
Async XLA Ops:
  2.9 8.5 %collective-permute-start = (f32[21,8,128]{2,1,0:T(8,128)}, f32[21,8,128]{2,1,0:T(8,128)S(1)}, u32[]{:S(2)}, u32[]{:S(2)}) collective-permute-start(f32[21,8,128]{2,1,0:T(8,128)} %get-tuple-element.35), channel_id=1, source_target_pairs={{8,16},{16,8},{9,17},{17,9},{10,18},{18,10},{11,19},{19,11},{12,20... | collective-permute-start | bytes 258056 | tf_op jit(solution)/shard_map/ppermute | solution.py:555
  3.6 8.6 %collective-permute-start.1 = (f32[21,8,128]{2,1,0:T(8,128)}, f32[21,8,128]{2,1,0:T(8,128)S(1)}, u32[]{:S(2)}, u32[]{:S(2)}) collective-permute-start(f32[21,8,128]{2,1,0:T(8,128)} %get-tuple-element.36), channel_id=1, source_target_pairs={{0,8},{8,0},{16,24},{24,16},{1,9},{9,1},{17,25},{25,17},{2,10},{10... | collective-permute-start | bytes 258056 | tf_op jit(solution)/shard_map/ppermute | solution.py:555
  9.5 1.0 %copy-start = (f32[90,8,128]{2,1,0:T(8,128)S(1)}, f32[90,8,128]{2,1,0:T(8,128)}, u32[]{:S(2)}) copy-start(f32[90,8,128]{2,1,0:T(8,128)} %get-tuple-element.37.stack_ref) | copy-start | bytes 1105924
  10.6 8.1 %collective-permute-start.3 = (f32[84,4,128]{2,1,0:T(4,128)S(1)}, f32[84,4,128]{2,1,0:T(4,128)S(1)}, u32[]{:S(2)}, u32[]{:S(2)}) collective-permute-start(f32[84,4,128]{2,1,0:T(4,128)S(1)} %get-tuple-element.51), channel_id=1, source_target_pairs={{0,1},{1,0},{2,3},{3,2},{4,5},{5,4},{6,7},{7,6},{8,9},{9,8},{10,11... | collective-permute-start | bytes 516104 | tf_op jit(solution)/shard_map/ppermute | solution.py:555
  10.7 9.2 %collective-permute-start.4 = (f32[84,4,128]{2,1,0:T(4,128)S(1)}, f32[84,4,128]{2,1,0:T(4,128)S(1)}, u32[]{:S(2)}, u32[]{:S(2)}) collective-permute-start(f32[84,4,128]{2,1,0:T(4,128)S(1)} %get-tuple-element.52), channel_id=1, source_target_pairs={{1,2},{2,1},{5,6},{6,5},{9,10},{10,9},{13,14},{14,13},{17,18},{18,... | collective-permute-start | bytes 516104 | tf_op jit(solution)/shard_map/ppermute | solution.py:555
  12.3 4.2 %collective-permute-start.2 = (f32[12,8,128]{2,1,0:T(8,128)S(1)}, f32[12,8,128]{2,1,0:T(8,128)S(1)}, u32[]{:S(2)}, u32[]{:S(2)}) collective-permute-start(f32[12,8,128]{2,1,0:T(8,128)S(1)} %shard_map.121._edge_ref), channel_id=1, source_target_pairs={{0,4},{4,0},{1,5},{5,1},{2,6},{6,2},{3,7},{7,3},{8,12},{12,8},{9,1... | collective-permute-start | bytes 147464 | tf_op jit(solution)/shard_map/ppermute | solution.py:555
  13.9 6.1 %collective-permute-start.5 = (f32[43,4,128]{2,1,0:T(4,128)S(1)}, f32[43,4,128]{2,1,0:T(4,128)S(1)}, u32[]{:S(2)}, u32[]{:S(2)}) collective-permute-start(f32[43,4,128]{2,1,0:T(4,128)S(1)} %get-tuple-element.53), channel_id=1, source_target_pairs={{0,1},{1,0},{2,3},{3,2},{4,5},{5,4},{6,7},{7,6},{8,9},{9,8},{10,11... | collective-permute-start | bytes 264200 | tf_op jit(solution)/shard_map/ppermute | solution.py:555
  15.9 4.1 %collective-permute-start.6 = (f32[43,4,128]{2,1,0:T(4,128)S(1)}, f32[43,4,128]{2,1,0:T(4,128)S(1)}, u32[]{:S(2)}, u32[]{:S(2)}) collective-permute-start(f32[43,4,128]{2,1,0:T(4,128)S(1)} %get-tuple-element.54), channel_id=1, source_target_pairs={{1,2},{2,1},{5,6},{6,5},{9,10},{10,9},{13,14},{14,13},{17,18},{18,... | collective-permute-start | bytes 264200 | tf_op jit(solution)/shard_map/ppermute | solution.py:555
  16.6 3.6 %collective-permute-start.7 = (f32[15,4,128]{2,1,0:T(4,128)S(1)}, f32[15,4,128]{2,1,0:T(4,128)S(1)}, u32[]{:S(2)}, u32[]{:S(2)}) collective-permute-start(f32[15,4,128]{2,1,0:T(4,128)S(1)} %get-tuple-element.57), channel_id=1, source_target_pairs={{0,1},{1,0},{2,3},{3,2},{4,5},{5,4},{6,7},{7,6},{8,9},{9,8},{10,11... | collective-permute-start | bytes 92168 | tf_op jit(solution)/shard_map/ppermute | solution.py:555
  18.8 1.4 %collective-permute-start.8 = (f32[15,4,128]{2,1,0:T(4,128)S(1)}, f32[15,4,128]{2,1,0:T(4,128)S(1)}, u32[]{:S(2)}, u32[]{:S(2)}) collective-permute-start(f32[15,4,128]{2,1,0:T(4,128)S(1)} %get-tuple-element.58), channel_id=1, source_target_pairs={{1,2},{2,1},{5,6},{6,5},{9,10},{10,9},{13,14},{14,13},{17,18},{18,... | collective-permute-start | bytes 92168 | tf_op jit(solution)/shard_map/ppermute | solution.py:555
  28.2 4.6 %collective-permute-start.9 = (f32[8,128]{1,0:T(8,128)S(1)}, f32[8,128]{1,0:T(8,128)S(1)}, u32[]{:S(2)}, u32[]{:S(2)}) collective-permute-start(f32[8,128]{1,0:T(8,128)S(1)} %get-tuple-element.63), channel_id=1, source_target_pairs={{0,1},{1,0},{2,3},{3,2},{4,5},{5,4},{6,7},{7,6},{8,9},{9,8},{10,11... | collective-permute-start | bytes 12296 | tf_op jit(solution)/shard_map/ppermute | solution.py:561

commit v15 on v14

--- a/solution.py
+++ b/solution.py
@@ -12,7 +12,7 @@
 FIELDS = 5
 DEPTH = ITERS
 LANE_STEP = 2 * DEPTH + 1
-UNROLL = 4
+UNROLL = 6
 GROUP = 4
 
 VMEM = pl.BlockSpec(memory_space=pltpu.VMEM)
@@ -169,6 +169,11 @@
         copy.wait()
 
 
+def x_neighbours():
+    ix = lax.axis_index("gx")
+    return ix < lax.axis_size("gx") - 1, ix > 0
+
+
 def side_edge_kernel(x_1_ref, x_0_ref, own_edge_ref, edge_ref):
     bz, by = edge_ref.shape[1:]
     own = own_edge_ref.shape[0]
@@ -176,11 +181,14 @@
 
     def body(above, below):
         edge = jnp.zeros((DEPTH, bz, by), jnp.float32)
+        inside = x_neighbours()
         for upper, (ref, at) in enumerate(((above, 0), (below, 1))):
             block = ref[pl.ds(at, DEPTH * FIELDS)].reshape(DEPTH, FIELDS, bz, by)
+            block = jnp.where(inside[upper], block, 0.0)
             edge = add_edges(edge, [block[:, f] for f in range(FIELDS)], upper)
         edge_ref[own:] = edge
-        edge_ref[own] = add_edge(edge[0], above[DEPTH * FIELDS], FIELDS * LANE_STEP)
+        vx = jnp.where(inside[0], above[DEPTH * FIELDS], 0.0)
+        edge_ref[own] = add_edge(edge[0], vx, FIELDS * LANE_STEP)
 
     by_parity("gx", (x_0_ref, x_1_ref), body)
 
@@ -203,9 +211,10 @@
     bz, by = sides_ref.shape[1:]
 
     def body(above, below):
-        sides_ref[0:count] = above[0:count]
-        sides_ref[count : 2 * count] = below[1 : count + 1]
-        sides_ref[2 * count] = above[count]
+        inside = x_neighbours()
+        sides_ref[0:count] = jnp.where(inside[0], above[0:count], 0.0)
+        sides_ref[count : 2 * count] = jnp.where(inside[1], below[1 : count + 1], 0.0)
+        sides_ref[2 * count] = jnp.where(inside[0], above[count], 0.0)
 
     by_parity("gx", (x_0_ref, x_1_ref), body)
     tiles = sides_ref[...]
@@ -224,6 +233,8 @@
 
 def lookups(fields, ok, keep, table_ref):
     *rest, phase = fields
+    if ok is not True:
+        rest = [jnp.where(ok, a, 0.0) for a in rest]
     for number in range(3):
         rows = [divmod(number * PHASES + index, table_ref.shape[1]) for index in range(PHASES)]
         table = [table_ref[n, r : r + 1, :] for n, r in rows]
@@ -285,15 +296,14 @@
 
 
 def side_places(bx):
-    ix = lax.axis_index("gx")
-    return (pl.ds(DEPTH + bx, DEPTH), ix < lax.axis_size("gx") - 1), (pl.ds(0, DEPTH), ix > 0)
+    return zip((pl.ds(DEPTH + bx, DEPTH), pl.ds(0, DEPTH)), x_neighbours())
 
 
 def unpack_sides(load, bx, ok, tables, store, vx_ref):
     count = DEPTH * FIELDS
     for n, (planes, inside) in enumerate(side_places(bx)):
         store(planes, 0, own_lanes(load(n * count, count), ok & inside, tables))
-    vx = load(2 * count, 1)
+    vx = jnp.where(ok, load(2 * count, 1), 0.0)
     vx_ref[pl.ds(bx + 2 * DEPTH, 1), :, 0 : vx.shape[-1]] = vx
 
 
@@ -303,7 +313,7 @@
     for upper, (planes, inside) in enumerate(side_places(bx)):
         store(planes, 1, edge_lanes(edge, upper, ok & inside, tables))
     by = edge.shape[-1]
-    vx_ref[pl.ds(bx + 2 * DEPTH, 1), :, by : 2 * by] = beside(edge[0:1], FIELDS, 0)
+    vx_ref[pl.ds(bx + 2 * DEPTH, 1), :, by : 2 * by] = jnp.where(ok, beside(edge[0:1], FIELDS, 0), 0.0)
 
 
 def own_kernel(stack_ref, z_0_ref, z_1_ref, edge_ref, tables_ref, v_ref, *rest):
@@ -359,14 +369,16 @@
         unpack_own(load_both(above, below), bx, ok, tables_ref, store)
         for i in range(bx):
             n = i % half
-            next_ref[DEPTH + i, half - 1 : half, 0:by] = above[bx * FIELDS + i // half, n : n + 1, :]
+            row = above[bx * FIELDS + i // half, n : n + 1, :]
+            next_ref[DEPTH + i, half - 1 : half, 0:by] = jnp.where(ok[0, 0:1], row, 0.0)
 
     def corners(above, below):
         unpack_sides(load_both(above, below), bx, ok, tables_ref, store, halo_ref.at[0])
         for i in range(2 * DEPTH):
             n = i % half
             to = DEPTH + bx + i if i < DEPTH else i - DEPTH
-            next_ref[to, half - 1 : half, 0:by] = above[2 * DEPTH * FIELDS + 1 + i // half, n : n + 1, :]
+            row = above[2 * DEPTH * FIELDS + 1 + i // half, n : n + 1, :]
+            next_ref[to, half - 1 : half, 0:by] = jnp.where(ok[0, 0:1], row, 0.0)
 
     by_parity("gz", (face_0_ref, face_1_ref), faces)
     by_parity("gz", (corner_0_ref, corner_1_ref), corners)
@@ -386,7 +398,7 @@
         for n in range(tiles // half):
             rows = above[tiles + n]
             for upper in range(2):
-                values = beside(rows, 1, upper)
+                values = jnp.where(ok[0, 0:1], beside(rows, 1, upper), 0.0)
                 for i in range(half):
                     tile = n * half + i
                     if tile < bx // 2:
@@ -552,7 +564,10 @@
 
 def swap(a, axis, start):
     count = lax.axis_size(axis)
-    return lax.ppermute(a, axis, [(i, j) for k in range(start, count - 1, 2) for i, j in ((k, k + 1), (k + 1, k))])
+    partner = {i: i for i in range(count)}
+    for i in range(start, count - 1, 2):
+        partner[i], partner[i + 1] = i + 1, i
+    return lax.ppermute(a, axis, list(partner.items()))
 
 
 def sum_everywhere(total):

time: 44.8 us -> 44.1 us (0.984)
  Pallas kernels: 12.1 us -> 11.3 us
    pallas_call x1, Pallas kernels: 7.97 us -> 7.22 us  [local(): pl.pallas_call(main_kernel, out_shape=(block,) * 5 + (shape(bz, by),) + t...]
  transfers between devices with their start and end apart: 10 -> 10, of which waited for: 2 -> 2; matrix products, arithmetic and copies ran while one was open for 0% -> 0% of each run, Pallas kernels for 2% -> 3%
where the time goes in v15:
time: 44.1 us; the launch traced here: 43.7 us
  starting transfers between devices  18.1 us (41%)
  Pallas kernels  11.3 us (26%)
  blocking collectives  10.9 us (25%)
  waiting for transfers between devices  1.57 us (4%)
  local copies, waits for them, and re-layouts  1 us (2%)
  between operations  0.78 us (2%)
    ppermute x9, starting transfers between devices, swap(): return lax.ppermute(a, axis, list(partner.items()))  14.4 us
    all_to_all x1, blocking collectives, sum_everywhere(): lax.all_to_all(total, axes, 0, 0, tiled=True, axis_index_groups=groups)  10.9 us
    pallas_call x1, Pallas kernels, local(): pl.pallas_call(main_kernel, out_shape=(block,) * 5 + (shape(bz, by),) + t...  7.22 us
    ppermute x1, starting transfers between devices, sum_everywhere(): lax.ppermute(total, axes, [(i, i ^ 1) for i in range(devices)])  3.77 us
    pallas_call x1, Pallas kernels, local(): pl.pallas_call(pack_kernel, out_shape=(shape(bx // 2, bz, by), sent, sent...  2.24 us
    unnamed x2, local copies, waits for them, and re-layouts  0.99 us
    pallas_call x3, Pallas kernels, unpacking(): pl.pallas_call(kernel, out_shape=out_shape, in_specs=[VMEM] * len(args),...  0.91 us
  transfers between devices with their start and end apart: 10, of which 2 were waited for; matrix products, arithmetic and copies ran while one was open for 0% of the time, Pallas kernels for 3%

profile of v15, /device:TPU:0, one launch (start us, length us, event | category | flops | bytes accessed | tf_op | source)
XLA Modules:
  0.0 43.7 jit_solution(469025084558176332)
XLA Ops:
  0.6 2.2 %shard_map.119 = (f32[8,8,128]{2,1,0:T(8,128)}, f32[21,8,128]{2,1,0:T(8,128)}, f32[21,8,128]{2,1,0:T(8,128)}, f32[90,8,128]{2,1,0:T(8,128)}) custom-call(f32[16,8,128]{2,1,0:T(8,128)} %vx_hbm.1, f32[16,8,128]{2,1,0:T(8,128)} %vz_hbm.1, f32[16,8,128]{2,1,0:T(8,128)} %vy_hbm.1, f32[16,8,128]{2,1,0:T(8,128)} %p_hbm.1, s32[16,8,128]{2,1,0:T(8,128)} %phase_hbm.1, ...), custom_call_target="tpu_custom_call" | custom-call | tf_op jit(solution)/shard_map/pallas_call | solution.py:597
  2.9 1.5 %collective-permute-start = (f32[21,8,128]{2,1,0:T(8,128)}, f32[21,8,128]{2,1,0:T(8,128)S(1)}, u32[]{:S(2)}, u32[]{:S(2)}) collective-permute-start(f32[21,8,128]{2,1,0:T(8,128)} %get-tuple-element.35), channel_id=1, source_target_pairs={{0,0},{8,16},{16,8},{24,24},{1,1},{9,17},{17,9},{25,25},{2,2},{10,... | collective-permute-start | bytes 258056 | tf_op jit(solution)/shard_map/ppermute | solution.py:570
  4.4 5.0 %collective-permute-start.1 = (f32[21,8,128]{2,1,0:T(8,128)}, f32[21,8,128]{2,1,0:T(8,128)S(1)}, u32[]{:S(2)}, u32[]{:S(2)}) collective-permute-start(f32[21,8,128]{2,1,0:T(8,128)} %get-tuple-element.36), channel_id=1, source_target_pairs={{0,8},{8,0},{16,24},{24,16},{1,9},{9,1},{17,25},{25,17},{2,10},{10... | collective-permute-start | bytes 258056 | tf_op jit(solution)/shard_map/ppermute | solution.py:570
  9.5 1.0 %copy-done = f32[90,8,128]{2,1,0:T(8,128)S(1)} copy-done((f32[90,8,128]{2,1,0:T(8,128)S(1)}, f32[90,8,128]{2,1,0:T(8,128)}, u32[]{:S(2)}) %copy-start) | copy-done | bytes 368664
  10.4 0.2 shard_map.120
  10.6 0.1 collective-permute-start.3
  10.7 0.7 %collective-permute-start.4 = (f32[84,4,128]{2,1,0:T(4,128)S(1)}, f32[84,4,128]{2,1,0:T(4,128)S(1)}, u32[]{:S(2)}, u32[]{:S(2)}) collective-permute-start(f32[84,4,128]{2,1,0:T(4,128)S(1)} %get-tuple-element.52), channel_id=1, source_target_pairs={{0,0},{1,2},{2,1},{3,3},{4,4},{5,6},{6,5},{7,7},{8,8},{9,10},{10,9... | collective-permute-start | bytes 516104 | tf_op jit(solution)/shard_map/ppermute | solution.py:570
  11.4 0.0 collective-permute-done.x_1_ref
  11.4 0.7 %collective-permute-done.1.x_0_ref = f32[21,8,128]{2,1,0:T(8,128)S(1)} collective-permute-done((f32[21,8,128]{2,1,0:T(8,128)}, f32[21,8,128]{2,1,0:T(8,128)S(1)}, u32[]{:S(2)}, u32[]{:S(2)}) %collective-permute-start.1) | collective-permute-done | bytes 86048 | tf_op jit(solution)/shard_map/ppermute | solution.py:570
  12.1 0.2 shard_map.121._edge_ref
  12.3 1.6 %collective-permute-start.2 = (f32[12,8,128]{2,1,0:T(8,128)S(1)}, f32[12,8,128]{2,1,0:T(8,128)S(1)}, u32[]{:S(2)}, u32[]{:S(2)}) collective-permute-start(f32[12,8,128]{2,1,0:T(8,128)S(1)} %shard_map.121._edge_ref), channel_id=1, source_target_pairs={{0,4},{4,0},{1,5},{5,1},{2,6},{6,2},{3,7},{7,3},{8,12},{12,8},{9,1... | collective-permute-start | bytes 147464 | tf_op jit(solution)/shard_map/ppermute | solution.py:570
  13.9 0.1 shard_map.122
  13.9 2.0 %collective-permute-start.5 = (f32[43,4,128]{2,1,0:T(4,128)S(1)}, f32[43,4,128]{2,1,0:T(4,128)S(1)}, u32[]{:S(2)}, u32[]{:S(2)}) collective-permute-start(f32[43,4,128]{2,1,0:T(4,128)S(1)} %get-tuple-element.53), channel_id=1, source_target_pairs={{0,1},{1,0},{2,3},{3,2},{4,5},{5,4},{6,7},{7,6},{8,9},{9,8},{10,11... | collective-permute-start | bytes 264200 | tf_op jit(solution)/shard_map/ppermute | solution.py:570
  15.9 0.7 %collective-permute-start.6 = (f32[43,4,128]{2,1,0:T(4,128)S(1)}, f32[43,4,128]{2,1,0:T(4,128)S(1)}, u32[]{:S(2)}, u32[]{:S(2)}) collective-permute-start(f32[43,4,128]{2,1,0:T(4,128)S(1)} %get-tuple-element.54), channel_id=1, source_target_pairs={{0,0},{1,2},{2,1},{3,3},{4,4},{5,6},{6,5},{7,7},{8,8},{9,10},{10,9... | collective-permute-start | bytes 264200 | tf_op jit(solution)/shard_map/ppermute | solution.py:570
  16.5 0.0 collective-permute-done.2.edge_ref
  16.6 2.2 %collective-permute-start.7 = (f32[15,4,128]{2,1,0:T(4,128)S(1)}, f32[15,4,128]{2,1,0:T(4,128)S(1)}, u32[]{:S(2)}, u32[]{:S(2)}) collective-permute-start(f32[15,4,128]{2,1,0:T(4,128)S(1)} %get-tuple-element.57), channel_id=1, source_target_pairs={{0,1},{1,0},{2,3},{3,2},{4,5},{5,4},{6,7},{7,6},{8,9},{9,8},{10,11... | collective-permute-start | bytes 92168 | tf_op jit(solution)/shard_map/ppermute | solution.py:570
  18.8 0.7 %collective-permute-start.8 = (f32[15,4,128]{2,1,0:T(4,128)S(1)}, f32[15,4,128]{2,1,0:T(4,128)S(1)}, u32[]{:S(2)}, u32[]{:S(2)}) collective-permute-start(f32[15,4,128]{2,1,0:T(4,128)S(1)} %get-tuple-element.58), channel_id=1, source_target_pairs={{0,0},{1,2},{2,1},{3,3},{4,4},{5,6},{6,5},{7,7},{8,8},{9,10},{10,9... | collective-permute-start | bytes 92168 | tf_op jit(solution)/shard_map/ppermute | solution.py:570
  19.4 0.5 %shard_map.123 = (f32[3,25,8,256]{3,2,1,0:T(8,128)S(1)}, f32[25,8,256]{2,1,0:T(8,128)S(1)}, f32[25,8,256]{2,1,0:T(8,128)S(1)}, f32[25,8,256]{2,1,0:T(8,128)S(1)}, f32[25,8,256]{2,1,0:T(8,128)S(1)}) custom-call(f32[41,8,128]{2,1,0:T(8,128)S(1)} %get-tuple-element.39.sides_ref, ...), custom_call_target="tpu_custom_call", output_to_operand_aliasing={{0}: (3, {}), {1}: (4, {}), {2}: (5, {}), {3}: (6, {}), {4}... | custom-call | flops 2662400 | bytes 2662400 | tf_op jit(solution)/shard_map/pallas_call | solution.py:629
  20.0 0.2 shard_map.124
  20.2 7.2 %shard_map.126 = (f32[16,8,128]{2,1,0:T(8,128)}, f32[16,8,128]{2,1,0:T(8,128)}, f32[16,8,128]{2,1,0:T(8,128)}, f32[16,8,128]{2,1,0:T(8,128)S(1)}, f32[16,8,128]{...) custom-call(f32[3,25,8,256]{3,2,1,0:T(8,128)S(1)} %get-tuple-element, ...), custom_call_target="tpu_custom_call", output_to_operand_aliasing={{6}: (5, {}), {7}: (6, {})} | custom-call | tf_op jit(solution)/shard_map/pallas_call | solution.py:682
  27.4 3.8 %collective-permute-start.9 = (f32[8,128]{1,0:T(8,128)S(1)}, f32[8,128]{1,0:T(8,128)S(1)}, u32[]{:S(2)}, u32[]{:S(2)}) collective-permute-start(f32[8,128]{1,0:T(8,128)S(1)} %get-tuple-element.63), channel_id=1, source_target_pairs={{0,1},{1,0},{2,3},{3,2},{4,5},{5,4},{6,7},{7,6},{8,9},{9,8},{10,11... | collective-permute-start | bytes 12296 | tf_op jit(solution)/shard_map/ppermute | solution.py:576
  31.2 0.8 %collective-permute-done.9 = f32[8,128]{1,0:T(8,128)S(1)} collective-permute-done((f32[8,128]{1,0:T(8,128)S(1)}, f32[8,128]{1,0:T(8,128)S(1)}, u32[]{:S(2)}, u32[]{:S(2)}) %collective-permute-start.9) | collective-permute-done | bytes 4128 | tf_op jit(solution)/shard_map/ppermute | solution.py:576
  32.1 10.9 %all_to_all.8 = f32[16,1,128]{2,1,0:T(1,128)S(1)} all-to-all(f32[16,1,128]{2,1,0:T(1,128)S(1)} %broadcast_in_dim.2), channel_id=1, replica_groups={{0,2,4,6,8,10,12,14,16,18,20,22,24,26,28,30},{1,3,5,7,9,11,13,15,17,19,..., dimensions={0} | all-to-all | bytes 16384 | tf_op jit(solution)/shard_map/all_to_all | solution.py:579
  43.0 0.8 %shard_map.127 = f32[16,8,128]{2,1,0:T(8,128)} custom-call(f32[16,8,128]{2,1,0:T(8,128)S(1)} %get-tuple-element.62.refs_0_, f32[16,128]{1,0:T(8,128)S(1)} %bitcast.1), custom_call_target="tpu_custom_call" | custom-call | tf_op jit(solution)/shard_map/pallas_call | solution.py:698
  (10 shorter events, 0.1 us)
Async XLA Ops:
  2.9 8.5 %collective-permute-start = (f32[21,8,128]{2,1,0:T(8,128)}, f32[21,8,128]{2,1,0:T(8,128)S(1)}, u32[]{:S(2)}, u32[]{:S(2)}) collective-permute-start(f32[21,8,128]{2,1,0:T(8,128)} %get-tuple-element.35), channel_id=1, source_target_pairs={{0,0},{8,16},{16,8},{24,24},{1,1},{9,17},{17,9},{25,25},{2,2},{10,... | collective-permute-start | bytes 258056 | tf_op jit(solution)/shard_map/ppermute | solution.py:570
  4.4 7.7 %collective-permute-start.1 = (f32[21,8,128]{2,1,0:T(8,128)}, f32[21,8,128]{2,1,0:T(8,128)S(1)}, u32[]{:S(2)}, u32[]{:S(2)}) collective-permute-start(f32[21,8,128]{2,1,0:T(8,128)} %get-tuple-element.36), channel_id=1, source_target_pairs={{0,8},{8,0},{16,24},{24,16},{1,9},{9,1},{17,25},{25,17},{2,10},{10... | collective-permute-start | bytes 258056 | tf_op jit(solution)/shard_map/ppermute | solution.py:570
  9.5 1.0 %copy-start = (f32[90,8,128]{2,1,0:T(8,128)S(1)}, f32[90,8,128]{2,1,0:T(8,128)}, u32[]{:S(2)}) copy-start(f32[90,8,128]{2,1,0:T(8,128)} %get-tuple-element.37.stack_ref) | copy-start | bytes 1105924
  10.6 8.1 %collective-permute-start.3 = (f32[84,4,128]{2,1,0:T(4,128)S(1)}, f32[84,4,128]{2,1,0:T(4,128)S(1)}, u32[]{:S(2)}, u32[]{:S(2)}) collective-permute-start(f32[84,4,128]{2,1,0:T(4,128)S(1)} %get-tuple-element.51), channel_id=1, source_target_pairs={{0,1},{1,0},{2,3},{3,2},{4,5},{5,4},{6,7},{7,6},{8,9},{9,8},{10,11... | collective-permute-start | bytes 516104 | tf_op jit(solution)/shard_map/ppermute | solution.py:570
  10.7 9.2 %collective-permute-start.4 = (f32[84,4,128]{2,1,0:T(4,128)S(1)}, f32[84,4,128]{2,1,0:T(4,128)S(1)}, u32[]{:S(2)}, u32[]{:S(2)}) collective-permute-start(f32[84,4,128]{2,1,0:T(4,128)S(1)} %get-tuple-element.52), channel_id=1, source_target_pairs={{0,0},{1,2},{2,1},{3,3},{4,4},{5,6},{6,5},{7,7},{8,8},{9,10},{10,9... | collective-permute-start | bytes 516104 | tf_op jit(solution)/shard_map/ppermute | solution.py:570
  12.3 4.2 %collective-permute-start.2 = (f32[12,8,128]{2,1,0:T(8,128)S(1)}, f32[12,8,128]{2,1,0:T(8,128)S(1)}, u32[]{:S(2)}, u32[]{:S(2)}) collective-permute-start(f32[12,8,128]{2,1,0:T(8,128)S(1)} %shard_map.121._edge_ref), channel_id=1, source_target_pairs={{0,4},{4,0},{1,5},{5,1},{2,6},{6,2},{3,7},{7,3},{8,12},{12,8},{9,1... | collective-permute-start | bytes 147464 | tf_op jit(solution)/shard_map/ppermute | solution.py:570
  13.9 6.1 %collective-permute-start.5 = (f32[43,4,128]{2,1,0:T(4,128)S(1)}, f32[43,4,128]{2,1,0:T(4,128)S(1)}, u32[]{:S(2)}, u32[]{:S(2)}) collective-permute-start(f32[43,4,128]{2,1,0:T(4,128)S(1)} %get-tuple-element.53), channel_id=1, source_target_pairs={{0,1},{1,0},{2,3},{3,2},{4,5},{5,4},{6,7},{7,6},{8,9},{9,8},{10,11... | collective-permute-start | bytes 264200 | tf_op jit(solution)/shard_map/ppermute | solution.py:570
  15.9 4.1 %collective-permute-start.6 = (f32[43,4,128]{2,1,0:T(4,128)S(1)}, f32[43,4,128]{2,1,0:T(4,128)S(1)}, u32[]{:S(2)}, u32[]{:S(2)}) collective-permute-start(f32[43,4,128]{2,1,0:T(4,128)S(1)} %get-tuple-element.54), channel_id=1, source_target_pairs={{0,0},{1,2},{2,1},{3,3},{4,4},{5,6},{6,5},{7,7},{8,8},{9,10},{10,9... | collective-permute-start | bytes 264200 | tf_op jit(solution)/shard_map/ppermute | solution.py:570
  16.6 3.6 %collective-permute-start.7 = (f32[15,4,128]{2,1,0:T(4,128)S(1)}, f32[15,4,128]{2,1,0:T(4,128)S(1)}, u32[]{:S(2)}, u32[]{:S(2)}) collective-permute-start(f32[15,4,128]{2,1,0:T(4,128)S(1)} %get-tuple-element.57), channel_id=1, source_target_pairs={{0,1},{1,0},{2,3},{3,2},{4,5},{5,4},{6,7},{7,6},{8,9},{9,8},{10,11... | collective-permute-start | bytes 92168 | tf_op jit(solution)/shard_map/ppermute | solution.py:570
  18.8 1.4 %collective-permute-start.8 = (f32[15,4,128]{2,1,0:T(4,128)S(1)}, f32[15,4,128]{2,1,0:T(4,128)S(1)}, u32[]{:S(2)}, u32[]{:S(2)}) collective-permute-start(f32[15,4,128]{2,1,0:T(4,128)S(1)} %get-tuple-element.58), channel_id=1, source_target_pairs={{0,0},{1,2},{2,1},{3,3},{4,4},{5,6},{6,5},{7,7},{8,8},{9,10},{10,9... | collective-permute-start | bytes 92168 | tf_op jit(solution)/shard_map/ppermute | solution.py:570
  27.4 4.6 %collective-permute-start.9 = (f32[8,128]{1,0:T(8,128)S(1)}, f32[8,128]{1,0:T(8,128)S(1)}, u32[]{:S(2)}, u32[]{:S(2)}) collective-permute-start(f32[8,128]{1,0:T(8,128)S(1)} %get-tuple-element.63), channel_id=1, source_target_pairs={{0,1},{1,0},{2,3},{3,2},{4,5},{5,4},{6,7},{7,6},{8,9},{9,8},{10,11... | collective-permute-start | bytes 12296 | tf_op jit(solution)/shard_map/ppermute | solution.py:576

commit v16 on v14

--- a/solution.py
+++ b/solution.py
@@ -12,7 +12,7 @@
 FIELDS = 5
 DEPTH = ITERS
 LANE_STEP = 2 * DEPTH + 1
-UNROLL = 4
+UNROLL = 8
 GROUP = 4
 
 VMEM = pl.BlockSpec(memory_space=pltpu.VMEM)
@@ -36,8 +36,7 @@
 
 
 def reciprocal(a):
-    r = pl.reciprocal(a, approx=True)
-    return r * (2.0 - a * r)
+    return pl.reciprocal(a, approx=True)
 
 
 def iota(shape, axis):

time: 44.8 us -> 43.7 us (0.975)
  Pallas kernels: 12.1 us -> 11 us
    pallas_call x1, Pallas kernels: 7.97 us -> 6.93 us  [local(): pl.pallas_call(main_kernel, out_shape=(block,) * 5 + (shape(bz, by),) + t...]
where the time goes in v16:
time: 43.7 us; the launch traced here: 43.4 us
  starting transfers between devices  18.1 us (41%)
  Pallas kernels  11 us (25%)
  blocking collectives  10.9 us (25%)
  waiting for transfers between devices  1.58 us (4%)
  local copies, waits for them, and re-layouts  1 us (2%)
  between operations  0.79 us (2%)
    ppermute x9, starting transfers between devices, swap(): lax.ppermute(a, axis, [(i, j) for k in range(start, count - 1, 2) for i,...  14.3 us
    all_to_all x1, blocking collectives, sum_everywhere(): lax.all_to_all(total, axes, 0, 0, tiled=True, axis_index_groups=groups)  10.9 us
    pallas_call x1, Pallas kernels, local(): pl.pallas_call(main_kernel, out_shape=(block,) * 5 + (shape(bz, by),) + t...  6.93 us
    ppermute x1, starting transfers between devices, sum_everywhere(): lax.ppermute(total, axes, [(i, i ^ 1) for i in range(devices)])  3.81 us
    pallas_call x1, Pallas kernels, local(): pl.pallas_call(pack_kernel, out_shape=(shape(bx // 2, bz, by), sent, sent...  2.24 us
    unnamed x2, local copies, waits for them, and re-layouts  0.99 us
  transfers between devices with their start and end apart: 10, of which 2 were waited for; matrix products, arithmetic and copies ran while one was open for 0% of the time, Pallas kernels for 2%

profile of v16, /device:TPU:0, one launch (start us, length us, event | category | flops | bytes accessed | tf_op | source)
XLA Modules:
  0.0 43.4 jit_solution(16370489349064468884)
XLA Ops:
  0.6 2.2 %shard_map.119 = (f32[8,8,128]{2,1,0:T(8,128)}, f32[21,8,128]{2,1,0:T(8,128)}, f32[21,8,128]{2,1,0:T(8,128)}, f32[90,8,128]{2,1,0:T(8,128)}) custom-call(f32[16,8,128]{2,1,0:T(8,128)} %vx_hbm.1, f32[16,8,128]{2,1,0:T(8,128)} %vz_hbm.1, f32[16,8,128]{2,1,0:T(8,128)} %vy_hbm.1, f32[16,8,128]{2,1,0:T(8,128)} %p_hbm.1, s32[16,8,128]{2,1,0:T(8,128)} %phase_hbm.1, ...), custom_call_target="tpu_custom_call" | custom-call | tf_op jit(solution)/shard_map/pallas_call | solution.py:581
  2.9 0.7 %collective-permute-start = (f32[21,8,128]{2,1,0:T(8,128)}, f32[21,8,128]{2,1,0:T(8,128)S(1)}, u32[]{:S(2)}, u32[]{:S(2)}) collective-permute-start(f32[21,8,128]{2,1,0:T(8,128)} %get-tuple-element.35), channel_id=1, source_target_pairs={{8,16},{16,8},{9,17},{17,9},{10,18},{18,10},{11,19},{19,11},{12,20... | collective-permute-start | bytes 258056 | tf_op jit(solution)/shard_map/ppermute | solution.py:554
  3.6 5.9 %collective-permute-start.1 = (f32[21,8,128]{2,1,0:T(8,128)}, f32[21,8,128]{2,1,0:T(8,128)S(1)}, u32[]{:S(2)}, u32[]{:S(2)}) collective-permute-start(f32[21,8,128]{2,1,0:T(8,128)} %get-tuple-element.36), channel_id=1, source_target_pairs={{0,8},{8,0},{16,24},{24,16},{1,9},{9,1},{17,25},{25,17},{2,10},{10... | collective-permute-start | bytes 258056 | tf_op jit(solution)/shard_map/ppermute | solution.py:554
  9.5 1.0 %copy-done = f32[90,8,128]{2,1,0:T(8,128)S(1)} copy-done((f32[90,8,128]{2,1,0:T(8,128)S(1)}, f32[90,8,128]{2,1,0:T(8,128)}, u32[]{:S(2)}) %copy-start) | copy-done | bytes 368664
  10.4 0.2 shard_map.120
  10.6 0.1 collective-permute-start.3
  10.7 0.7 %collective-permute-start.4 = (f32[84,4,128]{2,1,0:T(4,128)S(1)}, f32[84,4,128]{2,1,0:T(4,128)S(1)}, u32[]{:S(2)}, u32[]{:S(2)}) collective-permute-start(f32[84,4,128]{2,1,0:T(4,128)S(1)} %get-tuple-element.52), channel_id=1, source_target_pairs={{1,2},{2,1},{5,6},{6,5},{9,10},{10,9},{13,14},{14,13},{17,18},{18,... | collective-permute-start | bytes 516104 | tf_op jit(solution)/shard_map/ppermute | solution.py:554
  11.4 0.7 %collective-permute-done.1.x_0_ref = f32[21,8,128]{2,1,0:T(8,128)S(1)} collective-permute-done((f32[21,8,128]{2,1,0:T(8,128)}, f32[21,8,128]{2,1,0:T(8,128)S(1)}, u32[]{:S(2)}, u32[]{:S(2)}) %collective-permute-start.1) | collective-permute-done | bytes 86048 | tf_op jit(solution)/shard_map/ppermute | solution.py:554
  12.1 0.1 shard_map.121._edge_ref
  12.3 1.6 %collective-permute-start.2 = (f32[12,8,128]{2,1,0:T(8,128)S(1)}, f32[12,8,128]{2,1,0:T(8,128)S(1)}, u32[]{:S(2)}, u32[]{:S(2)}) collective-permute-start(f32[12,8,128]{2,1,0:T(8,128)S(1)} %shard_map.121._edge_ref), channel_id=1, source_target_pairs={{0,4},{4,0},{1,5},{5,1},{2,6},{6,2},{3,7},{7,3},{8,12},{12,8},{9,1... | collective-permute-start | bytes 147464 | tf_op jit(solution)/shard_map/ppermute | solution.py:554
  13.9 1.9 %collective-permute-start.5 = (f32[43,4,128]{2,1,0:T(4,128)S(1)}, f32[43,4,128]{2,1,0:T(4,128)S(1)}, u32[]{:S(2)}, u32[]{:S(2)}) collective-permute-start(f32[43,4,128]{2,1,0:T(4,128)S(1)} %get-tuple-element.53), channel_id=1, source_target_pairs={{0,1},{1,0},{2,3},{3,2},{4,5},{5,4},{6,7},{7,6},{8,9},{9,8},{10,11... | collective-permute-start | bytes 264200 | tf_op jit(solution)/shard_map/ppermute | solution.py:554
  15.8 0.7 %collective-permute-start.6 = (f32[43,4,128]{2,1,0:T(4,128)S(1)}, f32[43,4,128]{2,1,0:T(4,128)S(1)}, u32[]{:S(2)}, u32[]{:S(2)}) collective-permute-start(f32[43,4,128]{2,1,0:T(4,128)S(1)} %get-tuple-element.54), channel_id=1, source_target_pairs={{1,2},{2,1},{5,6},{6,5},{9,10},{10,9},{13,14},{14,13},{17,18},{18,... | collective-permute-start | bytes 264200 | tf_op jit(solution)/shard_map/ppermute | solution.py:554
  16.5 2.2 %collective-permute-start.7 = (f32[15,4,128]{2,1,0:T(4,128)S(1)}, f32[15,4,128]{2,1,0:T(4,128)S(1)}, u32[]{:S(2)}, u32[]{:S(2)}) collective-permute-start(f32[15,4,128]{2,1,0:T(4,128)S(1)} %get-tuple-element.57), channel_id=1, source_target_pairs={{0,1},{1,0},{2,3},{3,2},{4,5},{5,4},{6,7},{7,6},{8,9},{9,8},{10,11... | collective-permute-start | bytes 92168 | tf_op jit(solution)/shard_map/ppermute | solution.py:554
  18.8 0.7 %collective-permute-start.8 = (f32[15,4,128]{2,1,0:T(4,128)S(1)}, f32[15,4,128]{2,1,0:T(4,128)S(1)}, u32[]{:S(2)}, u32[]{:S(2)}) collective-permute-start(f32[15,4,128]{2,1,0:T(4,128)S(1)} %get-tuple-element.58), channel_id=1, source_target_pairs={{1,2},{2,1},{5,6},{6,5},{9,10},{10,9},{13,14},{14,13},{17,18},{18,... | collective-permute-start | bytes 92168 | tf_op jit(solution)/shard_map/ppermute | solution.py:554
  19.4 0.5 %shard_map.123 = (f32[3,25,8,256]{3,2,1,0:T(8,128)S(1)}, f32[25,8,256]{2,1,0:T(8,128)S(1)}, f32[25,8,256]{2,1,0:T(8,128)S(1)}, f32[25,8,256]{2,1,0:T(8,128)S(1)}, f32[25,8,256]{2,1,0:T(8,128)S(1)}) custom-call(f32[41,8,128]{2,1,0:T(8,128)S(1)} %get-tuple-element.39.sides_ref, ...), custom_call_target="tpu_custom_call", output_to_operand_aliasing={{0}: (3, {}), {1}: (4, {}), {2}: (5, {}), {3}: (6, {}), {4}... | custom-call | flops 2662400 | bytes 2662400 | tf_op jit(solution)/shard_map/pallas_call | solution.py:613
  19.9 0.0 collective-permute-done.4.face_1_ref
  19.9 0.0 collective-permute-done.5.corner_0_ref
  20.0 0.2 shard_map.124
  20.1 0.0 collective-permute-done.7.edge_0_ref
  20.2 6.9 %shard_map.126 = (f32[16,8,128]{2,1,0:T(8,128)}, f32[16,8,128]{2,1,0:T(8,128)}, f32[16,8,128]{2,1,0:T(8,128)}, f32[16,8,128]{2,1,0:T(8,128)S(1)}, f32[16,8,128]{...) custom-call(f32[3,25,8,256]{3,2,1,0:T(8,128)S(1)} %get-tuple-element, ...), custom_call_target="tpu_custom_call", output_to_operand_aliasing={{6}: (5, {}), {7}: (6, {})} | custom-call | tf_op jit(solution)/shard_map/pallas_call | solution.py:666
  27.1 3.8 %collective-permute-start.9 = (f32[8,128]{1,0:T(8,128)S(1)}, f32[8,128]{1,0:T(8,128)S(1)}, u32[]{:S(2)}, u32[]{:S(2)}) collective-permute-start(f32[8,128]{1,0:T(8,128)S(1)} %get-tuple-element.63), channel_id=1, source_target_pairs={{0,1},{1,0},{2,3},{3,2},{4,5},{5,4},{6,7},{7,6},{8,9},{9,8},{10,11... | collective-permute-start | bytes 12296 | tf_op jit(solution)/shard_map/ppermute | solution.py:560
  30.9 0.8 %collective-permute-done.9 = f32[8,128]{1,0:T(8,128)S(1)} collective-permute-done((f32[8,128]{1,0:T(8,128)S(1)}, f32[8,128]{1,0:T(8,128)S(1)}, u32[]{:S(2)}, u32[]{:S(2)}) %collective-permute-start.9) | collective-permute-done | bytes 4128 | tf_op jit(solution)/shard_map/ppermute | solution.py:560
  31.7 10.9 %all_to_all.8 = f32[16,1,128]{2,1,0:T(1,128)S(1)} all-to-all(f32[16,1,128]{2,1,0:T(1,128)S(1)} %broadcast_in_dim.2), channel_id=1, replica_groups={{0,2,4,6,8,10,12,14,16,18,20,22,24,26,28,30},{1,3,5,7,9,11,13,15,17,19,..., dimensions={0} | all-to-all | bytes 16384 | tf_op jit(solution)/shard_map/all_to_all | solution.py:563
  42.7 0.8 %shard_map.127 = f32[16,8,128]{2,1,0:T(8,128)} custom-call(f32[16,8,128]{2,1,0:T(8,128)S(1)} %get-tuple-element.62.refs_0_, f32[16,128]{1,0:T(8,128)S(1)} %bitcast.1), custom_call_target="tpu_custom_call" | custom-call | tf_op jit(solution)/shard_map/pallas_call | solution.py:682
  (10 shorter events, 0.1 us)
Async XLA Ops:
  2.9 8.5 %collective-permute-start = (f32[21,8,128]{2,1,0:T(8,128)}, f32[21,8,128]{2,1,0:T(8,128)S(1)}, u32[]{:S(2)}, u32[]{:S(2)}) collective-permute-start(f32[21,8,128]{2,1,0:T(8,128)} %get-tuple-element.35), channel_id=1, source_target_pairs={{8,16},{16,8},{9,17},{17,9},{10,18},{18,10},{11,19},{19,11},{12,20... | collective-permute-start | bytes 258056 | tf_op jit(solution)/shard_map/ppermute | solution.py:554
  3.6 8.6 %collective-permute-start.1 = (f32[21,8,128]{2,1,0:T(8,128)}, f32[21,8,128]{2,1,0:T(8,128)S(1)}, u32[]{:S(2)}, u32[]{:S(2)}) collective-permute-start(f32[21,8,128]{2,1,0:T(8,128)} %get-tuple-element.36), channel_id=1, source_target_pairs={{0,8},{8,0},{16,24},{24,16},{1,9},{9,1},{17,25},{25,17},{2,10},{10... | collective-permute-start | bytes 258056 | tf_op jit(solution)/shard_map/ppermute | solution.py:554
  9.5 1.0 %copy-start = (f32[90,8,128]{2,1,0:T(8,128)S(1)}, f32[90,8,128]{2,1,0:T(8,128)}, u32[]{:S(2)}) copy-start(f32[90,8,128]{2,1,0:T(8,128)} %get-tuple-element.37.stack_ref) | copy-start | bytes 1105924
  10.6 8.1 %collective-permute-start.3 = (f32[84,4,128]{2,1,0:T(4,128)S(1)}, f32[84,4,128]{2,1,0:T(4,128)S(1)}, u32[]{:S(2)}, u32[]{:S(2)}) collective-permute-start(f32[84,4,128]{2,1,0:T(4,128)S(1)} %get-tuple-element.51), channel_id=1, source_target_pairs={{0,1},{1,0},{2,3},{3,2},{4,5},{5,4},{6,7},{7,6},{8,9},{9,8},{10,11... | collective-permute-start | bytes 516104 | tf_op jit(solution)/shard_map/ppermute | solution.py:554
  10.7 9.2 %collective-permute-start.4 = (f32[84,4,128]{2,1,0:T(4,128)S(1)}, f32[84,4,128]{2,1,0:T(4,128)S(1)}, u32[]{:S(2)}, u32[]{:S(2)}) collective-permute-start(f32[84,4,128]{2,1,0:T(4,128)S(1)} %get-tuple-element.52), channel_id=1, source_target_pairs={{1,2},{2,1},{5,6},{6,5},{9,10},{10,9},{13,14},{14,13},{17,18},{18,... | collective-permute-start | bytes 516104 | tf_op jit(solution)/shard_map/ppermute | solution.py:554
  12.3 4.2 %collective-permute-start.2 = (f32[12,8,128]{2,1,0:T(8,128)S(1)}, f32[12,8,128]{2,1,0:T(8,128)S(1)}, u32[]{:S(2)}, u32[]{:S(2)}) collective-permute-start(f32[12,8,128]{2,1,0:T(8,128)S(1)} %shard_map.121._edge_ref), channel_id=1, source_target_pairs={{0,4},{4,0},{1,5},{5,1},{2,6},{6,2},{3,7},{7,3},{8,12},{12,8},{9,1... | collective-permute-start | bytes 147464 | tf_op jit(solution)/shard_map/ppermute | solution.py:554
  13.9 6.0 %collective-permute-start.5 = (f32[43,4,128]{2,1,0:T(4,128)S(1)}, f32[43,4,128]{2,1,0:T(4,128)S(1)}, u32[]{:S(2)}, u32[]{:S(2)}) collective-permute-start(f32[43,4,128]{2,1,0:T(4,128)S(1)} %get-tuple-element.53), channel_id=1, source_target_pairs={{0,1},{1,0},{2,3},{3,2},{4,5},{5,4},{6,7},{7,6},{8,9},{9,8},{10,11... | collective-permute-start | bytes 264200 | tf_op jit(solution)/shard_map/ppermute | solution.py:554
  15.8 4.1 %collective-permute-start.6 = (f32[43,4,128]{2,1,0:T(4,128)S(1)}, f32[43,4,128]{2,1,0:T(4,128)S(1)}, u32[]{:S(2)}, u32[]{:S(2)}) collective-permute-start(f32[43,4,128]{2,1,0:T(4,128)S(1)} %get-tuple-element.54), channel_id=1, source_target_pairs={{1,2},{2,1},{5,6},{6,5},{9,10},{10,9},{13,14},{14,13},{17,18},{18,... | collective-permute-start | bytes 264200 | tf_op jit(solution)/shard_map/ppermute | solution.py:554
  16.5 3.6 %collective-permute-start.7 = (f32[15,4,128]{2,1,0:T(4,128)S(1)}, f32[15,4,128]{2,1,0:T(4,128)S(1)}, u32[]{:S(2)}, u32[]{:S(2)}) collective-permute-start(f32[15,4,128]{2,1,0:T(4,128)S(1)} %get-tuple-element.57), channel_id=1, source_target_pairs={{0,1},{1,0},{2,3},{3,2},{4,5},{5,4},{6,7},{7,6},{8,9},{9,8},{10,11... | collective-permute-start | bytes 92168 | tf_op jit(solution)/shard_map/ppermute | solution.py:554
  18.8 1.4 %collective-permute-start.8 = (f32[15,4,128]{2,1,0:T(4,128)S(1)}, f32[15,4,128]{2,1,0:T(4,128)S(1)}, u32[]{:S(2)}, u32[]{:S(2)}) collective-permute-start(f32[15,4,128]{2,1,0:T(4,128)S(1)} %get-tuple-element.58), channel_id=1, source_target_pairs={{1,2},{2,1},{5,6},{6,5},{9,10},{10,9},{13,14},{14,13},{17,18},{18,... | collective-permute-start | bytes 92168 | tf_op jit(solution)/shard_map/ppermute | solution.py:554
  27.1 4.6 %collective-permute-start.9 = (f32[8,128]{1,0:T(8,128)S(1)}, f32[8,128]{1,0:T(8,128)S(1)}, u32[]{:S(2)}, u32[]{:S(2)}) collective-permute-start(f32[8,128]{1,0:T(8,128)S(1)} %get-tuple-element.63), channel_id=1, source_target_pairs={{0,1},{1,0},{2,3},{3,2},{4,5},{5,4},{6,7},{7,6},{8,9},{9,8},{10,11... | collective-permute-start | bytes 12296 | tf_op jit(solution)/shard_map/ppermute | solution.py:560

commit v17 on v16

--- a/solution.py
+++ b/solution.py
@@ -12,7 +12,7 @@
 FIELDS = 5
 DEPTH = ITERS
 LANE_STEP = 2 * DEPTH + 1
-UNROLL = 8
+UNROLL = 12
 GROUP = 4
 
 VMEM = pl.BlockSpec(memory_space=pltpu.VMEM)
@@ -116,31 +116,56 @@
     table_copies = [pltpu.make_async_copy(a, b, table_sems.at[n]) for n, (a, b) in enumerate(pairs)]
     for copy in table_copies:
         copy.start()
-    half = bx // GROUP // 2
+    groups = bx // GROUP
+    half = groups // 2
     outs = []
 
     def out(source, target):
         outs.append(pltpu.make_async_copy(source, target, out_sems.at[len(outs)]))
         outs[-1].start()
 
-    for g in range(half):
-        edge = jnp.zeros((GROUP, bz, by), jnp.float32)
-        for upper in range(2):
-            at = (g + upper * half) * GROUP
-            for copy in copies[g + upper * half]:
-                copy.wait()
-            fields = clean_group(g + upper * half, field_ref, phase_ref)
-            for f, a in enumerate(fields):
-                for i in range(GROUP):
-                    stack_ref[(at + i) * FIELDS + f] = a[i]
-            edge = add_edges(edge, fields, upper)
-            at = pl.ds(at * FIELDS, GROUP * FIELDS)
-            out(stack_ref.at[at], stack_hbm.at[at])
-        at = pl.ds(g * GROUP, GROUP)
-        edge_ref[at] = edge
-        out(edge_ref.at[at], edge_hbm.at[at])
-        stack_ref[pl.ds(bx * FIELDS + g * GROUP, GROUP)] = edge
-    count = bx * FIELDS + bx // 2
+    count = DEPTH * FIELDS
+    sems_x = [out_sems.at[out_sems.shape[0] - 1 - n] for n in range(3)]
+
+    def x_copies(to_above, to_below):
+        return (
+            pltpu.make_async_copy(stack_ref.at[pl.ds(0, count + 1)], to_below, sems_x[0]),
+            pltpu.make_async_copy(stack_ref.at[pl.ds(0, 1)], to_above.at[pl.ds(0, 1)], sems_x[1]),
+            pltpu.make_async_copy(
+                stack_ref.at[pl.ds(bx * FIELDS - count, count)], to_above.at[pl.ds(1, count)], sems_x[2]
+            ),
+        )
+
+    def start_x(above, below):
+        for copy in x_copies(above, below):
+            copy.start()
+
+    def wait_x(above, below):
+        for copy in x_copies(above, below):
+            copy.wait()
+
+    edges = {}
+    order = [0, groups - 1] + list(range(1, groups - 1))
+    for g in order:
+        for copy in copies[g]:
+            copy.wait()
+        fields = clean_group(g, field_ref, phase_ref)
+        for f, a in enumerate(fields):
+            for i in range(GROUP):
+                stack_ref[(g * GROUP + i) * FIELDS + f] = a[i]
+        at = pl.ds(g * GROUP * FIELDS, GROUP * FIELDS)
+        out(stack_ref.at[at], stack_hbm.at[at])
+        if g == 1:
+            by_parity("gx", (x_0_hbm, x_1_hbm), start_x)
+        upper, n = divmod(g, half)
+        edge = edges.get(n, jnp.zeros((GROUP, bz, by), jnp.float32))
+        edges[n] = add_edges(edge, fields, upper)
+        if n + half * (1 - upper) in order[: order.index(g)]:
+            at = pl.ds(n * GROUP, GROUP)
+            edge_ref[at] = edges[n]
+            out(edge_ref.at[at], edge_hbm.at[at])
+            stack_ref[pl.ds(bx * FIELDS + n * GROUP, GROUP)] = edges[n]
+    end = bx * FIELDS + bx // 2
     row = iota((bz, by), 0)
     for copy in table_copies:
         copy.wait()
@@ -149,21 +174,10 @@
         tile = jnp.zeros((bz, by), jnp.float32)
         for r, entry in enumerate(entries[n * bz : (n + 1) * bz]):
             tile = jnp.where(row == r, entry, tile)
-        stack_ref[count + n] = tile
-    at = pl.ds(bx * FIELDS, count + 2 - bx * FIELDS)
+        stack_ref[end + n] = tile
+    at = pl.ds(bx * FIELDS, end + 2 - bx * FIELDS)
     out(stack_ref.at[at], stack_hbm.at[at])
-    count = x_0_hbm.shape[0]
-    down, up = stack_ref.at[pl.ds(0, count)], stack_ref.at[pl.ds(bx * FIELDS - count, count)]
-    sem = out_sems.at[len(outs)], out_sems.at[len(outs) + 1]
-
-    def send(to_above, to_below):
-        pair = pltpu.make_async_copy(up, to_above, sem[0]), pltpu.make_async_copy(down, to_below, sem[1])
-        for copy in pair:
-            copy.start()
-        for copy in pair:
-            copy.wait()
-
-    by_parity("gx", (x_0_hbm, x_1_hbm), send)
+    by_parity("gx", (x_0_hbm, x_1_hbm), wait_x)
     for copy in outs:
         copy.wait()
 
@@ -305,8 +319,26 @@
     vx_ref[pl.ds(bx + 2 * DEPTH, 1), :, by : 2 * by] = beside(edge[0:1], FIELDS, 0)
 
 
-def own_kernel(stack_ref, z_0_ref, z_1_ref, edge_ref, tables_ref, v_ref, *rest):
+def make_weights(weight_ref):
+    shape = weight_ref.shape[1:]
+    rows, lanes = shape
+    bz, by = rows // 2, lanes // 2
+    nz, ny = lax.axis_size("gz"), lax.axis_size("gy")
+    iz, iy = lax.axis_index("gz"), lax.axis_index("gy")
+    r, c = iota(shape, 0), iota(shape, 1)
+    zg = iz * bz + jnp.where(r < bz + bz // 2, r, r - rows)
+    yg = iy * by + jnp.where(c <= by + DEPTH, c, c - lanes)
+    filled = (c <= by + DEPTH) | (c >= lanes - DEPTH)
+    inside = filled & (zg >= 0) & (zg < nz * bz) & (yg >= 0) & (yg < ny * by)
+    weight_ref[0] = jnp.where(inside, 0.05, 0.0)
+    weight_ref[1] = jnp.where(inside & (zg > 0), 0.05, 0.0)
+    weight_ref[2] = jnp.where(inside & (yg > 0), 0.05, 0.0)
+    weight_ref[3] = jnp.where(inside, 0.0, 1.0)
+
+
+def own_kernel(stack_ref, z_0_ref, z_1_ref, edge_ref, tables_ref, weight_ref, v_ref, *rest):
     bx = v_ref.shape[1] - 2 * DEPTH - 1
+    make_weights(weight_ref)
     count = bx * FIELDS
     edge_ref[...] = stack_ref[count : count + bx // 2]
     tables_ref[...] = stack_ref[count + bx // 2 :]
@@ -398,26 +430,14 @@
 
 
 def main_kernel(
-    v_ref, p0_ref, pre_ref, power_field_ref, rho_ref, _halo, _next, edge_0_ref, edge_1_ref, tables_ref,
+    v_ref, p0_ref, pre_ref, power_field_ref, rho_ref, _halo, _next, edge_0_ref, edge_1_ref, tables_ref, weight_ref,
     out_vx_ref, out_vz_ref, out_vy_ref, out_p_ref, out_eta_ref, sum_ref, halo_ref, next_ref,
-    va_ref, vb_ref, p_ref, weight_ref,
+    va_ref, vb_ref, p_ref,
 ):
     bx, bz, by = out_p_ref.shape
     rows, lanes = 2 * bz, 2 * by
-    nx, nz, ny = lax.axis_size("gx"), lax.axis_size("gz"), lax.axis_size("gy")
-    ix, iz, iy = lax.axis_index("gx"), lax.axis_index("gz"), lax.axis_index("gy")
+    nx, ix = lax.axis_size("gx"), lax.axis_index("gx")
     unpack_halo_edges(edge_0_ref, edge_1_ref, tables_ref, halo_ref, next_ref)
-
-    shape = (rows, lanes)
-    r, c = iota(shape, 0), iota(shape, 1)
-    zg = iz * bz + jnp.where(r < bz + bz // 2, r, r - rows)
-    yg = iy * by + jnp.where(c <= by + DEPTH, c, c - lanes)
-    filled = (c <= by + DEPTH) | (c >= lanes - DEPTH)
-    inside = filled & (zg >= 0) & (zg < nz * bz) & (yg >= 0) & (yg < ny * by)
-    weight_ref[0] = jnp.where(inside, 0.05, 0.0)
-    weight_ref[1] = jnp.where(inside & (zg > 0), 0.05, 0.0)
-    weight_ref[2] = jnp.where(inside & (yg > 0), 0.05, 0.0)
-    weight_ref[3] = jnp.where(inside, 0.0, 1.0)
 
     def with_halo(own, n, planes):
         return jnp.concatenate([own[planes], halo_ref[n, planes]], axis=1)
@@ -592,7 +612,7 @@
             pltpu.SMEM((PHASES,), f32),
             pltpu.SMEM((PHASES,), f32),
             pltpu.SemaphoreType.DMA((groups, FIELDS)),
-            pltpu.SemaphoreType.DMA((groups + groups // 2 + 3,)),
+            pltpu.SemaphoreType.DMA((groups + groups // 2 + 4,)),
             pltpu.SemaphoreType.DMA((3,)),
         ],
         compiler_params=limit(58),
@@ -625,8 +645,8 @@
     half = lambda tiles, planes: shape(tiles + planes // (bz // 2), bz // 2, by)
     x_1, x_0 = swap(x_1, "gx", 1), swap(x_0, "gx", 0)
     face = half(bx * FIELDS, bx)
-    extra = (shape(bx // 2, bz, by), shape(2, bz, by))
-    z_0, z_1, edge, tables, *own = unpacking(own_kernel, bx, (face, face) + extra + own_shape, stack)
+    extra = (shape(bx // 2, bz, by), shape(2, bz, by), shape(4, rows, lanes))
+    z_0, z_1, edge, tables, weights, *own = unpacking(own_kernel, bx, (face, face) + extra + own_shape, stack)
     face_1, face_0 = swap(z_1, "gz", 1), swap(z_0, "gz", 0)
 
     tiles = bx // 2 + DEPTH
@@ -666,17 +686,16 @@
     vx, vz, vy, p, eta, total, _, _ = pl.pallas_call(
         main_kernel,
         out_shape=(block,) * 5 + (shape(bz, by),) + tuple(shape(*a.shape) for a in halo),
-        in_specs=[VMEM] * 10,
+        in_specs=[VMEM] * 11,
         out_specs=(VMEM,) * 8,
         input_output_aliases={5: 6, 6: 7},
         scratch_shapes=[
             scratch(3, deep, rows, lanes),
             scratch(3, deep, rows, lanes),
             scratch(deep, rows, lanes),
-            scratch(4, rows, lanes),
         ],
         compiler_params=limit(32),
-    )(*own, *halo, edge_0, edge_1, tables)
+    )(*own, *halo, edge_0, edge_1, tables, weights)
 
     total = sum_everywhere(total)
     p = pl.pallas_call(

time: 43.7 us -> 43.1 us (0.986)
  Pallas kernels: 11 us -> 10.3 us
    pallas_call x1, Pallas kernels: 6.93 us -> 6.31 us  [local(): pl.pallas_call(main_kernel, out_shape=(block,) * 5 + (shape(bz, by),) + t...]
where the time goes in v17:
time: 43.1 us; the launch traced here: 42.8 us
  starting transfers between devices  18.1 us (42%)
  blocking collectives  10.9 us (25%)
  Pallas kernels  10.3 us (24%)
  waiting for transfers between devices  1.59 us (4%)
  local copies, waits for them, and re-layouts  1 us (2%)
  between operations  0.79 us (2%)
    ppermute x9, starting transfers between devices, swap(): lax.ppermute(a, axis, [(i, j) for k in range(start, count - 1, 2) for i,...  14.3 us
    all_to_all x1, blocking collectives, sum_everywhere(): lax.all_to_all(total, axes, 0, 0, tiled=True, axis_index_groups=groups)  10.9 us
    pallas_call x1, Pallas kernels, local(): pl.pallas_call(main_kernel, out_shape=(block,) * 5 + (shape(bz, by),) + t...  6.31 us
    ppermute x1, starting transfers between devices, sum_everywhere(): lax.ppermute(total, axes, [(i, i ^ 1) for i in range(devices)])  3.81 us
    pallas_call x1, Pallas kernels, local(): pl.pallas_call(pack_kernel, out_shape=(shape(bx // 2, bz, by), sent, sent...  2.18 us
    unnamed x2, local copies, waits for them, and re-layouts  0.99 us
  transfers between devices with their start and end apart: 10, of which 2 were waited for; matrix products, arithmetic and copies ran while one was open for 0% of the time, Pallas kernels for 2%

profile of v17, /device:TPU:0, one launch (start us, length us, event | category | flops | bytes accessed | tf_op | source)
XLA Modules:
  0.0 42.8 jit_solution(1670891473094532587)
XLA Ops:
  0.6 2.2 %shard_map.119 = (f32[8,8,128]{2,1,0:T(8,128)}, f32[21,8,128]{2,1,0:T(8,128)}, f32[21,8,128]{2,1,0:T(8,128)}, f32[90,8,128]{2,1,0:T(8,128)}) custom-call(f32[16,8,128]{2,1,0:T(8,128)} %vx_hbm.1, f32[16,8,128]{2,1,0:T(8,128)} %vz_hbm.1, f32[16,8,128]{2,1,0:T(8,128)} %vy_hbm.1, f32[16,8,128]{2,1,0:T(8,128)} %p_hbm.1, s32[16,8,128]{2,1,0:T(8,128)} %phase_hbm.1, ...), custom_call_target="tpu_custom_call" | custom-call | tf_op jit(solution)/shard_map/pallas_call | solution.py:601
  2.8 0.7 %collective-permute-start = (f32[21,8,128]{2,1,0:T(8,128)}, f32[21,8,128]{2,1,0:T(8,128)S(1)}, u32[]{:S(2)}, u32[]{:S(2)}) collective-permute-start(f32[21,8,128]{2,1,0:T(8,128)} %get-tuple-element.36), channel_id=1, source_target_pairs={{8,16},{16,8},{9,17},{17,9},{10,18},{18,10},{11,19},{19,11},{12,20... | collective-permute-start | bytes 258056 | tf_op jit(solution)/shard_map/ppermute | solution.py:574
  3.5 5.9 %collective-permute-start.1 = (f32[21,8,128]{2,1,0:T(8,128)}, f32[21,8,128]{2,1,0:T(8,128)S(1)}, u32[]{:S(2)}, u32[]{:S(2)}) collective-permute-start(f32[21,8,128]{2,1,0:T(8,128)} %get-tuple-element.37), channel_id=1, source_target_pairs={{0,8},{8,0},{16,24},{24,16},{1,9},{9,1},{17,25},{25,17},{2,10},{10... | collective-permute-start | bytes 258056 | tf_op jit(solution)/shard_map/ppermute | solution.py:574
  9.4 1.0 %copy-done = f32[90,8,128]{2,1,0:T(8,128)S(1)} copy-done((f32[90,8,128]{2,1,0:T(8,128)S(1)}, f32[90,8,128]{2,1,0:T(8,128)}, u32[]{:S(2)}) %copy-start) | copy-done | bytes 368664
  10.4 0.2 shard_map.120
  10.6 0.1 collective-permute-start.3
  10.6 0.7 %collective-permute-start.4 = (f32[84,4,128]{2,1,0:T(4,128)S(1)}, f32[84,4,128]{2,1,0:T(4,128)S(1)}, u32[]{:S(2)}, u32[]{:S(2)}) collective-permute-start(f32[84,4,128]{2,1,0:T(4,128)S(1)} %get-tuple-element.53), channel_id=1, source_target_pairs={{1,2},{2,1},{5,6},{6,5},{9,10},{10,9},{13,14},{14,13},{17,18},{18,... | collective-permute-start | bytes 516104 | tf_op jit(solution)/shard_map/ppermute | solution.py:574
  11.3 0.0 collective-permute-done.x_1_ref
  11.3 0.7 %collective-permute-done.1.x_0_ref = f32[21,8,128]{2,1,0:T(8,128)S(1)} collective-permute-done((f32[21,8,128]{2,1,0:T(8,128)}, f32[21,8,128]{2,1,0:T(8,128)S(1)}, u32[]{:S(2)}, u32[]{:S(2)}) %collective-permute-start.1) | collective-permute-done | bytes 86048 | tf_op jit(solution)/shard_map/ppermute | solution.py:574
  12.1 0.1 shard_map.121._edge_ref
  12.2 1.6 %collective-permute-start.2 = (f32[12,8,128]{2,1,0:T(8,128)S(1)}, f32[12,8,128]{2,1,0:T(8,128)S(1)}, u32[]{:S(2)}, u32[]{:S(2)}) collective-permute-start(f32[12,8,128]{2,1,0:T(8,128)S(1)} %shard_map.121._edge_ref), channel_id=1, source_target_pairs={{0,4},{4,0},{1,5},{5,1},{2,6},{6,2},{3,7},{7,3},{8,12},{12,8},{9,1... | collective-permute-start | bytes 147464 | tf_op jit(solution)/shard_map/ppermute | solution.py:574
  13.8 1.9 %collective-permute-start.5 = (f32[43,4,128]{2,1,0:T(4,128)S(1)}, f32[43,4,128]{2,1,0:T(4,128)S(1)}, u32[]{:S(2)}, u32[]{:S(2)}) collective-permute-start(f32[43,4,128]{2,1,0:T(4,128)S(1)} %get-tuple-element.54), channel_id=1, source_target_pairs={{0,1},{1,0},{2,3},{3,2},{4,5},{5,4},{6,7},{7,6},{8,9},{9,8},{10,11... | collective-permute-start | bytes 264200 | tf_op jit(solution)/shard_map/ppermute | solution.py:574
  15.8 0.7 %collective-permute-start.6 = (f32[43,4,128]{2,1,0:T(4,128)S(1)}, f32[43,4,128]{2,1,0:T(4,128)S(1)}, u32[]{:S(2)}, u32[]{:S(2)}) collective-permute-start(f32[43,4,128]{2,1,0:T(4,128)S(1)} %get-tuple-element.55), channel_id=1, source_target_pairs={{1,2},{2,1},{5,6},{6,5},{9,10},{10,9},{13,14},{14,13},{17,18},{18,... | collective-permute-start | bytes 264200 | tf_op jit(solution)/shard_map/ppermute | solution.py:574
  16.5 2.2 %collective-permute-start.7 = (f32[15,4,128]{2,1,0:T(4,128)S(1)}, f32[15,4,128]{2,1,0:T(4,128)S(1)}, u32[]{:S(2)}, u32[]{:S(2)}) collective-permute-start(f32[15,4,128]{2,1,0:T(4,128)S(1)} %get-tuple-element.58), channel_id=1, source_target_pairs={{0,1},{1,0},{2,3},{3,2},{4,5},{5,4},{6,7},{7,6},{8,9},{9,8},{10,11... | collective-permute-start | bytes 92168 | tf_op jit(solution)/shard_map/ppermute | solution.py:574
  18.7 0.0 collective-permute-done.3.face_0_ref
  18.7 0.7 %collective-permute-start.8 = (f32[15,4,128]{2,1,0:T(4,128)S(1)}, f32[15,4,128]{2,1,0:T(4,128)S(1)}, u32[]{:S(2)}, u32[]{:S(2)}) collective-permute-start(f32[15,4,128]{2,1,0:T(4,128)S(1)} %get-tuple-element.59), channel_id=1, source_target_pairs={{1,2},{2,1},{5,6},{6,5},{9,10},{10,9},{13,14},{14,13},{17,18},{18,... | collective-permute-start | bytes 92168 | tf_op jit(solution)/shard_map/ppermute | solution.py:574
  19.4 0.5 %shard_map.123 = (f32[3,25,8,256]{3,2,1,0:T(8,128)S(1)}, f32[25,8,256]{2,1,0:T(8,128)S(1)}, f32[25,8,256]{2,1,0:T(8,128)S(1)}, f32[25,8,256]{2,1,0:T(8,128)S(1)}, f32[25,8,256]{2,1,0:T(8,128)S(1)}) custom-call(f32[41,8,128]{2,1,0:T(8,128)S(1)} %get-tuple-element.40.sides_ref, ...), custom_call_target="tpu_custom_call", output_to_operand_aliasing={{0}: (3, {}), {1}: (4, {}), {2}: (5, {}), {3}: (6, {}), {4}... | custom-call | flops 2662400 | bytes 2662400 | tf_op jit(solution)/shard_map/pallas_call | solution.py:633
  19.9 0.0 collective-permute-done.5.corner_0_ref
  19.9 0.2 shard_map.124
  20.1 6.3 %shard_map.126 = (f32[16,8,128]{2,1,0:T(8,128)}, f32[16,8,128]{2,1,0:T(8,128)}, f32[16,8,128]{2,1,0:T(8,128)}, f32[16,8,128]{2,1,0:T(8,128)S(1)}, f32[16,8,128]{...) custom-call(f32[3,25,8,256]{3,2,1,0:T(8,128)S(1)} %get-tuple-element, ...), custom_call_target="tpu_custom_call", output_to_operand_aliasing={{6}: (5, {}), {7}: (6, {})} | custom-call | tf_op jit(solution)/shard_map/pallas_call | solution.py:686
  26.4 3.8 %collective-permute-start.9 = (f32[8,128]{1,0:T(8,128)S(1)}, f32[8,128]{1,0:T(8,128)S(1)}, u32[]{:S(2)}, u32[]{:S(2)}) collective-permute-start(f32[8,128]{1,0:T(8,128)S(1)} %get-tuple-element.65), channel_id=1, source_target_pairs={{0,1},{1,0},{2,3},{3,2},{4,5},{5,4},{6,7},{7,6},{8,9},{9,8},{10,11... | collective-permute-start | bytes 12296 | tf_op jit(solution)/shard_map/ppermute | solution.py:580
  30.2 0.8 %collective-permute-done.9 = f32[8,128]{1,0:T(8,128)S(1)} collective-permute-done((f32[8,128]{1,0:T(8,128)S(1)}, f32[8,128]{1,0:T(8,128)S(1)}, u32[]{:S(2)}, u32[]{:S(2)}) %collective-permute-start.9) | collective-permute-done | bytes 4128 | tf_op jit(solution)/shard_map/ppermute | solution.py:580
  31.1 10.9 %all_to_all.8 = f32[16,1,128]{2,1,0:T(1,128)S(1)} all-to-all(f32[16,1,128]{2,1,0:T(1,128)S(1)} %broadcast_in_dim.2), channel_id=1, replica_groups={{0,2,4,6,8,10,12,14,16,18,20,22,24,26,28,30},{1,3,5,7,9,11,13,15,17,19,..., dimensions={0} | all-to-all | bytes 16384 | tf_op jit(solution)/shard_map/all_to_all | solution.py:583
  42.0 0.8 %shard_map.127 = f32[16,8,128]{2,1,0:T(8,128)} custom-call(f32[16,8,128]{2,1,0:T(8,128)S(1)} %get-tuple-element.64.refs_0_, f32[16,128]{1,0:T(8,128)S(1)} %bitcast.1), custom_call_target="tpu_custom_call" | custom-call | tf_op jit(solution)/shard_map/pallas_call | solution.py:701
  (10 shorter events, 0.1 us)
Async XLA Ops:
  2.8 8.5 %collective-permute-start = (f32[21,8,128]{2,1,0:T(8,128)}, f32[21,8,128]{2,1,0:T(8,128)S(1)}, u32[]{:S(2)}, u32[]{:S(2)}) collective-permute-start(f32[21,8,128]{2,1,0:T(8,128)} %get-tuple-element.36), channel_id=1, source_target_pairs={{8,16},{16,8},{9,17},{17,9},{10,18},{18,10},{11,19},{19,11},{12,20... | collective-permute-start | bytes 258056 | tf_op jit(solution)/shard_map/ppermute | solution.py:574
  3.5 8.6 %collective-permute-start.1 = (f32[21,8,128]{2,1,0:T(8,128)}, f32[21,8,128]{2,1,0:T(8,128)S(1)}, u32[]{:S(2)}, u32[]{:S(2)}) collective-permute-start(f32[21,8,128]{2,1,0:T(8,128)} %get-tuple-element.37), channel_id=1, source_target_pairs={{0,8},{8,0},{16,24},{24,16},{1,9},{9,1},{17,25},{25,17},{2,10},{10... | collective-permute-start | bytes 258056 | tf_op jit(solution)/shard_map/ppermute | solution.py:574
  9.4 1.0 %copy-start = (f32[90,8,128]{2,1,0:T(8,128)S(1)}, f32[90,8,128]{2,1,0:T(8,128)}, u32[]{:S(2)}) copy-start(f32[90,8,128]{2,1,0:T(8,128)} %get-tuple-element.38.stack_ref) | copy-start | bytes 1105924
  10.6 8.1 %collective-permute-start.3 = (f32[84,4,128]{2,1,0:T(4,128)S(1)}, f32[84,4,128]{2,1,0:T(4,128)S(1)}, u32[]{:S(2)}, u32[]{:S(2)}) collective-permute-start(f32[84,4,128]{2,1,0:T(4,128)S(1)} %get-tuple-element.52), channel_id=1, source_target_pairs={{0,1},{1,0},{2,3},{3,2},{4,5},{5,4},{6,7},{7,6},{8,9},{9,8},{10,11... | collective-permute-start | bytes 516104 | tf_op jit(solution)/shard_map/ppermute | solution.py:574
  10.6 9.2 %collective-permute-start.4 = (f32[84,4,128]{2,1,0:T(4,128)S(1)}, f32[84,4,128]{2,1,0:T(4,128)S(1)}, u32[]{:S(2)}, u32[]{:S(2)}) collective-permute-start(f32[84,4,128]{2,1,0:T(4,128)S(1)} %get-tuple-element.53), channel_id=1, source_target_pairs={{1,2},{2,1},{5,6},{6,5},{9,10},{10,9},{13,14},{14,13},{17,18},{18,... | collective-permute-start | bytes 516104 | tf_op jit(solution)/shard_map/ppermute | solution.py:574
  12.2 4.2 %collective-permute-start.2 = (f32[12,8,128]{2,1,0:T(8,128)S(1)}, f32[12,8,128]{2,1,0:T(8,128)S(1)}, u32[]{:S(2)}, u32[]{:S(2)}) collective-permute-start(f32[12,8,128]{2,1,0:T(8,128)S(1)} %shard_map.121._edge_ref), channel_id=1, source_target_pairs={{0,4},{4,0},{1,5},{5,1},{2,6},{6,2},{3,7},{7,3},{8,12},{12,8},{9,1... | collective-permute-start | bytes 147464 | tf_op jit(solution)/shard_map/ppermute | solution.py:574
  13.8 6.0 %collective-permute-start.5 = (f32[43,4,128]{2,1,0:T(4,128)S(1)}, f32[43,4,128]{2,1,0:T(4,128)S(1)}, u32[]{:S(2)}, u32[]{:S(2)}) collective-permute-start(f32[43,4,128]{2,1,0:T(4,128)S(1)} %get-tuple-element.54), channel_id=1, source_target_pairs={{0,1},{1,0},{2,3},{3,2},{4,5},{5,4},{6,7},{7,6},{8,9},{9,8},{10,11... | collective-permute-start | bytes 264200 | tf_op jit(solution)/shard_map/ppermute | solution.py:574
  15.8 4.1 %collective-permute-start.6 = (f32[43,4,128]{2,1,0:T(4,128)S(1)}, f32[43,4,128]{2,1,0:T(4,128)S(1)}, u32[]{:S(2)}, u32[]{:S(2)}) collective-permute-start(f32[43,4,128]{2,1,0:T(4,128)S(1)} %get-tuple-element.55), channel_id=1, source_target_pairs={{1,2},{2,1},{5,6},{6,5},{9,10},{10,9},{13,14},{14,13},{17,18},{18,... | collective-permute-start | bytes 264200 | tf_op jit(solution)/shard_map/ppermute | solution.py:574
  16.5 3.6 %collective-permute-start.7 = (f32[15,4,128]{2,1,0:T(4,128)S(1)}, f32[15,4,128]{2,1,0:T(4,128)S(1)}, u32[]{:S(2)}, u32[]{:S(2)}) collective-permute-start(f32[15,4,128]{2,1,0:T(4,128)S(1)} %get-tuple-element.58), channel_id=1, source_target_pairs={{0,1},{1,0},{2,3},{3,2},{4,5},{5,4},{6,7},{7,6},{8,9},{9,8},{10,11... | collective-permute-start | bytes 92168 | tf_op jit(solution)/shard_map/ppermute | solution.py:574
  18.7 1.4 %collective-permute-start.8 = (f32[15,4,128]{2,1,0:T(4,128)S(1)}, f32[15,4,128]{2,1,0:T(4,128)S(1)}, u32[]{:S(2)}, u32[]{:S(2)}) collective-permute-start(f32[15,4,128]{2,1,0:T(4,128)S(1)} %get-tuple-element.59), channel_id=1, source_target_pairs={{1,2},{2,1},{5,6},{6,5},{9,10},{10,9},{13,14},{14,13},{17,18},{18,... | collective-permute-start | bytes 92168 | tf_op jit(solution)/shard_map/ppermute | solution.py:574
  26.4 4.6 %collective-permute-start.9 = (f32[8,128]{1,0:T(8,128)S(1)}, f32[8,128]{1,0:T(8,128)S(1)}, u32[]{:S(2)}, u32[]{:S(2)}) collective-permute-start(f32[8,128]{1,0:T(8,128)S(1)} %get-tuple-element.65), channel_id=1, source_target_pairs={{0,1},{1,0},{2,3},{3,2},{4,5},{5,4},{6,7},{7,6},{8,9},{9,8},{10,11... | collective-permute-start | bytes 12296 | tf_op jit(solution)/shard_map/ppermute | solution.py:580

commit v18 on v17

--- a/solution.py
+++ b/solution.py
@@ -12,7 +12,6 @@
 FIELDS = 5
 DEPTH = ITERS
 LANE_STEP = 2 * DEPTH + 1
-UNROLL = 12
 GROUP = 4
 
 VMEM = pl.BlockSpec(memory_space=pltpu.VMEM)
@@ -52,14 +51,14 @@
     pl.when(odd(axis))(lambda: body(pair[1], pair[0]))
 
 
-def start_copies(sources, targets, sems):
-    copies = []
-    for g in range(sources[0].shape[0] // GROUP):
+def start_copies(sources, targets, sems, order):
+    copies = {}
+    for g in order:
         at = pl.ds(g * GROUP, GROUP)
-        copies.append(
-            [pltpu.make_async_copy(a.at[at], b.at[at], sems.at[g, f]) for f, (a, b) in enumerate(zip(sources, targets))]
-        )
-        for copy in copies[-1]:
+        copies[g] = [
+            pltpu.make_async_copy(a.at[at], b.at[at], sems.at[g, f]) for f, (a, b) in enumerate(zip(sources, targets))
+        ]
+        for copy in copies[g]:
             copy.start()
     return copies
 
@@ -110,13 +109,14 @@
 ):
     bx, bz, by = phase_ref.shape
     targets = [field_ref.at[f] for f in range(FIELDS - 1)] + [phase_ref]
-    copies = start_copies((vx_hbm, vz_hbm, vy_hbm, p_hbm, phase_hbm), targets, sems)
+    groups = bx // GROUP
+    order = [0, groups - 1] + list(range(1, groups - 1))
+    copies = start_copies((vx_hbm, vz_hbm, vy_hbm, p_hbm, phase_hbm), targets, sems, order)
     table_refs = (scale_ref, power_ref, rho_ref)
     pairs = zip((scale_hbm, power_hbm, rho_hbm), table_refs)
     table_copies = [pltpu.make_async_copy(a, b, table_sems.at[n]) for n, (a, b) in enumerate(pairs)]
     for copy in table_copies:
         copy.start()
-    groups = bx // GROUP
     half = groups // 2
     outs = []
 
@@ -145,7 +145,6 @@
             copy.wait()
 
     edges = {}
-    order = [0, groups - 1] + list(range(1, groups - 1))
     for g in order:
         for copy in copies[g]:
             copy.wait()
@@ -476,78 +475,46 @@
             sy = quarter + y_down(quarter)
             return vx, vz, vy, eta, p, quarter, tx, tz, ty, sz, sy
 
-        def chunk(j, count, carry=None, final=False):
-            if carry is None:
-                below = cells(j - 1, count + 1)
-                if not last:
-                    p_ref[pl.ds(j - 1, 1)] = below[4][:1]
-                vx, vz, vy, eta, p, quarter, tx, tz, ty, sz, sy = (a[1:] for a in below)
-                join = lambda n, a: below[n][:-1]
-            else:
-                vx, vz, vy, eta, p, quarter, tx, tz, ty, sz, sy = cells(j, count)
-                first = {1: load(1, j - 1, 1), 2: load(2, j - 1, 1), 5: carry[0], 6: carry[1], 9: carry[2], 10: carry[3]}
-                join = lambda n, a: jnp.concatenate([first[n], a[:-1]], axis=0)
-            planes = pl.ds(j, count)
-            bias = weight_ref[3:4]
-            sx = quarter + join(5, quarter)
-            exz = sz + join(9, sz)
-            exy = sy + join(10, sy)
-            ezy = sz + y_down(sz)
-            fxz = exz * (vx - z_down(vx))
-            fxy = exy * (vx - y_down(vx))
-            low_vz, low_vy = join(1, vz), join(2, vy)
-            gzx = exz * (vz - low_vz)
-            hyx = exy * (vy - low_vy)
-            gzy = ezy * (vz - y_down(vz))
-            hyz = ezy * (vy - z_down(vy))
-            res_x = (tx - join(6, tx)) + ((z_up(fxz) - fxz) + (y_up(fxy) - fxy))
-            new_vx = vx + weight_ref[0:1] * reciprocal(sx + bias) * res_x
-            part_z = (tz - z_down(tz)) - with_halo(rho_ref, 6, planes) + ((y_up(gzy) - gzy) - gzx)
-            part_y = (ty - y_down(ty)) + ((z_up(hyz) - hyz) - hyx)
-            scale_z = weight_ref[1:2] * reciprocal(sz + bias)
-            scale_y = weight_ref[2:3] * reciprocal(sy + bias)
-
-            def lower(n, a):
-                return a[:-1] if carry is None else jnp.concatenate([carry[n], a[:-1]], axis=0)
-
-            skip = 1 if carry is None else 0
-            new_vz = low_vz[skip:] + lower(6, scale_z) * (lower(4, part_z) + gzx[skip:])
-            new_vy = low_vy[skip:] + lower(7, scale_y) * (lower(5, part_y) + hyx[skip:])
-            at = pl.ds(j - 1 + skip - (DEPTH if last else 0), count - skip)
-            if last:
-                own = count - 1 if final else count
-                here = pl.ds(j - DEPTH, own)
-                out_vx_ref[here] = new_vx[:own, 0:bz, 0:by]
-                out_p_ref[here] = p[:own, 0:bz, 0:by]
-                out_eta_ref[here] = eta[:own, 0:bz, 0:by]
-                sum_ref[...] += jnp.sum(p[:own, 0:bz, 0:by], axis=0)
-                out_vz_ref[at] = new_vz[:, 0:bz, 0:by]
-                out_vy_ref[at] = new_vy[:, 0:bz, 0:by]
-            else:
-                p_ref[planes] = p
-                new[0, planes] = new_vx
-                new[1, at] = new_vz
-                new[2, at] = new_vy
-            return tuple(a[-1:] for a in (quarter, tx, sz, sy, part_z, part_y, scale_z, scale_y))
-
         first, end = k, bx + 2 * DEPTH - k
+        count = end - first + 1
+        below = cells(first - 1, count + 1)
+        vx, vz, vy, eta, p, quarter, tx, tz, ty, sz, sy = (a[1:] for a in below)
+        vx0, vz0, vy0, _, _, quarter0, tx0, _, _, sz0, sy0 = (a[:-1] for a in below)
+        bias = weight_ref[3:4]
+        sx = quarter + quarter0
+        exz = sz + sz0
+        exy = sy + sy0
+        ezy = sz + y_down(sz)
+        fxz = exz * (vx - z_down(vx))
+        fxy = exy * (vx - y_down(vx))
+        gzx = exz * (vz - vz0)
+        hyx = exy * (vy - vy0)
+        gzy = ezy * (vz - y_down(vz))
+        hyz = ezy * (vy - z_down(vy))
+        res_x = (tx - tx0) + ((z_up(fxz) - fxz) + (y_up(fxy) - fxy))
+        new_vx = vx + weight_ref[0:1] * reciprocal(sx + bias) * res_x
+        part_z = (tz - z_down(tz)) - with_halo(rho_ref, 6, pl.ds(first, count)) + ((y_up(gzy) - gzy) - gzx)
+        part_y = (ty - y_down(ty)) + ((z_up(hyz) - hyz) - hyx)
+        scale_z = weight_ref[1:2] * reciprocal(sz + bias)
+        scale_y = weight_ref[2:3] * reciprocal(sy + bias)
+        new_vz = vz[:-1] + scale_z[:-1] * (part_z[:-1] + gzx[1:])
+        new_vy = vy[:-1] + scale_y[:-1] * (part_y[:-1] + hyx[1:])
         if last:
-            sum_ref[...] = jnp.zeros((bz, by), jnp.float32)
-        count = end - first + 1
-        steps = (count - 2) // UNROLL
-        start = count - steps * UNROLL
-        carry = chunk(first, start)
-        loops = steps - 1 if last else steps
-        carry = lax.fori_loop(
-            0, loops, lambda s, carry: chunk(first + start + s * UNROLL, UNROLL, carry), carry
-        )
-        if last:
-            chunk(end + 1 - UNROLL, UNROLL, carry, final=True)
+            out_vx_ref[...] = new_vx[:-1, 0:bz, 0:by]
+            out_vz_ref[...] = new_vz[:, 0:bz, 0:by]
+            out_vy_ref[...] = new_vy[:, 0:bz, 0:by]
+            out_p_ref[...] = p[:-1, 0:bz, 0:by]
+            out_eta_ref[...] = eta[:-1, 0:bz, 0:by]
+            sum_ref[...] = jnp.sum(p[:-1, 0:bz, 0:by], axis=0)
 
             @pl.when(ix == 0)
             def _():
                 out_vx_ref[0] = jnp.zeros((bz, by), jnp.float32)
         else:
+            p_ref[pl.ds(first - 1, count + 1)] = below[4]
+            new[0, pl.ds(first, count)] = new_vx
+            new[1, pl.ds(first, count - 1)] = new_vz
+            new[2, pl.ds(first, count - 1)] = new_vy
             plane = jnp.zeros((rows, lanes), jnp.float32)
 
             @pl.when(ix == 0)

time: 43.1 us -> 43 us (level)
  no operation moved by 1% of the time
where the time goes in v18:
time: 43 us; the launch traced here: 42.7 us
  starting transfers between devices  18.1 us (42%)
  blocking collectives  10.9 us (25%)
  Pallas kernels  10.3 us (24%)
  waiting for transfers between devices  1.59 us (4%)
  local copies, waits for them, and re-layouts  1 us (2%)
  between operations  0.79 us (2%)
    ppermute x9, starting transfers between devices, swap(): lax.ppermute(a, axis, [(i, j) for k in range(start, count - 1, 2) for i,...  14.3 us
    all_to_all x1, blocking collectives, sum_everywhere(): lax.all_to_all(total, axes, 0, 0, tiled=True, axis_index_groups=groups)  10.9 us
    pallas_call x1, Pallas kernels, local(): pl.pallas_call(main_kernel, out_shape=(block,) * 5 + (shape(bz, by),) + t...  6.29 us
    ppermute x1, starting transfers between devices, sum_everywhere(): lax.ppermute(total, axes, [(i, i ^ 1) for i in range(devices)])  3.81 us
    pallas_call x1, Pallas kernels, local(): pl.pallas_call(pack_kernel, out_shape=(shape(bx // 2, bz, by), sent, sent...  2.17 us
    unnamed x2, local copies, waits for them, and re-layouts  0.99 us
  transfers between devices with their start and end apart: 10, of which 2 were waited for; matrix products, arithmetic and copies ran while one was open for 0% of the time, Pallas kernels for 2%

profile of v18, /device:TPU:0, one launch (start us, length us, event | category | flops | bytes accessed | tf_op | source)
XLA Modules:
  0.0 42.7 jit_solution(16702996589094430711)
XLA Ops:
  0.6 2.2 %shard_map.119 = (f32[8,8,128]{2,1,0:T(8,128)}, f32[21,8,128]{2,1,0:T(8,128)}, f32[21,8,128]{2,1,0:T(8,128)}, f32[90,8,128]{2,1,0:T(8,128)}) custom-call(f32[16,8,128]{2,1,0:T(8,128)} %vx_hbm.1, f32[16,8,128]{2,1,0:T(8,128)} %vz_hbm.1, f32[16,8,128]{2,1,0:T(8,128)} %vy_hbm.1, f32[16,8,128]{2,1,0:T(8,128)} %p_hbm.1, s32[16,8,128]{2,1,0:T(8,128)} %phase_hbm.1, ...), custom_call_target="tpu_custom_call" | custom-call | tf_op jit(solution)/shard_map/pallas_call | solution.py:568
  2.8 0.7 %collective-permute-start = (f32[21,8,128]{2,1,0:T(8,128)}, f32[21,8,128]{2,1,0:T(8,128)S(1)}, u32[]{:S(2)}, u32[]{:S(2)}) collective-permute-start(f32[21,8,128]{2,1,0:T(8,128)} %get-tuple-element.36), channel_id=1, source_target_pairs={{8,16},{16,8},{9,17},{17,9},{10,18},{18,10},{11,19},{19,11},{12,20... | collective-permute-start | bytes 258056 | tf_op jit(solution)/shard_map/ppermute | solution.py:541
  3.5 5.9 %collective-permute-start.1 = (f32[21,8,128]{2,1,0:T(8,128)}, f32[21,8,128]{2,1,0:T(8,128)S(1)}, u32[]{:S(2)}, u32[]{:S(2)}) collective-permute-start(f32[21,8,128]{2,1,0:T(8,128)} %get-tuple-element.37), channel_id=1, source_target_pairs={{0,8},{8,0},{16,24},{24,16},{1,9},{9,1},{17,25},{25,17},{2,10},{10... | collective-permute-start | bytes 258056 | tf_op jit(solution)/shard_map/ppermute | solution.py:541
  9.4 1.0 %copy-done = f32[90,8,128]{2,1,0:T(8,128)S(1)} copy-done((f32[90,8,128]{2,1,0:T(8,128)S(1)}, f32[90,8,128]{2,1,0:T(8,128)}, u32[]{:S(2)}) %copy-start) | copy-done | bytes 368664
  10.4 0.2 shard_map.120
  10.6 0.1 collective-permute-start.3
  10.6 0.7 %collective-permute-start.4 = (f32[84,4,128]{2,1,0:T(4,128)S(1)}, f32[84,4,128]{2,1,0:T(4,128)S(1)}, u32[]{:S(2)}, u32[]{:S(2)}) collective-permute-start(f32[84,4,128]{2,1,0:T(4,128)S(1)} %get-tuple-element.53), channel_id=1, source_target_pairs={{1,2},{2,1},{5,6},{6,5},{9,10},{10,9},{13,14},{14,13},{17,18},{18,... | collective-permute-start | bytes 516104 | tf_op jit(solution)/shard_map/ppermute | solution.py:541
  11.3 0.0 collective-permute-done.x_1_ref
  11.3 0.7 %collective-permute-done.1.x_0_ref = f32[21,8,128]{2,1,0:T(8,128)S(1)} collective-permute-done((f32[21,8,128]{2,1,0:T(8,128)}, f32[21,8,128]{2,1,0:T(8,128)S(1)}, u32[]{:S(2)}, u32[]{:S(2)}) %collective-permute-start.1) | collective-permute-done | bytes 86048 | tf_op jit(solution)/shard_map/ppermute | solution.py:541
  12.1 0.1 shard_map.121._edge_ref
  12.2 1.6 %collective-permute-start.2 = (f32[12,8,128]{2,1,0:T(8,128)S(1)}, f32[12,8,128]{2,1,0:T(8,128)S(1)}, u32[]{:S(2)}, u32[]{:S(2)}) collective-permute-start(f32[12,8,128]{2,1,0:T(8,128)S(1)} %shard_map.121._edge_ref), channel_id=1, source_target_pairs={{0,4},{4,0},{1,5},{5,1},{2,6},{6,2},{3,7},{7,3},{8,12},{12,8},{9,1... | collective-permute-start | bytes 147464 | tf_op jit(solution)/shard_map/ppermute | solution.py:541
  13.8 1.9 %collective-permute-start.5 = (f32[43,4,128]{2,1,0:T(4,128)S(1)}, f32[43,4,128]{2,1,0:T(4,128)S(1)}, u32[]{:S(2)}, u32[]{:S(2)}) collective-permute-start(f32[43,4,128]{2,1,0:T(4,128)S(1)} %get-tuple-element.54), channel_id=1, source_target_pairs={{0,1},{1,0},{2,3},{3,2},{4,5},{5,4},{6,7},{7,6},{8,9},{9,8},{10,11... | collective-permute-start | bytes 264200 | tf_op jit(solution)/shard_map/ppermute | solution.py:541
  15.8 0.7 %collective-permute-start.6 = (f32[43,4,128]{2,1,0:T(4,128)S(1)}, f32[43,4,128]{2,1,0:T(4,128)S(1)}, u32[]{:S(2)}, u32[]{:S(2)}) collective-permute-start(f32[43,4,128]{2,1,0:T(4,128)S(1)} %get-tuple-element.55), channel_id=1, source_target_pairs={{1,2},{2,1},{5,6},{6,5},{9,10},{10,9},{13,14},{14,13},{17,18},{18,... | collective-permute-start | bytes 264200 | tf_op jit(solution)/shard_map/ppermute | solution.py:541
  16.4 0.0 collective-permute-done.2.edge_ref
  16.5 2.2 %collective-permute-start.7 = (f32[15,4,128]{2,1,0:T(4,128)S(1)}, f32[15,4,128]{2,1,0:T(4,128)S(1)}, u32[]{:S(2)}, u32[]{:S(2)}) collective-permute-start(f32[15,4,128]{2,1,0:T(4,128)S(1)} %get-tuple-element.58), channel_id=1, source_target_pairs={{0,1},{1,0},{2,3},{3,2},{4,5},{5,4},{6,7},{7,6},{8,9},{9,8},{10,11... | collective-permute-start | bytes 92168 | tf_op jit(solution)/shard_map/ppermute | solution.py:541
  18.7 0.0 collective-permute-done.3.face_0_ref
  18.7 0.7 %collective-permute-start.8 = (f32[15,4,128]{2,1,0:T(4,128)S(1)}, f32[15,4,128]{2,1,0:T(4,128)S(1)}, u32[]{:S(2)}, u32[]{:S(2)}) collective-permute-start(f32[15,4,128]{2,1,0:T(4,128)S(1)} %get-tuple-element.59), channel_id=1, source_target_pairs={{1,2},{2,1},{5,6},{6,5},{9,10},{10,9},{13,14},{14,13},{17,18},{18,... | collective-permute-start | bytes 92168 | tf_op jit(solution)/shard_map/ppermute | solution.py:541
  19.3 0.5 %shard_map.123 = (f32[3,25,8,256]{3,2,1,0:T(8,128)S(1)}, f32[25,8,256]{2,1,0:T(8,128)S(1)}, f32[25,8,256]{2,1,0:T(8,128)S(1)}, f32[25,8,256]{2,1,0:T(8,128)S(1)}, f32[25,8,256]{2,1,0:T(8,128)S(1)}) custom-call(f32[41,8,128]{2,1,0:T(8,128)S(1)} %get-tuple-element.40.sides_ref, ...), custom_call_target="tpu_custom_call", output_to_operand_aliasing={{0}: (3, {}), {1}: (4, {}), {2}: (5, {}), {3}: (6, {}), {4}... | custom-call | flops 2662400 | bytes 2662400 | tf_op jit(solution)/shard_map/pallas_call | solution.py:600
  19.9 0.2 shard_map.124
  20.1 6.3 %shard_map.126 = (f32[16,8,128]{2,1,0:T(8,128)}, f32[16,8,128]{2,1,0:T(8,128)}, f32[16,8,128]{2,1,0:T(8,128)}, f32[16,8,128]{2,1,0:T(8,128)S(1)}, f32[16,8,128]{...) custom-call(f32[3,25,8,256]{3,2,1,0:T(8,128)S(1)} %get-tuple-element, ...), custom_call_target="tpu_custom_call", output_to_operand_aliasing={{6}: (5, {}), {7}: (6, {})} | custom-call | tf_op jit(solution)/shard_map/pallas_call | solution.py:653
  26.4 3.8 %collective-permute-start.9 = (f32[8,128]{1,0:T(8,128)S(1)}, f32[8,128]{1,0:T(8,128)S(1)}, u32[]{:S(2)}, u32[]{:S(2)}) collective-permute-start(f32[8,128]{1,0:T(8,128)S(1)} %get-tuple-element.65), channel_id=1, source_target_pairs={{0,1},{1,0},{2,3},{3,2},{4,5},{5,4},{6,7},{7,6},{8,9},{9,8},{10,11... | collective-permute-start | bytes 12296 | tf_op jit(solution)/shard_map/ppermute | solution.py:547
  30.2 0.8 %collective-permute-done.9 = f32[8,128]{1,0:T(8,128)S(1)} collective-permute-done((f32[8,128]{1,0:T(8,128)S(1)}, f32[8,128]{1,0:T(8,128)S(1)}, u32[]{:S(2)}, u32[]{:S(2)}) %collective-permute-start.9) | collective-permute-done | bytes 4128 | tf_op jit(solution)/shard_map/ppermute | solution.py:547
  31.0 10.9 %all_to_all.8 = f32[16,1,128]{2,1,0:T(1,128)S(1)} all-to-all(f32[16,1,128]{2,1,0:T(1,128)S(1)} %broadcast_in_dim.2), channel_id=1, replica_groups={{0,2,4,6,8,10,12,14,16,18,20,22,24,26,28,30},{1,3,5,7,9,11,13,15,17,19,..., dimensions={0} | all-to-all | bytes 16384 | tf_op jit(solution)/shard_map/all_to_all | solution.py:550
  42.0 0.8 %shard_map.127 = f32[16,8,128]{2,1,0:T(8,128)} custom-call(f32[16,8,128]{2,1,0:T(8,128)S(1)} %get-tuple-element.64.refs_0_, f32[16,128]{1,0:T(8,128)S(1)} %bitcast.1), custom_call_target="tpu_custom_call" | custom-call | tf_op jit(solution)/shard_map/pallas_call | solution.py:668
  (10 shorter events, 0.1 us)
Async XLA Ops:
  2.8 8.5 %collective-permute-start = (f32[21,8,128]{2,1,0:T(8,128)}, f32[21,8,128]{2,1,0:T(8,128)S(1)}, u32[]{:S(2)}, u32[]{:S(2)}) collective-permute-start(f32[21,8,128]{2,1,0:T(8,128)} %get-tuple-element.36), channel_id=1, source_target_pairs={{8,16},{16,8},{9,17},{17,9},{10,18},{18,10},{11,19},{19,11},{12,20... | collective-permute-start | bytes 258056 | tf_op jit(solution)/shard_map/ppermute | solution.py:541
  3.5 8.6 %collective-permute-start.1 = (f32[21,8,128]{2,1,0:T(8,128)}, f32[21,8,128]{2,1,0:T(8,128)S(1)}, u32[]{:S(2)}, u32[]{:S(2)}) collective-permute-start(f32[21,8,128]{2,1,0:T(8,128)} %get-tuple-element.37), channel_id=1, source_target_pairs={{0,8},{8,0},{16,24},{24,16},{1,9},{9,1},{17,25},{25,17},{2,10},{10... | collective-permute-start | bytes 258056 | tf_op jit(solution)/shard_map/ppermute | solution.py:541
  9.4 1.0 %copy-start = (f32[90,8,128]{2,1,0:T(8,128)S(1)}, f32[90,8,128]{2,1,0:T(8,128)}, u32[]{:S(2)}) copy-start(f32[90,8,128]{2,1,0:T(8,128)} %get-tuple-element.38.stack_ref) | copy-start | bytes 1105924
  10.6 8.1 %collective-permute-start.3 = (f32[84,4,128]{2,1,0:T(4,128)S(1)}, f32[84,4,128]{2,1,0:T(4,128)S(1)}, u32[]{:S(2)}, u32[]{:S(2)}) collective-permute-start(f32[84,4,128]{2,1,0:T(4,128)S(1)} %get-tuple-element.52), channel_id=1, source_target_pairs={{0,1},{1,0},{2,3},{3,2},{4,5},{5,4},{6,7},{7,6},{8,9},{9,8},{10,11... | collective-permute-start | bytes 516104 | tf_op jit(solution)/shard_map/ppermute | solution.py:541
  10.6 9.2 %collective-permute-start.4 = (f32[84,4,128]{2,1,0:T(4,128)S(1)}, f32[84,4,128]{2,1,0:T(4,128)S(1)}, u32[]{:S(2)}, u32[]{:S(2)}) collective-permute-start(f32[84,4,128]{2,1,0:T(4,128)S(1)} %get-tuple-element.53), channel_id=1, source_target_pairs={{1,2},{2,1},{5,6},{6,5},{9,10},{10,9},{13,14},{14,13},{17,18},{18,... | collective-permute-start | bytes 516104 | tf_op jit(solution)/shard_map/ppermute | solution.py:541
  12.2 4.2 %collective-permute-start.2 = (f32[12,8,128]{2,1,0:T(8,128)S(1)}, f32[12,8,128]{2,1,0:T(8,128)S(1)}, u32[]{:S(2)}, u32[]{:S(2)}) collective-permute-start(f32[12,8,128]{2,1,0:T(8,128)S(1)} %shard_map.121._edge_ref), channel_id=1, source_target_pairs={{0,4},{4,0},{1,5},{5,1},{2,6},{6,2},{3,7},{7,3},{8,12},{12,8},{9,1... | collective-permute-start | bytes 147464 | tf_op jit(solution)/shard_map/ppermute | solution.py:541
  13.8 6.0 %collective-permute-start.5 = (f32[43,4,128]{2,1,0:T(4,128)S(1)}, f32[43,4,128]{2,1,0:T(4,128)S(1)}, u32[]{:S(2)}, u32[]{:S(2)}) collective-permute-start(f32[43,4,128]{2,1,0:T(4,128)S(1)} %get-tuple-element.54), channel_id=1, source_target_pairs={{0,1},{1,0},{2,3},{3,2},{4,5},{5,4},{6,7},{7,6},{8,9},{9,8},{10,11... | collective-permute-start | bytes 264200 | tf_op jit(solution)/shard_map/ppermute | solution.py:541
  15.8 4.1 %collective-permute-start.6 = (f32[43,4,128]{2,1,0:T(4,128)S(1)}, f32[43,4,128]{2,1,0:T(4,128)S(1)}, u32[]{:S(2)}, u32[]{:S(2)}) collective-permute-start(f32[43,4,128]{2,1,0:T(4,128)S(1)} %get-tuple-element.55), channel_id=1, source_target_pairs={{1,2},{2,1},{5,6},{6,5},{9,10},{10,9},{13,14},{14,13},{17,18},{18,... | collective-permute-start | bytes 264200 | tf_op jit(solution)/shard_map/ppermute | solution.py:541
  16.5 3.6 %collective-permute-start.7 = (f32[15,4,128]{2,1,0:T(4,128)S(1)}, f32[15,4,128]{2,1,0:T(4,128)S(1)}, u32[]{:S(2)}, u32[]{:S(2)}) collective-permute-start(f32[15,4,128]{2,1,0:T(4,128)S(1)} %get-tuple-element.58), channel_id=1, source_target_pairs={{0,1},{1,0},{2,3},{3,2},{4,5},{5,4},{6,7},{7,6},{8,9},{9,8},{10,11... | collective-permute-start | bytes 92168 | tf_op jit(solution)/shard_map/ppermute | solution.py:541
  18.7 1.4 %collective-permute-start.8 = (f32[15,4,128]{2,1,0:T(4,128)S(1)}, f32[15,4,128]{2,1,0:T(4,128)S(1)}, u32[]{:S(2)}, u32[]{:S(2)}) collective-permute-start(f32[15,4,128]{2,1,0:T(4,128)S(1)} %get-tuple-element.59), channel_id=1, source_target_pairs={{1,2},{2,1},{5,6},{6,5},{9,10},{10,9},{13,14},{14,13},{17,18},{18,... | collective-permute-start | bytes 92168 | tf_op jit(solution)/shard_map/ppermute | solution.py:541
  26.4 4.6 %collective-permute-start.9 = (f32[8,128]{1,0:T(8,128)S(1)}, f32[8,128]{1,0:T(8,128)S(1)}, u32[]{:S(2)}, u32[]{:S(2)}) collective-permute-start(f32[8,128]{1,0:T(8,128)S(1)} %get-tuple-element.65), channel_id=1, source_target_pairs={{0,1},{1,0},{2,3},{3,2},{4,5},{5,4},{6,7},{7,6},{8,9},{9,8},{10,11... | collective-permute-start | bytes 12296 | tf_op jit(solution)/shard_map/ppermute | solution.py:547

commit v19 on v18

--- a/solution.py
+++ b/solution.py
@@ -428,107 +428,177 @@
     by_parity("gz", (edge_0_ref, edge_1_ref), body)
 
 
+class Cells:
+    def __init__(self, own, side):
+        self.own, self.side = own, side
+
+    def map(self, f, *others):
+        parts = [(o.own, o.side) if isinstance(o, Cells) else (o, o) for o in others]
+        return Cells(f(self.own, *(p[0] for p in parts)), f(self.side, *(p[1] for p in parts)))
+
+    def __getitem__(self, at):
+        return Cells(self.own[at], self.side[at])
+
+    def __add__(self, other):
+        return self.map(jnp.add, other)
+
+    def __sub__(self, other):
+        return self.map(jnp.subtract, other)
+
+    def __mul__(self, other):
+        return self.map(jnp.multiply, other)
+
+    def along_z(self, up):
+        bz, by = self.side.shape[-2:]
+        move = z_up if up else z_down
+        side = move(self.side)
+        across = iota((1, bz, by), 1) == (bz - 1 if up else 0)
+        return Cells(move(self.own), jnp.where(across, pltpu.roll(side, by // 2, 2), side))
+
+    def along_y(self, up):
+        bz, by = self.side.shape[-2:]
+        one, half = (by - 1, by // 2 - 1) if up else (1, by // 2 + 1)
+        lane = iota((1, bz, by), 2)
+        own_end, side_end, halo_end = (by - 1, by - 1, by // 2 - 1) if up else (0, 0, by // 2)
+        first, second = self.own[:, 0:bz], self.own[:, bz:]
+        side = pltpu.roll(self.side, one, 2)
+        first_moved = pltpu.roll(first, one, 2)
+        own = jnp.concatenate(
+            [
+                jnp.where(lane == own_end, side, first_moved),
+                jnp.where(lane == own_end, pltpu.roll(self.side, half, 2), pltpu.roll(second, one, 2)),
+            ],
+            axis=1,
+        )
+        side = jnp.where(lane == halo_end, pltpu.roll(second, half, 2), side)
+        return Cells(own, jnp.where(lane == side_end, first_moved, side))
+
+
+def join_sides(own, halo):
+    by = own.shape[-1]
+    lane = iota((1,) * (own.ndim - 1) + (by,), own.ndim - 1)
+    middle = (lane >= by // 4) & (lane < by - by // 4)
+    return jnp.where(middle, pltpu.roll(halo, by // 2, own.ndim - 1), own)
+
+
 def main_kernel(
     v_ref, p0_ref, pre_ref, power_field_ref, rho_ref, _halo, _next, edge_0_ref, edge_1_ref, tables_ref, weight_ref,
     out_vx_ref, out_vz_ref, out_vy_ref, out_p_ref, out_eta_ref, sum_ref, halo_ref, next_ref,
-    va_ref, vb_ref, p_ref,
+    own_a_ref, own_b_ref, side_a_ref, side_b_ref, side_constant_ref,
 ):
     bx, bz, by = out_p_ref.shape
     rows, lanes = 2 * bz, 2 * by
+    deep = halo_ref.shape[1]
     nx, ix = lax.axis_size("gx"), lax.axis_index("gx")
     unpack_halo_edges(edge_0_ref, edge_1_ref, tables_ref, halo_ref, next_ref)
 
-    def with_halo(own, n, planes):
-        return jnp.concatenate([own[planes], halo_ref[n, planes]], axis=1)
+    fields = [v_ref.at[d] for d in range(3)] + [p0_ref, pre_ref, power_field_ref, rho_ref]
+    for n, ref in enumerate(fields):
+        target = side_b_ref.at[n] if n < 4 else side_constant_ref.at[n - 4]
+        target[...] = join_sides(ref[:, :, by:lanes], halo_ref[n, :, :, by:lanes])
+    weights = [
+        Cells(weight_ref[n : n + 1, :, 0:by], join_sides(weight_ref[n : n + 1, 0:bz, by:lanes], weight_ref[n : n + 1, bz:rows, by:lanes]))
+        for n in range(4)
+    ]
+
+    def own_rows(n, planes):
+        return jnp.concatenate([fields[n][planes, :, 0:by], halo_ref[n, planes, :, 0:by]], axis=1)
+
+    def constant(n, planes):
+        return Cells(own_rows(4 + n, planes), side_constant_ref[n, planes])
 
     for k in range(1, ITERS + 1):
-        old, new = (va_ref, vb_ref) if k % 2 else (vb_ref, va_ref)
+        old = (own_a_ref, side_a_ref) if k % 2 == 0 else (own_b_ref, side_b_ref)
+        new = (own_b_ref, side_b_ref) if k % 2 == 0 else (own_a_ref, side_a_ref)
         last = k == ITERS
 
-        def load(d, j, count):
+        def load(n, j, count):
             planes = pl.ds(j, count)
-            return with_halo(v_ref.at[d], d, planes) if k == 1 else old[d, planes]
-
-        def cells(j, count):
-            planes = pl.ds(j, count)
-            vx1 = load(0, j, count + 1)
-            vx = vx1[:count]
-            vz, vy = load(1, j, count), load(2, j, count)
-            p = with_halo(p0_ref, 3, planes) if k == 1 else p_ref[planes]
-            up = z_up(vz)
-            if k == 1:
-                after = next_ref[planes]
-                after = jnp.concatenate([after, after], axis=1)
-                up = jnp.where(iota((1, rows, lanes), 1) == bz + bz // 2 - 1, after, up)
-            rx = vx1[1:] - vx
-            rz = up - vz
-            ry = y_up(vy) - vy
-            a = rx - ry
-            b = ry - rz
-            inv = (a * (a + b) + b * b) * (1.0 / 3.0) + 1.0
-            eta = with_halo(pre_ref, 4, planes) * jnp.exp2(with_halo(power_field_ref, 5, planes) * jnp.log(inv))
-            quarter = 0.25 * eta
-            div = rx + ry + rz
-            p = p - quarter * (div + div)
-            tx, tz, ty = eta * rx - p, eta * rz - p, eta * ry - p
-            sz = quarter + z_down(quarter)
-            sy = quarter + y_down(quarter)
-            return vx, vz, vy, eta, p, quarter, tx, tz, ty, sz, sy
+            return Cells(own_rows(n, planes) if k == 1 else old[0][n, planes], old[1][n, planes])
 
         first, end = k, bx + 2 * DEPTH - k
         count = end - first + 1
-        below = cells(first - 1, count + 1)
-        vx, vz, vy, eta, p, quarter, tx, tz, ty, sz, sy = (a[1:] for a in below)
-        vx0, vz0, vy0, _, _, quarter0, tx0, _, _, sz0, sy0 = (a[:-1] for a in below)
-        bias = weight_ref[3:4]
+        planes = pl.ds(first - 1, count + 1)
+        vx1 = load(0, first - 1, count + 2)
+        vx, vz, vy, p = (load(n, first - 1, count + 1) for n in range(4))
+        up = vz.along_z(True)
+        if k == 1:
+            after = next_ref[planes]
+            both = jnp.concatenate([after[..., 0:by]] * 2, axis=1)
+            own = jnp.where(iota((1, rows, by), 1) == bz + bz // 2 - 1, both, up.own)
+            lane = iota((1, bz, by), 2)
+            here = (iota((1, bz, by), 1) == bz // 2 - 1) & (lane >= by // 4) & (lane < by - by // 4)
+            up = Cells(own, jnp.where(here, pltpu.roll(after[..., by:lanes], by // 2, 2), up.side))
+        rx = vx1[1:] - vx
+        rz = up - vz
+        ry = vy.along_y(True) - vy
+        a = rx - ry
+        b = ry - rz
+        inv = (a * (a + b) + b * b) * (1.0 / 3.0) + 1.0
+        exponent = constant(1, planes) * inv.map(jnp.log)
+        eta = constant(0, planes) * exponent.map(jnp.exp2)
+        quarter = eta * 0.25
+        div = rx + ry + rz
+        p = p - quarter * (div + div)
+        tx, tz, ty = eta * rx - p, eta * rz - p, eta * ry - p
+        sz = quarter + quarter.along_z(False)
+        sy = quarter + quarter.along_y(False)
+        if not last:
+            new[0][3, planes], new[1][3, planes] = p.own, p.side
+        vx0, vz0, vy0, quarter0, tx0, sz0, sy0 = (c[:-1] for c in (vx, vz, vy, quarter, tx, sz, sy))
+        vx, vz, vy, eta, p, quarter, tx, tz, ty, sz, sy = (c[1:] for c in (vx, vz, vy, eta, p, quarter, tx, tz, ty, sz, sy))
         sx = quarter + quarter0
         exz = sz + sz0
         exy = sy + sy0
-        ezy = sz + y_down(sz)
-        fxz = exz * (vx - z_down(vx))
-        fxy = exy * (vx - y_down(vx))
+        ezy = sz + sz.along_y(False)
+        fxz = exz * (vx - vx.along_z(False))
+        fxy = exy * (vx - vx.along_y(False))
         gzx = exz * (vz - vz0)
         hyx = exy * (vy - vy0)
-        gzy = ezy * (vz - y_down(vz))
-        hyz = ezy * (vy - z_down(vy))
-        res_x = (tx - tx0) + ((z_up(fxz) - fxz) + (y_up(fxy) - fxy))
-        new_vx = vx + weight_ref[0:1] * reciprocal(sx + bias) * res_x
-        part_z = (tz - z_down(tz)) - with_halo(rho_ref, 6, pl.ds(first, count)) + ((y_up(gzy) - gzy) - gzx)
-        part_y = (ty - y_down(ty)) + ((z_up(hyz) - hyz) - hyx)
-        scale_z = weight_ref[1:2] * reciprocal(sz + bias)
-        scale_y = weight_ref[2:3] * reciprocal(sy + bias)
+        gzy = ezy * (vz - vz.along_y(False))
+        hyz = ezy * (vy - vy.along_z(False))
+        res_x = (tx - tx0) + ((fxz.along_z(True) - fxz) + (fxy.along_y(True) - fxy))
+        rho = constant(2, pl.ds(first, count))
+        part_z = (tz - tz.along_z(False)) - rho + ((gzy.along_y(True) - gzy) - gzx)
+        part_y = (ty - ty.along_y(False)) + ((hyz.along_z(True) - hyz) - hyx)
+        scale_x, scale_z, scale_y = (
+            (total + weights[3]).map(reciprocal) * weight for total, weight in zip((sx, sz, sy), weights)
+        )
+        new_vx = vx + scale_x * res_x
         new_vz = vz[:-1] + scale_z[:-1] * (part_z[:-1] + gzx[1:])
         new_vy = vy[:-1] + scale_y[:-1] * (part_y[:-1] + hyx[1:])
         if last:
-            out_vx_ref[...] = new_vx[:-1, 0:bz, 0:by]
-            out_vz_ref[...] = new_vz[:, 0:bz, 0:by]
-            out_vy_ref[...] = new_vy[:, 0:bz, 0:by]
-            out_p_ref[...] = p[:-1, 0:bz, 0:by]
-            out_eta_ref[...] = eta[:-1, 0:bz, 0:by]
-            sum_ref[...] = jnp.sum(p[:-1, 0:bz, 0:by], axis=0)
+            out_vx_ref[...] = new_vx.own[:-1, 0:bz]
+            out_vz_ref[...] = new_vz.own[:, 0:bz]
+            out_vy_ref[...] = new_vy.own[:, 0:bz]
+            out_p_ref[...] = p.own[:-1, 0:bz]
+            out_eta_ref[...] = eta.own[:-1, 0:bz]
+            sum_ref[...] = jnp.sum(p.own[:-1, 0:bz], axis=0)
 
             @pl.when(ix == 0)
             def _():
                 out_vx_ref[0] = jnp.zeros((bz, by), jnp.float32)
         else:
-            p_ref[pl.ds(first - 1, count + 1)] = below[4]
-            new[0, pl.ds(first, count)] = new_vx
-            new[1, pl.ds(first, count - 1)] = new_vz
-            new[2, pl.ds(first, count - 1)] = new_vy
-            plane = jnp.zeros((rows, lanes), jnp.float32)
+            for d, value in enumerate((new_vx, new_vz, new_vy)):
+                at = pl.ds(first, count if d == 0 else count - 1)
+                new[0][d, at], new[1][d, at] = value.own, value.side
+
+            def clear(d, i):
+                for ref in new:
+                    ref[d, i] = jnp.zeros(ref.shape[2:], jnp.float32)
 
             @pl.when(ix == 0)
             def _():
                 for i in range(first, DEPTH):
                     for d in range(3):
-                        new[d, i] = plane
-                new[0, DEPTH] = plane
+                        clear(d, i)
+                clear(0, DEPTH)
 
             @pl.when(ix == nx - 1)
             def _():
                 for i in range(DEPTH + bx, end + 1):
                     for d in range(3):
-                        new[d, i] = plane
+                        clear(d, i)
 
 
 def final_kernel(p_ref, sum_ref, out_ref, *, cells):
@@ -657,9 +727,11 @@
         out_specs=(VMEM,) * 8,
         input_output_aliases={5: 6, 6: 7},
         scratch_shapes=[
-            scratch(3, deep, rows, lanes),
-            scratch(3, deep, rows, lanes),
-            scratch(deep, rows, lanes),
+            scratch(4, deep, rows, by),
+            scratch(4, deep, rows, by),
+            scratch(4, deep, bz, by),
+            scratch(4, deep, bz, by),
+            scratch(3, deep, bz, by),
         ],
         compiler_params=limit(32),
     )(*own, *halo, edge_0, edge_1, tables, weights)

time: 43 us -> 43.5 us (1.012)
    pallas_call x1, Pallas kernels: 6.29 us -> 6.75 us  [local(): pl.pallas_call(main_kernel, out_shape=(block,) * 5 + (shape(bz, by),) + t...]
where the time goes in v19:
time: 43.5 us; the launch traced here: 43.2 us
  starting transfers between devices  18.1 us (42%)
  blocking collectives  10.9 us (25%)
  Pallas kernels  10.7 us (25%)
  waiting for transfers between devices  1.59 us (4%)
  local copies, waits for them, and re-layouts  1 us (2%)
  between operations  0.79 us (2%)
    ppermute x9, starting transfers between devices, swap(): lax.ppermute(a, axis, [(i, j) for k in range(start, count - 1, 2) for i,...  14.3 us
    all_to_all x1, blocking collectives, sum_everywhere(): lax.all_to_all(total, axes, 0, 0, tiled=True, axis_index_groups=groups)  10.9 us
    pallas_call x1, Pallas kernels, local(): pl.pallas_call(main_kernel, out_shape=(block,) * 5 + (shape(bz, by),) + t...  6.75 us
    ppermute x1, starting transfers between devices, sum_everywhere(): lax.ppermute(total, axes, [(i, i ^ 1) for i in range(devices)])  3.81 us
    pallas_call x1, Pallas kernels, local(): pl.pallas_call(pack_kernel, out_shape=(shape(bx // 2, bz, by), sent, sent...  2.17 us
    unnamed x2, local copies, waits for them, and re-layouts  0.99 us
  transfers between devices with their start and end apart: 10, of which 2 were waited for; matrix products, arithmetic and copies ran while one was open for 0% of the time, Pallas kernels for 2%

profile of v19, /device:TPU:0, one launch (start us, length us, event | category | flops | bytes accessed | tf_op | source)
XLA Modules:
  0.0 43.2 jit_solution(6499771881544120550)
XLA Ops:
  0.6 2.2 %shard_map.119 = (f32[8,8,128]{2,1,0:T(8,128)}, f32[21,8,128]{2,1,0:T(8,128)}, f32[21,8,128]{2,1,0:T(8,128)}, f32[90,8,128]{2,1,0:T(8,128)}) custom-call(f32[16,8,128]{2,1,0:T(8,128)} %vx_hbm.1, f32[16,8,128]{2,1,0:T(8,128)} %vz_hbm.1, f32[16,8,128]{2,1,0:T(8,128)} %vy_hbm.1, f32[16,8,128]{2,1,0:T(8,128)} %p_hbm.1, s32[16,8,128]{2,1,0:T(8,128)} %phase_hbm.1, ...), custom_call_target="tpu_custom_call" | custom-call | tf_op jit(solution)/shard_map/pallas_call | solution.py:638
  2.8 0.7 %collective-permute-start = (f32[21,8,128]{2,1,0:T(8,128)}, f32[21,8,128]{2,1,0:T(8,128)S(1)}, u32[]{:S(2)}, u32[]{:S(2)}) collective-permute-start(f32[21,8,128]{2,1,0:T(8,128)} %get-tuple-element.36), channel_id=1, source_target_pairs={{8,16},{16,8},{9,17},{17,9},{10,18},{18,10},{11,19},{19,11},{12,20... | collective-permute-start | bytes 258056 | tf_op jit(solution)/shard_map/ppermute | solution.py:611
  3.5 5.9 %collective-permute-start.1 = (f32[21,8,128]{2,1,0:T(8,128)}, f32[21,8,128]{2,1,0:T(8,128)S(1)}, u32[]{:S(2)}, u32[]{:S(2)}) collective-permute-start(f32[21,8,128]{2,1,0:T(8,128)} %get-tuple-element.37), channel_id=1, source_target_pairs={{0,8},{8,0},{16,24},{24,16},{1,9},{9,1},{17,25},{25,17},{2,10},{10... | collective-permute-start | bytes 258056 | tf_op jit(solution)/shard_map/ppermute | solution.py:611
  9.4 1.0 %copy-done = f32[90,8,128]{2,1,0:T(8,128)S(1)} copy-done((f32[90,8,128]{2,1,0:T(8,128)S(1)}, f32[90,8,128]{2,1,0:T(8,128)}, u32[]{:S(2)}) %copy-start) | copy-done | bytes 368664
  10.4 0.2 shard_map.120
  10.6 0.1 collective-permute-start.3
  10.6 0.7 %collective-permute-start.4 = (f32[84,4,128]{2,1,0:T(4,128)S(1)}, f32[84,4,128]{2,1,0:T(4,128)S(1)}, u32[]{:S(2)}, u32[]{:S(2)}) collective-permute-start(f32[84,4,128]{2,1,0:T(4,128)S(1)} %get-tuple-element.53), channel_id=1, source_target_pairs={{1,2},{2,1},{5,6},{6,5},{9,10},{10,9},{13,14},{14,13},{17,18},{18,... | collective-permute-start | bytes 516104 | tf_op jit(solution)/shard_map/ppermute | solution.py:611
  11.3 0.0 collective-permute-done.x_1_ref
  11.3 0.7 %collective-permute-done.1.x_0_ref = f32[21,8,128]{2,1,0:T(8,128)S(1)} collective-permute-done((f32[21,8,128]{2,1,0:T(8,128)}, f32[21,8,128]{2,1,0:T(8,128)S(1)}, u32[]{:S(2)}, u32[]{:S(2)}) %collective-permute-start.1) | collective-permute-done | bytes 86048 | tf_op jit(solution)/shard_map/ppermute | solution.py:611
  12.1 0.1 shard_map.121._edge_ref
  12.2 1.6 %collective-permute-start.2 = (f32[12,8,128]{2,1,0:T(8,128)S(1)}, f32[12,8,128]{2,1,0:T(8,128)S(1)}, u32[]{:S(2)}, u32[]{:S(2)}) collective-permute-start(f32[12,8,128]{2,1,0:T(8,128)S(1)} %shard_map.121._edge_ref), channel_id=1, source_target_pairs={{0,4},{4,0},{1,5},{5,1},{2,6},{6,2},{3,7},{7,3},{8,12},{12,8},{9,1... | collective-permute-start | bytes 147464 | tf_op jit(solution)/shard_map/ppermute | solution.py:611
  13.8 1.9 %collective-permute-start.5 = (f32[43,4,128]{2,1,0:T(4,128)S(1)}, f32[43,4,128]{2,1,0:T(4,128)S(1)}, u32[]{:S(2)}, u32[]{:S(2)}) collective-permute-start(f32[43,4,128]{2,1,0:T(4,128)S(1)} %get-tuple-element.54), channel_id=1, source_target_pairs={{0,1},{1,0},{2,3},{3,2},{4,5},{5,4},{6,7},{7,6},{8,9},{9,8},{10,11... | collective-permute-start | bytes 264200 | tf_op jit(solution)/shard_map/ppermute | solution.py:611
  15.8 0.7 %collective-permute-start.6 = (f32[43,4,128]{2,1,0:T(4,128)S(1)}, f32[43,4,128]{2,1,0:T(4,128)S(1)}, u32[]{:S(2)}, u32[]{:S(2)}) collective-permute-start(f32[43,4,128]{2,1,0:T(4,128)S(1)} %get-tuple-element.55), channel_id=1, source_target_pairs={{1,2},{2,1},{5,6},{6,5},{9,10},{10,9},{13,14},{14,13},{17,18},{18,... | collective-permute-start | bytes 264200 | tf_op jit(solution)/shard_map/ppermute | solution.py:611
  16.4 0.0 collective-permute-done.2.edge_ref
  16.5 2.2 %collective-permute-start.7 = (f32[15,4,128]{2,1,0:T(4,128)S(1)}, f32[15,4,128]{2,1,0:T(4,128)S(1)}, u32[]{:S(2)}, u32[]{:S(2)}) collective-permute-start(f32[15,4,128]{2,1,0:T(4,128)S(1)} %get-tuple-element.58), channel_id=1, source_target_pairs={{0,1},{1,0},{2,3},{3,2},{4,5},{5,4},{6,7},{7,6},{8,9},{9,8},{10,11... | collective-permute-start | bytes 92168 | tf_op jit(solution)/shard_map/ppermute | solution.py:611
  18.7 0.0 collective-permute-done.3.face_0_ref
  18.7 0.7 %collective-permute-start.8 = (f32[15,4,128]{2,1,0:T(4,128)S(1)}, f32[15,4,128]{2,1,0:T(4,128)S(1)}, u32[]{:S(2)}, u32[]{:S(2)}) collective-permute-start(f32[15,4,128]{2,1,0:T(4,128)S(1)} %get-tuple-element.59), channel_id=1, source_target_pairs={{1,2},{2,1},{5,6},{6,5},{9,10},{10,9},{13,14},{14,13},{17,18},{18,... | collective-permute-start | bytes 92168 | tf_op jit(solution)/shard_map/ppermute | solution.py:611
  19.3 0.5 %shard_map.123 = (f32[3,25,8,256]{3,2,1,0:T(8,128)S(1)}, f32[25,8,256]{2,1,0:T(8,128)S(1)}, f32[25,8,256]{2,1,0:T(8,128)S(1)}, f32[25,8,256]{2,1,0:T(8,128)S(1)}, f32[25,8,256]{2,1,0:T(8,128)S(1)}) custom-call(f32[41,8,128]{2,1,0:T(8,128)S(1)} %get-tuple-element.40.sides_ref, ...), custom_call_target="tpu_custom_call", output_to_operand_aliasing={{0}: (3, {}), {1}: (4, {}), {2}: (5, {}), {3}: (6, {}), {4}... | custom-call | flops 2662400 | bytes 2662400 | tf_op jit(solution)/shard_map/pallas_call | solution.py:670
  19.9 0.2 shard_map.124
  20.1 6.8 %shard_map.126 = (f32[16,8,128]{2,1,0:T(8,128)}, f32[16,8,128]{2,1,0:T(8,128)}, f32[16,8,128]{2,1,0:T(8,128)}, f32[16,8,128]{2,1,0:T(8,128)S(1)}, f32[16,8,128]{...) custom-call(f32[3,25,8,256]{3,2,1,0:T(8,128)S(1)} %get-tuple-element, ...), custom_call_target="tpu_custom_call", output_to_operand_aliasing={{6}: (5, {}), {7}: (6, {})} | custom-call | tf_op jit(solution)/shard_map/pallas_call | solution.py:723
  26.8 3.8 %collective-permute-start.9 = (f32[8,128]{1,0:T(8,128)S(1)}, f32[8,128]{1,0:T(8,128)S(1)}, u32[]{:S(2)}, u32[]{:S(2)}) collective-permute-start(f32[8,128]{1,0:T(8,128)S(1)} %get-tuple-element.65), channel_id=1, source_target_pairs={{0,1},{1,0},{2,3},{3,2},{4,5},{5,4},{6,7},{7,6},{8,9},{9,8},{10,11... | collective-permute-start | bytes 12296 | tf_op jit(solution)/shard_map/ppermute | solution.py:617
  30.6 0.8 %collective-permute-done.9 = f32[8,128]{1,0:T(8,128)S(1)} collective-permute-done((f32[8,128]{1,0:T(8,128)S(1)}, f32[8,128]{1,0:T(8,128)S(1)}, u32[]{:S(2)}, u32[]{:S(2)}) %collective-permute-start.9) | collective-permute-done | bytes 4128 | tf_op jit(solution)/shard_map/ppermute | solution.py:617
  31.5 10.9 %all_to_all.8 = f32[16,1,128]{2,1,0:T(1,128)S(1)} all-to-all(f32[16,1,128]{2,1,0:T(1,128)S(1)} %broadcast_in_dim.2), channel_id=1, replica_groups={{0,2,4,6,8,10,12,14,16,18,20,22,24,26,28,30},{1,3,5,7,9,11,13,15,17,19,..., dimensions={0} | all-to-all | bytes 16384 | tf_op jit(solution)/shard_map/all_to_all | solution.py:620
  42.4 0.8 %shard_map.127 = f32[16,8,128]{2,1,0:T(8,128)} custom-call(f32[16,8,128]{2,1,0:T(8,128)S(1)} %get-tuple-element.64.refs_0_, f32[16,128]{1,0:T(8,128)S(1)} %bitcast.1), custom_call_target="tpu_custom_call" | custom-call | tf_op jit(solution)/shard_map/pallas_call | solution.py:740
  (10 shorter events, 0.1 us)
Async XLA Ops:
  2.8 8.5 %collective-permute-start = (f32[21,8,128]{2,1,0:T(8,128)}, f32[21,8,128]{2,1,0:T(8,128)S(1)}, u32[]{:S(2)}, u32[]{:S(2)}) collective-permute-start(f32[21,8,128]{2,1,0:T(8,128)} %get-tuple-element.36), channel_id=1, source_target_pairs={{8,16},{16,8},{9,17},{17,9},{10,18},{18,10},{11,19},{19,11},{12,20... | collective-permute-start | bytes 258056 | tf_op jit(solution)/shard_map/ppermute | solution.py:611
  3.5 8.6 %collective-permute-start.1 = (f32[21,8,128]{2,1,0:T(8,128)}, f32[21,8,128]{2,1,0:T(8,128)S(1)}, u32[]{:S(2)}, u32[]{:S(2)}) collective-permute-start(f32[21,8,128]{2,1,0:T(8,128)} %get-tuple-element.37), channel_id=1, source_target_pairs={{0,8},{8,0},{16,24},{24,16},{1,9},{9,1},{17,25},{25,17},{2,10},{10... | collective-permute-start | bytes 258056 | tf_op jit(solution)/shard_map/ppermute | solution.py:611
  9.4 1.0 %copy-start = (f32[90,8,128]{2,1,0:T(8,128)S(1)}, f32[90,8,128]{2,1,0:T(8,128)}, u32[]{:S(2)}) copy-start(f32[90,8,128]{2,1,0:T(8,128)} %get-tuple-element.38.stack_ref) | copy-start | bytes 1105924
  10.6 8.1 %collective-permute-start.3 = (f32[84,4,128]{2,1,0:T(4,128)S(1)}, f32[84,4,128]{2,1,0:T(4,128)S(1)}, u32[]{:S(2)}, u32[]{:S(2)}) collective-permute-start(f32[84,4,128]{2,1,0:T(4,128)S(1)} %get-tuple-element.52), channel_id=1, source_target_pairs={{0,1},{1,0},{2,3},{3,2},{4,5},{5,4},{6,7},{7,6},{8,9},{9,8},{10,11... | collective-permute-start | bytes 516104 | tf_op jit(solution)/shard_map/ppermute | solution.py:611
  10.6 9.2 %collective-permute-start.4 = (f32[84,4,128]{2,1,0:T(4,128)S(1)}, f32[84,4,128]{2,1,0:T(4,128)S(1)}, u32[]{:S(2)}, u32[]{:S(2)}) collective-permute-start(f32[84,4,128]{2,1,0:T(4,128)S(1)} %get-tuple-element.53), channel_id=1, source_target_pairs={{1,2},{2,1},{5,6},{6,5},{9,10},{10,9},{13,14},{14,13},{17,18},{18,... | collective-permute-start | bytes 516104 | tf_op jit(solution)/shard_map/ppermute | solution.py:611
  12.2 4.2 %collective-permute-start.2 = (f32[12,8,128]{2,1,0:T(8,128)S(1)}, f32[12,8,128]{2,1,0:T(8,128)S(1)}, u32[]{:S(2)}, u32[]{:S(2)}) collective-permute-start(f32[12,8,128]{2,1,0:T(8,128)S(1)} %shard_map.121._edge_ref), channel_id=1, source_target_pairs={{0,4},{4,0},{1,5},{5,1},{2,6},{6,2},{3,7},{7,3},{8,12},{12,8},{9,1... | collective-permute-start | bytes 147464 | tf_op jit(solution)/shard_map/ppermute | solution.py:611
  13.8 6.0 %collective-permute-start.5 = (f32[43,4,128]{2,1,0:T(4,128)S(1)}, f32[43,4,128]{2,1,0:T(4,128)S(1)}, u32[]{:S(2)}, u32[]{:S(2)}) collective-permute-start(f32[43,4,128]{2,1,0:T(4,128)S(1)} %get-tuple-element.54), channel_id=1, source_target_pairs={{0,1},{1,0},{2,3},{3,2},{4,5},{5,4},{6,7},{7,6},{8,9},{9,8},{10,11... | collective-permute-start | bytes 264200 | tf_op jit(solution)/shard_map/ppermute | solution.py:611
  15.8 4.1 %collective-permute-start.6 = (f32[43,4,128]{2,1,0:T(4,128)S(1)}, f32[43,4,128]{2,1,0:T(4,128)S(1)}, u32[]{:S(2)}, u32[]{:S(2)}) collective-permute-start(f32[43,4,128]{2,1,0:T(4,128)S(1)} %get-tuple-element.55), channel_id=1, source_target_pairs={{1,2},{2,1},{5,6},{6,5},{9,10},{10,9},{13,14},{14,13},{17,18},{18,... | collective-permute-start | bytes 264200 | tf_op jit(solution)/shard_map/ppermute | solution.py:611
  16.5 3.6 %collective-permute-start.7 = (f32[15,4,128]{2,1,0:T(4,128)S(1)}, f32[15,4,128]{2,1,0:T(4,128)S(1)}, u32[]{:S(2)}, u32[]{:S(2)}) collective-permute-start(f32[15,4,128]{2,1,0:T(4,128)S(1)} %get-tuple-element.58), channel_id=1, source_target_pairs={{0,1},{1,0},{2,3},{3,2},{4,5},{5,4},{6,7},{7,6},{8,9},{9,8},{10,11... | collective-permute-start | bytes 92168 | tf_op jit(solution)/shard_map/ppermute | solution.py:611
  18.7 1.4 %collective-permute-start.8 = (f32[15,4,128]{2,1,0:T(4,128)S(1)}, f32[15,4,128]{2,1,0:T(4,128)S(1)}, u32[]{:S(2)}, u32[]{:S(2)}) collective-permute-start(f32[15,4,128]{2,1,0:T(4,128)S(1)} %get-tuple-element.59), channel_id=1, source_target_pairs={{1,2},{2,1},{5,6},{6,5},{9,10},{10,9},{13,14},{14,13},{17,18},{18,... | collective-permute-start | bytes 92168 | tf_op jit(solution)/shard_map/ppermute | solution.py:611
  26.8 4.6 %collective-permute-start.9 = (f32[8,128]{1,0:T(8,128)S(1)}, f32[8,128]{1,0:T(8,128)S(1)}, u32[]{:S(2)}, u32[]{:S(2)}) collective-permute-start(f32[8,128]{1,0:T(8,128)S(1)} %get-tuple-element.65), channel_id=1, source_target_pairs={{0,1},{1,0},{2,3},{3,2},{4,5},{5,4},{6,7},{7,6},{8,9},{9,8},{10,11... | collective-permute-start | bytes 12296 | tf_op jit(solution)/shard_map/ppermute | solution.py:617

commit v20 on v18

--- a/solution.py
+++ b/solution.py
@@ -484,7 +484,7 @@
         sx = quarter + quarter0
         exz = sz + sz0
         exy = sy + sy0
-        ezy = sz + y_down(sz)
+        ezy = sy + z_down(sy)
         fxz = exz * (vx - z_down(vx))
         fxy = exy * (vx - y_down(vx))
         gzx = exz * (vz - vz0)

time: 43 us -> 42.9 us (level)
  no operation moved by 1% of the time
where the time goes in v20:
time: 42.9 us; the launch traced here: 42.6 us
  starting transfers between devices  18.1 us (42%)
  blocking collectives  10.9 us (25%)
  Pallas kernels  10.1 us (24%)
  waiting for transfers between devices  1.59 us (4%)
  local copies, waits for them, and re-layouts  1 us (2%)
  between operations  0.79 us (2%)
    ppermute x9, starting transfers between devices, swap(): lax.ppermute(a, axis, [(i, j) for k in range(start, count - 1, 2) for i,...  14.3 us
    all_to_all x1, blocking collectives, sum_everywhere(): lax.all_to_all(total, axes, 0, 0, tiled=True, axis_index_groups=groups)  10.9 us
    pallas_call x1, Pallas kernels, local(): pl.pallas_call(main_kernel, out_shape=(block,) * 5 + (shape(bz, by),) + t...  6.13 us
    ppermute x1, starting transfers between devices, sum_everywhere(): lax.ppermute(total, axes, [(i, i ^ 1) for i in range(devices)])  3.81 us
    pallas_call x1, Pallas kernels, local(): pl.pallas_call(pack_kernel, out_shape=(shape(bx // 2, bz, by), sent, sent...  2.17 us
    unnamed x2, local copies, waits for them, and re-layouts  0.99 us
  transfers between devices with their start and end apart: 10, of which 2 were waited for; matrix products, arithmetic and copies ran while one was open for 0% of the time, Pallas kernels for 2%

profile of v20, /device:TPU:0, one launch (start us, length us, event | category | flops | bytes accessed | tf_op | source)
XLA Modules:
  0.0 42.6 jit_solution(15107574257361443555)
XLA Ops:
  0.6 2.2 %shard_map.119 = (f32[8,8,128]{2,1,0:T(8,128)}, f32[21,8,128]{2,1,0:T(8,128)}, f32[21,8,128]{2,1,0:T(8,128)}, f32[90,8,128]{2,1,0:T(8,128)}) custom-call(f32[16,8,128]{2,1,0:T(8,128)} %vx_hbm.1, f32[16,8,128]{2,1,0:T(8,128)} %vz_hbm.1, f32[16,8,128]{2,1,0:T(8,128)} %vy_hbm.1, f32[16,8,128]{2,1,0:T(8,128)} %p_hbm.1, s32[16,8,128]{2,1,0:T(8,128)} %phase_hbm.1, ...), custom_call_target="tpu_custom_call" | custom-call | tf_op jit(solution)/shard_map/pallas_call | solution.py:568
  2.8 0.7 %collective-permute-start = (f32[21,8,128]{2,1,0:T(8,128)}, f32[21,8,128]{2,1,0:T(8,128)S(1)}, u32[]{:S(2)}, u32[]{:S(2)}) collective-permute-start(f32[21,8,128]{2,1,0:T(8,128)} %get-tuple-element.36), channel_id=1, source_target_pairs={{8,16},{16,8},{9,17},{17,9},{10,18},{18,10},{11,19},{19,11},{12,20... | collective-permute-start | bytes 258056 | tf_op jit(solution)/shard_map/ppermute | solution.py:541
  3.5 5.9 %collective-permute-start.1 = (f32[21,8,128]{2,1,0:T(8,128)}, f32[21,8,128]{2,1,0:T(8,128)S(1)}, u32[]{:S(2)}, u32[]{:S(2)}) collective-permute-start(f32[21,8,128]{2,1,0:T(8,128)} %get-tuple-element.37), channel_id=1, source_target_pairs={{0,8},{8,0},{16,24},{24,16},{1,9},{9,1},{17,25},{25,17},{2,10},{10... | collective-permute-start | bytes 258056 | tf_op jit(solution)/shard_map/ppermute | solution.py:541
  9.4 1.0 %copy-done = f32[90,8,128]{2,1,0:T(8,128)S(1)} copy-done((f32[90,8,128]{2,1,0:T(8,128)S(1)}, f32[90,8,128]{2,1,0:T(8,128)}, u32[]{:S(2)}) %copy-start) | copy-done | bytes 368664
  10.4 0.2 shard_map.120
  10.6 0.1 collective-permute-start.3
  10.6 0.7 %collective-permute-start.4 = (f32[84,4,128]{2,1,0:T(4,128)S(1)}, f32[84,4,128]{2,1,0:T(4,128)S(1)}, u32[]{:S(2)}, u32[]{:S(2)}) collective-permute-start(f32[84,4,128]{2,1,0:T(4,128)S(1)} %get-tuple-element.53), channel_id=1, source_target_pairs={{1,2},{2,1},{5,6},{6,5},{9,10},{10,9},{13,14},{14,13},{17,18},{18,... | collective-permute-start | bytes 516104 | tf_op jit(solution)/shard_map/ppermute | solution.py:541
  11.3 0.0 collective-permute-done.x_1_ref
  11.3 0.7 %collective-permute-done.1.x_0_ref = f32[21,8,128]{2,1,0:T(8,128)S(1)} collective-permute-done((f32[21,8,128]{2,1,0:T(8,128)}, f32[21,8,128]{2,1,0:T(8,128)S(1)}, u32[]{:S(2)}, u32[]{:S(2)}) %collective-permute-start.1) | collective-permute-done | bytes 86048 | tf_op jit(solution)/shard_map/ppermute | solution.py:541
  12.1 0.1 shard_map.121._edge_ref
  12.2 1.6 %collective-permute-start.2 = (f32[12,8,128]{2,1,0:T(8,128)S(1)}, f32[12,8,128]{2,1,0:T(8,128)S(1)}, u32[]{:S(2)}, u32[]{:S(2)}) collective-permute-start(f32[12,8,128]{2,1,0:T(8,128)S(1)} %shard_map.121._edge_ref), channel_id=1, source_target_pairs={{0,4},{4,0},{1,5},{5,1},{2,6},{6,2},{3,7},{7,3},{8,12},{12,8},{9,1... | collective-permute-start | bytes 147464 | tf_op jit(solution)/shard_map/ppermute | solution.py:541
  13.8 1.9 %collective-permute-start.5 = (f32[43,4,128]{2,1,0:T(4,128)S(1)}, f32[43,4,128]{2,1,0:T(4,128)S(1)}, u32[]{:S(2)}, u32[]{:S(2)}) collective-permute-start(f32[43,4,128]{2,1,0:T(4,128)S(1)} %get-tuple-element.54), channel_id=1, source_target_pairs={{0,1},{1,0},{2,3},{3,2},{4,5},{5,4},{6,7},{7,6},{8,9},{9,8},{10,11... | collective-permute-start | bytes 264200 | tf_op jit(solution)/shard_map/ppermute | solution.py:541
  15.8 0.7 %collective-permute-start.6 = (f32[43,4,128]{2,1,0:T(4,128)S(1)}, f32[43,4,128]{2,1,0:T(4,128)S(1)}, u32[]{:S(2)}, u32[]{:S(2)}) collective-permute-start(f32[43,4,128]{2,1,0:T(4,128)S(1)} %get-tuple-element.55), channel_id=1, source_target_pairs={{1,2},{2,1},{5,6},{6,5},{9,10},{10,9},{13,14},{14,13},{17,18},{18,... | collective-permute-start | bytes 264200 | tf_op jit(solution)/shard_map/ppermute | solution.py:541
  16.4 0.0 collective-permute-done.2.edge_ref
  16.5 2.2 %collective-permute-start.7 = (f32[15,4,128]{2,1,0:T(4,128)S(1)}, f32[15,4,128]{2,1,0:T(4,128)S(1)}, u32[]{:S(2)}, u32[]{:S(2)}) collective-permute-start(f32[15,4,128]{2,1,0:T(4,128)S(1)} %get-tuple-element.58), channel_id=1, source_target_pairs={{0,1},{1,0},{2,3},{3,2},{4,5},{5,4},{6,7},{7,6},{8,9},{9,8},{10,11... | collective-permute-start | bytes 92168 | tf_op jit(solution)/shard_map/ppermute | solution.py:541
  18.7 0.0 collective-permute-done.3.face_0_ref
  18.7 0.7 %collective-permute-start.8 = (f32[15,4,128]{2,1,0:T(4,128)S(1)}, f32[15,4,128]{2,1,0:T(4,128)S(1)}, u32[]{:S(2)}, u32[]{:S(2)}) collective-permute-start(f32[15,4,128]{2,1,0:T(4,128)S(1)} %get-tuple-element.59), channel_id=1, source_target_pairs={{1,2},{2,1},{5,6},{6,5},{9,10},{10,9},{13,14},{14,13},{17,18},{18,... | collective-permute-start | bytes 92168 | tf_op jit(solution)/shard_map/ppermute | solution.py:541
  19.3 0.5 %shard_map.123 = (f32[3,25,8,256]{3,2,1,0:T(8,128)S(1)}, f32[25,8,256]{2,1,0:T(8,128)S(1)}, f32[25,8,256]{2,1,0:T(8,128)S(1)}, f32[25,8,256]{2,1,0:T(8,128)S(1)}, f32[25,8,256]{2,1,0:T(8,128)S(1)}) custom-call(f32[41,8,128]{2,1,0:T(8,128)S(1)} %get-tuple-element.40.sides_ref, ...), custom_call_target="tpu_custom_call", output_to_operand_aliasing={{0}: (3, {}), {1}: (4, {}), {2}: (5, {}), {3}: (6, {}), {4}... | custom-call | flops 2662400 | bytes 2662400 | tf_op jit(solution)/shard_map/pallas_call | solution.py:600
  19.9 0.2 shard_map.124
  20.1 6.1 %shard_map.126 = (f32[16,8,128]{2,1,0:T(8,128)}, f32[16,8,128]{2,1,0:T(8,128)}, f32[16,8,128]{2,1,0:T(8,128)}, f32[16,8,128]{2,1,0:T(8,128)S(1)}, f32[16,8,128]{...) custom-call(f32[3,25,8,256]{3,2,1,0:T(8,128)S(1)} %get-tuple-element, ...), custom_call_target="tpu_custom_call", output_to_operand_aliasing={{6}: (5, {}), {7}: (6, {})} | custom-call | tf_op jit(solution)/shard_map/pallas_call | solution.py:653
  26.2 3.8 %collective-permute-start.9 = (f32[8,128]{1,0:T(8,128)S(1)}, f32[8,128]{1,0:T(8,128)S(1)}, u32[]{:S(2)}, u32[]{:S(2)}) collective-permute-start(f32[8,128]{1,0:T(8,128)S(1)} %get-tuple-element.65), channel_id=1, source_target_pairs={{0,1},{1,0},{2,3},{3,2},{4,5},{5,4},{6,7},{7,6},{8,9},{9,8},{10,11... | collective-permute-start | bytes 12296 | tf_op jit(solution)/shard_map/ppermute | solution.py:547
  30.0 0.8 %collective-permute-done.9 = f32[8,128]{1,0:T(8,128)S(1)} collective-permute-done((f32[8,128]{1,0:T(8,128)S(1)}, f32[8,128]{1,0:T(8,128)S(1)}, u32[]{:S(2)}, u32[]{:S(2)}) %collective-permute-start.9) | collective-permute-done | bytes 4128 | tf_op jit(solution)/shard_map/ppermute | solution.py:547
  30.9 10.9 %all_to_all.8 = f32[16,1,128]{2,1,0:T(1,128)S(1)} all-to-all(f32[16,1,128]{2,1,0:T(1,128)S(1)} %broadcast_in_dim.2), channel_id=1, replica_groups={{0,2,4,6,8,10,12,14,16,18,20,22,24,26,28,30},{1,3,5,7,9,11,13,15,17,19,..., dimensions={0} | all-to-all | bytes 16384 | tf_op jit(solution)/shard_map/all_to_all | solution.py:550
  41.8 0.8 %shard_map.127 = f32[16,8,128]{2,1,0:T(8,128)} custom-call(f32[16,8,128]{2,1,0:T(8,128)S(1)} %get-tuple-element.64.refs_0_, f32[16,128]{1,0:T(8,128)S(1)} %bitcast.1), custom_call_target="tpu_custom_call" | custom-call | tf_op jit(solution)/shard_map/pallas_call | solution.py:668
  (10 shorter events, 0.1 us)
Async XLA Ops:
  2.8 8.5 %collective-permute-start = (f32[21,8,128]{2,1,0:T(8,128)}, f32[21,8,128]{2,1,0:T(8,128)S(1)}, u32[]{:S(2)}, u32[]{:S(2)}) collective-permute-start(f32[21,8,128]{2,1,0:T(8,128)} %get-tuple-element.36), channel_id=1, source_target_pairs={{8,16},{16,8},{9,17},{17,9},{10,18},{18,10},{11,19},{19,11},{12,20... | collective-permute-start | bytes 258056 | tf_op jit(solution)/shard_map/ppermute | solution.py:541
  3.5 8.6 %collective-permute-start.1 = (f32[21,8,128]{2,1,0:T(8,128)}, f32[21,8,128]{2,1,0:T(8,128)S(1)}, u32[]{:S(2)}, u32[]{:S(2)}) collective-permute-start(f32[21,8,128]{2,1,0:T(8,128)} %get-tuple-element.37), channel_id=1, source_target_pairs={{0,8},{8,0},{16,24},{24,16},{1,9},{9,1},{17,25},{25,17},{2,10},{10... | collective-permute-start | bytes 258056 | tf_op jit(solution)/shard_map/ppermute | solution.py:541
  9.4 1.0 %copy-start = (f32[90,8,128]{2,1,0:T(8,128)S(1)}, f32[90,8,128]{2,1,0:T(8,128)}, u32[]{:S(2)}) copy-start(f32[90,8,128]{2,1,0:T(8,128)} %get-tuple-element.38.stack_ref) | copy-start | bytes 1105924
  10.6 8.1 %collective-permute-start.3 = (f32[84,4,128]{2,1,0:T(4,128)S(1)}, f32[84,4,128]{2,1,0:T(4,128)S(1)}, u32[]{:S(2)}, u32[]{:S(2)}) collective-permute-start(f32[84,4,128]{2,1,0:T(4,128)S(1)} %get-tuple-element.52), channel_id=1, source_target_pairs={{0,1},{1,0},{2,3},{3,2},{4,5},{5,4},{6,7},{7,6},{8,9},{9,8},{10,11... | collective-permute-start | bytes 516104 | tf_op jit(solution)/shard_map/ppermute | solution.py:541
  10.6 9.2 %collective-permute-start.4 = (f32[84,4,128]{2,1,0:T(4,128)S(1)}, f32[84,4,128]{2,1,0:T(4,128)S(1)}, u32[]{:S(2)}, u32[]{:S(2)}) collective-permute-start(f32[84,4,128]{2,1,0:T(4,128)S(1)} %get-tuple-element.53), channel_id=1, source_target_pairs={{1,2},{2,1},{5,6},{6,5},{9,10},{10,9},{13,14},{14,13},{17,18},{18,... | collective-permute-start | bytes 516104 | tf_op jit(solution)/shard_map/ppermute | solution.py:541
  12.2 4.2 %collective-permute-start.2 = (f32[12,8,128]{2,1,0:T(8,128)S(1)}, f32[12,8,128]{2,1,0:T(8,128)S(1)}, u32[]{:S(2)}, u32[]{:S(2)}) collective-permute-start(f32[12,8,128]{2,1,0:T(8,128)S(1)} %shard_map.121._edge_ref), channel_id=1, source_target_pairs={{0,4},{4,0},{1,5},{5,1},{2,6},{6,2},{3,7},{7,3},{8,12},{12,8},{9,1... | collective-permute-start | bytes 147464 | tf_op jit(solution)/shard_map/ppermute | solution.py:541
  13.8 6.0 %collective-permute-start.5 = (f32[43,4,128]{2,1,0:T(4,128)S(1)}, f32[43,4,128]{2,1,0:T(4,128)S(1)}, u32[]{:S(2)}, u32[]{:S(2)}) collective-permute-start(f32[43,4,128]{2,1,0:T(4,128)S(1)} %get-tuple-element.54), channel_id=1, source_target_pairs={{0,1},{1,0},{2,3},{3,2},{4,5},{5,4},{6,7},{7,6},{8,9},{9,8},{10,11... | collective-permute-start | bytes 264200 | tf_op jit(solution)/shard_map/ppermute | solution.py:541
  15.8 4.1 %collective-permute-start.6 = (f32[43,4,128]{2,1,0:T(4,128)S(1)}, f32[43,4,128]{2,1,0:T(4,128)S(1)}, u32[]{:S(2)}, u32[]{:S(2)}) collective-permute-start(f32[43,4,128]{2,1,0:T(4,128)S(1)} %get-tuple-element.55), channel_id=1, source_target_pairs={{1,2},{2,1},{5,6},{6,5},{9,10},{10,9},{13,14},{14,13},{17,18},{18,... | collective-permute-start | bytes 264200 | tf_op jit(solution)/shard_map/ppermute | solution.py:541
  16.5 3.6 %collective-permute-start.7 = (f32[15,4,128]{2,1,0:T(4,128)S(1)}, f32[15,4,128]{2,1,0:T(4,128)S(1)}, u32[]{:S(2)}, u32[]{:S(2)}) collective-permute-start(f32[15,4,128]{2,1,0:T(4,128)S(1)} %get-tuple-element.58), channel_id=1, source_target_pairs={{0,1},{1,0},{2,3},{3,2},{4,5},{5,4},{6,7},{7,6},{8,9},{9,8},{10,11... | collective-permute-start | bytes 92168 | tf_op jit(solution)/shard_map/ppermute | solution.py:541
  18.7 1.4 %collective-permute-start.8 = (f32[15,4,128]{2,1,0:T(4,128)S(1)}, f32[15,4,128]{2,1,0:T(4,128)S(1)}, u32[]{:S(2)}, u32[]{:S(2)}) collective-permute-start(f32[15,4,128]{2,1,0:T(4,128)S(1)} %get-tuple-element.59), channel_id=1, source_target_pairs={{1,2},{2,1},{5,6},{6,5},{9,10},{10,9},{13,14},{14,13},{17,18},{18,... | collective-permute-start | bytes 92168 | tf_op jit(solution)/shard_map/ppermute | solution.py:541
  26.2 4.6 %collective-permute-start.9 = (f32[8,128]{1,0:T(8,128)S(1)}, f32[8,128]{1,0:T(8,128)S(1)}, u32[]{:S(2)}, u32[]{:S(2)}) collective-permute-start(f32[8,128]{1,0:T(8,128)S(1)} %get-tuple-element.65), channel_id=1, source_target_pairs={{0,1},{1,0},{2,3},{3,2},{4,5},{5,4},{6,7},{7,6},{8,9},{9,8},{10,11... | collective-permute-start | bytes 12296 | tf_op jit(solution)/shard_map/ppermute | solution.py:547

commit v21 on v20

--- a/solution.py
+++ b/solution.py
@@ -275,25 +275,16 @@
 
 
 def unpack_own(load, bx, ok, tables, store):
-    def group(g, carry):
-        at = g * GROUP
+    for at in range(0, bx, GROUP):
         store(pl.ds(DEPTH + at, GROUP), 0, own_lanes(load(at * FIELDS, GROUP * FIELDS), ok, tables))
-        return carry
-
-    lax.fori_loop(0, bx // GROUP, group, 0)
 
 
 def unpack_own_edges(load, bx, ok, tables, store):
     half = bx // 2
-    for upper in range(2):
-
-        def group(g, carry):
-            at = g * GROUP
-            values = edge_lanes(load(at, GROUP), upper, ok, tables)
-            store(pl.ds(DEPTH + upper * half + at, GROUP), 1, values)
-            return carry
-
-        lax.fori_loop(0, half // GROUP, group, 0)
+    for at in range(0, half, GROUP):
+        edge = load(at, GROUP)
+        for upper in range(2):
+            store(pl.ds(DEPTH + upper * half + at, GROUP), 1, edge_lanes(edge, upper, ok, tables))
 
 
 def side_places(bx):
@@ -343,15 +334,11 @@
     tables_ref[...] = stack_ref[count + bx // 2 :]
     size = GROUP * FIELDS
 
-    def group(g, carry):
+    for g in range(bx // GROUP):
         at = pl.ds(g * size, size)
         tiles = stack_ref[at]
         for swap, ref in enumerate((z_0_ref, z_1_ref)):
             ref[at] = half_rows(tiles, swap)
-        return carry
-
-    lax.fori_loop(0, bx // GROUP, group, 0)
-    for g in range(bx // GROUP):
         vz = stack_ref[pl.ds(g * size, size)].reshape(GROUP, FIELDS, *stack_ref.shape[1:])[:, 1]
         store_next_rows((z_0_ref, z_1_ref), count + g * GROUP // (stack_ref.shape[1] // 2), vz)
     store = store_to([v_ref.at[d] for d in range(3)] + list(rest))

time: 42.9 us -> 42.5 us (level)
  Pallas kernels: 10.1 us -> 9.44 us
where the time goes in v21:
time: 42.5 us; the launch traced here: 42.2 us
  starting transfers between devices  18.4 us (43%)
  blocking collectives  10.9 us (26%)
  Pallas kernels  9.44 us (22%)
  waiting for transfers between devices  1.66 us (4%)
  local copies, waits for them, and re-layouts  1 us (2%)
  between operations  0.78 us (2%)
    ppermute x9, starting transfers between devices, swap(): lax.ppermute(a, axis, [(i, j) for k in range(start, count - 1, 2) for i,...  14.3 us
    all_to_all x1, blocking collectives, sum_everywhere(): lax.all_to_all(total, axes, 0, 0, tiled=True, axis_index_groups=groups)  10.9 us
    pallas_call x1, Pallas kernels, local(): pl.pallas_call(main_kernel, out_shape=(block,) * 5 + (shape(bz, by),) + t...  5.86 us
    ppermute x1, starting transfers between devices, sum_everywhere(): lax.ppermute(total, axes, [(i, i ^ 1) for i in range(devices)])  4.14 us
    pallas_call x1, Pallas kernels, local(): pl.pallas_call(pack_kernel, out_shape=(shape(bx // 2, bz, by), sent, sent...  2.17 us
    unnamed x2, local copies, waits for them, and re-layouts  0.99 us
  transfers between devices with their start and end apart: 10, of which 2 were waited for; matrix products, arithmetic and copies ran while one was open for 0% of the time, Pallas kernels for 2%

profile of v21, /device:TPU:0, one launch (start us, length us, event | category | flops | bytes accessed | tf_op | source)
XLA Modules:
  0.0 42.2 jit_solution(10109740439209199162)
XLA Ops:
  0.6 2.2 %shard_map.119 = (f32[8,8,128]{2,1,0:T(8,128)}, f32[21,8,128]{2,1,0:T(8,128)}, f32[21,8,128]{2,1,0:T(8,128)}, f32[90,8,128]{2,1,0:T(8,128)}) custom-call(f32[16,8,128]{2,1,0:T(8,128)} %vx_hbm.1, f32[16,8,128]{2,1,0:T(8,128)} %vz_hbm.1, f32[16,8,128]{2,1,0:T(8,128)} %vy_hbm.1, f32[16,8,128]{2,1,0:T(8,128)} %p_hbm.1, s32[16,8,128]{2,1,0:T(8,128)} %phase_hbm.1, ...), custom_call_target="tpu_custom_call" | custom-call | tf_op jit(solution)/shard_map/pallas_call | solution.py:555
  2.8 0.7 %collective-permute-start = (f32[21,8,128]{2,1,0:T(8,128)}, f32[21,8,128]{2,1,0:T(8,128)S(1)}, u32[]{:S(2)}, u32[]{:S(2)}) collective-permute-start(f32[21,8,128]{2,1,0:T(8,128)} %get-tuple-element.36), channel_id=1, source_target_pairs={{8,16},{16,8},{9,17},{17,9},{10,18},{18,10},{11,19},{19,11},{12,20... | collective-permute-start | bytes 258056 | tf_op jit(solution)/shard_map/ppermute | solution.py:528
  3.5 5.9 %collective-permute-start.1 = (f32[21,8,128]{2,1,0:T(8,128)}, f32[21,8,128]{2,1,0:T(8,128)S(1)}, u32[]{:S(2)}, u32[]{:S(2)}) collective-permute-start(f32[21,8,128]{2,1,0:T(8,128)} %get-tuple-element.37), channel_id=1, source_target_pairs={{0,8},{8,0},{16,24},{24,16},{1,9},{9,1},{17,25},{25,17},{2,10},{10... | collective-permute-start | bytes 258056 | tf_op jit(solution)/shard_map/ppermute | solution.py:528
  9.4 1.0 %copy-done = f32[90,8,128]{2,1,0:T(8,128)S(1)} copy-done((f32[90,8,128]{2,1,0:T(8,128)S(1)}, f32[90,8,128]{2,1,0:T(8,128)}, u32[]{:S(2)}) %copy-start) | copy-done | bytes 368664
  10.4 0.1 shard_map.120
  10.5 0.1 collective-permute-start.3
  10.6 0.7 %collective-permute-start.4 = (f32[84,4,128]{2,1,0:T(4,128)S(1)}, f32[84,4,128]{2,1,0:T(4,128)S(1)}, u32[]{:S(2)}, u32[]{:S(2)}) collective-permute-start(f32[84,4,128]{2,1,0:T(4,128)S(1)} %get-tuple-element.53), channel_id=1, source_target_pairs={{1,2},{2,1},{5,6},{6,5},{9,10},{10,9},{13,14},{14,13},{17,18},{18,... | collective-permute-start | bytes 516104 | tf_op jit(solution)/shard_map/ppermute | solution.py:528
  11.2 0.0 collective-permute-done.x_1_ref
  11.3 0.8 %collective-permute-done.1.x_0_ref = f32[21,8,128]{2,1,0:T(8,128)S(1)} collective-permute-done((f32[21,8,128]{2,1,0:T(8,128)}, f32[21,8,128]{2,1,0:T(8,128)S(1)}, u32[]{:S(2)}, u32[]{:S(2)}) %collective-permute-start.1) | collective-permute-done | bytes 86048 | tf_op jit(solution)/shard_map/ppermute | solution.py:528
  12.1 0.1 shard_map.121._edge_ref
  12.2 1.6 %collective-permute-start.2 = (f32[12,8,128]{2,1,0:T(8,128)S(1)}, f32[12,8,128]{2,1,0:T(8,128)S(1)}, u32[]{:S(2)}, u32[]{:S(2)}) collective-permute-start(f32[12,8,128]{2,1,0:T(8,128)S(1)} %shard_map.121._edge_ref), channel_id=1, source_target_pairs={{0,4},{4,0},{1,5},{5,1},{2,6},{6,2},{3,7},{7,3},{8,12},{12,8},{9,1... | collective-permute-start | bytes 147464 | tf_op jit(solution)/shard_map/ppermute | solution.py:528
  13.8 1.9 %collective-permute-start.5 = (f32[43,4,128]{2,1,0:T(4,128)S(1)}, f32[43,4,128]{2,1,0:T(4,128)S(1)}, u32[]{:S(2)}, u32[]{:S(2)}) collective-permute-start(f32[43,4,128]{2,1,0:T(4,128)S(1)} %get-tuple-element.54), channel_id=1, source_target_pairs={{0,1},{1,0},{2,3},{3,2},{4,5},{5,4},{6,7},{7,6},{8,9},{9,8},{10,11... | collective-permute-start | bytes 264200 | tf_op jit(solution)/shard_map/ppermute | solution.py:528
  15.7 0.7 %collective-permute-start.6 = (f32[43,4,128]{2,1,0:T(4,128)S(1)}, f32[43,4,128]{2,1,0:T(4,128)S(1)}, u32[]{:S(2)}, u32[]{:S(2)}) collective-permute-start(f32[43,4,128]{2,1,0:T(4,128)S(1)} %get-tuple-element.55), channel_id=1, source_target_pairs={{1,2},{2,1},{5,6},{6,5},{9,10},{10,9},{13,14},{14,13},{17,18},{18,... | collective-permute-start | bytes 264200 | tf_op jit(solution)/shard_map/ppermute | solution.py:528
  16.4 0.0 collective-permute-done.2.edge_ref
  16.4 2.2 %collective-permute-start.7 = (f32[15,4,128]{2,1,0:T(4,128)S(1)}, f32[15,4,128]{2,1,0:T(4,128)S(1)}, u32[]{:S(2)}, u32[]{:S(2)}) collective-permute-start(f32[15,4,128]{2,1,0:T(4,128)S(1)} %get-tuple-element.58), channel_id=1, source_target_pairs={{0,1},{1,0},{2,3},{3,2},{4,5},{5,4},{6,7},{7,6},{8,9},{9,8},{10,11... | collective-permute-start | bytes 92168 | tf_op jit(solution)/shard_map/ppermute | solution.py:528
  18.6 0.0 collective-permute-done.3.face_0_ref
  18.6 0.7 %collective-permute-start.8 = (f32[15,4,128]{2,1,0:T(4,128)S(1)}, f32[15,4,128]{2,1,0:T(4,128)S(1)}, u32[]{:S(2)}, u32[]{:S(2)}) collective-permute-start(f32[15,4,128]{2,1,0:T(4,128)S(1)} %get-tuple-element.59), channel_id=1, source_target_pairs={{1,2},{2,1},{5,6},{6,5},{9,10},{10,9},{13,14},{14,13},{17,18},{18,... | collective-permute-start | bytes 92168 | tf_op jit(solution)/shard_map/ppermute | solution.py:528
  19.3 0.2 shard_map.123
  19.5 0.1 shard_map.124
  19.7 5.9 %shard_map.126 = (f32[16,8,128]{2,1,0:T(8,128)}, f32[16,8,128]{2,1,0:T(8,128)}, f32[16,8,128]{2,1,0:T(8,128)}, f32[16,8,128]{2,1,0:T(8,128)S(1)}, f32[16,8,128]{...) custom-call(f32[3,25,8,256]{3,2,1,0:T(8,128)S(1)} %get-tuple-element, ...), custom_call_target="tpu_custom_call", output_to_operand_aliasing={{6}: (5, {}), {7}: (6, {})} | custom-call | tf_op jit(solution)/shard_map/pallas_call | solution.py:640
  25.5 4.1 %collective-permute-start.9 = (f32[8,128]{1,0:T(8,128)S(1)}, f32[8,128]{1,0:T(8,128)S(1)}, u32[]{:S(2)}, u32[]{:S(2)}) collective-permute-start(f32[8,128]{1,0:T(8,128)S(1)} %get-tuple-element.65), channel_id=1, source_target_pairs={{0,1},{1,0},{2,3},{3,2},{4,5},{5,4},{6,7},{7,6},{8,9},{9,8},{10,11... | collective-permute-start | bytes 12296 | tf_op jit(solution)/shard_map/ppermute | solution.py:534
  29.7 0.8 %collective-permute-done.9 = f32[8,128]{1,0:T(8,128)S(1)} collective-permute-done((f32[8,128]{1,0:T(8,128)S(1)}, f32[8,128]{1,0:T(8,128)S(1)}, u32[]{:S(2)}, u32[]{:S(2)}) %collective-permute-start.9) | collective-permute-done | bytes 4128 | tf_op jit(solution)/shard_map/ppermute | solution.py:534
  30.5 10.9 %all_to_all.8 = f32[16,1,128]{2,1,0:T(1,128)S(1)} all-to-all(f32[16,1,128]{2,1,0:T(1,128)S(1)} %broadcast_in_dim.2), channel_id=1, replica_groups={{0,2,4,6,8,10,12,14,16,18,20,22,24,26,28,30},{1,3,5,7,9,11,13,15,17,19,..., dimensions={0} | all-to-all | bytes 16384 | tf_op jit(solution)/shard_map/all_to_all | solution.py:537
  41.5 0.8 %shard_map.127 = f32[16,8,128]{2,1,0:T(8,128)} custom-call(f32[16,8,128]{2,1,0:T(8,128)S(1)} %get-tuple-element.64.refs_0_, f32[16,128]{1,0:T(8,128)S(1)} %bitcast.1), custom_call_target="tpu_custom_call" | custom-call | tf_op jit(solution)/shard_map/pallas_call | solution.py:655
  (10 shorter events, 0.1 us)
Async XLA Ops:
  2.8 8.4 %collective-permute-start = (f32[21,8,128]{2,1,0:T(8,128)}, f32[21,8,128]{2,1,0:T(8,128)S(1)}, u32[]{:S(2)}, u32[]{:S(2)}) collective-permute-start(f32[21,8,128]{2,1,0:T(8,128)} %get-tuple-element.36), channel_id=1, source_target_pairs={{8,16},{16,8},{9,17},{17,9},{10,18},{18,10},{11,19},{19,11},{12,20... | collective-permute-start | bytes 258056 | tf_op jit(solution)/shard_map/ppermute | solution.py:528
  3.5 8.6 %collective-permute-start.1 = (f32[21,8,128]{2,1,0:T(8,128)}, f32[21,8,128]{2,1,0:T(8,128)S(1)}, u32[]{:S(2)}, u32[]{:S(2)}) collective-permute-start(f32[21,8,128]{2,1,0:T(8,128)} %get-tuple-element.37), channel_id=1, source_target_pairs={{0,8},{8,0},{16,24},{24,16},{1,9},{9,1},{17,25},{25,17},{2,10},{10... | collective-permute-start | bytes 258056 | tf_op jit(solution)/shard_map/ppermute | solution.py:528
  9.4 1.0 %copy-start = (f32[90,8,128]{2,1,0:T(8,128)S(1)}, f32[90,8,128]{2,1,0:T(8,128)}, u32[]{:S(2)}) copy-start(f32[90,8,128]{2,1,0:T(8,128)} %get-tuple-element.38.stack_ref) | copy-start | bytes 1105924
  10.5 8.1 %collective-permute-start.3 = (f32[84,4,128]{2,1,0:T(4,128)S(1)}, f32[84,4,128]{2,1,0:T(4,128)S(1)}, u32[]{:S(2)}, u32[]{:S(2)}) collective-permute-start(f32[84,4,128]{2,1,0:T(4,128)S(1)} %get-tuple-element.52), channel_id=1, source_target_pairs={{0,1},{1,0},{2,3},{3,2},{4,5},{5,4},{6,7},{7,6},{8,9},{9,8},{10,11... | collective-permute-start | bytes 516104 | tf_op jit(solution)/shard_map/ppermute | solution.py:528
  10.6 8.9 %collective-permute-start.4 = (f32[84,4,128]{2,1,0:T(4,128)S(1)}, f32[84,4,128]{2,1,0:T(4,128)S(1)}, u32[]{:S(2)}, u32[]{:S(2)}) collective-permute-start(f32[84,4,128]{2,1,0:T(4,128)S(1)} %get-tuple-element.53), channel_id=1, source_target_pairs={{1,2},{2,1},{5,6},{6,5},{9,10},{10,9},{13,14},{14,13},{17,18},{18,... | collective-permute-start | bytes 516104 | tf_op jit(solution)/shard_map/ppermute | solution.py:528
  12.2 4.2 %collective-permute-start.2 = (f32[12,8,128]{2,1,0:T(8,128)S(1)}, f32[12,8,128]{2,1,0:T(8,128)S(1)}, u32[]{:S(2)}, u32[]{:S(2)}) collective-permute-start(f32[12,8,128]{2,1,0:T(8,128)S(1)} %shard_map.121._edge_ref), channel_id=1, source_target_pairs={{0,4},{4,0},{1,5},{5,1},{2,6},{6,2},{3,7},{7,3},{8,12},{12,8},{9,1... | collective-permute-start | bytes 147464 | tf_op jit(solution)/shard_map/ppermute | solution.py:528
  13.8 5.7 %collective-permute-start.5 = (f32[43,4,128]{2,1,0:T(4,128)S(1)}, f32[43,4,128]{2,1,0:T(4,128)S(1)}, u32[]{:S(2)}, u32[]{:S(2)}) collective-permute-start(f32[43,4,128]{2,1,0:T(4,128)S(1)} %get-tuple-element.54), channel_id=1, source_target_pairs={{0,1},{1,0},{2,3},{3,2},{4,5},{5,4},{6,7},{7,6},{8,9},{9,8},{10,11... | collective-permute-start | bytes 264200 | tf_op jit(solution)/shard_map/ppermute | solution.py:528
  15.7 3.8 %collective-permute-start.6 = (f32[43,4,128]{2,1,0:T(4,128)S(1)}, f32[43,4,128]{2,1,0:T(4,128)S(1)}, u32[]{:S(2)}, u32[]{:S(2)}) collective-permute-start(f32[43,4,128]{2,1,0:T(4,128)S(1)} %get-tuple-element.55), channel_id=1, source_target_pairs={{1,2},{2,1},{5,6},{6,5},{9,10},{10,9},{13,14},{14,13},{17,18},{18,... | collective-permute-start | bytes 264200 | tf_op jit(solution)/shard_map/ppermute | solution.py:528
  16.4 3.3 %collective-permute-start.7 = (f32[15,4,128]{2,1,0:T(4,128)S(1)}, f32[15,4,128]{2,1,0:T(4,128)S(1)}, u32[]{:S(2)}, u32[]{:S(2)}) collective-permute-start(f32[15,4,128]{2,1,0:T(4,128)S(1)} %get-tuple-element.58), channel_id=1, source_target_pairs={{0,1},{1,0},{2,3},{3,2},{4,5},{5,4},{6,7},{7,6},{8,9},{9,8},{10,11... | collective-permute-start | bytes 92168 | tf_op jit(solution)/shard_map/ppermute | solution.py:528
  18.6 1.1 %collective-permute-start.8 = (f32[15,4,128]{2,1,0:T(4,128)S(1)}, f32[15,4,128]{2,1,0:T(4,128)S(1)}, u32[]{:S(2)}, u32[]{:S(2)}) collective-permute-start(f32[15,4,128]{2,1,0:T(4,128)S(1)} %get-tuple-element.59), channel_id=1, source_target_pairs={{1,2},{2,1},{5,6},{6,5},{9,10},{10,9},{13,14},{14,13},{17,18},{18,... | collective-permute-start | bytes 92168 | tf_op jit(solution)/shard_map/ppermute | solution.py:528
  25.5 5.0 %collective-permute-start.9 = (f32[8,128]{1,0:T(8,128)S(1)}, f32[8,128]{1,0:T(8,128)S(1)}, u32[]{:S(2)}, u32[]{:S(2)}) collective-permute-start(f32[8,128]{1,0:T(8,128)S(1)} %get-tuple-element.65), channel_id=1, source_target_pairs={{0,1},{1,0},{2,3},{3,2},{4,5},{5,4},{6,7},{7,6},{8,9},{9,8},{10,11... | collective-permute-start | bytes 12296 | tf_op jit(solution)/shard_map/ppermute | solution.py:534

commit v22 on v21

--- a/solution.py
+++ b/solution.py
@@ -51,14 +51,16 @@
     pl.when(odd(axis))(lambda: body(pair[1], pair[0]))
 
 
-def start_copies(sources, targets, sems, order):
+def start_copies(sources, targets, sems):
+    half = sources[0].shape[0] // 2
     copies = {}
-    for g in order:
-        at = pl.ds(g * GROUP, GROUP)
-        copies[g] = [
-            pltpu.make_async_copy(a.at[at], b.at[at], sems.at[g, f]) for f, (a, b) in enumerate(zip(sources, targets))
+    for n in range(2):
+        at = pl.ds(n * half, half)
+        copies[n * (half // GROUP)] = [
+            pltpu.make_async_copy(a.at[at], b.at[at], sems.at[n, f]) for f, (a, b) in enumerate(zip(sources, targets))
         ]
-        for copy in copies[g]:
+    for half_copies in copies.values():
+        for copy in half_copies:
             copy.start()
     return copies
 
@@ -109,15 +111,15 @@
 ):
     bx, bz, by = phase_ref.shape
     targets = [field_ref.at[f] for f in range(FIELDS - 1)] + [phase_ref]
-    groups = bx // GROUP
-    order = [0, groups - 1] + list(range(1, groups - 1))
-    copies = start_copies((vx_hbm, vz_hbm, vy_hbm, p_hbm, phase_hbm), targets, sems, order)
+    copies = start_copies((vx_hbm, vz_hbm, vy_hbm, p_hbm, phase_hbm), targets, sems)
     table_refs = (scale_ref, power_ref, rho_ref)
     pairs = zip((scale_hbm, power_hbm, rho_hbm), table_refs)
     table_copies = [pltpu.make_async_copy(a, b, table_sems.at[n]) for n, (a, b) in enumerate(pairs)]
     for copy in table_copies:
         copy.start()
+    groups = bx // GROUP
     half = groups // 2
+    order = list(range(half)) + list(range(groups - 1, half, -1)) + [half]
     outs = []
 
     def out(source, target):
@@ -146,15 +148,16 @@
 
     edges = {}
     for g in order:
-        for copy in copies[g]:
-            copy.wait()
+        if g in (0, groups - 1):
+            for copy in copies[0 if g == 0 else half]:
+                copy.wait()
         fields = clean_group(g, field_ref, phase_ref)
         for f, a in enumerate(fields):
             for i in range(GROUP):
                 stack_ref[(g * GROUP + i) * FIELDS + f] = a[i]
         at = pl.ds(g * GROUP * FIELDS, GROUP * FIELDS)
         out(stack_ref.at[at], stack_hbm.at[at])
-        if g == 1:
+        if g == groups - 1:
             by_parity("gx", (x_0_hbm, x_1_hbm), start_x)
         upper, n = divmod(g, half)
         edge = edges.get(n, jnp.zeros((GROUP, bz, by), jnp.float32))

time: 42.5 us -> 42.4 us (level)
  no operation moved by 1% of the time
where the time goes in v22:
time: 42.4 us; the launch traced here: 42.1 us
  starting transfers between devices  18.4 us (43%)
  blocking collectives  10.9 us (26%)
  Pallas kernels  9.33 us (22%)
  waiting for transfers between devices  1.66 us (4%)
  local copies, waits for them, and re-layouts  1 us (2%)
  between operations  0.78 us (2%)
    ppermute x9, starting transfers between devices, swap(): lax.ppermute(a, axis, [(i, j) for k in range(start, count - 1, 2) for i,...  14.3 us
    all_to_all x1, blocking collectives, sum_everywhere(): lax.all_to_all(total, axes, 0, 0, tiled=True, axis_index_groups=groups)  10.9 us
    pallas_call x1, Pallas kernels, local(): pl.pallas_call(main_kernel, out_shape=(block,) * 5 + (shape(bz, by),) + t...  5.86 us
    ppermute x1, starting transfers between devices, sum_everywhere(): lax.ppermute(total, axes, [(i, i ^ 1) for i in range(devices)])  4.14 us
    pallas_call x1, Pallas kernels, local(): pl.pallas_call(pack_kernel, out_shape=(shape(bx // 2, bz, by), sent, sent...  2.06 us
    unnamed x2, local copies, waits for them, and re-layouts  0.99 us
  transfers between devices with their start and end apart: 10, of which 2 were waited for; matrix products, arithmetic and copies ran while one was open for 0% of the time, Pallas kernels for 2%

profile of v22, /device:TPU:0, one launch (start us, length us, event | category | flops | bytes accessed | tf_op | source)
XLA Modules:
  0.0 42.1 jit_solution(3173594383624657554)
XLA Ops:
  0.6 2.1 %shard_map.119 = (f32[8,8,128]{2,1,0:T(8,128)}, f32[21,8,128]{2,1,0:T(8,128)}, f32[21,8,128]{2,1,0:T(8,128)}, f32[90,8,128]{2,1,0:T(8,128)}) custom-call(f32[16,8,128]{2,1,0:T(8,128)} %vx_hbm.1, f32[16,8,128]{2,1,0:T(8,128)} %vz_hbm.1, f32[16,8,128]{2,1,0:T(8,128)} %vy_hbm.1, f32[16,8,128]{2,1,0:T(8,128)} %p_hbm.1, s32[16,8,128]{2,1,0:T(8,128)} %phase_hbm.1, ...), custom_call_target="tpu_custom_call" | custom-call | tf_op jit(solution)/shard_map/pallas_call | solution.py:558
  2.7 0.7 %collective-permute-start = (f32[21,8,128]{2,1,0:T(8,128)}, f32[21,8,128]{2,1,0:T(8,128)S(1)}, u32[]{:S(2)}, u32[]{:S(2)}) collective-permute-start(f32[21,8,128]{2,1,0:T(8,128)} %get-tuple-element.36), channel_id=1, source_target_pairs={{8,16},{16,8},{9,17},{17,9},{10,18},{18,10},{11,19},{19,11},{12,20... | collective-permute-start | bytes 258056 | tf_op jit(solution)/shard_map/ppermute | solution.py:531
  3.4 5.9 %collective-permute-start.1 = (f32[21,8,128]{2,1,0:T(8,128)}, f32[21,8,128]{2,1,0:T(8,128)S(1)}, u32[]{:S(2)}, u32[]{:S(2)}) collective-permute-start(f32[21,8,128]{2,1,0:T(8,128)} %get-tuple-element.37), channel_id=1, source_target_pairs={{0,8},{8,0},{16,24},{24,16},{1,9},{9,1},{17,25},{25,17},{2,10},{10... | collective-permute-start | bytes 258056 | tf_op jit(solution)/shard_map/ppermute | solution.py:531
  9.3 1.0 %copy-done = f32[90,8,128]{2,1,0:T(8,128)S(1)} copy-done((f32[90,8,128]{2,1,0:T(8,128)S(1)}, f32[90,8,128]{2,1,0:T(8,128)}, u32[]{:S(2)}) %copy-start) | copy-done | bytes 368664
  10.3 0.1 shard_map.120
  10.4 0.1 collective-permute-start.3
  10.5 0.7 %collective-permute-start.4 = (f32[84,4,128]{2,1,0:T(4,128)S(1)}, f32[84,4,128]{2,1,0:T(4,128)S(1)}, u32[]{:S(2)}, u32[]{:S(2)}) collective-permute-start(f32[84,4,128]{2,1,0:T(4,128)S(1)} %get-tuple-element.53), channel_id=1, source_target_pairs={{1,2},{2,1},{5,6},{6,5},{9,10},{10,9},{13,14},{14,13},{17,18},{18,... | collective-permute-start | bytes 516104 | tf_op jit(solution)/shard_map/ppermute | solution.py:531
  11.2 0.8 %collective-permute-done.1.x_0_ref = f32[21,8,128]{2,1,0:T(8,128)S(1)} collective-permute-done((f32[21,8,128]{2,1,0:T(8,128)}, f32[21,8,128]{2,1,0:T(8,128)S(1)}, u32[]{:S(2)}, u32[]{:S(2)}) %collective-permute-start.1) | collective-permute-done | bytes 86048 | tf_op jit(solution)/shard_map/ppermute | solution.py:531
  12.0 0.1 shard_map.121._edge_ref
  12.1 1.6 %collective-permute-start.2 = (f32[12,8,128]{2,1,0:T(8,128)S(1)}, f32[12,8,128]{2,1,0:T(8,128)S(1)}, u32[]{:S(2)}, u32[]{:S(2)}) collective-permute-start(f32[12,8,128]{2,1,0:T(8,128)S(1)} %shard_map.121._edge_ref), channel_id=1, source_target_pairs={{0,4},{4,0},{1,5},{5,1},{2,6},{6,2},{3,7},{7,3},{8,12},{12,8},{9,1... | collective-permute-start | bytes 147464 | tf_op jit(solution)/shard_map/ppermute | solution.py:531
  13.7 1.9 %collective-permute-start.5 = (f32[43,4,128]{2,1,0:T(4,128)S(1)}, f32[43,4,128]{2,1,0:T(4,128)S(1)}, u32[]{:S(2)}, u32[]{:S(2)}) collective-permute-start(f32[43,4,128]{2,1,0:T(4,128)S(1)} %get-tuple-element.54), channel_id=1, source_target_pairs={{0,1},{1,0},{2,3},{3,2},{4,5},{5,4},{6,7},{7,6},{8,9},{9,8},{10,11... | collective-permute-start | bytes 264200 | tf_op jit(solution)/shard_map/ppermute | solution.py:531
  15.6 0.7 %collective-permute-start.6 = (f32[43,4,128]{2,1,0:T(4,128)S(1)}, f32[43,4,128]{2,1,0:T(4,128)S(1)}, u32[]{:S(2)}, u32[]{:S(2)}) collective-permute-start(f32[43,4,128]{2,1,0:T(4,128)S(1)} %get-tuple-element.55), channel_id=1, source_target_pairs={{1,2},{2,1},{5,6},{6,5},{9,10},{10,9},{13,14},{14,13},{17,18},{18,... | collective-permute-start | bytes 264200 | tf_op jit(solution)/shard_map/ppermute | solution.py:531
  16.3 0.0 collective-permute-done.2.edge_ref
  16.3 2.2 %collective-permute-start.7 = (f32[15,4,128]{2,1,0:T(4,128)S(1)}, f32[15,4,128]{2,1,0:T(4,128)S(1)}, u32[]{:S(2)}, u32[]{:S(2)}) collective-permute-start(f32[15,4,128]{2,1,0:T(4,128)S(1)} %get-tuple-element.58), channel_id=1, source_target_pairs={{0,1},{1,0},{2,3},{3,2},{4,5},{5,4},{6,7},{7,6},{8,9},{9,8},{10,11... | collective-permute-start | bytes 92168 | tf_op jit(solution)/shard_map/ppermute | solution.py:531
  18.5 0.7 %collective-permute-start.8 = (f32[15,4,128]{2,1,0:T(4,128)S(1)}, f32[15,4,128]{2,1,0:T(4,128)S(1)}, u32[]{:S(2)}, u32[]{:S(2)}) collective-permute-start(f32[15,4,128]{2,1,0:T(4,128)S(1)} %get-tuple-element.59), channel_id=1, source_target_pairs={{1,2},{2,1},{5,6},{6,5},{9,10},{10,9},{13,14},{14,13},{17,18},{18,... | collective-permute-start | bytes 92168 | tf_op jit(solution)/shard_map/ppermute | solution.py:531
  19.2 0.2 shard_map.123
  19.4 0.0 collective-permute-done.5.corner_0_ref
  19.4 0.0 collective-permute-done.6.corner_1_ref
  19.4 0.1 shard_map.124
  19.6 5.9 %shard_map.126 = (f32[16,8,128]{2,1,0:T(8,128)}, f32[16,8,128]{2,1,0:T(8,128)}, f32[16,8,128]{2,1,0:T(8,128)}, f32[16,8,128]{2,1,0:T(8,128)S(1)}, f32[16,8,128]{...) custom-call(f32[3,25,8,256]{3,2,1,0:T(8,128)S(1)} %get-tuple-element, ...), custom_call_target="tpu_custom_call", output_to_operand_aliasing={{6}: (5, {}), {7}: (6, {})} | custom-call | tf_op jit(solution)/shard_map/pallas_call | solution.py:643
  25.4 4.1 %collective-permute-start.9 = (f32[8,128]{1,0:T(8,128)S(1)}, f32[8,128]{1,0:T(8,128)S(1)}, u32[]{:S(2)}, u32[]{:S(2)}) collective-permute-start(f32[8,128]{1,0:T(8,128)S(1)} %get-tuple-element.65), channel_id=1, source_target_pairs={{0,1},{1,0},{2,3},{3,2},{4,5},{5,4},{6,7},{7,6},{8,9},{9,8},{10,11... | collective-permute-start | bytes 12296 | tf_op jit(solution)/shard_map/ppermute | solution.py:537
  29.6 0.8 %collective-permute-done.9 = f32[8,128]{1,0:T(8,128)S(1)} collective-permute-done((f32[8,128]{1,0:T(8,128)S(1)}, f32[8,128]{1,0:T(8,128)S(1)}, u32[]{:S(2)}, u32[]{:S(2)}) %collective-permute-start.9) | collective-permute-done | bytes 4128 | tf_op jit(solution)/shard_map/ppermute | solution.py:537
  30.4 10.9 %all_to_all.8 = f32[16,1,128]{2,1,0:T(1,128)S(1)} all-to-all(f32[16,1,128]{2,1,0:T(1,128)S(1)} %broadcast_in_dim.2), channel_id=1, replica_groups={{0,2,4,6,8,10,12,14,16,18,20,22,24,26,28,30},{1,3,5,7,9,11,13,15,17,19,..., dimensions={0} | all-to-all | bytes 16384 | tf_op jit(solution)/shard_map/all_to_all | solution.py:540
  41.4 0.8 %shard_map.127 = f32[16,8,128]{2,1,0:T(8,128)} custom-call(f32[16,8,128]{2,1,0:T(8,128)S(1)} %get-tuple-element.64.refs_0_, f32[16,128]{1,0:T(8,128)S(1)} %bitcast.1), custom_call_target="tpu_custom_call" | custom-call | tf_op jit(solution)/shard_map/pallas_call | solution.py:658
  (10 shorter events, 0.1 us)
Async XLA Ops:
  2.7 8.4 %collective-permute-start = (f32[21,8,128]{2,1,0:T(8,128)}, f32[21,8,128]{2,1,0:T(8,128)S(1)}, u32[]{:S(2)}, u32[]{:S(2)}) collective-permute-start(f32[21,8,128]{2,1,0:T(8,128)} %get-tuple-element.36), channel_id=1, source_target_pairs={{8,16},{16,8},{9,17},{17,9},{10,18},{18,10},{11,19},{19,11},{12,20... | collective-permute-start | bytes 258056 | tf_op jit(solution)/shard_map/ppermute | solution.py:531
  3.4 8.6 %collective-permute-start.1 = (f32[21,8,128]{2,1,0:T(8,128)}, f32[21,8,128]{2,1,0:T(8,128)S(1)}, u32[]{:S(2)}, u32[]{:S(2)}) collective-permute-start(f32[21,8,128]{2,1,0:T(8,128)} %get-tuple-element.37), channel_id=1, source_target_pairs={{0,8},{8,0},{16,24},{24,16},{1,9},{9,1},{17,25},{25,17},{2,10},{10... | collective-permute-start | bytes 258056 | tf_op jit(solution)/shard_map/ppermute | solution.py:531
  9.3 1.0 %copy-start = (f32[90,8,128]{2,1,0:T(8,128)S(1)}, f32[90,8,128]{2,1,0:T(8,128)}, u32[]{:S(2)}) copy-start(f32[90,8,128]{2,1,0:T(8,128)} %get-tuple-element.38.stack_ref) | copy-start | bytes 1105924
  10.4 8.1 %collective-permute-start.3 = (f32[84,4,128]{2,1,0:T(4,128)S(1)}, f32[84,4,128]{2,1,0:T(4,128)S(1)}, u32[]{:S(2)}, u32[]{:S(2)}) collective-permute-start(f32[84,4,128]{2,1,0:T(4,128)S(1)} %get-tuple-element.52), channel_id=1, source_target_pairs={{0,1},{1,0},{2,3},{3,2},{4,5},{5,4},{6,7},{7,6},{8,9},{9,8},{10,11... | collective-permute-start | bytes 516104 | tf_op jit(solution)/shard_map/ppermute | solution.py:531
  10.5 8.9 %collective-permute-start.4 = (f32[84,4,128]{2,1,0:T(4,128)S(1)}, f32[84,4,128]{2,1,0:T(4,128)S(1)}, u32[]{:S(2)}, u32[]{:S(2)}) collective-permute-start(f32[84,4,128]{2,1,0:T(4,128)S(1)} %get-tuple-element.53), channel_id=1, source_target_pairs={{1,2},{2,1},{5,6},{6,5},{9,10},{10,9},{13,14},{14,13},{17,18},{18,... | collective-permute-start | bytes 516104 | tf_op jit(solution)/shard_map/ppermute | solution.py:531
  12.1 4.2 %collective-permute-start.2 = (f32[12,8,128]{2,1,0:T(8,128)S(1)}, f32[12,8,128]{2,1,0:T(8,128)S(1)}, u32[]{:S(2)}, u32[]{:S(2)}) collective-permute-start(f32[12,8,128]{2,1,0:T(8,128)S(1)} %shard_map.121._edge_ref), channel_id=1, source_target_pairs={{0,4},{4,0},{1,5},{5,1},{2,6},{6,2},{3,7},{7,3},{8,12},{12,8},{9,1... | collective-permute-start | bytes 147464 | tf_op jit(solution)/shard_map/ppermute | solution.py:531
  13.7 5.7 %collective-permute-start.5 = (f32[43,4,128]{2,1,0:T(4,128)S(1)}, f32[43,4,128]{2,1,0:T(4,128)S(1)}, u32[]{:S(2)}, u32[]{:S(2)}) collective-permute-start(f32[43,4,128]{2,1,0:T(4,128)S(1)} %get-tuple-element.54), channel_id=1, source_target_pairs={{0,1},{1,0},{2,3},{3,2},{4,5},{5,4},{6,7},{7,6},{8,9},{9,8},{10,11... | collective-permute-start | bytes 264200 | tf_op jit(solution)/shard_map/ppermute | solution.py:531
  15.6 3.8 %collective-permute-start.6 = (f32[43,4,128]{2,1,0:T(4,128)S(1)}, f32[43,4,128]{2,1,0:T(4,128)S(1)}, u32[]{:S(2)}, u32[]{:S(2)}) collective-permute-start(f32[43,4,128]{2,1,0:T(4,128)S(1)} %get-tuple-element.55), channel_id=1, source_target_pairs={{1,2},{2,1},{5,6},{6,5},{9,10},{10,9},{13,14},{14,13},{17,18},{18,... | collective-permute-start | bytes 264200 | tf_op jit(solution)/shard_map/ppermute | solution.py:531
  16.3 3.3 %collective-permute-start.7 = (f32[15,4,128]{2,1,0:T(4,128)S(1)}, f32[15,4,128]{2,1,0:T(4,128)S(1)}, u32[]{:S(2)}, u32[]{:S(2)}) collective-permute-start(f32[15,4,128]{2,1,0:T(4,128)S(1)} %get-tuple-element.58), channel_id=1, source_target_pairs={{0,1},{1,0},{2,3},{3,2},{4,5},{5,4},{6,7},{7,6},{8,9},{9,8},{10,11... | collective-permute-start | bytes 92168 | tf_op jit(solution)/shard_map/ppermute | solution.py:531
  18.5 1.1 %collective-permute-start.8 = (f32[15,4,128]{2,1,0:T(4,128)S(1)}, f32[15,4,128]{2,1,0:T(4,128)S(1)}, u32[]{:S(2)}, u32[]{:S(2)}) collective-permute-start(f32[15,4,128]{2,1,0:T(4,128)S(1)} %get-tuple-element.59), channel_id=1, source_target_pairs={{1,2},{2,1},{5,6},{6,5},{9,10},{10,9},{13,14},{14,13},{17,18},{18,... | collective-permute-start | bytes 92168 | tf_op jit(solution)/shard_map/ppermute | solution.py:531
  25.4 5.0 %collective-permute-start.9 = (f32[8,128]{1,0:T(8,128)S(1)}, f32[8,128]{1,0:T(8,128)S(1)}, u32[]{:S(2)}, u32[]{:S(2)}) collective-permute-start(f32[8,128]{1,0:T(8,128)S(1)} %get-tuple-element.65), channel_id=1, source_target_pairs={{0,1},{1,0},{2,3},{3,2},{4,5},{5,4},{6,7},{7,6},{8,9},{9,8},{10,11... | collective-permute-start | bytes 12296 | tf_op jit(solution)/shard_map/ppermute | solution.py:537

commit v23 on v22

--- a/solution.py
+++ b/solution.py
@@ -79,12 +79,8 @@
 
 
 def add_edge(edge, a, base):
-    by = edge.shape[-1]
-    lane = iota((1,) * (edge.ndim - 1) + (by,), edge.ndim - 1)
-    first = pltpu.roll(a, base, a.ndim - 1) if base else a
-    edge = jnp.where((lane >= base) & (lane <= base + DEPTH), first, edge)
-    last = pltpu.roll(a, (base + LANE_STEP) % by, a.ndim - 1)
-    return jnp.where((lane > base + DEPTH) & (lane < base + LANE_STEP), last, edge)
+    lane = iota((1,) * (edge.ndim - 1) + edge.shape[-1:], edge.ndim - 1)
+    return jnp.where((lane >= base) & (lane < base + LANE_STEP), pltpu.roll(a, base + DEPTH, a.ndim - 1), edge)
 
 
 def add_edges(edge, fields, upper):
@@ -100,9 +96,7 @@
     right = (lane <= DEPTH) & (iy < lax.axis_size("gy") - 1)
     left = (lane >= by - DEPTH) & (iy > 0)
     shift = by // 2 * upper + LANE_STEP * f
-    a = pltpu.roll(edge, by - shift, edge.ndim - 1) if shift else edge
-    b = pltpu.roll(edge, (by - LANE_STEP - shift) % by, edge.ndim - 1)
-    return jnp.where(right, a, jnp.where(left, b, 0.0))
+    return jnp.where(right | left, pltpu.roll(edge, by - DEPTH - shift, edge.ndim - 1), 0.0)
 
 
 def pack_kernel(
@@ -580,7 +574,7 @@
         if ny == 2:
             return side
         lane = iota(side.shape, 2) % (by // 2) % LANE_STEP
-        return jnp.where((lane <= DEPTH) == (lax.rem(iy, 2) == 0), side, swap(edge, "gy", 1))
+        return jnp.where((lane >= DEPTH) == (lax.rem(iy, 2) == 0), side, swap(edge, "gy", 1))
 
     estimate = lambda size: pl.CostEstimate(
         flops=4 * size * bz * by, bytes_accessed=size * bz * by * 4, transcendentals=0

time: 42.4 us -> 42.3 us (level)
  transfers between devices with their start and end apart: 10 -> 10, of which waited for: 2 -> 2; matrix products, arithmetic and copies ran while one was open for 0% -> 0% of each run, Pallas kernels for 2% -> 1%
where the time goes in v23:
time: 42.3 us; the launch traced here: 42 us
  starting transfers between devices  18.4 us (43%)
  blocking collectives  10.9 us (26%)
  Pallas kernels  9.18 us (22%)
  waiting for transfers between devices  1.66 us (4%)
  local copies, waits for them, and re-layouts  1 us (2%)
  between operations  0.78 us (2%)
    ppermute x9, starting transfers between devices, swap(): lax.ppermute(a, axis, [(i, j) for k in range(start, count - 1, 2) for i,...  14.3 us
    all_to_all x1, blocking collectives, sum_everywhere(): lax.all_to_all(total, axes, 0, 0, tiled=True, axis_index_groups=groups)  10.9 us
    pallas_call x1, Pallas kernels, local(): pl.pallas_call(main_kernel, out_shape=(block,) * 5 + (shape(bz, by),) + t...  5.84 us
    ppermute x1, starting transfers between devices, sum_everywhere(): lax.ppermute(total, axes, [(i, i ^ 1) for i in range(devices)])  4.16 us
    pallas_call x1, Pallas kernels, local(): pl.pallas_call(pack_kernel, out_shape=(shape(bx // 2, bz, by), sent, sent...  1.98 us
    unnamed x2, local copies, waits for them, and re-layouts  0.99 us
  transfers between devices with their start and end apart: 10, of which 2 were waited for; matrix products, arithmetic and copies ran while one was open for 0% of the time, Pallas kernels for 1%

profile of v23, /device:TPU:0, one launch (start us, length us, event | category | flops | bytes accessed | tf_op | source)
XLA Modules:
  0.0 42.0 jit_solution(10001273474589665631)
XLA Ops:
  0.6 2.0 %shard_map.119 = (f32[8,8,128]{2,1,0:T(8,128)}, f32[21,8,128]{2,1,0:T(8,128)}, f32[21,8,128]{2,1,0:T(8,128)}, f32[90,8,128]{2,1,0:T(8,128)}) custom-call(f32[16,8,128]{2,1,0:T(8,128)} %vx_hbm.1, f32[16,8,128]{2,1,0:T(8,128)} %vz_hbm.1, f32[16,8,128]{2,1,0:T(8,128)} %vy_hbm.1, f32[16,8,128]{2,1,0:T(8,128)} %p_hbm.1, s32[16,8,128]{2,1,0:T(8,128)} %phase_hbm.1, ...), custom_call_target="tpu_custom_call" | custom-call | tf_op jit(solution)/shard_map/pallas_call | solution.py:552
  2.6 0.7 %collective-permute-start = (f32[21,8,128]{2,1,0:T(8,128)}, f32[21,8,128]{2,1,0:T(8,128)S(1)}, u32[]{:S(2)}, u32[]{:S(2)}) collective-permute-start(f32[21,8,128]{2,1,0:T(8,128)} %get-tuple-element.36), channel_id=1, source_target_pairs={{8,16},{16,8},{9,17},{17,9},{10,18},{18,10},{11,19},{19,11},{12,20... | collective-permute-start | bytes 258056 | tf_op jit(solution)/shard_map/ppermute | solution.py:525
  3.3 5.9 %collective-permute-start.1 = (f32[21,8,128]{2,1,0:T(8,128)}, f32[21,8,128]{2,1,0:T(8,128)S(1)}, u32[]{:S(2)}, u32[]{:S(2)}) collective-permute-start(f32[21,8,128]{2,1,0:T(8,128)} %get-tuple-element.37), channel_id=1, source_target_pairs={{0,8},{8,0},{16,24},{24,16},{1,9},{9,1},{17,25},{25,17},{2,10},{10... | collective-permute-start | bytes 258056 | tf_op jit(solution)/shard_map/ppermute | solution.py:525
  9.2 1.0 %copy-done = f32[90,8,128]{2,1,0:T(8,128)S(1)} copy-done((f32[90,8,128]{2,1,0:T(8,128)S(1)}, f32[90,8,128]{2,1,0:T(8,128)}, u32[]{:S(2)}) %copy-start) | copy-done | bytes 368664
  10.2 0.1 shard_map.120
  10.3 0.1 collective-permute-start.3
  10.4 0.7 %collective-permute-start.4 = (f32[84,4,128]{2,1,0:T(4,128)S(1)}, f32[84,4,128]{2,1,0:T(4,128)S(1)}, u32[]{:S(2)}, u32[]{:S(2)}) collective-permute-start(f32[84,4,128]{2,1,0:T(4,128)S(1)} %get-tuple-element.53), channel_id=1, source_target_pairs={{1,2},{2,1},{5,6},{6,5},{9,10},{10,9},{13,14},{14,13},{17,18},{18,... | collective-permute-start | bytes 516104 | tf_op jit(solution)/shard_map/ppermute | solution.py:525
  11.1 0.0 collective-permute-done.x_1_ref
  11.1 0.8 %collective-permute-done.1.x_0_ref = f32[21,8,128]{2,1,0:T(8,128)S(1)} collective-permute-done((f32[21,8,128]{2,1,0:T(8,128)}, f32[21,8,128]{2,1,0:T(8,128)S(1)}, u32[]{:S(2)}, u32[]{:S(2)}) %collective-permute-start.1) | collective-permute-done | bytes 86048 | tf_op jit(solution)/shard_map/ppermute | solution.py:525
  11.9 0.1 shard_map.121._edge_ref
  12.0 1.6 %collective-permute-start.2 = (f32[12,8,128]{2,1,0:T(8,128)S(1)}, f32[12,8,128]{2,1,0:T(8,128)S(1)}, u32[]{:S(2)}, u32[]{:S(2)}) collective-permute-start(f32[12,8,128]{2,1,0:T(8,128)S(1)} %shard_map.121._edge_ref), channel_id=1, source_target_pairs={{0,4},{4,0},{1,5},{5,1},{2,6},{6,2},{3,7},{7,3},{8,12},{12,8},{9,1... | collective-permute-start | bytes 147464 | tf_op jit(solution)/shard_map/ppermute | solution.py:525
  13.6 1.9 %collective-permute-start.5 = (f32[43,4,128]{2,1,0:T(4,128)S(1)}, f32[43,4,128]{2,1,0:T(4,128)S(1)}, u32[]{:S(2)}, u32[]{:S(2)}) collective-permute-start(f32[43,4,128]{2,1,0:T(4,128)S(1)} %get-tuple-element.54), channel_id=1, source_target_pairs={{0,1},{1,0},{2,3},{3,2},{4,5},{5,4},{6,7},{7,6},{8,9},{9,8},{10,11... | collective-permute-start | bytes 264200 | tf_op jit(solution)/shard_map/ppermute | solution.py:525
  15.5 0.7 %collective-permute-start.6 = (f32[43,4,128]{2,1,0:T(4,128)S(1)}, f32[43,4,128]{2,1,0:T(4,128)S(1)}, u32[]{:S(2)}, u32[]{:S(2)}) collective-permute-start(f32[43,4,128]{2,1,0:T(4,128)S(1)} %get-tuple-element.55), channel_id=1, source_target_pairs={{1,2},{2,1},{5,6},{6,5},{9,10},{10,9},{13,14},{14,13},{17,18},{18,... | collective-permute-start | bytes 264200 | tf_op jit(solution)/shard_map/ppermute | solution.py:525
  16.1 0.0 collective-permute-done.2.edge_ref
  16.2 2.2 %collective-permute-start.7 = (f32[15,4,128]{2,1,0:T(4,128)S(1)}, f32[15,4,128]{2,1,0:T(4,128)S(1)}, u32[]{:S(2)}, u32[]{:S(2)}) collective-permute-start(f32[15,4,128]{2,1,0:T(4,128)S(1)} %get-tuple-element.58), channel_id=1, source_target_pairs={{0,1},{1,0},{2,3},{3,2},{4,5},{5,4},{6,7},{7,6},{8,9},{9,8},{10,11... | collective-permute-start | bytes 92168 | tf_op jit(solution)/shard_map/ppermute | solution.py:525
  18.4 0.0 collective-permute-done.3.face_0_ref
  18.4 0.7 %collective-permute-start.8 = (f32[15,4,128]{2,1,0:T(4,128)S(1)}, f32[15,4,128]{2,1,0:T(4,128)S(1)}, u32[]{:S(2)}, u32[]{:S(2)}) collective-permute-start(f32[15,4,128]{2,1,0:T(4,128)S(1)} %get-tuple-element.59), channel_id=1, source_target_pairs={{1,2},{2,1},{5,6},{6,5},{9,10},{10,9},{13,14},{14,13},{17,18},{18,... | collective-permute-start | bytes 92168 | tf_op jit(solution)/shard_map/ppermute | solution.py:525
  19.0 0.2 shard_map.123
  19.3 0.1 shard_map.124
  19.4 5.8 %shard_map.126 = (f32[16,8,128]{2,1,0:T(8,128)}, f32[16,8,128]{2,1,0:T(8,128)}, f32[16,8,128]{2,1,0:T(8,128)}, f32[16,8,128]{2,1,0:T(8,128)S(1)}, f32[16,8,128]{...) custom-call(f32[3,25,8,256]{3,2,1,0:T(8,128)S(1)} %get-tuple-element, ...), custom_call_target="tpu_custom_call", output_to_operand_aliasing={{6}: (5, {}), {7}: (6, {})} | custom-call | tf_op jit(solution)/shard_map/pallas_call | solution.py:637
  25.3 4.2 %collective-permute-start.9 = (f32[8,128]{1,0:T(8,128)S(1)}, f32[8,128]{1,0:T(8,128)S(1)}, u32[]{:S(2)}, u32[]{:S(2)}) collective-permute-start(f32[8,128]{1,0:T(8,128)S(1)} %get-tuple-element.65), channel_id=1, source_target_pairs={{0,1},{1,0},{2,3},{3,2},{4,5},{5,4},{6,7},{7,6},{8,9},{9,8},{10,11... | collective-permute-start | bytes 12296 | tf_op jit(solution)/shard_map/ppermute | solution.py:531
  29.4 0.8 %collective-permute-done.9 = f32[8,128]{1,0:T(8,128)S(1)} collective-permute-done((f32[8,128]{1,0:T(8,128)S(1)}, f32[8,128]{1,0:T(8,128)S(1)}, u32[]{:S(2)}, u32[]{:S(2)}) %collective-permute-start.9) | collective-permute-done | bytes 4128 | tf_op jit(solution)/shard_map/ppermute | solution.py:531
  30.3 10.9 %all_to_all.8 = f32[16,1,128]{2,1,0:T(1,128)S(1)} all-to-all(f32[16,1,128]{2,1,0:T(1,128)S(1)} %broadcast_in_dim.2), channel_id=1, replica_groups={{0,2,4,6,8,10,12,14,16,18,20,22,24,26,28,30},{1,3,5,7,9,11,13,15,17,19,..., dimensions={0} | all-to-all | bytes 16384 | tf_op jit(solution)/shard_map/all_to_all | solution.py:534
  41.2 0.8 %shard_map.127 = f32[16,8,128]{2,1,0:T(8,128)} custom-call(f32[16,8,128]{2,1,0:T(8,128)S(1)} %get-tuple-element.64.refs_0_, f32[16,128]{1,0:T(8,128)S(1)} %bitcast.1), custom_call_target="tpu_custom_call" | custom-call | tf_op jit(solution)/shard_map/pallas_call | solution.py:652
  (10 shorter events, 0.1 us)
Async XLA Ops:
  2.6 8.4 %collective-permute-start = (f32[21,8,128]{2,1,0:T(8,128)}, f32[21,8,128]{2,1,0:T(8,128)S(1)}, u32[]{:S(2)}, u32[]{:S(2)}) collective-permute-start(f32[21,8,128]{2,1,0:T(8,128)} %get-tuple-element.36), channel_id=1, source_target_pairs={{8,16},{16,8},{9,17},{17,9},{10,18},{18,10},{11,19},{19,11},{12,20... | collective-permute-start | bytes 258056 | tf_op jit(solution)/shard_map/ppermute | solution.py:525
  3.3 8.6 %collective-permute-start.1 = (f32[21,8,128]{2,1,0:T(8,128)}, f32[21,8,128]{2,1,0:T(8,128)S(1)}, u32[]{:S(2)}, u32[]{:S(2)}) collective-permute-start(f32[21,8,128]{2,1,0:T(8,128)} %get-tuple-element.37), channel_id=1, source_target_pairs={{0,8},{8,0},{16,24},{24,16},{1,9},{9,1},{17,25},{25,17},{2,10},{10... | collective-permute-start | bytes 258056 | tf_op jit(solution)/shard_map/ppermute | solution.py:525
  9.2 1.0 %copy-start = (f32[90,8,128]{2,1,0:T(8,128)S(1)}, f32[90,8,128]{2,1,0:T(8,128)}, u32[]{:S(2)}) copy-start(f32[90,8,128]{2,1,0:T(8,128)} %get-tuple-element.38.stack_ref) | copy-start | bytes 1105924
  10.3 8.1 %collective-permute-start.3 = (f32[84,4,128]{2,1,0:T(4,128)S(1)}, f32[84,4,128]{2,1,0:T(4,128)S(1)}, u32[]{:S(2)}, u32[]{:S(2)}) collective-permute-start(f32[84,4,128]{2,1,0:T(4,128)S(1)} %get-tuple-element.52), channel_id=1, source_target_pairs={{0,1},{1,0},{2,3},{3,2},{4,5},{5,4},{6,7},{7,6},{8,9},{9,8},{10,11... | collective-permute-start | bytes 516104 | tf_op jit(solution)/shard_map/ppermute | solution.py:525
  10.4 8.9 %collective-permute-start.4 = (f32[84,4,128]{2,1,0:T(4,128)S(1)}, f32[84,4,128]{2,1,0:T(4,128)S(1)}, u32[]{:S(2)}, u32[]{:S(2)}) collective-permute-start(f32[84,4,128]{2,1,0:T(4,128)S(1)} %get-tuple-element.53), channel_id=1, source_target_pairs={{1,2},{2,1},{5,6},{6,5},{9,10},{10,9},{13,14},{14,13},{17,18},{18,... | collective-permute-start | bytes 516104 | tf_op jit(solution)/shard_map/ppermute | solution.py:525
  12.0 4.2 %collective-permute-start.2 = (f32[12,8,128]{2,1,0:T(8,128)S(1)}, f32[12,8,128]{2,1,0:T(8,128)S(1)}, u32[]{:S(2)}, u32[]{:S(2)}) collective-permute-start(f32[12,8,128]{2,1,0:T(8,128)S(1)} %shard_map.121._edge_ref), channel_id=1, source_target_pairs={{0,4},{4,0},{1,5},{5,1},{2,6},{6,2},{3,7},{7,3},{8,12},{12,8},{9,1... | collective-permute-start | bytes 147464 | tf_op jit(solution)/shard_map/ppermute | solution.py:525
  13.6 5.7 %collective-permute-start.5 = (f32[43,4,128]{2,1,0:T(4,128)S(1)}, f32[43,4,128]{2,1,0:T(4,128)S(1)}, u32[]{:S(2)}, u32[]{:S(2)}) collective-permute-start(f32[43,4,128]{2,1,0:T(4,128)S(1)} %get-tuple-element.54), channel_id=1, source_target_pairs={{0,1},{1,0},{2,3},{3,2},{4,5},{5,4},{6,7},{7,6},{8,9},{9,8},{10,11... | collective-permute-start | bytes 264200 | tf_op jit(solution)/shard_map/ppermute | solution.py:525
  15.5 3.8 %collective-permute-start.6 = (f32[43,4,128]{2,1,0:T(4,128)S(1)}, f32[43,4,128]{2,1,0:T(4,128)S(1)}, u32[]{:S(2)}, u32[]{:S(2)}) collective-permute-start(f32[43,4,128]{2,1,0:T(4,128)S(1)} %get-tuple-element.55), channel_id=1, source_target_pairs={{1,2},{2,1},{5,6},{6,5},{9,10},{10,9},{13,14},{14,13},{17,18},{18,... | collective-permute-start | bytes 264200 | tf_op jit(solution)/shard_map/ppermute | solution.py:525
  16.2 3.2 %collective-permute-start.7 = (f32[15,4,128]{2,1,0:T(4,128)S(1)}, f32[15,4,128]{2,1,0:T(4,128)S(1)}, u32[]{:S(2)}, u32[]{:S(2)}) collective-permute-start(f32[15,4,128]{2,1,0:T(4,128)S(1)} %get-tuple-element.58), channel_id=1, source_target_pairs={{0,1},{1,0},{2,3},{3,2},{4,5},{5,4},{6,7},{7,6},{8,9},{9,8},{10,11... | collective-permute-start | bytes 92168 | tf_op jit(solution)/shard_map/ppermute | solution.py:525
  18.4 1.0 %collective-permute-start.8 = (f32[15,4,128]{2,1,0:T(4,128)S(1)}, f32[15,4,128]{2,1,0:T(4,128)S(1)}, u32[]{:S(2)}, u32[]{:S(2)}) collective-permute-start(f32[15,4,128]{2,1,0:T(4,128)S(1)} %get-tuple-element.59), channel_id=1, source_target_pairs={{1,2},{2,1},{5,6},{6,5},{9,10},{10,9},{13,14},{14,13},{17,18},{18,... | collective-permute-start | bytes 92168 | tf_op jit(solution)/shard_map/ppermute | solution.py:525
  25.3 5.0 %collective-permute-start.9 = (f32[8,128]{1,0:T(8,128)S(1)}, f32[8,128]{1,0:T(8,128)S(1)}, u32[]{:S(2)}, u32[]{:S(2)}) collective-permute-start(f32[8,128]{1,0:T(8,128)S(1)} %get-tuple-element.65), channel_id=1, source_target_pairs={{0,1},{1,0},{2,3},{3,2},{4,5},{5,4},{6,7},{7,6},{8,9},{9,8},{10,11... | collective-permute-start | bytes 12296 | tf_op jit(solution)/shard_map/ppermute | solution.py:531
